TPU v7x, 256 devices: a whole 4x4x8 slice. The times are simulated.
256 devices in a mesh: row: 4 (over x), col: 2 (over core), depth: 32 (over z, y).
Axes of the slice: x: 4, y: 4, z: 8, core: 2. Of those that a mesh axis runs over, the one named last changes fastest.
Arguments:
- residual_in: float32 [32768, 6400], P(('col', 'depth'), 'row'), may hold values from -6 to 6
- integrals: bfloat16 [6400, 6400], P('row', ('col', 'depth')), may hold values from -0.078125 to 0.078125
- amplitudes: bfloat16 [6400, 32768], P('row', ('col', 'depth')), may hold values from -16 to 16
Outputs:
- residual_out: float32 [32768, 6400], P(('col', 'depth'), 'row')
All inputs are finite; a program needn't handle non-finite values.
Results may differ from a plain program's by a relative error of at most 0.0003.
Values may be sent and summed in bfloat16 or wider, within the bound.
No kernel may reach another device: no remote copies, remote signals or barrier semaphores. Data moves between devices by JAX's collectives and lax.ppermute only.
A program may use at most 128 MiB of HBM per device.

v0:
```python
import jax
import jax.numpy as jnp
from jax import lax
from jax.sharding import PartitionSpec as P


def contract(panel_rows, block):
    return lax.dot_general(
        panel_rows, block, (((0,), (1,)), ((), ())), preferred_element_type=jnp.float32
    )


def folder(source, piece):
    return contract(source, piece)


def per_device(residual_in, integrals, amplitudes):
    panel = lax.all_gather(amplitudes, "row", axis=0, tiled=True)
    share = folder(panel, lax.all_gather(integrals, ("col", "depth"), axis=1, tiled=True))
    return residual_in + share


def solution(mesh):
    placed = (P(("col", "depth"), "row"), P("row", ("col", "depth")), P("row", ("col", "depth")))
    return jax.shard_map(
        per_device,
        mesh=mesh,
        in_specs=placed,
        out_specs=P(("col", "depth"), "row"),
        check_vma=False,
    )
```

profile of v0, /device:TPU:1, one launch (start us, length us, event | category | flops | bytes accessed | tf_op | source)
XLA Modules:
  0.0 222.2 jit_solution(2079709472897072271)
XLA Ops:
  6.5 0.0 all-gather.6.cloned.1.call-start
  6.5 0.7 all-gather.6.cloned.1.call-update
  7.3 0.0 all-gather.4.cloned.1.call-start
  7.3 0.7 all-gather.4.cloned.1.call-update
  8.0 0.0 copy-start
  8.0 120.0 %all-gather.6.cloned.1.call-done = bf16[64,100,1600]{2,1,0:T(8,128)(2,1)} async-done(((bf16[1,100,1600]{2,1,0:T(8,128)(2,1)}), bf16[64,100,1600]{2,1,0:T(8,128)(2,1)}) %all-gather.6.cloned.1.call-update) | async-done | bytes 20480016 | tf_op jit(solution)/shard_map/all_gather | solution.py:19
  128.0 28.3 %reshape.1 = bf16[6400,1600]{1,0:T(8,128)(2,1)} reshape(bf16[64,100,1600]{2,1,0:T(8,128)(2,1)} %all-gather.6.cloned.1.call-done) | data formatting | bytes 40960000
  156.3 40.5 %all-gather.4.cloned.1.call-done = bf16[6400,512]{1,0:T(8,128)(2,1)} async-done(((bf16[1600,512]{1,0:T(8,128)(2,1)}), bf16[6400,512]{1,0:T(8,128)(2,1)}) %all-gather.4.cloned.1.call-update) | async-done | bytes 6553616 | tf_op jit(solution)/shard_map/all_gather | solution.py:18
  196.8 0.0 copy-done
  196.8 18.6 %convolution_add_fusion = f32[512,1600]{0,1:T(8,128)} fusion(f32[512,1600]{0,1:T(8,128)S(1)} %copy-done, bf16[6400,512]{1,0:T(8,128)(2,1)} %all-gather.4.cloned.1.call-done, bf16[6400,1600]{1,0:T(8,128)(2,1)} %reshape.1), kind=kOutput, calls=%fused_computation | convolution fusion | flops 10486579200 | bytes 33587200 | tf_op jit(solution)/shard_map/dot_general | solution.py:8
Async XLA Ops:
  6.5 121.5 %all-gather.6.cloned.1.call-start = ((), (), s32[]{:S(2)}) async-start(), calls=%async_computation.1 | async-start | bytes 22497280 | tf_op jit(solution)/shard_map/all_gather | solution.py:19
  7.3 189.5 %all-gather.4.cloned.1.call-start = ((), (), s32[]{:S(2)}) async-start(), calls=%async_computation | async-start | bytes 8192000 | tf_op jit(solution)/shard_map/all_gather | solution.py:18
  8.0 188.8 %copy-start = (f32[512,1600]{0,1:T(8,128)S(1)}, f32[512,1600]{0,1:T(8,128)}, u32[]{:S(2)}) copy-start(f32[512,1600]{0,1:T(8,128)} %param.3) | copy-start | bytes 9830404
Sparse Core Ops, SparseCore 0:
  10.0 117.9 all-gather.5
  129.8 66.8 all-gather.3
where the time goes:
time: 223 us; the launch traced here: 222 us
  waiting for transfers between devices  162 us (73%)
  local copies, waits for them, and re-layouts  28.3 us (13%)
  matrix products  18.6 us (8%)
  between operations  13.4 us (6%)
    all_gather x1, waiting for transfers between devices, per_device(): lax.all_gather(integrals, ('col', 'depth'), axis=1, tiled=True)  120 us
    all_gather x1, waiting for transfers between devices, per_device(): panel = lax.all_gather(amplitudes, 'row', axis=0, tiled=True)  40.5 us
    unnamed x3, local copies, waits for them, and re-layouts  28.3 us
    dot_general x1, matrix products, contract(): lax.dot_general(panel_rows, block, (((0,), (1,)), ((), ())), preferred_el...  18.6 us
  transfers between devices with their start and end apart: 2, of which 2 were waited for; matrix products, arithmetic and copies ran while one was open for 13% of the time, Pallas kernels for 0%

commit v1 on v0

v1 whole, which is shorter than its diff:
```python
import jax
import jax.numpy as jnp
from jax import lax
from jax.sharding import PartitionSpec as P


def shift(array, axis, size, step):
    return lax.ppermute(array, axis, [(i, (i + step) % size) for i in range(size)])


def padded(blocks, rows):
    extra = -rows % 8
    parts = blocks.reshape(-1, rows, blocks.shape[-1])
    return jnp.pad(parts, ((0, 0), (0, extra), (0, 0))).reshape(-1, blocks.shape[-1])


def row_panel(block, size):
    after, before = shift(block, "row", size, -1), shift(block, "row", size, 1)
    half = block.shape[0] // 2
    far = [shift(before[:half], "row", size, 1), shift(after[half:], "row", size, -1)]
    ring = jnp.concatenate([block, after, *far, before])
    start = (size - lax.axis_index("row")) % size * block.shape[0]
    return lax.dynamic_slice_in_dim(jnp.concatenate([ring, ring]), start, ring.shape[0])


def solution(mesh):
    size = mesh.shape["row"]

    def per_device(residual_in, integrals, amplitudes):
        rows = integrals.shape[1]
        columns = padded(integrals.T, rows)
        gathered = lax.all_gather(columns, ("col", "depth"), axis=0, tiled=True)
        panel = row_panel(padded(amplitudes, rows), size)
        share = lax.dot_general(
            panel, gathered, (((0,), (0,)), ((), ())), preferred_element_type=jnp.float32
        )
        return residual_in + share

    placed = (P(("col", "depth"), "row"), P("row", ("col", "depth")), P("row", ("col", "depth")))
    return jax.shard_map(
        per_device, mesh=mesh, in_specs=placed, out_specs=P(("col", "depth"), "row"), check_vma=False
    )
```

time: 223 us -> 155 us (0.70)
  waiting for transfers between devices: 162 us -> 89.1 us
  starting transfers between devices: 0.04 us -> 6.92 us
  local copies, waits for them, and re-layouts: 28.3 us -> 25.4 us
    all_gather x2 -> x1, waiting for transfers between devices: 160 us -> 43.6 us  [per_device(): gathered = lax.all_gather(columns, ('col', 'depth'), axis=0, tiled=True)]
    ppermute x0 -> x4, waiting for transfers between devices: none -> 45.5 us  [shift(): lax.ppermute(array, axis, [(i, (i + step) % size) for i in range(size)])]
    unnamed x3 -> x13, local copies, waits for them, and re-layouts: 28.3 us -> 18 us
    ppermute x0 -> x4, starting transfers between devices: none -> 6.92 us  [shift(): lax.ppermute(array, axis, [(i, (i + step) % size) for i in range(size)])]
    reshape x0 -> x1, local copies, waits for them, and re-layouts: none -> 2.32 us  [padded(): parts = blocks.reshape(-1, rows, blocks.shape[-1])]
  transfers between devices with their start and end apart: 2 -> 5, of which waited for: 2 -> 4; matrix products, arithmetic and copies ran while one was open for 13% -> 15% of each run, Pallas kernels for 0% -> 0%
where the time goes in v1:
time: 155 us
  waiting for transfers between devices  89.1 us (57%)
  local copies, waits for them, and re-layouts  25.4 us (16%)
  matrix products  19.7 us (13%)
  between operations  13.4 us (9%)
  starting transfers between devices  6.92 us (4%)
    ppermute x4, waiting for transfers between devices, shift(): lax.ppermute(array, axis, [(i, (i + step) % size) for i in range(size)])  45.5 us
    all_gather x1, waiting for transfers between devices, per_device(): gathered = lax.all_gather(columns, ('col', 'depth'), axis=0, tiled=True)  43.6 us
    dot_general x1, matrix products, per_device(): lax.dot_general(panel, gathered, (((0,), (0,)), ((), ())), preferred_elem...  19.7 us
    unnamed x13, local copies, waits for them, and re-layouts  18 us
    ppermute x4, starting transfers between devices, shift(): lax.ppermute(array, axis, [(i, (i + step) % size) for i in range(size)])  6.92 us
  transfers between devices with their start and end apart: 5, of which 4 were waited for; matrix products, arithmetic and copies ran while one was open for 15% of the time, Pallas kernels for 0%

profile of v1, /device:TPU:1, one launch (start us, length us, event | category | flops | bytes accessed | tf_op | source)
XLA Modules:
  0.0 154.6 jit_solution(17022055003137609008)
XLA Ops:
  6.5 0.0 all-gather.3.cloned.1.call-start
  6.5 1.7 %pad.9 = bf16[1,104,1600]{2,1,0:T(8,128)(2,1)} pad(bf16[1,100,1600]{2,1,0:T(8,128)(2,1)} %bitcast.13, bf16[]{:T(256)} %constant.18.clone.1), padding=0_0x0_4x0_0 | pad | bytes 652802 | tf_op jit(solution)/shard_map/jit(_pad)/pad | solution.py:14
  8.3 0.0 all-gather.3.cloned.1.call-update
  8.3 2.3 %reshape.12 = bf16[16,100,512]{2,1,0:T(8,128)(2,1)S(1)} reshape(bf16[1600,512]{1,0:T(8,128)(2,1)} %param.5) | data formatting | bytes 3276800 | tf_op jit(solution)/shard_map/reshape | solution.py:13
  10.6 0.1 pad.8
  10.8 2.1 %collective-permute-start.1 = (bf16[1664,512]{1,0:T(8,128)(2,1)S(1)}, bf16[1664,512]{1,0:T(8,128)(2,1)S(1)}, u32[]{:S(2)}, u32[]{:S(2)}) collective-permute-start(bf16[1664,512]{1,0:T(8,128)(2,1)S(1)} %bitcast.9), channel_id=1, source_target_pairs={{0,64},{64,128},{128,192},{192,0},{1,65},{65,129},{129,193},{193,1... | collective-permute-start | bytes 5111816 | tf_op jit(solution)/shard_map/ppermute | solution.py:8
  12.9 1.4 collective-permute-start
  14.2 34.6 %collective-permute-done.1 = bf16[1664,512]{1,0:T(8,128)(2,1)S(1)} collective-permute-done((bf16[1664,512]{1,0:T(8,128)(2,1)S(1)}, bf16[1664,512]{1,0:T(8,128)(2,1)S(1)}, u32[]{:S(2)}, u32[]{:S(2)}) %collective-permute-start.1) | collective-permute-done | bytes 1703968 | tf_op jit(solution)/shard_map/ppermute | solution.py:8
  48.9 1.0 slice.8
  49.9 1.9 %collective-permute-start.2 = (bf16[832,512]{1,0:T(8,128)(2,1)}, bf16[832,512]{1,0:T(8,128)(2,1)}, u32[]{:S(2)}, u32[]{:S(2)}) collective-permute-start(bf16[832,512]{1,0:T(8,128)(2,1)} %slice.8), channel_id=1, source_target_pairs={{0,64},{64,128},{128,192},{192,0},{1,65},{65,129},{129,193},{193,1... | collective-permute-start | bytes 2555912 | tf_op jit(solution)/shard_map/ppermute | solution.py:8
  51.7 0.0 collective-permute-done
  51.7 0.0 copy-start
  51.7 1.2 copy-done
  52.9 1.0 slice.9
  53.9 1.6 %collective-permute-start.3 = (bf16[832,512]{1,0:T(8,128)(2,1)}, bf16[832,512]{1,0:T(8,128)(2,1)}, u32[]{:S(2)}, u32[]{:S(2)}) collective-permute-start(bf16[832,512]{1,0:T(8,128)(2,1)} %slice.9), channel_id=1, source_target_pairs={{0,192},{64,0},{128,64},{192,128},{1,193},{65,1},{129,65},{193,129... | collective-permute-start | bytes 2555912 | tf_op jit(solution)/shard_map/ppermute | solution.py:8
  55.5 0.0 copy-start.1
  55.5 1.3 constant_dynamic-update-slice_fusion.9
  56.8 2.8 %constant_dynamic-update-slice_fusion.8 = bf16[13312,512]{1,0:T(8,128)(2,1)} fusion(bf16[13312,512]{1,0:T(8,128)(2,1)} %constant_dynamic-update-slice_fusion.9, bf16[1664,512]{1,0:T(8,128)(2,1)} %copy-done), kind=kLoop, calls=%fused_computation.12 | loop fusion | bytes 3407872
  59.6 10.3 %collective-permute-done.2 = bf16[832,512]{1,0:T(8,128)(2,1)} collective-permute-done((bf16[832,512]{1,0:T(8,128)(2,1)}, bf16[832,512]{1,0:T(8,128)(2,1)}, u32[]{:S(2)}, u32[]{:S(2)}) %collective-permute-start.2) | collective-permute-done | bytes 852000 | tf_op jit(solution)/shard_map/ppermute | solution.py:8
  69.9 2.2 %constant_dynamic-update-slice_fusion.7 = bf16[13312,512]{1,0:T(8,128)(2,1)} fusion(bf16[13312,512]{1,0:T(8,128)(2,1)} %constant_dynamic-update-slice_fusion.8, bf16[832,512]{1,0:T(8,128)(2,1)} %collective-permute-done.2), kind=kLoop, calls=%fused_computation.11 | loop fusion | bytes 1703936
  72.1 0.5 collective-permute-done.3
  72.7 2.1 %constant_dynamic-update-slice_fusion.6 = bf16[13312,512]{1,0:T(8,128)(2,1)} fusion(bf16[13312,512]{1,0:T(8,128)(2,1)} %constant_dynamic-update-slice_fusion.7, bf16[832,512]{1,0:T(8,128)(2,1)} %collective-permute-done.3), kind=kLoop, calls=%fused_computation.10 | loop fusion | bytes 1703936
  74.8 1.3 constant_dynamic-update-slice_fusion.5
  76.1 1.4 constant_dynamic-update-slice_fusion.4
  77.5 0.0 copy-done.1
  77.5 1.3 constant_dynamic-update-slice_fusion.3
  78.8 2.1 %constant_dynamic-update-slice_fusion.2 = bf16[13312,512]{1,0:T(8,128)(2,1)} fusion(bf16[13312,512]{1,0:T(8,128)(2,1)} %constant_dynamic-update-slice_fusion.3, bf16[832,512]{1,0:T(8,128)(2,1)} %collective-permute-done.2), kind=kLoop, calls=%fused_computation.6 | loop fusion | bytes 1703936
  80.9 2.2 %constant_dynamic-update-slice_fusion.1 = bf16[13312,512]{1,0:T(8,128)(2,1)} fusion(bf16[13312,512]{1,0:T(8,128)(2,1)} %constant_dynamic-update-slice_fusion.2, bf16[832,512]{1,0:T(8,128)(2,1)} %collective-permute-done.3), kind=kLoop, calls=%fused_computation.5 | loop fusion | bytes 1703936
  83.1 1.3 constant_dynamic-update-slice_fusion
  84.4 43.6 %all-gather.3.cloned.1.call-done = bf16[1,6656,1600]{2,1,0:T(8,128)(2,1)} async-done(((bf16[1,104,1600]{2,1,0:T(8,128)(2,1)}), bf16[1,6656,1600]{2,1,0:T(8,128)(2,1)}) %all-gather.3.cloned.1.call-update) | async-done | bytes 21299216 | tf_op jit(solution)/shard_map/all_gather | solution.py:32
  128.0 19.7 %fusion.3 = f32[512,1600]{0,1:T(8,128)} fusion(f32[512,1600]{0,1:T(8,128)} %param.3, bf16[1,6656,1600]{2,1,0:T(8,128)(2,1)} %all-gather.3.cloned.1.call-done, bf16[13312,512]{1,0:T(8,128)(2,1)} %constant_dynamic-update-slice_fusion, s32[]{:T(128)S(6)} %select_n.11), kind=kOutput, calls=%fused_computation.3 | convolution fusion | flops 10906009600 | bytes 35520516 | tf_op jit(solution)/shard_map/dot_general | solution.py:34
Async XLA Ops:
  6.5 121.5 %all-gather.3.cloned.1.call-start = ((), (), s32[]{:S(2)}) async-start(), calls=%async_computation | async-start | bytes 22497280 | tf_op jit(solution)/shard_map/all_gather | solution.py:32
  10.8 38.1 %collective-permute-start.1 = (bf16[1664,512]{1,0:T(8,128)(2,1)S(1)}, bf16[1664,512]{1,0:T(8,128)(2,1)S(1)}, u32[]{:S(2)}, u32[]{:S(2)}) collective-permute-start(bf16[1664,512]{1,0:T(8,128)(2,1)S(1)} %bitcast.9), channel_id=1, source_target_pairs={{0,64},{64,128},{128,192},{192,0},{1,65},{65,129},{129,193},{193,1... | collective-permute-start | bytes 5111816 | tf_op jit(solution)/shard_map/ppermute | solution.py:8
  12.9 38.9 %collective-permute-start = (bf16[1664,512]{1,0:T(8,128)(2,1)S(1)}, bf16[1664,512]{1,0:T(8,128)(2,1)S(1)}, u32[]{:S(2)}, u32[]{:S(2)}) collective-permute-start(bf16[1664,512]{1,0:T(8,128)(2,1)S(1)} %bitcast.10), channel_id=1, source_target_pairs={{0,192},{64,0},{128,64},{192,128},{1,193},{65,1},{129,65},{193,129... | collective-permute-start | bytes 5111816 | tf_op jit(solution)/shard_map/ppermute | solution.py:8
  49.9 20.1 %collective-permute-start.2 = (bf16[832,512]{1,0:T(8,128)(2,1)}, bf16[832,512]{1,0:T(8,128)(2,1)}, u32[]{:S(2)}, u32[]{:S(2)}) collective-permute-start(bf16[832,512]{1,0:T(8,128)(2,1)} %slice.8), channel_id=1, source_target_pairs={{0,64},{64,128},{128,192},{192,0},{1,65},{65,129},{129,193},{193,1... | collective-permute-start | bytes 2555912 | tf_op jit(solution)/shard_map/ppermute | solution.py:8
  51.7 1.2 copy-start
  53.9 18.8 %collective-permute-start.3 = (bf16[832,512]{1,0:T(8,128)(2,1)}, bf16[832,512]{1,0:T(8,128)(2,1)}, u32[]{:S(2)}, u32[]{:S(2)}) collective-permute-start(bf16[832,512]{1,0:T(8,128)(2,1)} %slice.9), channel_id=1, source_target_pairs={{0,192},{64,0},{128,64},{192,128},{1,193},{65,1},{129,65},{193,129... | collective-permute-start | bytes 2555912 | tf_op jit(solution)/shard_map/ppermute | solution.py:8
  55.5 22.0 %copy-start.1 = (bf16[1664,512]{1,0:T(8,128)(2,1)S(1)}, bf16[1664,512]{1,0:T(8,128)(2,1)}, u32[]{:S(2)}) copy-start(bf16[1664,512]{1,0:T(8,128)(2,1)} %copy-done) | copy-start | bytes 5111812
Sparse Core Ops, SparseCore 0:
  10.0 117.9 all-gather.2

commit v2 on v0

v2 whole, which is shorter than its diff:
```python
import jax
import jax.numpy as jnp
from jax import lax
from jax.experimental import pallas as pl
from jax.experimental.pallas import tpu as pltpu
from jax.sharding import PartitionSpec as P

Z, Y = 8, 4


def shift(array, size, step):
    return lax.ppermute(array, "row", [(i, (i + step) % size) for i in range(size)])


def travel(array, first, second):
    pairs = []
    for core, step in enumerate((first, second)):
        if step is not None:
            for z in range(Z):
                for y in range(Y):
                    target = (z + step[0]) % Z * Y + (y + step[1]) % Y
                    pairs.append(((core * Z + z) * Y + y, core * Z * Y + target))
    return lax.ppermute(array, ("col", "depth"), pairs)


def swap(array):
    return lax.ppermute(array, "col", [(0, 1), (1, 0)])


def padded(blocks, rows):
    parts = blocks.reshape(-1, rows, blocks.shape[-1])
    return jnp.pad(parts, ((0, 0), (0, -rows % 8), (0, 0)))


def pieces_of(block):
    along, back = ((0, 1), (1, 0)), ((0, -1), (-1, 0))
    a1 = travel(block, *along)
    b1 = travel(block, *back)
    a2 = travel(a1, *along)
    pack = jnp.concatenate([block, a1, b1, a2])
    b2 = travel(b1, None, back[1])
    a3 = travel(a2, None, along[1])
    b3 = travel(b2, None, back[1])
    a4 = travel(a3, None, along[1])
    rest = jnp.concatenate([b2, a3, b3, a4])
    up, down = ((1, 0), (0, 1)), ((-1, 0), (0, -1))
    u1, d1 = travel(pack, *up), travel(pack, *down)
    u2, d2 = travel(u1, *up), travel(d1, down[0], None)
    first = lax.axis_index("col") == 0
    kept = jnp.where(first, d2, rest)
    u3, d3 = travel(jnp.where(first, u2, rest), *up), travel(kept, *down)
    u4, d4 = travel(u3[:2], *up), travel(d3[2:], *down)
    return [pack, u1, d1, u2, kept, u3, d3, u4, d4]


def arrange(own, after, far_low, far_high, before, rows):
    count, height, width = own.shape

    def kernel(own_ref, after_ref, low_ref, high_ref, before_ref, out_ref, sems):
        x, core, depth = (lax.axis_index(name) for name in ("row", "col", "depth"))
        z, y = depth // Y, depth % Y
        copies = []
        sources = [(own_ref, 0, 0), (after_ref, 1, 0), (low_ref, 2, 0), (high_ref, 2, count // 2), (before_ref, 3, 0)]
        for ref, step, start in sources:
            block_row = lax.rem(x + step, rows)
            half = block_row // (rows // 2)
            for i in range(ref.shape[0]):
                there = lax.rem(block_row, rows // 2) * count + start + i
                dz = lax.rem(there // Y - z + Z, Z)
                dy = lax.rem((start + i) % Y - y + Y, Y)
                oz = jnp.where(dz < Z // 2, 2 * dz, 2 * (Z - dz) - 1)
                oy = jnp.where(dy < Y // 2, 2 * dy, 2 * (Y - dy) - 1)
                place = jnp.where(half == 0, oz * Y + oy, oz // Y * (Y * Y) + oy * Y + lax.rem(oz, Y))
                copy = pltpu.make_async_copy(
                    ref.at[i], out_ref.at[lax.rem(half + core, 2), place], sems.at[len(copies)]
                )
                copy.start()
                copies.append(copy)
        for copy in copies:
            copy.wait()

    return pl.pallas_call(
        kernel,
        out_shape=jax.ShapeDtypeStruct((2, Z * Y, height, width), own.dtype),
        in_specs=[pl.BlockSpec(memory_space=pl.ANY)] * 5,
        out_specs=pl.BlockSpec(memory_space=pl.ANY),
        scratch_shapes=[pltpu.SemaphoreType.DMA((rows * count,))],
        cost_estimate=pl.CostEstimate(flops=0, bytes_accessed=4 * rows * own.size, transcendentals=0),
        name="arrange",
    )(own, after, far_low, far_high, before)


def accumulate(total, factors, pieces, tile=256):
    columns, pairs = total.shape
    pieces = [piece.reshape(-1, columns) for piece in pieces]
    heights = [piece.shape[0] for piece in pieces]

    def kernel(total_ref, *refs):
        piece_refs, factor_refs, out_ref = refs[: len(pieces)], refs[len(pieces) : -1], refs[-1]
        result = total_ref[...]
        at = [0] * len(factors)
        for number, (ref, height) in enumerate(zip(piece_refs, heights)):
            which = number * len(factors) // len(pieces)
            factor = factor_refs[which][pl.ds(at[which], height), :]
            at[which] += height
            result += lax.dot_general(ref[...], factor, (((0,), (0,)), ((), ())), preferred_element_type=jnp.float32)
        out_ref[...] = result

    flops = 2 * columns * pairs * sum(heights)
    return pl.pallas_call(
        kernel,
        grid=(pl.cdiv(columns, tile),),
        out_shape=jax.ShapeDtypeStruct(total.shape, total.dtype),
        in_specs=[pl.BlockSpec((tile, pairs), lambda i: (i, 0))]
        + [pl.BlockSpec((height, tile), lambda i: (0, i)) for height in heights]
        + [pl.BlockSpec(factor.shape, lambda i: (0, 0)) for factor in factors],
        out_specs=pl.BlockSpec((tile, pairs), lambda i: (i, 0)),
        compiler_params=pltpu.CompilerParams(vmem_limit_bytes=48 << 20),
        cost_estimate=pl.CostEstimate(
            flops=flops, bytes_accessed=8 * total.size + 2 * sum(heights) * (columns + pairs), transcendentals=0
        ),
        name="accumulate",
    )(total, *pieces, *factors)


def solution(mesh):
    rows = mesh.shape["row"]

    def per_device(residual_in, integrals, amplitudes):
        depth = integrals.shape[1]
        own = padded(amplitudes, depth)
        after, before = shift(own, rows, -1), shift(own, rows, 1)
        half = own.shape[0] // 2
        far_low, far_high = shift(before[:half], rows, 1), shift(after[half:], rows, -1)
        mine = pieces_of(padded(integrals.T, depth))
        other = [swap(piece) for piece in mine]
        panel = arrange(own, after, far_low, far_high, before, rows)
        panel = panel.reshape(2, -1, panel.shape[-1])
        early = 5
        split = sum(piece.shape[0] for piece in mine[:early]) * own.shape[1]
        total = accumulate(residual_in.T, [panel[0, :split], panel[1, :split]], mine[:early] + other[:early])
        total = accumulate(total, [panel[0, split:], panel[1, split:]], mine[early:] + other[early:])
        return total.T

    placed = (P(("col", "depth"), "row"), P("row", ("col", "depth")), P("row", ("col", "depth")))
    return jax.shard_map(
        per_device, mesh=mesh, in_specs=placed, out_specs=P(("col", "depth"), "row"), check_vma=False
    )
```

time: 223 us -> 373 us (1.67)
  Pallas kernels: 0 us -> 234 us
  waiting for transfers between devices: 162 us -> 65.7 us
  starting transfers between devices: 0.04 us -> 48.2 us
  matrix products: 18.6 us -> 0 us
  between operations: 13.4 us -> 0.26 us
  local copies, waits for them, and re-layouts: 28.3 us -> 21 us
    pallas_call x0 -> x3, Pallas kernels: none -> 234 us  [the longest x1 208 us: arrange(): pl.pallas_call(kernel, out_shape=jax.ShapeDtypeStruct((2, Z * Y, height,...]
    all_gather x2 -> x0, waiting for transfers between devices: 160 us -> none  [the longest x1 120 us: per_device(): lax.all_gather(integrals, ('col', 'depth'), axis=1, tiled=True)]
    ppermute x0 -> x28, waiting for transfers between devices: none -> 65.7 us  [the longest x15 41.9 us: travel(): return lax.ppermute(array, ('col', 'depth'), pairs)]
    ppermute x0 -> x28, starting transfers between devices: none -> 48.2 us  [the longest x15 28.3 us: travel(): return lax.ppermute(array, ('col', 'depth'), pairs)]
    unnamed x3 -> x15, local copies, waits for them, and re-layouts: 28.3 us -> 3.68 us
    dot_general x1 -> x0, matrix products: 18.6 us -> none  [contract(): lax.dot_general(panel_rows, block, (((0,), (1,)), ((), ())), preferred_el...]
    squeeze x0 -> x2, local copies, waits for them, and re-layouts: none -> 6.48 us  [the longest x1 4.62 us: per_device(): panel[1, :split]]
    pad x0 -> x2, local copies, waits for them, and re-layouts: none -> 3.88 us  [padded(): return jnp.pad(parts, ((0, 0), (0, -rows % 8), (0, 0)))]
  transfers between devices with their start and end apart: 2 -> 28, of which waited for: 2 -> 8; matrix products, arithmetic and copies ran while one was open for 13% -> 5% of each run, Pallas kernels for 0% -> 60%
where the time goes in v2:
time: 373 us; the launch traced here: 372 us
  Pallas kernels  234 us (63%)
  waiting for transfers between devices  65.7 us (18%)
  starting transfers between devices  48.2 us (13%)
  local copies, waits for them, and re-layouts  21 us (6%)
    pallas_call x1, Pallas kernels, arrange(): pl.pallas_call(kernel, out_shape=jax.ShapeDtypeStruct((2, Z * Y, height,...  208 us
    ppermute x15, waiting for transfers between devices, travel(): return lax.ppermute(array, ('col', 'depth'), pairs)  41.9 us
    ppermute x15, starting transfers between devices, travel(): return lax.ppermute(array, ('col', 'depth'), pairs)  28.3 us
    pallas_call x2, Pallas kernels, accumulate(): pl.pallas_call(kernel, grid=(pl.cdiv(columns, tile),), out_shape=jax.Shap...  26 us
    ppermute x4, waiting for transfers between devices, shift(): lax.ppermute(array, 'row', [(i, (i + step) % size) for i in range(size)])  23.7 us
    ppermute x9, starting transfers between devices, swap(): return lax.ppermute(array, 'col', [(0, 1), (1, 0)])  14.3 us
  transfers between devices with their start and end apart: 28, of which 8 were waited for; matrix products, arithmetic and copies ran while one was open for 5% of the time, Pallas kernels for 60%

profile of v2, /device:TPU:1, one launch (start us, length us, event | category | flops | bytes accessed | tf_op | source)
XLA Modules:
  0.0 372.4 jit_solution(4522462150101686828)
XLA Ops:
  0.0 1.0 pad.8
  1.0 2.5 collective-permute-start
  3.6 4.0 %collective-permute-start.1 = (bf16[1,104,1600]{2,1,0:T(8,128)(2,1)S(1)}, bf16[1,104,1600]{2,1,0:T(8,128)(2,1)S(1)}, u32[]{:S(2)}, u32[]{:S(2)}) collective-permute-start(bf16[1,104,1600]{2,1,0:T(8,128)(2,1)S(1)} %pad.8), channel_id=1, source_target_pairs={{0,3},{1,0},{2,1},{3,2},{4,7},{5,4},{6,5},{7,6},{8,11},{9,8},{10,9... | collective-permute-start | bytes 998408 | tf_op jit(solution)/shard_map/ppermute | solution.py:23
  7.6 4.8 %collective-permute-done = bf16[1,104,1600]{2,1,0:T(8,128)(2,1)S(1)} collective-permute-done((bf16[1,104,1600]{2,1,0:T(8,128)(2,1)S(1)}, bf16[1,104,1600]{2,1,0:T(8,128)(2,1)S(1)}, u32[]{:S(2)}, u32[]{:S(2)}) %collective-permute-start) | collective-permute-done | bytes 332832 | tf_op jit(solution)/shard_map/ppermute | solution.py:23
  12.4 0.0 collective-permute-start.2
  12.4 0.0 collective-permute-done.1
  12.4 7.7 %collective-permute-done.2 = bf16[1,104,1600]{2,1,0:T(8,128)(2,1)} collective-permute-done((bf16[1,104,1600]{2,1,0:T(8,128)(2,1)S(1)}, bf16[1,104,1600]{2,1,0:T(8,128)(2,1)}, u32[]{:S(2)}, u32[]{:S(2)}) %collective-permute-start.2) | collective-permute-done | bytes 332832 | tf_op jit(solution)/shard_map/ppermute | solution.py:23
  20.2 1.2 pad_maximum_fusion
  21.4 0.8 collective-permute-start.3
  22.2 1.9 collective-permute-start.4
  24.1 2.3 collective-permute-start.7
  26.4 13.8 %collective-permute-done.3 = bf16[4,104,1600]{2,1,0:T(8,128)(2,1)} collective-permute-done((bf16[4,104,1600]{2,1,0:T(8,128)(2,1)S(1)}, bf16[4,104,1600]{2,1,0:T(8,128)(2,1)}, u32[]{:S(2)}, u32[]{:S(2)}) %collective-permute-start.3) | collective-permute-done | bytes 1331232 | tf_op jit(solution)/shard_map/ppermute | solution.py:23
  40.3 0.0 collective-permute-start.5
  40.3 0.0 collective-permute-done.4
  40.3 1.7 collective-permute-start.6
  42.0 1.9 collective-permute-start.8
  43.9 0.0 collective-permute-done.7
  44.0 4.6 %collective-permute-start.9 = (bf16[1,104,1600]{2,1,0:T(8,128)(2,1)S(1)}, bf16[1,104,1600]{2,1,0:T(8,128)(2,1)}, u32[]{:S(2)}, u32[]{:S(2)}) collective-permute-start(bf16[1,104,1600]{2,1,0:T(8,128)(2,1)S(1)} %collective-permute-done.7), channel_id=1, source_target_pairs={{32,60},{33,61},{34,62},{35,63},{36,32},{37,33},{38,34},{39,35},{4... | collective-permute-start | bytes 998408 | tf_op jit(solution)/shard_map/ppermute | solution.py:23
  48.5 3.4 reshape.74
  51.9 2.9 pad.9.own_ref
  54.8 0.7 collective-permute-start.17
  55.5 0.0 collective-permute-done.8
  55.6 2.0 collective-permute-start.16
  57.6 0.0 collective-permute-done.9
  57.6 1.9 collective-permute-start.10
  59.5 1.0 constant_dynamic-update-slice_fusion.1
  60.5 9.7 %collective-permute-done.10 = bf16[1,104,1600]{2,1,0:T(8,128)(2,1)S(1)} collective-permute-done((bf16[1,104,1600]{2,1,0:T(8,128)(2,1)S(1)}, bf16[1,104,1600]{2,1,0:T(8,128)(2,1)S(1)}, u32[]{:S(2)}, u32[]{:S(2)}) %collective-permute-start.10) | collective-permute-done | bytes 332832 | tf_op jit(solution)/shard_map/ppermute | solution.py:23
  70.3 0.0 collective-permute-done.6
  70.3 1.9 broadcast_select_fusion
  72.2 0.3 collective-permute-start.21
  72.5 17.4 %collective-permute-done.17.before_ref = bf16[16,104,512]{2,1,0:T(8,128)(2,1)} collective-permute-done((bf16[16,104,512]{2,1,0:T(8,128)(2,1)}, bf16[16,104,512]{2,1,0:T(8,128)(2,1)}, u32[]{:S(2)}, u32[]{:S(2)}) %collective-permute-start.17) | collective-permute-done | bytes 1703968 | tf_op jit(solution)/shard_map/ppermute | solution.py:12
  89.9 1.2 slice.32
  91.1 0.1 collective-permute-start.18
  91.2 0.0 collective-permute-done.16.after_ref
  91.2 0.0 copy-start
  91.2 0.1 slice.33
  91.3 2.7 collective-permute-start.19
  94.0 2.1 collective-permute-start.20
  96.1 4.8 %collective-permute-start.11 = (bf16[4,104,1600]{2,1,0:T(8,128)(2,1)S(1)}, bf16[4,104,1600]{2,1,0:T(8,128)(2,1)}, u32[]{:S(2)}, u32[]{:S(2)}) collective-permute-start(bf16[4,104,1600]{2,1,0:T(8,128)(2,1)S(1)} %pad_maximum_fusion), channel_id=1, source_target_pairs={{0,32},{32,0},{1,33},{33,1},{2,34},{34,2},{3,35},{35,3},{4,36},{36... | collective-permute-start | bytes 3993608 | tf_op jit(solution)/shard_map/ppermute | solution.py:27
  100.9 6.4 %collective-permute-done.18.low_ref = bf16[8,104,512]{2,1,0:T(8,128)(2,1)S(1)} collective-permute-done((bf16[8,104,512]{2,1,0:T(8,128)(2,1)S(1)}, bf16[8,104,512]{2,1,0:T(8,128)(2,1)S(1)}, u32[]{:S(2)}, u32[]{:S(2)}) %collective-permute-start.18) | collective-permute-done | bytes 852000 | tf_op jit(solution)/shard_map/ppermute | solution.py:12
  107.3 6.8 %collective-permute-start.13 = (bf16[4,104,1600]{2,1,0:T(8,128)(2,1)}, bf16[4,104,1600]{2,1,0:T(8,128)(2,1)}, u32[]{:S(2)}, u32[]{:S(2)}) collective-permute-start(bf16[4,104,1600]{2,1,0:T(8,128)(2,1)} %collective-permute-done.4), channel_id=1, source_target_pairs={{0,32},{32,0},{1,33},{33,1},{2,34},{34,2},{3,35},{35,3},{4,36},{36... | collective-permute-start | bytes 3993608 | tf_op jit(solution)/shard_map/ppermute | solution.py:27
  114.1 1.0 collective-permute-start.12
  115.1 0.0 collective-permute-done.21
  115.1 1.0 collective-permute-start.15
  116.1 208.2 %arrange.1 = bf16[2,32,104,512]{3,2,1,0:T(8,128)(2,1)} custom-call(bf16[16,104,512]{2,1,0:T(8,128)(2,1)} %pad.9.own_ref, bf16[16,104,512]{2,1,0:T(8,128)(2,1)} %copy-done, bf16[8,104,512]{2,1,0:T(8,128)(2,1)} %copy-done.3, bf16[8,104,512]{2,1,0:T(8,128)(2,1)} %copy-done.4, bf16[16,104,512]{2,1,0:T(8,128)(2,1)} %collective-permute-done.17.before_ref), custom_call_target="tpu_custom_call" | custom-call | bytes 13631488 | tf_op jit(solution)/shard_map/arrange/pallas_call | solution.py:82
  324.3 1.2 slice.37
  325.4 0.1 collective-permute-start.14
  325.5 1.2 slice.36
  326.7 0.0 collective-permute-done.11
  326.7 4.1 %collective-permute-start.23 = (bf16[2,104,1600]{2,1,0:T(8,128)(2,1)S(1)}, bf16[2,104,1600]{2,1,0:T(8,128)(2,1)S(1)}, u32[]{:S(2)}, u32[]{:S(2)}) collective-permute-start(bf16[2,104,1600]{2,1,0:T(8,128)(2,1)S(1)} %slice.37), channel_id=1, source_target_pairs={{0,28},{1,29},{2,30},{3,31},{4,0},{5,1},{6,2},{7,3},{8,4},{9,5},{1... | collective-permute-start | bytes 1996808 | tf_op jit(solution)/shard_map/ppermute | solution.py:23
  330.8 0.0 collective-permute-done.13
  330.8 0.1 collective-permute-start.25
  330.9 0.0 collective-permute-done.15
  330.9 0.5 collective-permute-start.24
  331.4 4.6 %slice_bitcast_fusion = (bf16[2080,512]{1,0:T(8,128)(2,1)}, bf16[2080,512]{1,0:T(8,128)(2,1)}) fusion(bf16[2,3328,512]{2,1,0:T(8,128)(2,1)} %bitcast.38), kind=kLoop, calls=%fused_computation | loop fusion | bytes 8519680 | tf_op jit(solution)/shard_map/squeeze | solution.py:141
  336.0 2.7 collective-permute-done.23
  338.7 0.0 collective-permute-start.27
  338.7 3.1 collective-permute-done.22
  341.9 1.9 slice_bitcast_fusion.2
  343.7 1.1 copy-done.5
  344.8 15.6 %accumulate.2.total_ref = f32[1600,512]{1,0:T(8,128)} custom-call(f32[1600,512]{1,0:T(8,128)} %bitcast.43, bf16[416,1600]{1,0:T(8,128)(2,1)S(1)} %bitcast.32, bf16[416,1600]{1,0:T(8,128)(2,1)} %bitcast.4.refs_1_, bf16[416,1600]{1,0:T(8,128)(2,1)} %bitcast.5.refs_2_, bf16[416,1600]{1,0:T(8,128)(2,1)S(1)} %bitcast.33, bf16[416,1600]{1,0:T(8,128)(2,1)} %bitcast.7.refs_4_, ...), custom_call_target="tpu_custom_call" | custom-call | flops 6815744000 | bytes 24125440 | tf_op jit(solution)/shard_map/accumulate/pallas_call | solution.py:110
  360.5 1.1 copy-done.1
  361.6 0.4 copy-done.2
  362.0 10.4 %accumulate.3 = f32[1600,512]{1,0:T(8,128)} custom-call(f32[1600,512]{1,0:T(8,128)} %accumulate.2.total_ref, bf16[416,1600]{1,0:T(8,128)(2,1)} %bitcast.16.refs_0_, bf16[416,1600]{1,0:T(8,128)(2,1)} %bitcast.17.refs_1_, bf16[208,1600]{1,0:T(8,128)(2,1)S(1)} %bitcast.35, bf16[208,1600]{1,0:T(8,128)(2,1)S(1)} %bitcast.34, bf16[416,1600]{1,0:T(8,128)(2,1)} %bitcast.41, ...), custom_call_target="tpu_custom_call" | custom-call | flops 4089446400 | bytes 17096704 | tf_op jit(solution)/shard_map/accumulate/pallas_call | solution.py:110
  (22 shorter events, 0.1 us)
Async XLA Ops:
  1.0 11.4 %collective-permute-start = (bf16[1,104,1600]{2,1,0:T(8,128)(2,1)S(1)}, bf16[1,104,1600]{2,1,0:T(8,128)(2,1)S(1)}, u32[]{:S(2)}, u32[]{:S(2)}) collective-permute-start(bf16[1,104,1600]{2,1,0:T(8,128)(2,1)S(1)} %pad.8), channel_id=1, source_target_pairs={{0,1},{1,2},{2,3},{3,0},{4,5},{5,6},{6,7},{7,4},{8,9},{9,10},{10,1... | collective-permute-start | bytes 998408 | tf_op jit(solution)/shard_map/ppermute | solution.py:23
  3.6 8.9 %collective-permute-start.1 = (bf16[1,104,1600]{2,1,0:T(8,128)(2,1)S(1)}, bf16[1,104,1600]{2,1,0:T(8,128)(2,1)S(1)}, u32[]{:S(2)}, u32[]{:S(2)}) collective-permute-start(bf16[1,104,1600]{2,1,0:T(8,128)(2,1)S(1)} %pad.8), channel_id=1, source_target_pairs={{0,3},{1,0},{2,1},{3,2},{4,7},{5,4},{6,5},{7,6},{8,11},{9,8},{10,9... | collective-permute-start | bytes 998408 | tf_op jit(solution)/shard_map/ppermute | solution.py:23
  12.4 7.7 %collective-permute-start.2 = (bf16[1,104,1600]{2,1,0:T(8,128)(2,1)S(1)}, bf16[1,104,1600]{2,1,0:T(8,128)(2,1)}, u32[]{:S(2)}, u32[]{:S(2)}) collective-permute-start(bf16[1,104,1600]{2,1,0:T(8,128)(2,1)S(1)} %collective-permute-done), channel_id=1, source_target_pairs={{0,1},{1,2},{2,3},{3,0},{4,5},{5,6},{6,7},{7,4},{8,9},{9,10},{10,1... | collective-permute-start | bytes 998408 | tf_op jit(solution)/shard_map/ppermute | solution.py:23
  21.4 18.9 %collective-permute-start.3 = (bf16[4,104,1600]{2,1,0:T(8,128)(2,1)S(1)}, bf16[4,104,1600]{2,1,0:T(8,128)(2,1)}, u32[]{:S(2)}, u32[]{:S(2)}) collective-permute-start(bf16[4,104,1600]{2,1,0:T(8,128)(2,1)S(1)} %pad_maximum_fusion), channel_id=1, source_target_pairs={{0,4},{1,5},{2,6},{3,7},{4,8},{5,9},{6,10},{7,11},{8,12},{9,13},{1... | collective-permute-start | bytes 3993608 | tf_op jit(solution)/shard_map/ppermute | solution.py:23
  22.2 18.1 %collective-permute-start.4 = (bf16[4,104,1600]{2,1,0:T(8,128)(2,1)S(1)}, bf16[4,104,1600]{2,1,0:T(8,128)(2,1)}, u32[]{:S(2)}, u32[]{:S(2)}) collective-permute-start(bf16[4,104,1600]{2,1,0:T(8,128)(2,1)S(1)} %pad_maximum_fusion), channel_id=1, source_target_pairs={{0,28},{1,29},{2,30},{3,31},{4,0},{5,1},{6,2},{7,3},{8,4},{9,5},{1... | collective-permute-start | bytes 3993608 | tf_op jit(solution)/shard_map/ppermute | solution.py:23
  24.1 19.8 %collective-permute-start.7 = (bf16[1,104,1600]{2,1,0:T(8,128)(2,1)S(1)}, bf16[1,104,1600]{2,1,0:T(8,128)(2,1)S(1)}, u32[]{:S(2)}, u32[]{:S(2)}) collective-permute-start(bf16[1,104,1600]{2,1,0:T(8,128)(2,1)S(1)} %collective-permute-done.1), channel_id=1, source_target_pairs={{32,60},{33,61},{34,62},{35,63},{36,32},{37,33},{38,34},{39,35},{4... | collective-permute-start | bytes 998408 | tf_op jit(solution)/shard_map/ppermute | solution.py:23
  40.3 30.0 %collective-permute-start.5 = (bf16[4,104,1600]{2,1,0:T(8,128)(2,1)}, bf16[4,104,1600]{2,1,0:T(8,128)(2,1)S(1)}, u32[]{:S(2)}, u32[]{:S(2)}) collective-permute-start(bf16[4,104,1600]{2,1,0:T(8,128)(2,1)} %collective-permute-done.3), channel_id=1, source_target_pairs={{0,4},{1,5},{2,6},{3,7},{4,8},{5,9},{6,10},{7,11},{8,12},{9,13},{1... | collective-permute-start | bytes 3993608 | tf_op jit(solution)/shard_map/ppermute | solution.py:23
  40.3 30.0 %collective-permute-start.6 = (bf16[4,104,1600]{2,1,0:T(8,128)(2,1)}, bf16[4,104,1600]{2,1,0:T(8,128)(2,1)}, u32[]{:S(2)}, u32[]{:S(2)}) collective-permute-start(bf16[4,104,1600]{2,1,0:T(8,128)(2,1)} %collective-permute-done.4), channel_id=1, source_target_pairs={{0,28},{1,29},{2,30},{3,31},{4,0},{5,1},{6,2},{7,3},{8,4},{9,5},{1... | collective-permute-start | bytes 3993608 | tf_op jit(solution)/shard_map/ppermute | solution.py:23
  42.0 13.5 %collective-permute-start.8 = (bf16[1,104,1600]{2,1,0:T(8,128)(2,1)}, bf16[1,104,1600]{2,1,0:T(8,128)(2,1)S(1)}, u32[]{:S(2)}, u32[]{:S(2)}) collective-permute-start(bf16[1,104,1600]{2,1,0:T(8,128)(2,1)} %collective-permute-done.2), channel_id=1, source_target_pairs={{32,36},{33,37},{34,38},{35,39},{36,40},{37,41},{38,42},{39,43},{4... | collective-permute-start | bytes 998408 | tf_op jit(solution)/shard_map/ppermute | solution.py:23
  44.0 13.6 %collective-permute-start.9 = (bf16[1,104,1600]{2,1,0:T(8,128)(2,1)S(1)}, bf16[1,104,1600]{2,1,0:T(8,128)(2,1)}, u32[]{:S(2)}, u32[]{:S(2)}) collective-permute-start(bf16[1,104,1600]{2,1,0:T(8,128)(2,1)S(1)} %collective-permute-done.7), channel_id=1, source_target_pairs={{32,60},{33,61},{34,62},{35,63},{36,32},{37,33},{38,34},{39,35},{4... | collective-permute-start | bytes 998408 | tf_op jit(solution)/shard_map/ppermute | solution.py:23
  54.8 35.1 %collective-permute-start.17 = (bf16[16,104,512]{2,1,0:T(8,128)(2,1)}, bf16[16,104,512]{2,1,0:T(8,128)(2,1)}, u32[]{:S(2)}, u32[]{:S(2)}) collective-permute-start(bf16[16,104,512]{2,1,0:T(8,128)(2,1)} %pad.9.own_ref), channel_id=1, source_target_pairs={{0,64},{64,128},{128,192},{192,0},{1,65},{65,129},{129,193},{193,1... | collective-permute-start | bytes 5111816 | tf_op jit(solution)/shard_map/ppermute | solution.py:12
  55.6 35.6 %collective-permute-start.16 = (bf16[16,104,512]{2,1,0:T(8,128)(2,1)}, bf16[16,104,512]{2,1,0:T(8,128)(2,1)S(1)}, u32[]{:S(2)}, u32[]{:S(2)}) collective-permute-start(bf16[16,104,512]{2,1,0:T(8,128)(2,1)} %pad.9.own_ref), channel_id=1, source_target_pairs={{0,192},{64,0},{128,64},{192,128},{1,193},{65,1},{129,65},{193,129... | collective-permute-start | bytes 5111816 | tf_op jit(solution)/shard_map/ppermute | solution.py:12
  57.6 12.7 %collective-permute-start.10 = (bf16[1,104,1600]{2,1,0:T(8,128)(2,1)S(1)}, bf16[1,104,1600]{2,1,0:T(8,128)(2,1)S(1)}, u32[]{:S(2)}, u32[]{:S(2)}) collective-permute-start(bf16[1,104,1600]{2,1,0:T(8,128)(2,1)S(1)} %collective-permute-done.8), channel_id=1, source_target_pairs={{32,36},{33,37},{34,38},{35,39},{36,40},{37,41},{38,42},{39,43},{4... | collective-permute-start | bytes 998408 | tf_op jit(solution)/shard_map/ppermute | solution.py:23
  72.2 42.9 %collective-permute-start.21 = (bf16[4,104,1600]{2,1,0:T(8,128)(2,1)}, bf16[4,104,1600]{2,1,0:T(8,128)(2,1)}, u32[]{:S(2)}, u32[]{:S(2)}) collective-permute-start(bf16[4,104,1600]{2,1,0:T(8,128)(2,1)} %get-tuple-element.10), channel_id=1, source_target_pairs={{0,28},{1,29},{2,30},{3,31},{4,0},{5,1},{6,2},{7,3},{8,4},{9,5},{1... | collective-permute-start | bytes 3993608 | tf_op jit(solution)/shard_map/ppermute | solution.py:23
  91.1 16.2 %collective-permute-start.18 = (bf16[8,104,512]{2,1,0:T(8,128)(2,1)S(1)}, bf16[8,104,512]{2,1,0:T(8,128)(2,1)S(1)}, u32[]{:S(2)}, u32[]{:S(2)}) collective-permute-start(bf16[8,104,512]{2,1,0:T(8,128)(2,1)S(1)} %slice.32), channel_id=1, source_target_pairs={{0,64},{64,128},{128,192},{192,0},{1,65},{65,129},{129,193},{193,1... | collective-permute-start | bytes 2555912 | tf_op jit(solution)/shard_map/ppermute | solution.py:12
  91.2 2.8 copy-start
  91.3 22.8 %collective-permute-start.19 = (bf16[8,104,512]{2,1,0:T(8,128)(2,1)S(1)}, bf16[8,104,512]{2,1,0:T(8,128)(2,1)S(1)}, u32[]{:S(2)}, u32[]{:S(2)}) collective-permute-start(bf16[8,104,512]{2,1,0:T(8,128)(2,1)S(1)} %slice.33), channel_id=1, source_target_pairs={{0,192},{64,0},{128,64},{192,128},{1,193},{65,1},{129,65},{193,129... | collective-permute-start | bytes 2555912 | tf_op jit(solution)/shard_map/ppermute | solution.py:12
  94.0 231.4 %collective-permute-start.20 = (bf16[4,104,1600]{2,1,0:T(8,128)(2,1)}, bf16[4,104,1600]{2,1,0:T(8,128)(2,1)}, u32[]{:S(2)}, u32[]{:S(2)}) collective-permute-start(bf16[4,104,1600]{2,1,0:T(8,128)(2,1)} %get-tuple-element.9), channel_id=1, source_target_pairs={{0,4},{1,5},{2,6},{3,7},{4,8},{5,9},{6,10},{7,11},{8,12},{9,13},{1... | collective-permute-start | bytes 3993608 | tf_op jit(solution)/shard_map/ppermute | solution.py:23
  96.1 230.6 %collective-permute-start.11 = (bf16[4,104,1600]{2,1,0:T(8,128)(2,1)S(1)}, bf16[4,104,1600]{2,1,0:T(8,128)(2,1)}, u32[]{:S(2)}, u32[]{:S(2)}) collective-permute-start(bf16[4,104,1600]{2,1,0:T(8,128)(2,1)S(1)} %pad_maximum_fusion), channel_id=1, source_target_pairs={{0,32},{32,0},{1,33},{33,1},{2,34},{34,2},{3,35},{35,3},{4,36},{36... | collective-permute-start | bytes 3993608 | tf_op jit(solution)/shard_map/ppermute | solution.py:27
  107.3 6.8 %copy-start.3 = (bf16[8,104,512]{2,1,0:T(8,128)(2,1)}, bf16[8,104,512]{2,1,0:T(8,128)(2,1)S(1)}, u32[]{:S(2)}) copy-start(bf16[8,104,512]{2,1,0:T(8,128)(2,1)S(1)} %collective-permute-done.18.low_ref) | copy-start | bytes 2555908
  107.3 223.5 %collective-permute-start.13 = (bf16[4,104,1600]{2,1,0:T(8,128)(2,1)}, bf16[4,104,1600]{2,1,0:T(8,128)(2,1)}, u32[]{:S(2)}, u32[]{:S(2)}) collective-permute-start(bf16[4,104,1600]{2,1,0:T(8,128)(2,1)} %collective-permute-done.4), channel_id=1, source_target_pairs={{0,32},{32,0},{1,33},{33,1},{2,34},{34,2},{3,35},{35,3},{4,36},{36... | collective-permute-start | bytes 3993608 | tf_op jit(solution)/shard_map/ppermute | solution.py:27
  114.1 1.0 copy-start.4
  114.1 216.7 %collective-permute-start.12 = (bf16[4,104,1600]{2,1,0:T(8,128)(2,1)}, bf16[4,104,1600]{2,1,0:T(8,128)(2,1)}, u32[]{:S(2)}, u32[]{:S(2)}) collective-permute-start(bf16[4,104,1600]{2,1,0:T(8,128)(2,1)} %collective-permute-done.3), channel_id=1, source_target_pairs={{0,32},{32,0},{1,33},{33,1},{2,34},{34,2},{3,35},{35,3},{4,36},{36... | collective-permute-start | bytes 3993608 | tf_op jit(solution)/shard_map/ppermute | solution.py:27
  115.1 215.8 %collective-permute-start.15 = (bf16[4,104,1600]{2,1,0:T(8,128)(2,1)}, bf16[4,104,1600]{2,1,0:T(8,128)(2,1)}, u32[]{:S(2)}, u32[]{:S(2)}) collective-permute-start(bf16[4,104,1600]{2,1,0:T(8,128)(2,1)} %get-tuple-element.10), channel_id=1, source_target_pairs={{0,32},{32,0},{1,33},{33,1},{2,34},{34,2},{3,35},{35,3},{4,36},{36... | collective-permute-start | bytes 3993608 | tf_op jit(solution)/shard_map/ppermute | solution.py:27
  325.4 18.3 %collective-permute-start.14 = (bf16[4,104,1600]{2,1,0:T(8,128)(2,1)S(1)}, bf16[4,104,1600]{2,1,0:T(8,128)(2,1)S(1)}, u32[]{:S(2)}, u32[]{:S(2)}) collective-permute-start(bf16[4,104,1600]{2,1,0:T(8,128)(2,1)S(1)} %collective-permute-done.5), channel_id=1, source_target_pairs={{0,32},{32,0},{1,33},{33,1},{2,34},{34,2},{3,35},{35,3},{4,36},{36... | collective-permute-start | bytes 3993608 | tf_op jit(solution)/shard_map/ppermute | solution.py:27
  326.7 12.0 %collective-permute-start.23 = (bf16[2,104,1600]{2,1,0:T(8,128)(2,1)S(1)}, bf16[2,104,1600]{2,1,0:T(8,128)(2,1)S(1)}, u32[]{:S(2)}, u32[]{:S(2)}) collective-permute-start(bf16[2,104,1600]{2,1,0:T(8,128)(2,1)S(1)} %slice.37), channel_id=1, source_target_pairs={{0,28},{1,29},{2,30},{3,31},{4,0},{5,1},{6,2},{7,3},{8,4},{9,5},{1... | collective-permute-start | bytes 1996808 | tf_op jit(solution)/shard_map/ppermute | solution.py:23
  330.8 11.0 %collective-permute-start.22 = (bf16[2,104,1600]{2,1,0:T(8,128)(2,1)S(1)}, bf16[2,104,1600]{2,1,0:T(8,128)(2,1)S(1)}, u32[]{:S(2)}, u32[]{:S(2)}) collective-permute-start(bf16[2,104,1600]{2,1,0:T(8,128)(2,1)S(1)} %slice.36), channel_id=1, source_target_pairs={{0,4},{1,5},{2,6},{3,7},{4,8},{5,9},{6,10},{7,11},{8,12},{9,13},{1... | collective-permute-start | bytes 1996808 | tf_op jit(solution)/shard_map/ppermute | solution.py:23
  330.8 29.7 %collective-permute-start.25 = (bf16[4,104,1600]{2,1,0:T(8,128)(2,1)}, bf16[4,104,1600]{2,1,0:T(8,128)(2,1)S(1)}, u32[]{:S(2)}, u32[]{:S(2)}) collective-permute-start(bf16[4,104,1600]{2,1,0:T(8,128)(2,1)} %collective-permute-done.21), channel_id=1, source_target_pairs={{0,32},{32,0},{1,33},{33,1},{2,34},{34,2},{3,35},{35,3},{4,36},{36... | collective-permute-start | bytes 3993608 | tf_op jit(solution)/shard_map/ppermute | solution.py:27
  330.9 29.6 %collective-permute-start.24 = (bf16[4,104,1600]{2,1,0:T(8,128)(2,1)}, bf16[4,104,1600]{2,1,0:T(8,128)(2,1)S(1)}, u32[]{:S(2)}, u32[]{:S(2)}) collective-permute-start(bf16[4,104,1600]{2,1,0:T(8,128)(2,1)} %collective-permute-done.20), channel_id=1, source_target_pairs={{0,32},{32,0},{1,33},{33,1},{2,34},{34,2},{3,35},{35,3},{4,36},{36... | collective-permute-start | bytes 3993608 | tf_op jit(solution)/shard_map/ppermute | solution.py:27
  338.7 21.7 %collective-permute-start.27 = (bf16[2,104,1600]{2,1,0:T(8,128)(2,1)S(1)}, bf16[2,104,1600]{2,1,0:T(8,128)(2,1)S(1)}, u32[]{:S(2)}, u32[]{:S(2)}) collective-permute-start(bf16[2,104,1600]{2,1,0:T(8,128)(2,1)S(1)} %collective-permute-done.23), channel_id=1, source_target_pairs={{0,32},{32,0},{1,33},{33,1},{2,34},{34,2},{3,35},{35,3},{4,36},{36... | collective-permute-start | bytes 1996808 | tf_op jit(solution)/shard_map/ppermute | solution.py:27
  341.8 18.6 %collective-permute-start.26 = (bf16[2,104,1600]{2,1,0:T(8,128)(2,1)S(1)}, bf16[2,104,1600]{2,1,0:T(8,128)(2,1)S(1)}, u32[]{:S(2)}, u32[]{:S(2)}) collective-permute-start(bf16[2,104,1600]{2,1,0:T(8,128)(2,1)S(1)} %collective-permute-done.22), channel_id=1, source_target_pairs={{0,32},{32,0},{1,33},{33,1},{2,34},{34,2},{3,35},{35,3},{4,36},{36... | collective-permute-start | bytes 1996808 | tf_op jit(solution)/shard_map/ppermute | solution.py:27
  343.7 1.1 copy-start.5
  360.5 1.1 copy-start.1
  360.5 1.5 copy-start.2

commit v3 on v2

v3 whole, which is shorter than its diff:
```python
import jax
import jax.numpy as jnp
from jax import lax
from jax.experimental import pallas as pl
from jax.experimental.pallas import tpu as pltpu
from jax.sharding import PartitionSpec as P

Z, Y = 8, 4
VMEM = 16 << 20


def shift(array, size, step):
    return lax.ppermute(array, "row", [(i, (i + step) % size) for i in range(size)])


def travel(array, first, second):
    pairs = []
    for core, step in enumerate((first, second)):
        if step is not None:
            for z in range(Z):
                for y in range(Y):
                    target = (z + step[0]) % Z * Y + (y + step[1]) % Y
                    pairs.append(((core * Z + z) * Y + y, core * Z * Y + target))
    return lax.ppermute(array, ("col", "depth"), pairs)


def swap(array):
    return lax.ppermute(array, "col", [(0, 1), (1, 0)])


def padded(blocks, rows):
    parts = blocks.reshape(-1, rows, blocks.shape[-1])
    return jnp.pad(parts, ((0, 0), (0, -rows % 8), (0, 0)))


def gather(block, amplitudes, rows):
    along, back = ((0, 1), (1, 0)), ((0, -1), (-1, 0))
    after, before = shift(amplitudes, rows, -1), shift(amplitudes, rows, 1)
    a1 = travel(block, *along)
    b1 = travel(block, *back)
    a2 = travel(a1, *along)
    pack = jnp.concatenate([block, a1, b1, a2])
    b2 = travel(b1, None, back[1])
    a3 = travel(a2, None, along[1])
    b3 = travel(b2, None, back[1])
    a4 = travel(a3, None, along[1])
    rest = jnp.concatenate([b2, a3, b3, a4])
    up, down = ((1, 0), (0, 1)), ((-1, 0), (0, -1))
    u1, d1 = travel(pack, *up), travel(pack, *down)
    u2, d2 = travel(u1, *up), travel(d1, down[0], None)
    u2, d2, after, before = lax.optimization_barrier((u2, d2, after, before))
    half = amplitudes.shape[0] // 2
    far_low, far_high = shift(before[:half], rows, 1), shift(after[half:], rows, -1)
    first = lax.axis_index("col") == 0
    kept = jnp.where(first, d2, rest)
    u3, d3 = travel(jnp.where(first, u2, rest), *up), travel(kept, *down)
    u3, d3, far_low, far_high = lax.optimization_barrier((u3, d3, far_low, far_high))
    u4, d4 = travel(u3[:2], *up), travel(d3[2:], *down)
    return [pack, u1, d1, u2, kept, u3, d3, u4, d4], (after, far_low, far_high, before)


def arrange(own, after, far_low, far_high, before, rows, height, cuts):
    width = own.shape[1]
    count = own.shape[0] // height
    full = height + -height % 8

    def kernel(own_ref, after_ref, low_ref, high_ref, before_ref, *refs):
        out_refs, held = refs[:-1], refs[-1]
        x, core, depth = (lax.axis_index(name) for name in ("row", "col", "depth"))
        z, y = depth // Y, lax.rem(depth, Y)
        held[:, :, height:, :] = jnp.zeros((2, Z * Y, full - height, width), held.dtype)
        sources = [(own_ref, 0, 0), (after_ref, 1, 0), (low_ref, 2, 0), (high_ref, 2, count // 2), (before_ref, 3, 0)]
        for ref, step, start in sources:
            block_row = lax.rem(x + step, rows)
            half = block_row // (rows // 2)
            for i in range(ref.shape[0] // height):
                there = lax.rem(block_row, rows // 2) * count + start + i
                dz = lax.rem(there // Y - z + Z, Z)
                dy = lax.rem((start + i) % Y - y + Y, Y)
                oz = jnp.where(dz < Z // 2, 2 * dz, 2 * (Z - dz) - 1)
                oy = jnp.where(dy < Y // 2, 2 * dy, 2 * (Y - dy) - 1)
                place = jnp.where(half == 0, oz * Y + oy, oz // Y * (Y * Y) + oy * Y + lax.rem(oz, Y))
                held[lax.rem(half + core, 2), place, pl.ds(0, height), :] = ref[pl.ds(i * height, height), :]
        for side in range(2):
            at = 0
            for out_ref, blocks in zip(out_refs, cuts):
                part = held[side, pl.ds(at, blocks)].reshape(blocks * full, width)
                out_ref[side] = part.T
                at += blocks

    size = 2 * own.size * rows
    return pl.pallas_call(
        kernel,
        out_shape=[jax.ShapeDtypeStruct((2, width, blocks * full), own.dtype) for blocks in cuts],
        scratch_shapes=[pltpu.VMEM((2, Z * Y, full, width), own.dtype)],
        compiler_params=pltpu.CompilerParams(vmem_limit_bytes=VMEM),
        cost_estimate=pl.CostEstimate(flops=0, bytes_accessed=2 * size, transcendentals=0),
        name="arrange",
    )(own, after, far_low, far_high, before)


def accumulate(total, factor, mine, other, tile=256):
    columns, pairs = total.shape
    pieces = [piece.reshape(-1, columns) for piece in mine + other]
    depth = factor.shape[-1]

    def kernel(total_ref, factor_ref, *refs):
        piece_refs, out_ref = refs[:-1], refs[-1]

        def add(start, width):
            share = jnp.zeros((pairs, width), jnp.float32)
            for side in range(2):
                refs = piece_refs[side * len(mine) :][: len(mine)]
                part = jnp.concatenate([ref[:, pl.ds(start, width)] for ref in refs])
                share += jnp.dot(factor_ref[side], part, preferred_element_type=jnp.float32)
            out_ref[pl.ds(start, width), :] = total_ref[pl.ds(start, width), :] + share.T

        whole = columns // tile

        @pl.loop(0, whole)
        def _(i):
            add(pl.multiple_of(i * tile, tile), tile)

        if columns % tile:
            add(whole * tile, columns % tile)

    return pl.pallas_call(
        kernel,
        out_shape=jax.ShapeDtypeStruct(total.shape, total.dtype),
        compiler_params=pltpu.CompilerParams(vmem_limit_bytes=VMEM),
        cost_estimate=pl.CostEstimate(
            flops=4 * columns * pairs * depth,
            bytes_accessed=8 * total.size + 4 * depth * (columns + pairs),
            transcendentals=0,
        ),
        name="accumulate",
    )(total, factor, *pieces)


def solution(mesh):
    rows = mesh.shape["row"]

    def per_device(residual_in, integrals, amplitudes):
        height = integrals.shape[1]
        mine, others = gather(padded(integrals.T, height), amplitudes, rows)
        other = [swap(piece) for piece in mine]
        factors = arrange(amplitudes, *others, rows, height, [20, 8, 4])
        total = residual_in.T
        for factor, a, b in zip(factors, (0, 5, 7), (5, 7, 9)):
            total = accumulate(total, factor, mine[a:b], other[a:b])
        return total.T

    placed = (P(("col", "depth"), "row"), P("row", ("col", "depth")), P("row", ("col", "depth")))
    return jax.shard_map(
        per_device, mesh=mesh, in_specs=placed, out_specs=P(("col", "depth"), "row"), check_vma=False
    )
```

time: 373 us -> 134 us (0.36)
  Pallas kernels: 234 us -> 27.6 us
  waiting for transfers between devices: 65.7 us -> 48.1 us
  local copies, waits for them, and re-layouts: 21 us -> 4.32 us
  starting transfers between devices: 48.2 us -> 53.4 us
    pallas_call x3 -> x4, Pallas kernels: 234 us -> 27.6 us  [the longest x3 23.1 us: accumulate(): pl.pallas_call(kernel, out_shape=jax.ShapeDtypeStruct(total.shape, total....]
    ppermute x4, waiting for transfers between devices: 23.7 us -> 4.58 us  [shift(): lax.ppermute(array, 'row', [(i, (i + step) % size) for i in range(size)])]
    ppermute x9, starting transfers between devices: 14.3 us -> 22.7 us  [swap(): return lax.ppermute(array, 'col', [(0, 1), (1, 0)])]
    squeeze x2 -> x0, local copies, waits for them, and re-layouts: 6.48 us -> none  [the longest x1 4.62 us: per_device(): panel[1, :split]]
  transfers between devices with their start and end apart: 28 -> 28, of which waited for: 8 -> 9; matrix products, arithmetic and copies ran while one was open for 5% -> 2% of each run, Pallas kernels for 60% -> 16%
where the time goes in v3:
time: 134 us
  starting transfers between devices  53.4 us (40%)
  waiting for transfers between devices  48.1 us (36%)
  Pallas kernels  27.6 us (21%)
  local copies, waits for them, and re-layouts  4.32 us (3%)
    ppermute x15, waiting for transfers between devices, travel(): return lax.ppermute(array, ('col', 'depth'), pairs)  43.5 us
    ppermute x15, starting transfers between devices, travel(): return lax.ppermute(array, ('col', 'depth'), pairs)  25.3 us
    pallas_call x3, Pallas kernels, accumulate(): pl.pallas_call(kernel, out_shape=jax.ShapeDtypeStruct(total.shape, total....  23.1 us
    ppermute x9, starting transfers between devices, swap(): return lax.ppermute(array, 'col', [(0, 1), (1, 0)])  22.7 us
    ppermute x4, starting transfers between devices, shift(): lax.ppermute(array, 'row', [(i, (i + step) % size) for i in range(size)])  5.39 us
    ppermute x4, waiting for transfers between devices, shift(): lax.ppermute(array, 'row', [(i, (i + step) % size) for i in range(size)])  4.58 us
    pallas_call x1, Pallas kernels, arrange(): pl.pallas_call(kernel, out_shape=[jax.ShapeDtypeStruct((2, width, blocks...  4.46 us
    unnamed x9, local copies, waits for them, and re-layouts  3.07 us
  transfers between devices with their start and end apart: 28, of which 9 were waited for; matrix products, arithmetic and copies ran while one was open for 2% of the time, Pallas kernels for 16%

profile of v3, /device:TPU:1, one launch (start us, length us, event | category | flops | bytes accessed | tf_op | source)
XLA Modules:
  0.0 134.1 jit_solution(6278065339254735098)
XLA Ops:
  0.0 1.0 pad.4
  1.0 2.5 %collective-permute-start = (bf16[1,104,1600]{2,1,0:T(8,128)(2,1)S(1)}, bf16[1,104,1600]{2,1,0:T(8,128)(2,1)S(1)}, u32[]{:S(2)}, u32[]{:S(2)}) collective-permute-start(bf16[1,104,1600]{2,1,0:T(8,128)(2,1)S(1)} %pad.4), channel_id=1, source_target_pairs={{0,1},{1,2},{2,3},{3,0},{4,5},{5,6},{6,7},{7,4},{8,9},{9,10},{10,1... | collective-permute-start | bytes 998408 | tf_op jit(solution)/shard_map/ppermute | solution.py:24
  3.6 4.0 %collective-permute-start.1 = (bf16[1,104,1600]{2,1,0:T(8,128)(2,1)S(1)}, bf16[1,104,1600]{2,1,0:T(8,128)(2,1)S(1)}, u32[]{:S(2)}, u32[]{:S(2)}) collective-permute-start(bf16[1,104,1600]{2,1,0:T(8,128)(2,1)S(1)} %pad.4), channel_id=1, source_target_pairs={{0,3},{1,0},{2,1},{3,2},{4,7},{5,4},{6,5},{7,6},{8,11},{9,8},{10,9... | collective-permute-start | bytes 998408 | tf_op jit(solution)/shard_map/ppermute | solution.py:24
  7.6 4.8 %collective-permute-done = bf16[1,104,1600]{2,1,0:T(8,128)(2,1)S(1)} collective-permute-done((bf16[1,104,1600]{2,1,0:T(8,128)(2,1)S(1)}, bf16[1,104,1600]{2,1,0:T(8,128)(2,1)S(1)}, u32[]{:S(2)}, u32[]{:S(2)}) %collective-permute-start) | collective-permute-done | bytes 332832 | tf_op jit(solution)/shard_map/ppermute | solution.py:24
  12.4 0.0 collective-permute-start.2
  12.4 0.0 collective-permute-done.1
  12.4 7.6 %collective-permute-done.2 = bf16[1,104,1600]{2,1,0:T(8,128)(2,1)S(1)} collective-permute-done((bf16[1,104,1600]{2,1,0:T(8,128)(2,1)S(1)}, bf16[1,104,1600]{2,1,0:T(8,128)(2,1)S(1)}, u32[]{:S(2)}, u32[]{:S(2)}) %collective-permute-start.2) | collective-permute-done | bytes 332832 | tf_op jit(solution)/shard_map/ppermute | solution.py:24
  20.0 0.2 pad_maximum_fusion
  20.3 0.0 copy-start
  20.3 0.8 collective-permute-start.3
  21.1 1.9 %collective-permute-start.5 = (bf16[4,104,1600]{2,1,0:T(8,128)(2,1)S(1)}, bf16[4,104,1600]{2,1,0:T(8,128)(2,1)}, u32[]{:S(2)}, u32[]{:S(2)}) collective-permute-start(bf16[4,104,1600]{2,1,0:T(8,128)(2,1)S(1)} %pad_maximum_fusion), channel_id=1, source_target_pairs={{0,28},{1,29},{2,30},{3,31},{4,0},{5,1},{6,2},{7,3},{8,4},{9,5},{1... | collective-permute-start | bytes 3993608 | tf_op jit(solution)/shard_map/ppermute | solution.py:24
  23.0 2.3 %collective-permute-start.9 = (bf16[1,104,1600]{2,1,0:T(8,128)(2,1)S(1)}, bf16[1,104,1600]{2,1,0:T(8,128)(2,1)}, u32[]{:S(2)}, u32[]{:S(2)}) collective-permute-start(bf16[1,104,1600]{2,1,0:T(8,128)(2,1)S(1)} %collective-permute-done.1), channel_id=1, source_target_pairs={{32,60},{33,61},{34,62},{35,63},{36,32},{37,33},{38,34},{39,35},{4... | collective-permute-start | bytes 998408 | tf_op jit(solution)/shard_map/ppermute | solution.py:24
  25.4 2.6 %collective-permute-start.7 = (bf16[1600,512]{1,0:T(8,128)(2,1)}, bf16[1600,512]{1,0:T(8,128)(2,1)S(1)}, u32[]{:S(2)}, u32[]{:S(2)}) collective-permute-start(bf16[1600,512]{1,0:T(8,128)(2,1)} %own_ref.1), channel_id=1, source_target_pairs={{0,192},{64,0},{128,64},{192,128},{1,193},{65,1},{129,65},{193,129... | collective-permute-start | bytes 4915208 | tf_op jit(solution)/shard_map/ppermute | solution.py:13
  27.9 0.0 collective-permute-start.8
  27.9 7.3 %collective-permute-done.9 = bf16[1,104,1600]{2,1,0:T(8,128)(2,1)} collective-permute-done((bf16[1,104,1600]{2,1,0:T(8,128)(2,1)S(1)}, bf16[1,104,1600]{2,1,0:T(8,128)(2,1)}, u32[]{:S(2)}, u32[]{:S(2)}) %collective-permute-start.9) | collective-permute-done | bytes 332832 | tf_op jit(solution)/shard_map/ppermute | solution.py:24
  35.2 1.9 %collective-permute-start.10 = (bf16[1,104,1600]{2,1,0:T(8,128)(2,1)S(1)}, bf16[1,104,1600]{2,1,0:T(8,128)(2,1)}, u32[]{:S(2)}, u32[]{:S(2)}) collective-permute-start(bf16[1,104,1600]{2,1,0:T(8,128)(2,1)S(1)} %collective-permute-done.2), channel_id=1, source_target_pairs={{32,36},{33,37},{34,38},{35,39},{36,40},{37,41},{38,42},{39,43},{4... | collective-permute-start | bytes 998408 | tf_op jit(solution)/shard_map/ppermute | solution.py:24
  37.1 2.1 %collective-permute-done.3 = bf16[4,104,1600]{2,1,0:T(8,128)(2,1)} collective-permute-done((bf16[4,104,1600]{2,1,0:T(8,128)(2,1)S(1)}, bf16[4,104,1600]{2,1,0:T(8,128)(2,1)}, u32[]{:S(2)}, u32[]{:S(2)}) %collective-permute-start.3) | collective-permute-done | bytes 1331232 | tf_op jit(solution)/shard_map/ppermute | solution.py:24
  39.2 0.0 collective-permute-start.4
  39.2 0.0 collective-permute-done.5
  39.2 1.8 %collective-permute-start.6 = (bf16[4,104,1600]{2,1,0:T(8,128)(2,1)}, bf16[4,104,1600]{2,1,0:T(8,128)(2,1)}, u32[]{:S(2)}, u32[]{:S(2)}) collective-permute-start(bf16[4,104,1600]{2,1,0:T(8,128)(2,1)} %collective-permute-done.5), channel_id=1, source_target_pairs={{0,28},{1,29},{2,30},{3,31},{4,0},{5,1},{6,2},{7,3},{8,4},{9,5},{1... | collective-permute-start | bytes 3993608 | tf_op jit(solution)/shard_map/ppermute | solution.py:24
  41.0 4.4 %collective-permute-done.10 = bf16[1,104,1600]{2,1,0:T(8,128)(2,1)} collective-permute-done((bf16[1,104,1600]{2,1,0:T(8,128)(2,1)S(1)}, bf16[1,104,1600]{2,1,0:T(8,128)(2,1)}, u32[]{:S(2)}, u32[]{:S(2)}) %collective-permute-start.10) | collective-permute-done | bytes 332832 | tf_op jit(solution)/shard_map/ppermute | solution.py:24
  45.5 3.7 %collective-permute-start.11 = (bf16[1,104,1600]{2,1,0:T(8,128)(2,1)}, bf16[1,104,1600]{2,1,0:T(8,128)(2,1)}, u32[]{:S(2)}, u32[]{:S(2)}) collective-permute-start(bf16[1,104,1600]{2,1,0:T(8,128)(2,1)} %collective-permute-done.9), channel_id=1, source_target_pairs={{32,60},{33,61},{34,62},{35,63},{36,32},{37,33},{38,34},{39,35},{4... | collective-permute-start | bytes 998408 | tf_op jit(solution)/shard_map/ppermute | solution.py:24
  49.2 1.0 constant_dynamic-update-slice_fusion.3
  50.2 7.6 %collective-permute-done.11 = bf16[1,104,1600]{2,1,0:T(8,128)(2,1)} collective-permute-done((bf16[1,104,1600]{2,1,0:T(8,128)(2,1)}, bf16[1,104,1600]{2,1,0:T(8,128)(2,1)}, u32[]{:S(2)}, u32[]{:S(2)}) %collective-permute-start.11) | collective-permute-done | bytes 332832 | tf_op jit(solution)/shard_map/ppermute | solution.py:24
  57.8 1.9 %collective-permute-start.12 = (bf16[1,104,1600]{2,1,0:T(8,128)(2,1)}, bf16[1,104,1600]{2,1,0:T(8,128)(2,1)S(1)}, u32[]{:S(2)}, u32[]{:S(2)}) collective-permute-start(bf16[1,104,1600]{2,1,0:T(8,128)(2,1)} %collective-permute-done.10), channel_id=1, source_target_pairs={{32,36},{33,37},{34,38},{35,39},{36,40},{37,41},{38,42},{39,43},{4... | collective-permute-start | bytes 998408 | tf_op jit(solution)/shard_map/ppermute | solution.py:24
  59.7 1.0 constant_dynamic-update-slice_fusion.2
  60.7 1.0 constant_dynamic-update-slice_fusion.1
  61.7 5.5 %collective-permute-done.12 = bf16[1,104,1600]{2,1,0:T(8,128)(2,1)S(1)} collective-permute-done((bf16[1,104,1600]{2,1,0:T(8,128)(2,1)}, bf16[1,104,1600]{2,1,0:T(8,128)(2,1)S(1)}, u32[]{:S(2)}, u32[]{:S(2)}) %collective-permute-start.12) | collective-permute-done | bytes 332832 | tf_op jit(solution)/shard_map/ppermute | solution.py:24
  67.3 0.0 collective-permute-done.7.after_ref
  67.3 0.0 collective-permute-done.8.before_ref
  67.3 0.0 collective-permute-done.6
  67.3 0.3 broadcast_select_fusion
  67.6 0.0 copy-start.1
  67.6 0.7 collective-permute-start.14
  68.3 0.1 slice.12
  68.3 0.5 collective-permute-start.15
  68.8 0.1 slice.13
  68.9 2.3 %collective-permute-start.16 = (bf16[800,512]{1,0:T(8,128)(2,1)S(1)}, bf16[800,512]{1,0:T(8,128)(2,1)S(1)}, u32[]{:S(2)}, u32[]{:S(2)}) collective-permute-start(bf16[800,512]{1,0:T(8,128)(2,1)S(1)} %slice.13), channel_id=1, source_target_pairs={{0,192},{64,0},{128,64},{192,128},{1,193},{65,1},{129,65},{193,129... | collective-permute-start | bytes 2457608 | tf_op jit(solution)/shard_map/ppermute | solution.py:13
  71.2 0.9 collective-permute-start.13
  72.1 6.2 %collective-permute-start.17 = (bf16[4,104,1600]{2,1,0:T(8,128)(2,1)S(1)}, bf16[4,104,1600]{2,1,0:T(8,128)(2,1)S(1)}, u32[]{:S(2)}, u32[]{:S(2)}) collective-permute-start(bf16[4,104,1600]{2,1,0:T(8,128)(2,1)S(1)} %copy-done.1), channel_id=1, source_target_pairs={{0,32},{32,0},{1,33},{33,1},{2,34},{34,2},{3,35},{35,3},{4,36},{36... | collective-permute-start | bytes 3993608 | tf_op jit(solution)/shard_map/ppermute | solution.py:28
  78.3 4.6 %collective-permute-done.15.low_ref = bf16[800,512]{1,0:T(8,128)(2,1)S(1)} collective-permute-done((bf16[800,512]{1,0:T(8,128)(2,1)S(1)}, bf16[800,512]{1,0:T(8,128)(2,1)S(1)}, u32[]{:S(2)}, u32[]{:S(2)}) %collective-permute-start.15) | collective-permute-done | bytes 819232 | tf_op jit(solution)/shard_map/ppermute | solution.py:13
  82.8 7.4 %collective-permute-start.19 = (bf16[4,104,1600]{2,1,0:T(8,128)(2,1)}, bf16[4,104,1600]{2,1,0:T(8,128)(2,1)S(1)}, u32[]{:S(2)}, u32[]{:S(2)}) collective-permute-start(bf16[4,104,1600]{2,1,0:T(8,128)(2,1)} %collective-permute-done.5), channel_id=1, source_target_pairs={{0,32},{32,0},{1,33},{33,1},{2,34},{34,2},{3,35},{35,3},{4,36},{36... | collective-permute-start | bytes 3993608 | tf_op jit(solution)/shard_map/ppermute | solution.py:28
  90.3 0.0 collective-permute-done.16.high_ref
  90.3 0.0 collective-permute-start.18
  90.3 0.5 collective-permute-start.21
  90.8 0.0 collective-permute-done.13
  90.8 7.1 %collective-permute-start.20 = (bf16[4,104,1600]{2,1,0:T(8,128)(2,1)}, bf16[4,104,1600]{2,1,0:T(8,128)(2,1)S(1)}, u32[]{:S(2)}, u32[]{:S(2)}) collective-permute-start(bf16[4,104,1600]{2,1,0:T(8,128)(2,1)} %collective-permute-done.4), channel_id=1, source_target_pairs={{0,32},{32,0},{1,33},{33,1},{2,34},{34,2},{3,35},{35,3},{4,36},{36... | collective-permute-start | bytes 3993608 | tf_op jit(solution)/shard_map/ppermute | solution.py:28
  97.9 0.0 collective-permute-done.17
  97.9 0.0 collective-permute-start.22
  97.9 0.0 collective-permute-done.19
  97.9 0.5 collective-permute-start.23
  98.4 0.1 slice.14
  98.4 0.1 slice.15
  98.5 0.0 copy-start.2
  98.5 0.0 collective-permute-done.18
  98.5 0.1 collective-permute-start.24
  98.6 2.7 %collective-permute-start.25 = (bf16[2,104,1600]{2,1,0:T(8,128)(2,1)S(1)}, bf16[2,104,1600]{2,1,0:T(8,128)(2,1)S(1)}, u32[]{:S(2)}, u32[]{:S(2)}) collective-permute-start(bf16[2,104,1600]{2,1,0:T(8,128)(2,1)S(1)} %slice.15), channel_id=1, source_target_pairs={{0,28},{1,29},{2,30},{3,31},{4,0},{5,1},{6,2},{7,3},{8,4},{9,5},{1... | collective-permute-start | bytes 1996808 | tf_op jit(solution)/shard_map/ppermute | solution.py:24
  101.3 4.5 %arrange.1 = (bf16[2,512,2080]{2,1,0:T(8,128)(2,1)S(1)}, bf16[2,512,832]{2,1,0:T(8,128)(2,1)S(1)}, bf16[2,512,416]{2,1,0:T(8,128)(2,1)S(1)}) custom-call(bf16[1600,512]{1,0:T(8,128)(2,1)} %own_ref.1, bf16[1600,512]{1,0:T(8,128)(2,1)S(1)} %collective-permute-done.7.after_ref, bf16[800,512]{1,0:T(8,128)(2,1)S(1)} %collective-permute-done.15.low_ref, ...), custom_call_target="tpu_custom_call" | custom-call | bytes 13107200 | tf_op jit(solution)/shard_map/arrange/pallas_call | solution.py:92
  105.7 4.2 %collective-permute-done.24 = bf16[2,104,1600]{2,1,0:T(8,128)(2,1)S(1)} collective-permute-done((bf16[2,104,1600]{2,1,0:T(8,128)(2,1)S(1)}, bf16[2,104,1600]{2,1,0:T(8,128)(2,1)S(1)}, u32[]{:S(2)}, u32[]{:S(2)}) %collective-permute-start.24) | collective-permute-done | bytes 665632 | tf_op jit(solution)/shard_map/ppermute | solution.py:24
  109.9 0.9 collective-permute-start.26
  110.9 0.0 collective-permute-start.27
  110.9 12.2 %accumulate.3.total_ref = f32[1600,512]{1,0:T(8,128)S(1)} custom-call(f32[1600,512]{1,0:T(8,128)S(1)} %bitcast.33, bf16[2,512,2080]{2,1,0:T(8,128)(2,1)S(1)} %get-tuple-element.22.factor_ref, bf16[416,1600]{1,0:T(8,128)(2,1)S(1)} %bitcast.25, bf16[416,1600]{1,0:T(8,128)(2,1)} %bitcast.4.refs_1_, bf16[416,1600]{1,0:T(8,128)(2,1)} %bitcast.5.refs_2_, ...), custom_call_target="tpu_custom_call" | custom-call | flops 6815744000 | bytes 24125440 | tf_op jit(solution)/shard_map/accumulate/pallas_call | solution.py:127
  123.1 5.3 %accumulate.4.total_ref = f32[1600,512]{1,0:T(8,128)S(1)} custom-call(f32[1600,512]{1,0:T(8,128)S(1)} %accumulate.3.total_ref, bf16[2,512,832]{2,1,0:T(8,128)(2,1)S(1)} %get-tuple-element.23.factor_ref, bf16[416,1600]{1,0:T(8,128)(2,1)S(1)} %bitcast.24, bf16[416,1600]{1,0:T(8,128)(2,1)S(1)} %bitcast.23, bf16[416,1600]{1,0:T(8,128)(2,1)S(1)} %bitcast.27, ...), custom_call_target="tpu_custom_call" | custom-call | flops 2726297600 | bytes 13582336 | tf_op jit(solution)/shard_map/accumulate/pallas_call | solution.py:127
  128.5 5.6 %accumulate.5 = f32[1600,512]{1,0:T(8,128)} custom-call(f32[1600,512]{1,0:T(8,128)S(1)} %accumulate.4.total_ref, bf16[2,512,416]{2,1,0:T(8,128)(2,1)S(1)} %get-tuple-element.26.factor_ref, bf16[208,1600]{1,0:T(8,128)(2,1)S(1)} %bitcast.29, bf16[208,1600]{1,0:T(8,128)(2,1)S(1)} %bitcast.30, bf16[208,1600]{1,0:T(8,128)(2,1)S(1)} %bitcast.31, ...), custom_call_target="tpu_custom_call" | custom-call | flops 1363148800 | bytes 10067968 | tf_op jit(solution)/shard_map/accumulate/pallas_call | solution.py:127
  (13 shorter events, 0.1 us)
Async XLA Ops:
  1.0 11.4 %collective-permute-start = (bf16[1,104,1600]{2,1,0:T(8,128)(2,1)S(1)}, bf16[1,104,1600]{2,1,0:T(8,128)(2,1)S(1)}, u32[]{:S(2)}, u32[]{:S(2)}) collective-permute-start(bf16[1,104,1600]{2,1,0:T(8,128)(2,1)S(1)} %pad.4), channel_id=1, source_target_pairs={{0,1},{1,2},{2,3},{3,0},{4,5},{5,6},{6,7},{7,4},{8,9},{9,10},{10,1... | collective-permute-start | bytes 998408 | tf_op jit(solution)/shard_map/ppermute | solution.py:24
  3.6 8.9 %collective-permute-start.1 = (bf16[1,104,1600]{2,1,0:T(8,128)(2,1)S(1)}, bf16[1,104,1600]{2,1,0:T(8,128)(2,1)S(1)}, u32[]{:S(2)}, u32[]{:S(2)}) collective-permute-start(bf16[1,104,1600]{2,1,0:T(8,128)(2,1)S(1)} %pad.4), channel_id=1, source_target_pairs={{0,3},{1,0},{2,1},{3,2},{4,7},{5,4},{6,5},{7,6},{8,11},{9,8},{10,9... | collective-permute-start | bytes 998408 | tf_op jit(solution)/shard_map/ppermute | solution.py:24
  12.4 7.6 %collective-permute-start.2 = (bf16[1,104,1600]{2,1,0:T(8,128)(2,1)S(1)}, bf16[1,104,1600]{2,1,0:T(8,128)(2,1)S(1)}, u32[]{:S(2)}, u32[]{:S(2)}) collective-permute-start(bf16[1,104,1600]{2,1,0:T(8,128)(2,1)S(1)} %collective-permute-done), channel_id=1, source_target_pairs={{0,1},{1,2},{2,3},{3,0},{4,5},{5,6},{6,7},{7,4},{8,9},{9,10},{10,1... | collective-permute-start | bytes 998408 | tf_op jit(solution)/shard_map/ppermute | solution.py:24
  20.3 5.1 %copy-start = (bf16[4,104,1600]{2,1,0:T(8,128)(2,1)}, bf16[4,104,1600]{2,1,0:T(8,128)(2,1)S(1)}, u32[]{:S(2)}) copy-start(bf16[4,104,1600]{2,1,0:T(8,128)(2,1)S(1)} %pad_maximum_fusion) | copy-start | bytes 3993604
  20.3 18.9 %collective-permute-start.3 = (bf16[4,104,1600]{2,1,0:T(8,128)(2,1)S(1)}, bf16[4,104,1600]{2,1,0:T(8,128)(2,1)}, u32[]{:S(2)}, u32[]{:S(2)}) collective-permute-start(bf16[4,104,1600]{2,1,0:T(8,128)(2,1)S(1)} %pad_maximum_fusion), channel_id=1, source_target_pairs={{0,4},{1,5},{2,6},{3,7},{4,8},{5,9},{6,10},{7,11},{8,12},{9,13},{1... | collective-permute-start | bytes 3993608 | tf_op jit(solution)/shard_map/ppermute | solution.py:24
  21.1 18.1 %collective-permute-start.5 = (bf16[4,104,1600]{2,1,0:T(8,128)(2,1)S(1)}, bf16[4,104,1600]{2,1,0:T(8,128)(2,1)}, u32[]{:S(2)}, u32[]{:S(2)}) collective-permute-start(bf16[4,104,1600]{2,1,0:T(8,128)(2,1)S(1)} %pad_maximum_fusion), channel_id=1, source_target_pairs={{0,28},{1,29},{2,30},{3,31},{4,0},{5,1},{6,2},{7,3},{8,4},{9,5},{1... | collective-permute-start | bytes 3993608 | tf_op jit(solution)/shard_map/ppermute | solution.py:24
  23.0 12.2 %collective-permute-start.9 = (bf16[1,104,1600]{2,1,0:T(8,128)(2,1)S(1)}, bf16[1,104,1600]{2,1,0:T(8,128)(2,1)}, u32[]{:S(2)}, u32[]{:S(2)}) collective-permute-start(bf16[1,104,1600]{2,1,0:T(8,128)(2,1)S(1)} %collective-permute-done.1), channel_id=1, source_target_pairs={{32,60},{33,61},{34,62},{35,63},{36,32},{37,33},{38,34},{39,35},{4... | collective-permute-start | bytes 998408 | tf_op jit(solution)/shard_map/ppermute | solution.py:24
  25.4 41.9 %collective-permute-start.7 = (bf16[1600,512]{1,0:T(8,128)(2,1)}, bf16[1600,512]{1,0:T(8,128)(2,1)S(1)}, u32[]{:S(2)}, u32[]{:S(2)}) collective-permute-start(bf16[1600,512]{1,0:T(8,128)(2,1)} %own_ref.1), channel_id=1, source_target_pairs={{0,192},{64,0},{128,64},{192,128},{1,193},{65,1},{129,65},{193,129... | collective-permute-start | bytes 4915208 | tf_op jit(solution)/shard_map/ppermute | solution.py:13
  27.9 39.3 %collective-permute-start.8 = (bf16[1600,512]{1,0:T(8,128)(2,1)}, bf16[1600,512]{1,0:T(8,128)(2,1)S(1)}, u32[]{:S(2)}, u32[]{:S(2)}) collective-permute-start(bf16[1600,512]{1,0:T(8,128)(2,1)} %own_ref.1), channel_id=1, source_target_pairs={{0,64},{64,128},{128,192},{192,0},{1,65},{65,129},{129,193},{193,1... | collective-permute-start | bytes 4915208 | tf_op jit(solution)/shard_map/ppermute | solution.py:13
  35.2 10.2 %collective-permute-start.10 = (bf16[1,104,1600]{2,1,0:T(8,128)(2,1)S(1)}, bf16[1,104,1600]{2,1,0:T(8,128)(2,1)}, u32[]{:S(2)}, u32[]{:S(2)}) collective-permute-start(bf16[1,104,1600]{2,1,0:T(8,128)(2,1)S(1)} %collective-permute-done.2), channel_id=1, source_target_pairs={{32,36},{33,37},{34,38},{35,39},{36,40},{37,41},{38,42},{39,43},{4... | collective-permute-start | bytes 998408 | tf_op jit(solution)/shard_map/ppermute | solution.py:24
  39.2 28.0 %collective-permute-start.4 = (bf16[4,104,1600]{2,1,0:T(8,128)(2,1)}, bf16[4,104,1600]{2,1,0:T(8,128)(2,1)}, u32[]{:S(2)}, u32[]{:S(2)}) collective-permute-start(bf16[4,104,1600]{2,1,0:T(8,128)(2,1)} %collective-permute-done.3), channel_id=1, source_target_pairs={{0,4},{1,5},{2,6},{3,7},{4,8},{5,9},{6,10},{7,11},{8,12},{9,13},{1... | collective-permute-start | bytes 3993608 | tf_op jit(solution)/shard_map/ppermute | solution.py:24
  39.2 28.1 %collective-permute-start.6 = (bf16[4,104,1600]{2,1,0:T(8,128)(2,1)}, bf16[4,104,1600]{2,1,0:T(8,128)(2,1)}, u32[]{:S(2)}, u32[]{:S(2)}) collective-permute-start(bf16[4,104,1600]{2,1,0:T(8,128)(2,1)} %collective-permute-done.5), channel_id=1, source_target_pairs={{0,28},{1,29},{2,30},{3,31},{4,0},{5,1},{6,2},{7,3},{8,4},{9,5},{1... | collective-permute-start | bytes 3993608 | tf_op jit(solution)/shard_map/ppermute | solution.py:24
  45.5 12.3 %collective-permute-start.11 = (bf16[1,104,1600]{2,1,0:T(8,128)(2,1)}, bf16[1,104,1600]{2,1,0:T(8,128)(2,1)}, u32[]{:S(2)}, u32[]{:S(2)}) collective-permute-start(bf16[1,104,1600]{2,1,0:T(8,128)(2,1)} %collective-permute-done.9), channel_id=1, source_target_pairs={{32,60},{33,61},{34,62},{35,63},{36,32},{37,33},{38,34},{39,35},{4... | collective-permute-start | bytes 998408 | tf_op jit(solution)/shard_map/ppermute | solution.py:24
  57.8 9.4 %collective-permute-start.12 = (bf16[1,104,1600]{2,1,0:T(8,128)(2,1)}, bf16[1,104,1600]{2,1,0:T(8,128)(2,1)S(1)}, u32[]{:S(2)}, u32[]{:S(2)}) collective-permute-start(bf16[1,104,1600]{2,1,0:T(8,128)(2,1)} %collective-permute-done.10), channel_id=1, source_target_pairs={{32,36},{33,37},{34,38},{35,39},{36,40},{37,41},{38,42},{39,43},{4... | collective-permute-start | bytes 998408 | tf_op jit(solution)/shard_map/ppermute | solution.py:24
  67.6 4.5 %copy-start.1 = (bf16[4,104,1600]{2,1,0:T(8,128)(2,1)S(1)}, bf16[4,104,1600]{2,1,0:T(8,128)(2,1)}, u32[]{:S(2)}) copy-start(bf16[4,104,1600]{2,1,0:T(8,128)(2,1)} %copy-done) | copy-start | bytes 3993604
  67.6 22.7 %collective-permute-start.14 = (bf16[4,104,1600]{2,1,0:T(8,128)(2,1)S(1)}, bf16[4,104,1600]{2,1,0:T(8,128)(2,1)S(1)}, u32[]{:S(2)}, u32[]{:S(2)}) collective-permute-start(bf16[4,104,1600]{2,1,0:T(8,128)(2,1)S(1)} %get-tuple-element.27), channel_id=1, source_target_pairs={{0,28},{1,29},{2,30},{3,31},{4,0},{5,1},{6,2},{7,3},{8,4},{9,5},{1... | collective-permute-start | bytes 3993608 | tf_op jit(solution)/shard_map/ppermute | solution.py:24
  68.3 14.5 %collective-permute-start.15 = (bf16[800,512]{1,0:T(8,128)(2,1)S(1)}, bf16[800,512]{1,0:T(8,128)(2,1)S(1)}, u32[]{:S(2)}, u32[]{:S(2)}) collective-permute-start(bf16[800,512]{1,0:T(8,128)(2,1)S(1)} %slice.12), channel_id=1, source_target_pairs={{0,64},{64,128},{128,192},{192,0},{1,65},{65,129},{129,193},{193,1... | collective-permute-start | bytes 2457608 | tf_op jit(solution)/shard_map/ppermute | solution.py:13
  68.9 21.4 %collective-permute-start.16 = (bf16[800,512]{1,0:T(8,128)(2,1)S(1)}, bf16[800,512]{1,0:T(8,128)(2,1)S(1)}, u32[]{:S(2)}, u32[]{:S(2)}) collective-permute-start(bf16[800,512]{1,0:T(8,128)(2,1)S(1)} %slice.13), channel_id=1, source_target_pairs={{0,192},{64,0},{128,64},{192,128},{1,193},{65,1},{129,65},{193,129... | collective-permute-start | bytes 2457608 | tf_op jit(solution)/shard_map/ppermute | solution.py:13
  71.2 19.6 %collective-permute-start.13 = (bf16[4,104,1600]{2,1,0:T(8,128)(2,1)S(1)}, bf16[4,104,1600]{2,1,0:T(8,128)(2,1)S(1)}, u32[]{:S(2)}, u32[]{:S(2)}) collective-permute-start(bf16[4,104,1600]{2,1,0:T(8,128)(2,1)S(1)} %get-tuple-element.28), channel_id=1, source_target_pairs={{0,4},{1,5},{2,6},{3,7},{4,8},{5,9},{6,10},{7,11},{8,12},{9,13},{1... | collective-permute-start | bytes 3993608 | tf_op jit(solution)/shard_map/ppermute | solution.py:24
  72.1 25.8 %collective-permute-start.17 = (bf16[4,104,1600]{2,1,0:T(8,128)(2,1)S(1)}, bf16[4,104,1600]{2,1,0:T(8,128)(2,1)S(1)}, u32[]{:S(2)}, u32[]{:S(2)}) collective-permute-start(bf16[4,104,1600]{2,1,0:T(8,128)(2,1)S(1)} %copy-done.1), channel_id=1, source_target_pairs={{0,32},{32,0},{1,33},{33,1},{2,34},{34,2},{3,35},{35,3},{4,36},{36... | collective-permute-start | bytes 3993608 | tf_op jit(solution)/shard_map/ppermute | solution.py:28
  82.8 15.0 %collective-permute-start.19 = (bf16[4,104,1600]{2,1,0:T(8,128)(2,1)}, bf16[4,104,1600]{2,1,0:T(8,128)(2,1)S(1)}, u32[]{:S(2)}, u32[]{:S(2)}) collective-permute-start(bf16[4,104,1600]{2,1,0:T(8,128)(2,1)} %collective-permute-done.5), channel_id=1, source_target_pairs={{0,32},{32,0},{1,33},{33,1},{2,34},{34,2},{3,35},{35,3},{4,36},{36... | collective-permute-start | bytes 3993608 | tf_op jit(solution)/shard_map/ppermute | solution.py:28
  90.3 8.3 %collective-permute-start.18 = (bf16[4,104,1600]{2,1,0:T(8,128)(2,1)}, bf16[4,104,1600]{2,1,0:T(8,128)(2,1)S(1)}, u32[]{:S(2)}, u32[]{:S(2)}) collective-permute-start(bf16[4,104,1600]{2,1,0:T(8,128)(2,1)} %collective-permute-done.3), channel_id=1, source_target_pairs={{0,32},{32,0},{1,33},{33,1},{2,34},{34,2},{3,35},{35,3},{4,36},{36... | collective-permute-start | bytes 3993608 | tf_op jit(solution)/shard_map/ppermute | solution.py:28
  90.3 8.3 %collective-permute-start.21 = (bf16[4,104,1600]{2,1,0:T(8,128)(2,1)S(1)}, bf16[4,104,1600]{2,1,0:T(8,128)(2,1)S(1)}, u32[]{:S(2)}, u32[]{:S(2)}) collective-permute-start(bf16[4,104,1600]{2,1,0:T(8,128)(2,1)S(1)} %get-tuple-element.27), channel_id=1, source_target_pairs={{0,32},{32,0},{1,33},{33,1},{2,34},{34,2},{3,35},{35,3},{4,36},{36... | collective-permute-start | bytes 3993608 | tf_op jit(solution)/shard_map/ppermute | solution.py:28
  90.8 20.1 %collective-permute-start.20 = (bf16[4,104,1600]{2,1,0:T(8,128)(2,1)}, bf16[4,104,1600]{2,1,0:T(8,128)(2,1)S(1)}, u32[]{:S(2)}, u32[]{:S(2)}) collective-permute-start(bf16[4,104,1600]{2,1,0:T(8,128)(2,1)} %collective-permute-done.4), channel_id=1, source_target_pairs={{0,32},{32,0},{1,33},{33,1},{2,34},{34,2},{3,35},{35,3},{4,36},{36... | collective-permute-start | bytes 3993608 | tf_op jit(solution)/shard_map/ppermute | solution.py:28
  97.9 25.2 %collective-permute-start.22 = (bf16[4,104,1600]{2,1,0:T(8,128)(2,1)S(1)}, bf16[4,104,1600]{2,1,0:T(8,128)(2,1)S(1)}, u32[]{:S(2)}, u32[]{:S(2)}) collective-permute-start(bf16[4,104,1600]{2,1,0:T(8,128)(2,1)S(1)} %collective-permute-done.13), channel_id=1, source_target_pairs={{0,32},{32,0},{1,33},{33,1},{2,34},{34,2},{3,35},{35,3},{4,36},{36... | collective-permute-start | bytes 3993608 | tf_op jit(solution)/shard_map/ppermute | solution.py:28
  97.9 25.2 %collective-permute-start.23 = (bf16[4,104,1600]{2,1,0:T(8,128)(2,1)S(1)}, bf16[4,104,1600]{2,1,0:T(8,128)(2,1)S(1)}, u32[]{:S(2)}, u32[]{:S(2)}) collective-permute-start(bf16[4,104,1600]{2,1,0:T(8,128)(2,1)S(1)} %collective-permute-done.14), channel_id=1, source_target_pairs={{0,32},{32,0},{1,33},{33,1},{2,34},{34,2},{3,35},{35,3},{4,36},{36... | collective-permute-start | bytes 3993608 | tf_op jit(solution)/shard_map/ppermute | solution.py:28
  98.5 12.4 %copy-start.2 = (f32[512,1600]{0,1:T(8,128)S(1)}, f32[512,1600]{0,1:T(8,128)}, u32[]{:S(2)}) copy-start(f32[512,1600]{0,1:T(8,128)} %param.3) | copy-start | bytes 9830404
  98.5 11.4 %collective-permute-start.24 = (bf16[2,104,1600]{2,1,0:T(8,128)(2,1)S(1)}, bf16[2,104,1600]{2,1,0:T(8,128)(2,1)S(1)}, u32[]{:S(2)}, u32[]{:S(2)}) collective-permute-start(bf16[2,104,1600]{2,1,0:T(8,128)(2,1)S(1)} %slice.14), channel_id=1, source_target_pairs={{0,4},{1,5},{2,6},{3,7},{4,8},{5,9},{6,10},{7,11},{8,12},{9,13},{1... | collective-permute-start | bytes 1996808 | tf_op jit(solution)/shard_map/ppermute | solution.py:24
  98.6 12.3 %collective-permute-start.25 = (bf16[2,104,1600]{2,1,0:T(8,128)(2,1)S(1)}, bf16[2,104,1600]{2,1,0:T(8,128)(2,1)S(1)}, u32[]{:S(2)}, u32[]{:S(2)}) collective-permute-start(bf16[2,104,1600]{2,1,0:T(8,128)(2,1)S(1)} %slice.15), channel_id=1, source_target_pairs={{0,28},{1,29},{2,30},{3,31},{4,0},{5,1},{6,2},{7,3},{8,4},{9,5},{1... | collective-permute-start | bytes 1996808 | tf_op jit(solution)/shard_map/ppermute | solution.py:24
  109.9 18.5 %collective-permute-start.26 = (bf16[2,104,1600]{2,1,0:T(8,128)(2,1)S(1)}, bf16[2,104,1600]{2,1,0:T(8,128)(2,1)S(1)}, u32[]{:S(2)}, u32[]{:S(2)}) collective-permute-start(bf16[2,104,1600]{2,1,0:T(8,128)(2,1)S(1)} %collective-permute-done.24), channel_id=1, source_target_pairs={{0,32},{32,0},{1,33},{33,1},{2,34},{34,2},{3,35},{35,3},{4,36},{36... | collective-permute-start | bytes 1996808 | tf_op jit(solution)/shard_map/ppermute | solution.py:28
  110.9 17.6 %collective-permute-start.27 = (bf16[2,104,1600]{2,1,0:T(8,128)(2,1)S(1)}, bf16[2,104,1600]{2,1,0:T(8,128)(2,1)S(1)}, u32[]{:S(2)}, u32[]{:S(2)}) collective-permute-start(bf16[2,104,1600]{2,1,0:T(8,128)(2,1)S(1)} %collective-permute-done.25), channel_id=1, source_target_pairs={{0,32},{32,0},{1,33},{33,1},{2,34},{34,2},{3,35},{35,3},{4,36},{36... | collective-permute-start | bytes 1996808 | tf_op jit(solution)/shard_map/ppermute | solution.py:28

commit v4 on v3

--- a/solution.py
+++ b/solution.py
@@ -7,6 +7,7 @@
 
 Z, Y = 8, 4
 VMEM = 16 << 20
+LONGER = 192
 
 
 def shift(array, size, step):
@@ -33,9 +34,12 @@
     return jnp.pad(parts, ((0, 0), (0, -rows % 8), (0, 0)))
 
 
-def gather(block, amplitudes, rows):
+def gather(block, height, amplitudes, rows, multiply_first):
+    count = amplitudes.shape[0]
     along, back = ((0, 1), (1, 0)), ((0, -1), (-1, 0))
-    after, before = shift(amplitudes, rows, -1), shift(amplitudes, rows, 1)
+    up, down = ((1, 0), (0, 1)), ((-1, 0), (0, -1))
+    longer = jnp.pad(amplitudes, ((0, LONGER), (0, 0)))
+    after, before = shift(longer, rows, -1), shift(longer, rows, 1)
     a1 = travel(block, *along)
     b1 = travel(block, *back)
     a2 = travel(a1, *along)
@@ -45,18 +49,19 @@
     b3 = travel(b2, None, back[1])
     a4 = travel(a3, None, along[1])
     rest = jnp.concatenate([b2, a3, b3, a4])
-    up, down = ((1, 0), (0, 1)), ((-1, 0), (0, -1))
     u1, d1 = travel(pack, *up), travel(pack, *down)
     u2, d2 = travel(u1, *up), travel(d1, down[0], None)
-    u2, d2, after, before = lax.optimization_barrier((u2, d2, after, before))
-    half = amplitudes.shape[0] // 2
-    far_low, far_high = shift(before[:half], rows, 1), shift(after[half:], rows, -1)
+    far_low, far_high = shift(before[: count // 2], rows, 1), shift(after[count // 2 : count], rows, -1)
+    u2, d2, far_low, far_high = lax.optimization_barrier((u2, d2, far_low, far_high))
     first = lax.axis_index("col") == 0
     kept = jnp.where(first, d2, rest)
     u3, d3 = travel(jnp.where(first, u2, rest), *up), travel(kept, *down)
-    u3, d3, far_low, far_high = lax.optimization_barrier((u3, d3, far_low, far_high))
+    factors = arrange(amplitudes, after, far_low, far_high, before, rows, height, [20, 8, 4])
+    early = [pack, u1, d1, u2, kept]
+    total = multiply_first(factors[0], early + [swap(piece) for piece in early])
+    u3, d3, total = lax.optimization_barrier((u3, d3, total))
     u4, d4 = travel(u3[:2], *up), travel(d3[2:], *down)
-    return [pack, u1, d1, u2, kept, u3, d3, u4, d4], (after, far_low, far_high, before)
+    return factors[1:], total, [u3, d3, swap(u3), swap(d3)], [u4, d4, swap(u4), swap(d4)]
 
 
 def arrange(own, after, far_low, far_high, before, rows, height, cuts):
@@ -73,7 +78,7 @@
         for ref, step, start in sources:
             block_row = lax.rem(x + step, rows)
             half = block_row // (rows // 2)
-            for i in range(ref.shape[0] // height):
+            for i in range(min(count, ref.shape[0] // height)):
                 there = lax.rem(block_row, rows // 2) * count + start + i
                 dz = lax.rem(there // Y - z + Z, Z)
                 dy = lax.rem((start + i) % Y - y + Y, Y)
@@ -99,42 +104,73 @@
     )(own, after, far_low, far_high, before)
 
 
-def accumulate(total, factor, mine, other, tile=256):
-    columns, pairs = total.shape
-    pieces = [piece.reshape(-1, columns) for piece in mine + other]
-    depth = factor.shape[-1]
+def products(factor_ref, piece_refs, start, width):
+    share = 0.0
+    count = len(piece_refs) // 2
+    for side in range(2):
+        part = jnp.concatenate([ref[:, pl.ds(start, width)] for ref in piece_refs[side * count :][:count]])
+        share += jnp.dot(factor_ref[side], part, preferred_element_type=jnp.float32)
+    return share
 
-    def kernel(total_ref, factor_ref, *refs):
-        piece_refs, out_ref = refs[:-1], refs[-1]
 
-        def add(start, width):
-            share = jnp.zeros((pairs, width), jnp.float32)
-            for side in range(2):
-                refs = piece_refs[side * len(mine) :][: len(mine)]
-                part = jnp.concatenate([ref[:, pl.ds(start, width)] for ref in refs])
-                share += jnp.dot(factor_ref[side], part, preferred_element_type=jnp.float32)
-            out_ref[pl.ds(start, width), :] = total_ref[pl.ds(start, width), :] + share.T
+def multiply(body, shape, factor, pieces, *operands, **options):
+    columns = pieces[0].shape[-1]
+    flops = 4 * factor.shape[1] * factor.shape[2] * columns
+    return pl.pallas_call(
+        body,
+        out_shape=jax.ShapeDtypeStruct(shape, jnp.float32),
+        compiler_params=pltpu.CompilerParams(vmem_limit_bytes=VMEM),
+        cost_estimate=pl.CostEstimate(flops=flops, bytes_accessed=flops // 512, transcendentals=0),
+        **options,
+    )(*operands, factor, *[piece.reshape(-1, columns) for piece in pieces])
 
-        whole = columns // tile
 
-        @pl.loop(0, whole)
-        def _(i):
-            add(pl.multiple_of(i * tile, tile), tile)
+def tiles(columns, tile=256):
+    return [(start, min(tile, columns - start)) for start in range(0, columns, tile)]
 
-        if columns % tile:
-            add(whole * tile, columns % tile)
 
-    return pl.pallas_call(
-        kernel,
-        out_shape=jax.ShapeDtypeStruct(total.shape, total.dtype),
-        compiler_params=pltpu.CompilerParams(vmem_limit_bytes=VMEM),
-        cost_estimate=pl.CostEstimate(
-            flops=4 * columns * pairs * depth,
-            bytes_accessed=8 * total.size + 4 * depth * (columns + pairs),
-            transcendentals=0,
-        ),
-        name="accumulate",
-    )(total, factor, *pieces)
+def first_products(factor, pieces):
+    def body(factor_ref, *refs):
+        for start, width in tiles(refs[-1].shape[1]):
+            refs[-1][:, pl.ds(start, width)] = products(factor_ref, refs[:-1], start, width)
+
+    return multiply(body, (factor.shape[1], pieces[0].shape[-1]), factor, pieces, name="first")
+
+
+def more_products(residual, total, factor, pieces):
+    def body(residual_ref, total_ref, factor_ref, *refs):
+        for start, width in tiles(refs[-1].shape[0]):
+            part = pl.ds(start, width)
+            share = total_ref[:, part] + products(factor_ref, refs[:-1], start, width)
+            refs[-1][part, :] = residual_ref[part, :] + share.T
+
+    return multiply(body, residual.shape, factor, pieces, residual, total, name="more")
+
+
+def last_products(total, factor, pieces):
+    parts = tiles(total.shape[0])
+
+    def body(total_ref, factor_ref, *refs):
+        *piece_refs, out_ref, held, sems = refs
+        copies = []
+        for number, (start, width) in enumerate(parts):
+            part = pl.ds(start, width)
+            held[part, :] = total_ref[part, :] + products(factor_ref, piece_refs, start, width).T
+            copies.append(pltpu.make_async_copy(held.at[part], out_ref.at[part], sems.at[number]))
+            copies[-1].start()
+        for copy in copies:
+            copy.wait()
+
+    return multiply(
+        body,
+        total.shape,
+        factor,
+        pieces,
+        total,
+        out_specs=pl.BlockSpec(memory_space=pl.ANY),
+        scratch_shapes=[pltpu.VMEM(total.shape, jnp.float32), pltpu.SemaphoreType.DMA((len(parts),))],
+        name="last",
+    )
 
 
 def solution(mesh):
@@ -142,13 +178,10 @@
 
     def per_device(residual_in, integrals, amplitudes):
         height = integrals.shape[1]
-        mine, others = gather(padded(integrals.T, height), amplitudes, rows)
-        other = [swap(piece) for piece in mine]
-        factors = arrange(amplitudes, *others, rows, height, [20, 8, 4])
-        total = residual_in.T
-        for factor, a, b in zip(factors, (0, 5, 7), (5, 7, 9)):
-            total = accumulate(total, factor, mine[a:b], other[a:b])
-        return total.T
+        block = padded(integrals.T, height)
+        factors, total, more, last = gather(block, height, amplitudes, rows, first_products)
+        total = more_products(residual_in.T, total, factors[0], more)
+        return last_products(total, factors[1], last).T
 
     placed = (P(("col", "depth"), "row"), P("row", ("col", "depth")), P("row", ("col", "depth")))
     return jax.shard_map(

time: 134 us -> 133 us (level)
  starting transfers between devices: 53.4 us -> 42.5 us
  waiting for transfers between devices: 48.1 us -> 57.6 us
  Pallas kernels: 27.6 us -> 23.1 us
  local copies, waits for them, and re-layouts: 4.32 us -> 7.89 us
    ppermute x9, starting transfers between devices: 22.7 us -> 6.47 us  [swap(): return lax.ppermute(array, 'col', [(0, 1), (1, 0)])]
    ppermute x4, waiting for transfers between devices: 4.58 us -> 17.8 us  [shift(): lax.ppermute(array, 'row', [(i, (i + step) % size) for i in range(size)])]
    pallas_call x3, Pallas kernels: 23.1 us -> 18.3 us  [multiply(): pl.pallas_call(body, out_shape=jax.ShapeDtypeStruct(shape, jnp.float32),...]
    ppermute x15, starting transfers between devices: 25.3 us -> 30.1 us  [travel(): return lax.ppermute(array, ('col', 'depth'), pairs)]
    ppermute x15, waiting for transfers between devices: 43.5 us -> 39.7 us  [travel(): return lax.ppermute(array, ('col', 'depth'), pairs)]
    slice x2, local copies, waits for them, and re-layouts: 0.11 us -> 2.14 us  [the longest x1 1.2 us: gather(): before[:count // 2]]
    pad x0 -> x1, local copies, waits for them, and re-layouts: none -> 1.55 us  [gather(): longer = jnp.pad(amplitudes, ((0, LONGER), (0, 0)))]
    unnamed x9 -> x7, local copies, waits for them, and re-layouts: 3.07 us -> 3.06 us
  transfers between devices with their start and end apart: 28 -> 28, of which waited for: 9 -> 9; matrix products, arithmetic and copies ran while one was open for 2% -> 6% of each run, Pallas kernels for 16% -> 15%
where the time goes in v4:
time: 133 us
  waiting for transfers between devices  57.6 us (43%)
  starting transfers between devices  42.5 us (32%)
  Pallas kernels  23.1 us (17%)
  local copies, waits for them, and re-layouts  7.89 us (6%)
  other arithmetic  1.48 us (1%)
    ppermute x15, waiting for transfers between devices, travel(): return lax.ppermute(array, ('col', 'depth'), pairs)  39.7 us
    ppermute x15, starting transfers between devices, travel(): return lax.ppermute(array, ('col', 'depth'), pairs)  30.1 us
    pallas_call x3, Pallas kernels, multiply(): pl.pallas_call(body, out_shape=jax.ShapeDtypeStruct(shape, jnp.float32),...  18.3 us
    ppermute x4, waiting for transfers between devices, shift(): lax.ppermute(array, 'row', [(i, (i + step) % size) for i in range(size)])  17.8 us
    ppermute x9, starting transfers between devices, swap(): return lax.ppermute(array, 'col', [(0, 1), (1, 0)])  6.47 us
    ppermute x4, starting transfers between devices, shift(): lax.ppermute(array, 'row', [(i, (i + step) % size) for i in range(size)])  5.9 us
    pallas_call x1, Pallas kernels, arrange(): pl.pallas_call(kernel, out_shape=[jax.ShapeDtypeStruct((2, width, blocks...  4.78 us
    unnamed x7, local copies, waits for them, and re-layouts  3.06 us
  transfers between devices with their start and end apart: 28, of which 9 were waited for; matrix products, arithmetic and copies ran while one was open for 6% of the time, Pallas kernels for 15%

profile of v4, /device:TPU:1, one launch (start us, length us, event | category | flops | bytes accessed | tf_op | source)
XLA Modules:
  0.0 132.9 jit_solution(4808799780013735403)
XLA Ops:
  0.0 1.0 pad.8
  1.0 2.5 %collective-permute-start = (bf16[1,104,1600]{2,1,0:T(8,128)(2,1)S(1)}, bf16[1,104,1600]{2,1,0:T(8,128)(2,1)S(1)}, u32[]{:S(2)}, u32[]{:S(2)}) collective-permute-start(bf16[1,104,1600]{2,1,0:T(8,128)(2,1)S(1)} %pad.8), channel_id=1, source_target_pairs={{0,1},{1,2},{2,3},{3,0},{4,5},{5,6},{6,7},{7,4},{8,9},{9,10},{10,1... | collective-permute-start | bytes 998408 | tf_op jit(solution)/shard_map/ppermute | solution.py:25
  3.6 4.0 %collective-permute-start.1 = (bf16[1,104,1600]{2,1,0:T(8,128)(2,1)S(1)}, bf16[1,104,1600]{2,1,0:T(8,128)(2,1)S(1)}, u32[]{:S(2)}, u32[]{:S(2)}) collective-permute-start(bf16[1,104,1600]{2,1,0:T(8,128)(2,1)S(1)} %pad.8), channel_id=1, source_target_pairs={{0,3},{1,0},{2,1},{3,2},{4,7},{5,4},{6,5},{7,6},{8,11},{9,8},{10,9... | collective-permute-start | bytes 998408 | tf_op jit(solution)/shard_map/ppermute | solution.py:25
  7.6 4.8 %collective-permute-done = bf16[1,104,1600]{2,1,0:T(8,128)(2,1)S(1)} collective-permute-done((bf16[1,104,1600]{2,1,0:T(8,128)(2,1)S(1)}, bf16[1,104,1600]{2,1,0:T(8,128)(2,1)S(1)}, u32[]{:S(2)}, u32[]{:S(2)}) %collective-permute-start) | collective-permute-done | bytes 332832 | tf_op jit(solution)/shard_map/ppermute | solution.py:25
  12.4 0.0 collective-permute-start.2
  12.4 1.6 %pad.9 = bf16[1792,512]{1,0:T(8,128)(2,1)S(1)} pad(bf16[1600,512]{1,0:T(8,128)(2,1)} %own_ref.1, bf16[]{:T(256)} %constant.9.clone.1), padding=0_192x0_0 | pad | bytes 3473410 | tf_op jit(solution)/shard_map/jit(_pad)/pad | solution.py:41
  14.0 2.3 %collective-permute-start.9 = (bf16[1792,512]{1,0:T(8,128)(2,1)S(1)}, bf16[1792,512]{1,0:T(8,128)(2,1)S(1)}, u32[]{:S(2)}, u32[]{:S(2)}) collective-permute-start(bf16[1792,512]{1,0:T(8,128)(2,1)S(1)} %pad.9), channel_id=1, source_target_pairs={{0,192},{64,0},{128,64},{192,128},{1,193},{65,1},{129,65},{193,129... | collective-permute-start | bytes 5505032 | tf_op jit(solution)/shard_map/ppermute | solution.py:14
  16.3 0.0 collective-permute-start.7
  16.3 0.0 collective-permute-done.1
  16.3 3.9 %collective-permute-done.2 = bf16[1,104,1600]{2,1,0:T(8,128)(2,1)} collective-permute-done((bf16[1,104,1600]{2,1,0:T(8,128)(2,1)S(1)}, bf16[1,104,1600]{2,1,0:T(8,128)(2,1)}, u32[]{:S(2)}, u32[]{:S(2)}) %collective-permute-start.2) | collective-permute-done | bytes 332832 | tf_op jit(solution)/shard_map/ppermute | solution.py:25
  20.2 1.2 pad_maximum_fusion
  21.4 0.8 collective-permute-start.3
  22.2 2.1 %collective-permute-start.5 = (bf16[4,104,1600]{2,1,0:T(8,128)(2,1)S(1)}, bf16[4,104,1600]{2,1,0:T(8,128)(2,1)}, u32[]{:S(2)}, u32[]{:S(2)}) collective-permute-start(bf16[4,104,1600]{2,1,0:T(8,128)(2,1)S(1)} %pad_maximum_fusion), channel_id=1, source_target_pairs={{0,28},{1,29},{2,30},{3,31},{4,0},{5,1},{6,2},{7,3},{8,4},{9,5},{1... | collective-permute-start | bytes 3993608 | tf_op jit(solution)/shard_map/ppermute | solution.py:25
  24.3 2.1 %collective-permute-start.11 = (bf16[1,104,1600]{2,1,0:T(8,128)(2,1)S(1)}, bf16[1,104,1600]{2,1,0:T(8,128)(2,1)}, u32[]{:S(2)}, u32[]{:S(2)}) collective-permute-start(bf16[1,104,1600]{2,1,0:T(8,128)(2,1)S(1)} %collective-permute-done.1), channel_id=1, source_target_pairs={{32,60},{33,61},{34,62},{35,63},{36,32},{37,33},{38,34},{39,35},{4... | collective-permute-start | bytes 998408 | tf_op jit(solution)/shard_map/ppermute | solution.py:25
  26.4 13.9 %collective-permute-done.3 = bf16[4,104,1600]{2,1,0:T(8,128)(2,1)} collective-permute-done((bf16[4,104,1600]{2,1,0:T(8,128)(2,1)S(1)}, bf16[4,104,1600]{2,1,0:T(8,128)(2,1)}, u32[]{:S(2)}, u32[]{:S(2)}) %collective-permute-start.3) | collective-permute-done | bytes 1331232 | tf_op jit(solution)/shard_map/ppermute | solution.py:25
  40.4 0.0 collective-permute-start.4
  40.4 0.0 collective-permute-done.5
  40.4 1.7 %collective-permute-start.6 = (bf16[4,104,1600]{2,1,0:T(8,128)(2,1)}, bf16[4,104,1600]{2,1,0:T(8,128)(2,1)}, u32[]{:S(2)}, u32[]{:S(2)}) collective-permute-start(bf16[4,104,1600]{2,1,0:T(8,128)(2,1)} %collective-permute-done.5), channel_id=1, source_target_pairs={{0,28},{1,29},{2,30},{3,31},{4,0},{5,1},{6,2},{7,3},{8,4},{9,5},{1... | collective-permute-start | bytes 3993608 | tf_op jit(solution)/shard_map/ppermute | solution.py:25
  42.1 13.7 %collective-permute-done.9.after_ref = bf16[1792,512]{1,0:T(8,128)(2,1)S(1)} collective-permute-done((bf16[1792,512]{1,0:T(8,128)(2,1)S(1)}, bf16[1792,512]{1,0:T(8,128)(2,1)S(1)}, u32[]{:S(2)}, u32[]{:S(2)}) %collective-permute-start.9) | collective-permute-done | bytes 1835040 | tf_op jit(solution)/shard_map/ppermute | solution.py:14
  55.8 1.9 %collective-permute-start.12 = (bf16[1,104,1600]{2,1,0:T(8,128)(2,1)}, bf16[1,104,1600]{2,1,0:T(8,128)(2,1)}, u32[]{:S(2)}, u32[]{:S(2)}) collective-permute-start(bf16[1,104,1600]{2,1,0:T(8,128)(2,1)} %collective-permute-done.2), channel_id=1, source_target_pairs={{32,36},{33,37},{34,38},{35,39},{36,40},{37,41},{38,42},{39,43},{4... | collective-permute-start | bytes 998408 | tf_op jit(solution)/shard_map/ppermute | solution.py:25
  57.8 0.9 slice.17
  58.7 0.0 collective-permute-done.11
  58.7 3.5 %collective-permute-start.10 = (bf16[800,512]{1,0:T(8,128)(2,1)}, bf16[800,512]{1,0:T(8,128)(2,1)}, u32[]{:S(2)}, u32[]{:S(2)}) collective-permute-start(bf16[800,512]{1,0:T(8,128)(2,1)} %slice.17), channel_id=1, source_target_pairs={{0,192},{64,0},{128,64},{192,128},{1,193},{65,1},{129,65},{193,129... | collective-permute-start | bytes 2457608 | tf_op jit(solution)/shard_map/ppermute | solution.py:14
  62.2 0.0 collective-permute-done.7.before_ref
  62.2 4.6 %collective-permute-start.13 = (bf16[1,104,1600]{2,1,0:T(8,128)(2,1)}, bf16[1,104,1600]{2,1,0:T(8,128)(2,1)}, u32[]{:S(2)}, u32[]{:S(2)}) collective-permute-start(bf16[1,104,1600]{2,1,0:T(8,128)(2,1)} %collective-permute-done.11), channel_id=1, source_target_pairs={{32,60},{33,61},{34,62},{35,63},{36,32},{37,33},{38,34},{39,35},{4... | collective-permute-start | bytes 998408 | tf_op jit(solution)/shard_map/ppermute | solution.py:25
  66.8 1.2 slice.16
  68.0 0.0 collective-permute-done.12
  68.0 0.1 collective-permute-start.8
  68.1 1.0 constant_dynamic-update-slice_fusion.3
  69.1 2.2 %collective-permute-done.13 = bf16[1,104,1600]{2,1,0:T(8,128)(2,1)} collective-permute-done((bf16[1,104,1600]{2,1,0:T(8,128)(2,1)}, bf16[1,104,1600]{2,1,0:T(8,128)(2,1)}, u32[]{:S(2)}, u32[]{:S(2)}) %collective-permute-start.13) | collective-permute-done | bytes 332832 | tf_op jit(solution)/shard_map/ppermute | solution.py:25
  71.3 4.9 %collective-permute-start.14 = (bf16[1,104,1600]{2,1,0:T(8,128)(2,1)}, bf16[1,104,1600]{2,1,0:T(8,128)(2,1)S(1)}, u32[]{:S(2)}, u32[]{:S(2)}) collective-permute-start(bf16[1,104,1600]{2,1,0:T(8,128)(2,1)} %collective-permute-done.12), channel_id=1, source_target_pairs={{32,36},{33,37},{34,38},{35,39},{36,40},{37,41},{38,42},{39,43},{4... | collective-permute-start | bytes 998408 | tf_op jit(solution)/shard_map/ppermute | solution.py:25
  76.2 1.0 constant_dynamic-update-slice_fusion.2
  77.2 1.0 constant_dynamic-update-slice_fusion.1
  78.2 3.4 %collective-permute-done.14 = bf16[1,104,1600]{2,1,0:T(8,128)(2,1)S(1)} collective-permute-done((bf16[1,104,1600]{2,1,0:T(8,128)(2,1)}, bf16[1,104,1600]{2,1,0:T(8,128)(2,1)S(1)}, u32[]{:S(2)}, u32[]{:S(2)}) %collective-permute-start.14) | collective-permute-done | bytes 332832 | tf_op jit(solution)/shard_map/ppermute | solution.py:25
  81.7 0.0 collective-permute-start.17
  81.7 0.0 collective-permute-done.10.high_ref
  81.7 0.5 collective-permute-start.19
  82.2 0.0 copy-start
  82.2 4.1 %collective-permute-done.8.low_ref = bf16[800,512]{1,0:T(8,128)(2,1)S(1)} collective-permute-done((bf16[800,512]{1,0:T(8,128)(2,1)S(1)}, bf16[800,512]{1,0:T(8,128)(2,1)S(1)}, u32[]{:S(2)}, u32[]{:S(2)}) %collective-permute-start.8) | collective-permute-done | bytes 819232 | tf_op jit(solution)/shard_map/ppermute | solution.py:14
  86.4 0.3 broadcast_select_fusion
  86.6 2.3 %collective-permute-start.21 = (bf16[4,104,1600]{2,1,0:T(8,128)(2,1)S(1)}, bf16[4,104,1600]{2,1,0:T(8,128)(2,1)S(1)}, u32[]{:S(2)}, u32[]{:S(2)}) collective-permute-start(bf16[4,104,1600]{2,1,0:T(8,128)(2,1)S(1)} %get-tuple-element.25), channel_id=1, source_target_pairs={{0,32},{32,0},{1,33},{33,1},{2,34},{34,2},{3,35},{35,3},{4,36},{36... | collective-permute-start | bytes 3993608 | tf_op jit(solution)/shard_map/ppermute | solution.py:29
  89.0 0.1 collective-permute-start.20
  89.1 2.5 %collective-permute-start.16 = (bf16[4,104,1600]{2,1,0:T(8,128)(2,1)S(1)}, bf16[4,104,1600]{2,1,0:T(8,128)(2,1)S(1)}, u32[]{:S(2)}, u32[]{:S(2)}) collective-permute-start(bf16[4,104,1600]{2,1,0:T(8,128)(2,1)S(1)} %get-tuple-element.25), channel_id=1, source_target_pairs={{0,28},{1,29},{2,30},{3,31},{4,0},{5,1},{6,2},{7,3},{8,4},{9,5},{1... | collective-permute-start | bytes 3993608 | tf_op jit(solution)/shard_map/ppermute | solution.py:25
  91.6 0.0 collective-permute-done.19
  91.6 0.0 collective-permute-start.15
  91.6 4.8 %arrange.1 = (bf16[2,512,2080]{2,1,0:T(8,128)(2,1)S(1)}, bf16[2,512,832]{2,1,0:T(8,128)(2,1)S(1)}, bf16[2,512,416]{2,1,0:T(8,128)(2,1)S(1)}) custom-call(bf16[1600,512]{1,0:T(8,128)(2,1)S(1)} %copy-done, bf16[1792,512]{1,0:T(8,128)(2,1)S(1)} %collective-permute-done.9.after_ref, bf16[800,512]{1,0:T(8,128)(2,1)S(1)} %collective-permute-done.8.low_ref, ...), custom_call_target="tpu_custom_call" | custom-call | bytes 13107200 | tf_op jit(solution)/shard_map/arrange/pallas_call | solution.py:97
  96.4 0.0 collective-permute-done.18
  96.4 0.0 collective-permute-done.20
  96.4 0.0 copy-start.1
  96.5 11.0 %first.1.total_ref = f32[512,1600]{1,0:T(8,128)S(1)} custom-call(bf16[2,512,2080]{2,1,0:T(8,128)(2,1)S(1)} %get-tuple-element.19.factor_ref, bf16[416,1600]{1,0:T(8,128)(2,1)S(1)} %bitcast.26, bf16[416,1600]{1,0:T(8,128)(2,1)} %bitcast.4.refs_1_, bf16[416,1600]{1,0:T(8,128)(2,1)} %bitcast.5.refs_2_, bf16[416,1600]{1,0:T(8,128)(2,1)} %bitcast.6.refs_3_, ...), custom_call_target="tpu_custom_call" | custom-call | flops 6815744000 | bytes 13312000 | tf_op jit(solution)/shard_map/first/pallas_call | solution.py:119
  107.4 0.0 collective-permute-done.16
  107.4 2.9 %collective-permute-done.15 = bf16[4,104,1600]{2,1,0:T(8,128)(2,1)S(1)} collective-permute-done((bf16[4,104,1600]{2,1,0:T(8,128)(2,1)S(1)}, bf16[4,104,1600]{2,1,0:T(8,128)(2,1)S(1)}, u32[]{:S(2)}, u32[]{:S(2)}) %collective-permute-start.15) | collective-permute-done | bytes 1331232 | tf_op jit(solution)/shard_map/ppermute | solution.py:25
  110.4 2.2 %collective-permute-start.22 = (bf16[4,104,1600]{2,1,0:T(8,128)(2,1)S(1)}, bf16[4,104,1600]{2,1,0:T(8,128)(2,1)S(1)}, u32[]{:S(2)}, u32[]{:S(2)}) collective-permute-start(bf16[4,104,1600]{2,1,0:T(8,128)(2,1)S(1)} %collective-permute-done.15), channel_id=1, source_target_pairs={{0,32},{32,0},{1,33},{33,1},{2,34},{34,2},{3,35},{35,3},{4,36},{36... | collective-permute-start | bytes 3993608 | tf_op jit(solution)/shard_map/ppermute | solution.py:29
  112.5 0.0 collective-permute-start.23
  112.5 0.1 slice.14
  112.6 1.4 %collective-permute-start.24 = (bf16[2,104,1600]{2,1,0:T(8,128)(2,1)S(1)}, bf16[2,104,1600]{2,1,0:T(8,128)(2,1)S(1)}, u32[]{:S(2)}, u32[]{:S(2)}) collective-permute-start(bf16[2,104,1600]{2,1,0:T(8,128)(2,1)S(1)} %slice.14), channel_id=1, source_target_pairs={{0,4},{1,5},{2,6},{3,7},{4,8},{5,9},{6,10},{7,11},{8,12},{9,13},{1... | collective-permute-start | bytes 1996808 | tf_op jit(solution)/shard_map/ppermute | solution.py:25
  113.9 0.1 slice.15
  114.0 1.5 %collective-permute-start.25 = (bf16[2,104,1600]{2,1,0:T(8,128)(2,1)S(1)}, bf16[2,104,1600]{2,1,0:T(8,128)(2,1)S(1)}, u32[]{:S(2)}, u32[]{:S(2)}) collective-permute-start(bf16[2,104,1600]{2,1,0:T(8,128)(2,1)S(1)} %slice.15), channel_id=1, source_target_pairs={{0,28},{1,29},{2,30},{3,31},{4,0},{5,1},{6,2},{7,3},{8,4},{9,5},{1... | collective-permute-start | bytes 1996808 | tf_op jit(solution)/shard_map/ppermute | solution.py:25
  115.5 8.5 %collective-permute-done.24 = bf16[2,104,1600]{2,1,0:T(8,128)(2,1)S(1)} collective-permute-done((bf16[2,104,1600]{2,1,0:T(8,128)(2,1)S(1)}, bf16[2,104,1600]{2,1,0:T(8,128)(2,1)S(1)}, u32[]{:S(2)}, u32[]{:S(2)}) %collective-permute-start.24) | collective-permute-done | bytes 665632 | tf_op jit(solution)/shard_map/ppermute | solution.py:25
  124.0 1.4 %collective-permute-start.26 = (bf16[2,104,1600]{2,1,0:T(8,128)(2,1)S(1)}, bf16[2,104,1600]{2,1,0:T(8,128)(2,1)S(1)}, u32[]{:S(2)}, u32[]{:S(2)}) collective-permute-start(bf16[2,104,1600]{2,1,0:T(8,128)(2,1)S(1)} %collective-permute-done.24), channel_id=1, source_target_pairs={{0,32},{32,0},{1,33},{33,1},{2,34},{34,2},{3,35},{35,3},{4,36},{36... | collective-permute-start | bytes 1996808 | tf_op jit(solution)/shard_map/ppermute | solution.py:29
  125.4 0.0 collective-permute-start.27
  125.4 0.0 collective-permute-done.23
  125.4 4.0 %more.1.total_ref = f32[1600,512]{1,0:T(8,128)S(1)} custom-call(f32[1600,512]{1,0:T(8,128)S(1)} %bitcast.23, f32[512,1600]{1,0:T(8,128)S(1)} %first.1.total_ref, bf16[2,512,832]{2,1,0:T(8,128)(2,1)S(1)} %get-tuple-element.21.factor_ref, bf16[416,1600]{1,0:T(8,128)(2,1)S(1)} %bitcast.25, bf16[416,1600]{1,0:T(8,128)(2,1)S(1)} %bitcast.24, ...), custom_call_target="tpu_custom_call" | custom-call | flops 2726297600 | bytes 5324800 | tf_op jit(solution)/shard_map/more/pallas_call | solution.py:119
  129.4 3.3 %last.1 = f32[1600,512]{1,0:T(8,128)} custom-call(f32[1600,512]{1,0:T(8,128)S(1)} %more.1.total_ref, bf16[2,512,416]{2,1,0:T(8,128)(2,1)S(1)} %get-tuple-element.24.factor_ref, bf16[208,1600]{1,0:T(8,128)(2,1)S(1)} %bitcast.30, bf16[208,1600]{1,0:T(8,128)(2,1)S(1)} %bitcast.31, bf16[208,1600]{1,0:T(8,128)(2,1)S(1)} %bitcast.32, bf16[208,1600]{1,0:T(8,128)(2,1)S(1)} %bitcast.33), custom_call_target="tpu_custom_call" | custom-call | flops 1363148800 | bytes 2662400 | tf_op jit(solution)/shard_map/last/pallas_call | solution.py:119
  (12 shorter events, 0.1 us)
Async XLA Ops:
  1.0 11.4 %collective-permute-start = (bf16[1,104,1600]{2,1,0:T(8,128)(2,1)S(1)}, bf16[1,104,1600]{2,1,0:T(8,128)(2,1)S(1)}, u32[]{:S(2)}, u32[]{:S(2)}) collective-permute-start(bf16[1,104,1600]{2,1,0:T(8,128)(2,1)S(1)} %pad.8), channel_id=1, source_target_pairs={{0,1},{1,2},{2,3},{3,0},{4,5},{5,6},{6,7},{7,4},{8,9},{9,10},{10,1... | collective-permute-start | bytes 998408 | tf_op jit(solution)/shard_map/ppermute | solution.py:25
  3.6 12.7 %collective-permute-start.1 = (bf16[1,104,1600]{2,1,0:T(8,128)(2,1)S(1)}, bf16[1,104,1600]{2,1,0:T(8,128)(2,1)S(1)}, u32[]{:S(2)}, u32[]{:S(2)}) collective-permute-start(bf16[1,104,1600]{2,1,0:T(8,128)(2,1)S(1)} %pad.8), channel_id=1, source_target_pairs={{0,3},{1,0},{2,1},{3,2},{4,7},{5,4},{6,5},{7,6},{8,11},{9,8},{10,9... | collective-permute-start | bytes 998408 | tf_op jit(solution)/shard_map/ppermute | solution.py:25
  12.4 7.7 %collective-permute-start.2 = (bf16[1,104,1600]{2,1,0:T(8,128)(2,1)S(1)}, bf16[1,104,1600]{2,1,0:T(8,128)(2,1)}, u32[]{:S(2)}, u32[]{:S(2)}) collective-permute-start(bf16[1,104,1600]{2,1,0:T(8,128)(2,1)S(1)} %collective-permute-done), channel_id=1, source_target_pairs={{0,1},{1,2},{2,3},{3,0},{4,5},{5,6},{6,7},{7,4},{8,9},{9,10},{10,1... | collective-permute-start | bytes 998408 | tf_op jit(solution)/shard_map/ppermute | solution.py:25
  14.0 41.9 %collective-permute-start.9 = (bf16[1792,512]{1,0:T(8,128)(2,1)S(1)}, bf16[1792,512]{1,0:T(8,128)(2,1)S(1)}, u32[]{:S(2)}, u32[]{:S(2)}) collective-permute-start(bf16[1792,512]{1,0:T(8,128)(2,1)S(1)} %pad.9), channel_id=1, source_target_pairs={{0,192},{64,0},{128,64},{192,128},{1,193},{65,1},{129,65},{193,129... | collective-permute-start | bytes 5505032 | tf_op jit(solution)/shard_map/ppermute | solution.py:14
  16.3 46.0 %collective-permute-start.7 = (bf16[1792,512]{1,0:T(8,128)(2,1)S(1)}, bf16[1792,512]{1,0:T(8,128)(2,1)}, u32[]{:S(2)}, u32[]{:S(2)}) collective-permute-start(bf16[1792,512]{1,0:T(8,128)(2,1)S(1)} %pad.9), channel_id=1, source_target_pairs={{0,64},{64,128},{128,192},{192,0},{1,65},{65,129},{129,193},{193,1... | collective-permute-start | bytes 5505032 | tf_op jit(solution)/shard_map/ppermute | solution.py:14
  21.4 19.0 %collective-permute-start.3 = (bf16[4,104,1600]{2,1,0:T(8,128)(2,1)S(1)}, bf16[4,104,1600]{2,1,0:T(8,128)(2,1)}, u32[]{:S(2)}, u32[]{:S(2)}) collective-permute-start(bf16[4,104,1600]{2,1,0:T(8,128)(2,1)S(1)} %pad_maximum_fusion), channel_id=1, source_target_pairs={{0,4},{1,5},{2,6},{3,7},{4,8},{5,9},{6,10},{7,11},{8,12},{9,13},{1... | collective-permute-start | bytes 3993608 | tf_op jit(solution)/shard_map/ppermute | solution.py:25
  22.2 18.2 %collective-permute-start.5 = (bf16[4,104,1600]{2,1,0:T(8,128)(2,1)S(1)}, bf16[4,104,1600]{2,1,0:T(8,128)(2,1)}, u32[]{:S(2)}, u32[]{:S(2)}) collective-permute-start(bf16[4,104,1600]{2,1,0:T(8,128)(2,1)S(1)} %pad_maximum_fusion), channel_id=1, source_target_pairs={{0,28},{1,29},{2,30},{3,31},{4,0},{5,1},{6,2},{7,3},{8,4},{9,5},{1... | collective-permute-start | bytes 3993608 | tf_op jit(solution)/shard_map/ppermute | solution.py:25
  24.3 34.4 %collective-permute-start.11 = (bf16[1,104,1600]{2,1,0:T(8,128)(2,1)S(1)}, bf16[1,104,1600]{2,1,0:T(8,128)(2,1)}, u32[]{:S(2)}, u32[]{:S(2)}) collective-permute-start(bf16[1,104,1600]{2,1,0:T(8,128)(2,1)S(1)} %collective-permute-done.1), channel_id=1, source_target_pairs={{32,60},{33,61},{34,62},{35,63},{36,32},{37,33},{38,34},{39,35},{4... | collective-permute-start | bytes 998408 | tf_op jit(solution)/shard_map/ppermute | solution.py:25
  40.4 46.0 %collective-permute-start.4 = (bf16[4,104,1600]{2,1,0:T(8,128)(2,1)}, bf16[4,104,1600]{2,1,0:T(8,128)(2,1)}, u32[]{:S(2)}, u32[]{:S(2)}) collective-permute-start(bf16[4,104,1600]{2,1,0:T(8,128)(2,1)} %collective-permute-done.3), channel_id=1, source_target_pairs={{0,4},{1,5},{2,6},{3,7},{4,8},{5,9},{6,10},{7,11},{8,12},{9,13},{1... | collective-permute-start | bytes 3993608 | tf_op jit(solution)/shard_map/ppermute | solution.py:25
  40.4 45.9 %collective-permute-start.6 = (bf16[4,104,1600]{2,1,0:T(8,128)(2,1)}, bf16[4,104,1600]{2,1,0:T(8,128)(2,1)}, u32[]{:S(2)}, u32[]{:S(2)}) collective-permute-start(bf16[4,104,1600]{2,1,0:T(8,128)(2,1)} %collective-permute-done.5), channel_id=1, source_target_pairs={{0,28},{1,29},{2,30},{3,31},{4,0},{5,1},{6,2},{7,3},{8,4},{9,5},{1... | collective-permute-start | bytes 3993608 | tf_op jit(solution)/shard_map/ppermute | solution.py:25
  55.8 12.2 %collective-permute-start.12 = (bf16[1,104,1600]{2,1,0:T(8,128)(2,1)}, bf16[1,104,1600]{2,1,0:T(8,128)(2,1)}, u32[]{:S(2)}, u32[]{:S(2)}) collective-permute-start(bf16[1,104,1600]{2,1,0:T(8,128)(2,1)} %collective-permute-done.2), channel_id=1, source_target_pairs={{32,36},{33,37},{34,38},{35,39},{36,40},{37,41},{38,42},{39,43},{4... | collective-permute-start | bytes 998408 | tf_op jit(solution)/shard_map/ppermute | solution.py:25
  58.7 23.0 %collective-permute-start.10 = (bf16[800,512]{1,0:T(8,128)(2,1)}, bf16[800,512]{1,0:T(8,128)(2,1)}, u32[]{:S(2)}, u32[]{:S(2)}) collective-permute-start(bf16[800,512]{1,0:T(8,128)(2,1)} %slice.17), channel_id=1, source_target_pairs={{0,192},{64,0},{128,64},{192,128},{1,193},{65,1},{129,65},{193,129... | collective-permute-start | bytes 2457608 | tf_op jit(solution)/shard_map/ppermute | solution.py:14
  62.2 9.1 %collective-permute-start.13 = (bf16[1,104,1600]{2,1,0:T(8,128)(2,1)}, bf16[1,104,1600]{2,1,0:T(8,128)(2,1)}, u32[]{:S(2)}, u32[]{:S(2)}) collective-permute-start(bf16[1,104,1600]{2,1,0:T(8,128)(2,1)} %collective-permute-done.11), channel_id=1, source_target_pairs={{32,60},{33,61},{34,62},{35,63},{36,32},{37,33},{38,34},{39,35},{4... | collective-permute-start | bytes 998408 | tf_op jit(solution)/shard_map/ppermute | solution.py:25
  68.0 18.3 %collective-permute-start.8 = (bf16[800,512]{1,0:T(8,128)(2,1)S(1)}, bf16[800,512]{1,0:T(8,128)(2,1)S(1)}, u32[]{:S(2)}, u32[]{:S(2)}) collective-permute-start(bf16[800,512]{1,0:T(8,128)(2,1)S(1)} %slice.16), channel_id=1, source_target_pairs={{0,64},{64,128},{128,192},{192,0},{1,65},{65,129},{129,193},{193,1... | collective-permute-start | bytes 2457608 | tf_op jit(solution)/shard_map/ppermute | solution.py:14
  71.3 10.4 %collective-permute-start.14 = (bf16[1,104,1600]{2,1,0:T(8,128)(2,1)}, bf16[1,104,1600]{2,1,0:T(8,128)(2,1)S(1)}, u32[]{:S(2)}, u32[]{:S(2)}) collective-permute-start(bf16[1,104,1600]{2,1,0:T(8,128)(2,1)} %collective-permute-done.12), channel_id=1, source_target_pairs={{32,36},{33,37},{34,38},{35,39},{36,40},{37,41},{38,42},{39,43},{4... | collective-permute-start | bytes 998408 | tf_op jit(solution)/shard_map/ppermute | solution.py:25
  81.7 7.4 %collective-permute-start.17 = (bf16[4,104,1600]{2,1,0:T(8,128)(2,1)S(1)}, bf16[4,104,1600]{2,1,0:T(8,128)(2,1)S(1)}, u32[]{:S(2)}, u32[]{:S(2)}) collective-permute-start(bf16[4,104,1600]{2,1,0:T(8,128)(2,1)S(1)} %pad_maximum_fusion), channel_id=1, source_target_pairs={{0,32},{32,0},{1,33},{33,1},{2,34},{34,2},{3,35},{35,3},{4,36},{36... | collective-permute-start | bytes 3993608 | tf_op jit(solution)/shard_map/ppermute | solution.py:29
  81.7 9.9 %collective-permute-start.19 = (bf16[4,104,1600]{2,1,0:T(8,128)(2,1)}, bf16[4,104,1600]{2,1,0:T(8,128)(2,1)S(1)}, u32[]{:S(2)}, u32[]{:S(2)}) collective-permute-start(bf16[4,104,1600]{2,1,0:T(8,128)(2,1)} %collective-permute-done.5), channel_id=1, source_target_pairs={{0,32},{32,0},{1,33},{33,1},{2,34},{34,2},{3,35},{35,3},{4,36},{36... | collective-permute-start | bytes 3993608 | tf_op jit(solution)/shard_map/ppermute | solution.py:29
  82.2 9.4 %copy-start = (bf16[1600,512]{1,0:T(8,128)(2,1)S(1)}, bf16[1600,512]{1,0:T(8,128)(2,1)}, u32[]{:S(2)}) copy-start(bf16[1600,512]{1,0:T(8,128)(2,1)} %own_ref.1) | copy-start | bytes 4915204
  86.3 10.1 %collective-permute-start.18 = (bf16[4,104,1600]{2,1,0:T(8,128)(2,1)}, bf16[4,104,1600]{2,1,0:T(8,128)(2,1)S(1)}, u32[]{:S(2)}, u32[]{:S(2)}) collective-permute-start(bf16[4,104,1600]{2,1,0:T(8,128)(2,1)} %collective-permute-done.3), channel_id=1, source_target_pairs={{0,32},{32,0},{1,33},{33,1},{2,34},{34,2},{3,35},{35,3},{4,36},{36... | collective-permute-start | bytes 3993608 | tf_op jit(solution)/shard_map/ppermute | solution.py:29
  86.6 9.8 %collective-permute-start.21 = (bf16[4,104,1600]{2,1,0:T(8,128)(2,1)S(1)}, bf16[4,104,1600]{2,1,0:T(8,128)(2,1)S(1)}, u32[]{:S(2)}, u32[]{:S(2)}) collective-permute-start(bf16[4,104,1600]{2,1,0:T(8,128)(2,1)S(1)} %get-tuple-element.25), channel_id=1, source_target_pairs={{0,32},{32,0},{1,33},{33,1},{2,34},{34,2},{3,35},{35,3},{4,36},{36... | collective-permute-start | bytes 3993608 | tf_op jit(solution)/shard_map/ppermute | solution.py:29
  89.0 7.5 %collective-permute-start.20 = (bf16[4,104,1600]{2,1,0:T(8,128)(2,1)}, bf16[4,104,1600]{2,1,0:T(8,128)(2,1)S(1)}, u32[]{:S(2)}, u32[]{:S(2)}) collective-permute-start(bf16[4,104,1600]{2,1,0:T(8,128)(2,1)} %collective-permute-done.4), channel_id=1, source_target_pairs={{0,32},{32,0},{1,33},{33,1},{2,34},{34,2},{3,35},{35,3},{4,36},{36... | collective-permute-start | bytes 3993608 | tf_op jit(solution)/shard_map/ppermute | solution.py:29
  89.1 18.4 %collective-permute-start.16 = (bf16[4,104,1600]{2,1,0:T(8,128)(2,1)S(1)}, bf16[4,104,1600]{2,1,0:T(8,128)(2,1)S(1)}, u32[]{:S(2)}, u32[]{:S(2)}) collective-permute-start(bf16[4,104,1600]{2,1,0:T(8,128)(2,1)S(1)} %get-tuple-element.25), channel_id=1, source_target_pairs={{0,28},{1,29},{2,30},{3,31},{4,0},{5,1},{6,2},{7,3},{8,4},{9,5},{1... | collective-permute-start | bytes 3993608 | tf_op jit(solution)/shard_map/ppermute | solution.py:25
  91.6 18.8 %collective-permute-start.15 = (bf16[4,104,1600]{2,1,0:T(8,128)(2,1)S(1)}, bf16[4,104,1600]{2,1,0:T(8,128)(2,1)S(1)}, u32[]{:S(2)}, u32[]{:S(2)}) collective-permute-start(bf16[4,104,1600]{2,1,0:T(8,128)(2,1)S(1)} %get-tuple-element.26), channel_id=1, source_target_pairs={{0,4},{1,5},{2,6},{3,7},{4,8},{5,9},{6,10},{7,11},{8,12},{9,13},{1... | collective-permute-start | bytes 3993608 | tf_op jit(solution)/shard_map/ppermute | solution.py:25
  96.4 28.9 %copy-start.1 = (f32[512,1600]{0,1:T(8,128)S(1)}, f32[512,1600]{0,1:T(8,128)}, u32[]{:S(2)}) copy-start(f32[512,1600]{0,1:T(8,128)} %param.3) | copy-start | bytes 9830404
  110.4 15.0 %collective-permute-start.22 = (bf16[4,104,1600]{2,1,0:T(8,128)(2,1)S(1)}, bf16[4,104,1600]{2,1,0:T(8,128)(2,1)S(1)}, u32[]{:S(2)}, u32[]{:S(2)}) collective-permute-start(bf16[4,104,1600]{2,1,0:T(8,128)(2,1)S(1)} %collective-permute-done.15), channel_id=1, source_target_pairs={{0,32},{32,0},{1,33},{33,1},{2,34},{34,2},{3,35},{35,3},{4,36},{36... | collective-permute-start | bytes 3993608 | tf_op jit(solution)/shard_map/ppermute | solution.py:29
  112.5 12.8 %collective-permute-start.23 = (bf16[4,104,1600]{2,1,0:T(8,128)(2,1)S(1)}, bf16[4,104,1600]{2,1,0:T(8,128)(2,1)S(1)}, u32[]{:S(2)}, u32[]{:S(2)}) collective-permute-start(bf16[4,104,1600]{2,1,0:T(8,128)(2,1)S(1)} %collective-permute-done.16), channel_id=1, source_target_pairs={{0,32},{32,0},{1,33},{33,1},{2,34},{34,2},{3,35},{35,3},{4,36},{36... | collective-permute-start | bytes 3993608 | tf_op jit(solution)/shard_map/ppermute | solution.py:29
  112.6 11.4 %collective-permute-start.24 = (bf16[2,104,1600]{2,1,0:T(8,128)(2,1)S(1)}, bf16[2,104,1600]{2,1,0:T(8,128)(2,1)S(1)}, u32[]{:S(2)}, u32[]{:S(2)}) collective-permute-start(bf16[2,104,1600]{2,1,0:T(8,128)(2,1)S(1)} %slice.14), channel_id=1, source_target_pairs={{0,4},{1,5},{2,6},{3,7},{4,8},{5,9},{6,10},{7,11},{8,12},{9,13},{1... | collective-permute-start | bytes 1996808 | tf_op jit(solution)/shard_map/ppermute | solution.py:25
  114.0 11.4 %collective-permute-start.25 = (bf16[2,104,1600]{2,1,0:T(8,128)(2,1)S(1)}, bf16[2,104,1600]{2,1,0:T(8,128)(2,1)S(1)}, u32[]{:S(2)}, u32[]{:S(2)}) collective-permute-start(bf16[2,104,1600]{2,1,0:T(8,128)(2,1)S(1)} %slice.15), channel_id=1, source_target_pairs={{0,28},{1,29},{2,30},{3,31},{4,0},{5,1},{6,2},{7,3},{8,4},{9,5},{1... | collective-permute-start | bytes 1996808 | tf_op jit(solution)/shard_map/ppermute | solution.py:25
  124.0 5.4 %collective-permute-start.26 = (bf16[2,104,1600]{2,1,0:T(8,128)(2,1)S(1)}, bf16[2,104,1600]{2,1,0:T(8,128)(2,1)S(1)}, u32[]{:S(2)}, u32[]{:S(2)}) collective-permute-start(bf16[2,104,1600]{2,1,0:T(8,128)(2,1)S(1)} %collective-permute-done.24), channel_id=1, source_target_pairs={{0,32},{32,0},{1,33},{33,1},{2,34},{34,2},{3,35},{35,3},{4,36},{36... | collective-permute-start | bytes 1996808 | tf_op jit(solution)/shard_map/ppermute | solution.py:29
  125.4 4.1 %collective-permute-start.27 = (bf16[2,104,1600]{2,1,0:T(8,128)(2,1)S(1)}, bf16[2,104,1600]{2,1,0:T(8,128)(2,1)S(1)}, u32[]{:S(2)}, u32[]{:S(2)}) collective-permute-start(bf16[2,104,1600]{2,1,0:T(8,128)(2,1)S(1)} %collective-permute-done.25), channel_id=1, source_target_pairs={{0,32},{32,0},{1,33},{33,1},{2,34},{34,2},{3,35},{35,3},{4,36},{36... | collective-permute-start | bytes 1996808 | tf_op jit(solution)/shard_map/ppermute | solution.py:29

commit v5 on v4

--- a/solution.py
+++ b/solution.py
@@ -7,11 +7,11 @@
 
 Z, Y = 8, 4
 VMEM = 16 << 20
-LONGER = 192
 
 
-def shift(array, size, step):
-    return lax.ppermute(array, "row", [(i, (i + step) % size) for i in range(size)])
+def along_row(array, size, first, second):
+    pairs = [((row * 2 + core), (row + step) % size * 2 + core) for row in range(size) for core, step in enumerate((first, second))]
+    return lax.ppermute(array, ("row", "col"), pairs)
 
 
 def travel(array, first, second):
@@ -38,25 +38,28 @@
     count = amplitudes.shape[0]
     along, back = ((0, 1), (1, 0)), ((0, -1), (-1, 0))
     up, down = ((1, 0), (0, 1)), ((-1, 0), (0, -1))
-    longer = jnp.pad(amplitudes, ((0, LONGER), (0, 0)))
-    after, before = shift(longer, rows, -1), shift(longer, rows, 1)
+    near = along_row(amplitudes, rows, 1, -1)
     a1 = travel(block, *along)
     b1 = travel(block, *back)
     a2 = travel(a1, *along)
     pack = jnp.concatenate([block, a1, b1, a2])
     b2 = travel(b1, None, back[1])
     a3 = travel(a2, None, along[1])
+    own, near, b2, a3 = lax.optimization_barrier((amplitudes, near, b2, a3))
+    other = along_row(own, rows, -1, 1)
     b3 = travel(b2, None, back[1])
     a4 = travel(a3, None, along[1])
+    near, b3, a4 = lax.optimization_barrier((near, b3, a4))
+    far_low = along_row(near[: count // 2], rows, 1, -1)
     rest = jnp.concatenate([b2, a3, b3, a4])
     u1, d1 = travel(pack, *up), travel(pack, *down)
     u2, d2 = travel(u1, *up), travel(d1, down[0], None)
-    far_low, far_high = shift(before[: count // 2], rows, 1), shift(after[count // 2 : count], rows, -1)
+    far_high = along_row(other[count // 2 :], rows, -1, 1)
     u2, d2, far_low, far_high = lax.optimization_barrier((u2, d2, far_low, far_high))
     first = lax.axis_index("col") == 0
     kept = jnp.where(first, d2, rest)
     u3, d3 = travel(jnp.where(first, u2, rest), *up), travel(kept, *down)
-    factors = arrange(amplitudes, after, far_low, far_high, before, rows, height, [20, 8, 4])
+    factors = arrange(amplitudes, near, other, far_low, far_high, rows, height, [20, 8, 4])
     early = [pack, u1, d1, u2, kept]
     total = multiply_first(factors[0], early + [swap(piece) for piece in early])
     u3, d3, total = lax.optimization_barrier((u3, d3, total))
@@ -64,21 +67,22 @@
     return factors[1:], total, [u3, d3, swap(u3), swap(d3)], [u4, d4, swap(u4), swap(d4)]
 
 
-def arrange(own, after, far_low, far_high, before, rows, height, cuts):
+def arrange(own, near, other, far_low, far_high, rows, height, cuts):
     width = own.shape[1]
     count = own.shape[0] // height
     full = height + -height % 8
 
-    def kernel(own_ref, after_ref, low_ref, high_ref, before_ref, *refs):
+    def kernel(own_ref, near_ref, other_ref, low_ref, high_ref, *refs):
         out_refs, held = refs[:-1], refs[-1]
         x, core, depth = (lax.axis_index(name) for name in ("row", "col", "depth"))
         z, y = depth // Y, lax.rem(depth, Y)
         held[:, :, height:, :] = jnp.zeros((2, Z * Y, full - height, width), held.dtype)
-        sources = [(own_ref, 0, 0), (after_ref, 1, 0), (low_ref, 2, 0), (high_ref, 2, count // 2), (before_ref, 3, 0)]
+        steps = rows - 1 + core * (2 - rows), 1 + core * (rows - 2)
+        sources = [(own_ref, 0, 0), (near_ref, steps[0], 0), (other_ref, steps[1], 0), (low_ref, 2, 0), (high_ref, 2, count // 2)]
         for ref, step, start in sources:
             block_row = lax.rem(x + step, rows)
             half = block_row // (rows // 2)
-            for i in range(min(count, ref.shape[0] // height)):
+            for i in range(ref.shape[0] // height):
                 there = lax.rem(block_row, rows // 2) * count + start + i
                 dz = lax.rem(there // Y - z + Z, Z)
                 dy = lax.rem((start + i) % Y - y + Y, Y)
@@ -101,7 +105,7 @@
         compiler_params=pltpu.CompilerParams(vmem_limit_bytes=VMEM),
         cost_estimate=pl.CostEstimate(flops=0, bytes_accessed=2 * size, transcendentals=0),
         name="arrange",
-    )(own, after, far_low, far_high, before)
+    )(own, near, other, far_low, far_high)
 
 
 def products(factor_ref, piece_refs, start, width):

time: 133 us -> 125 us (0.940)
  waiting for transfers between devices: 57.6 us -> 38.6 us
  starting transfers between devices: 42.5 us -> 58.1 us
  local copies, waits for them, and re-layouts: 7.89 us -> 3.78 us
    ppermute x9, starting transfers between devices: 6.47 us -> 26.3 us  [swap(): return lax.ppermute(array, 'col', [(0, 1), (1, 0)])]
    ppermute x4, waiting for transfers between devices: 17.8 us -> 6.81 us  [along_row(): return lax.ppermute(array, ('row', 'col'), pairs)]
    ppermute x15, waiting for transfers between devices: 39.7 us -> 31.8 us  [travel(): return lax.ppermute(array, ('col', 'depth'), pairs)]
    ppermute x15, starting transfers between devices: 30.1 us -> 27.9 us  [travel(): return lax.ppermute(array, ('col', 'depth'), pairs)]
    ppermute x4, starting transfers between devices: 5.9 us -> 3.88 us  [along_row(): return lax.ppermute(array, ('row', 'col'), pairs)]
    pad x1 -> x0, local copies, waits for them, and re-layouts: 1.55 us -> none  [gather(): longer = jnp.pad(amplitudes, ((0, LONGER), (0, 0)))]
    unnamed x7 -> x25, local copies, waits for them, and re-layouts: 3.06 us -> 1.64 us
  transfers between devices with their start and end apart: 28 -> 28, of which waited for: 9 -> 9; matrix products, arithmetic and copies ran while one was open for 6% -> 2% of each run, Pallas kernels for 15% -> 16%
where the time goes in v5:
time: 125 us
  starting transfers between devices  58.1 us (46%)
  waiting for transfers between devices  38.6 us (31%)
  Pallas kernels  22.9 us (18%)
  local copies, waits for them, and re-layouts  3.78 us (3%)
    ppermute x15, waiting for transfers between devices, travel(): return lax.ppermute(array, ('col', 'depth'), pairs)  31.8 us
    ppermute x15, starting transfers between devices, travel(): return lax.ppermute(array, ('col', 'depth'), pairs)  27.9 us
    ppermute x9, starting transfers between devices, swap(): return lax.ppermute(array, 'col', [(0, 1), (1, 0)])  26.3 us
    pallas_call x3, Pallas kernels, multiply(): pl.pallas_call(body, out_shape=jax.ShapeDtypeStruct(shape, jnp.float32),...  18.2 us
    ppermute x4, waiting for transfers between devices, along_row(): return lax.ppermute(array, ('row', 'col'), pairs)  6.81 us
    pallas_call x1, Pallas kernels, arrange(): pl.pallas_call(kernel, out_shape=[jax.ShapeDtypeStruct((2, width, blocks...  4.67 us
    ppermute x4, starting transfers between devices, along_row(): return lax.ppermute(array, ('row', 'col'), pairs)  3.88 us
  transfers between devices with their start and end apart: 28, of which 9 were waited for; matrix products, arithmetic and copies ran while one was open for 2% of the time, Pallas kernels for 16%

profile of v5, /device:TPU:1, one launch (start us, length us, event | category | flops | bytes accessed | tf_op | source)
XLA Modules:
  0.0 124.5 jit_solution(13021047164107307007)
XLA Ops:
  0.0 3.3 %collective-permute-start.7 = (bf16[1600,512]{1,0:T(8,128)(2,1)}, bf16[1600,512]{1,0:T(8,128)(2,1)S(1)}, u32[]{:S(2)}, u32[]{:S(2)}) collective-permute-start(bf16[1600,512]{1,0:T(8,128)(2,1)} %own_ref.1), channel_id=1, source_target_pairs={{0,64},{32,224},{64,128},{96,32},{128,192},{160,96},{192,0},{224,1... | collective-permute-start | bytes 4915208 | tf_op jit(solution)/shard_map/ppermute | solution.py:14
  3.3 1.0 pad.4
  4.3 1.7 %collective-permute-start = (bf16[1,104,1600]{2,1,0:T(8,128)(2,1)S(1)}, bf16[1,104,1600]{2,1,0:T(8,128)(2,1)S(1)}, u32[]{:S(2)}, u32[]{:S(2)}) collective-permute-start(bf16[1,104,1600]{2,1,0:T(8,128)(2,1)S(1)} %pad.4), channel_id=1, source_target_pairs={{0,1},{1,2},{2,3},{3,0},{4,5},{5,6},{6,7},{7,4},{8,9},{9,10},{10,1... | collective-permute-start | bytes 998408 | tf_op jit(solution)/shard_map/ppermute | solution.py:25
  6.0 4.0 %collective-permute-start.1 = (bf16[1,104,1600]{2,1,0:T(8,128)(2,1)S(1)}, bf16[1,104,1600]{2,1,0:T(8,128)(2,1)S(1)}, u32[]{:S(2)}, u32[]{:S(2)}) collective-permute-start(bf16[1,104,1600]{2,1,0:T(8,128)(2,1)S(1)} %pad.4), channel_id=1, source_target_pairs={{0,3},{1,0},{2,1},{3,2},{4,7},{5,4},{6,5},{7,6},{8,11},{9,8},{10,9... | collective-permute-start | bytes 998408 | tf_op jit(solution)/shard_map/ppermute | solution.py:25
  10.1 4.9 %collective-permute-done = bf16[1,104,1600]{2,1,0:T(8,128)(2,1)S(1)} collective-permute-done((bf16[1,104,1600]{2,1,0:T(8,128)(2,1)S(1)}, bf16[1,104,1600]{2,1,0:T(8,128)(2,1)S(1)}, u32[]{:S(2)}, u32[]{:S(2)}) %collective-permute-start) | collective-permute-done | bytes 332832 | tf_op jit(solution)/shard_map/ppermute | solution.py:25
  14.9 0.0 collective-permute-start.2
  14.9 0.0 collective-permute-done.1
  14.9 4.7 %collective-permute-start.8 = (bf16[1,104,1600]{2,1,0:T(8,128)(2,1)S(1)}, bf16[1,104,1600]{2,1,0:T(8,128)(2,1)S(1)}, u32[]{:S(2)}, u32[]{:S(2)}) collective-permute-start(bf16[1,104,1600]{2,1,0:T(8,128)(2,1)S(1)} %collective-permute-done.1), channel_id=1, source_target_pairs={{32,60},{33,61},{34,62},{35,63},{36,32},{37,33},{38,34},{39,35},{4... | collective-permute-start | bytes 998408 | tf_op jit(solution)/shard_map/ppermute | solution.py:25
  19.6 3.0 %collective-permute-done.2 = bf16[1,104,1600]{2,1,0:T(8,128)(2,1)S(1)} collective-permute-done((bf16[1,104,1600]{2,1,0:T(8,128)(2,1)S(1)}, bf16[1,104,1600]{2,1,0:T(8,128)(2,1)S(1)}, u32[]{:S(2)}, u32[]{:S(2)}) %collective-permute-start.2) | collective-permute-done | bytes 332832 | tf_op jit(solution)/shard_map/ppermute | solution.py:25
  22.6 1.9 %collective-permute-start.9 = (bf16[1,104,1600]{2,1,0:T(8,128)(2,1)S(1)}, bf16[1,104,1600]{2,1,0:T(8,128)(2,1)S(1)}, u32[]{:S(2)}, u32[]{:S(2)}) collective-permute-start(bf16[1,104,1600]{2,1,0:T(8,128)(2,1)S(1)} %collective-permute-done.2), channel_id=1, source_target_pairs={{32,36},{33,37},{34,38},{35,39},{36,40},{37,41},{38,42},{39,43},{4... | collective-permute-start | bytes 998408 | tf_op jit(solution)/shard_map/ppermute | solution.py:25
  24.5 0.2 pad_maximum_fusion
  24.7 0.0 copy-start.1
  24.7 1.4 %collective-permute-start.3 = (bf16[4,104,1600]{2,1,0:T(8,128)(2,1)S(1)}, bf16[4,104,1600]{2,1,0:T(8,128)(2,1)}, u32[]{:S(2)}, u32[]{:S(2)}) collective-permute-start(bf16[4,104,1600]{2,1,0:T(8,128)(2,1)S(1)} %pad_maximum_fusion), channel_id=1, source_target_pairs={{0,4},{1,5},{2,6},{3,7},{4,8},{5,9},{6,10},{7,11},{8,12},{9,13},{1... | collective-permute-start | bytes 3993608 | tf_op jit(solution)/shard_map/ppermute | solution.py:25
  26.1 1.5 %collective-permute-start.5 = (bf16[4,104,1600]{2,1,0:T(8,128)(2,1)S(1)}, bf16[4,104,1600]{2,1,0:T(8,128)(2,1)}, u32[]{:S(2)}, u32[]{:S(2)}) collective-permute-start(bf16[4,104,1600]{2,1,0:T(8,128)(2,1)S(1)} %pad_maximum_fusion), channel_id=1, source_target_pairs={{0,28},{1,29},{2,30},{3,31},{4,0},{5,1},{6,2},{7,3},{8,4},{9,5},{1... | collective-permute-start | bytes 3993608 | tf_op jit(solution)/shard_map/ppermute | solution.py:25
  27.6 0.0 collective-permute-done.8
  27.6 7.6 %collective-permute-done.9 = bf16[1,104,1600]{2,1,0:T(8,128)(2,1)S(1)} collective-permute-done((bf16[1,104,1600]{2,1,0:T(8,128)(2,1)S(1)}, bf16[1,104,1600]{2,1,0:T(8,128)(2,1)S(1)}, u32[]{:S(2)}, u32[]{:S(2)}) %collective-permute-start.9) | collective-permute-done | bytes 332832 | tf_op jit(solution)/shard_map/ppermute | solution.py:25
  35.2 0.0 collective-permute-done.7.near_ref
  35.2 0.1 collective-permute-start.13
  35.3 1.9 %collective-permute-start.10 = (bf16[1,104,1600]{2,1,0:T(8,128)(2,1)S(1)}, bf16[1,104,1600]{2,1,0:T(8,128)(2,1)S(1)}, u32[]{:S(2)}, u32[]{:S(2)}) collective-permute-start(bf16[1,104,1600]{2,1,0:T(8,128)(2,1)S(1)} %collective-permute-done.8), channel_id=1, source_target_pairs={{32,60},{33,61},{34,62},{35,63},{36,32},{37,33},{38,34},{39,35},{4... | collective-permute-start | bytes 998408 | tf_op jit(solution)/shard_map/ppermute | solution.py:25
  37.3 3.4 %collective-permute-start.11 = (bf16[1,104,1600]{2,1,0:T(8,128)(2,1)S(1)}, bf16[1,104,1600]{2,1,0:T(8,128)(2,1)S(1)}, u32[]{:S(2)}, u32[]{:S(2)}) collective-permute-start(bf16[1,104,1600]{2,1,0:T(8,128)(2,1)S(1)} %collective-permute-done.9), channel_id=1, source_target_pairs={{32,36},{33,37},{34,38},{35,39},{36,40},{37,41},{38,42},{39,43},{4... | collective-permute-start | bytes 998408 | tf_op jit(solution)/shard_map/ppermute | solution.py:25
  40.6 3.1 %collective-permute-done.3 = bf16[4,104,1600]{2,1,0:T(8,128)(2,1)} collective-permute-done((bf16[4,104,1600]{2,1,0:T(8,128)(2,1)S(1)}, bf16[4,104,1600]{2,1,0:T(8,128)(2,1)}, u32[]{:S(2)}, u32[]{:S(2)}) %collective-permute-start.3) | collective-permute-done | bytes 1331232 | tf_op jit(solution)/shard_map/ppermute | solution.py:25
  43.7 0.0 collective-permute-start.4
  43.8 1.8 %collective-permute-start.6 = (bf16[4,104,1600]{2,1,0:T(8,128)(2,1)}, bf16[4,104,1600]{2,1,0:T(8,128)(2,1)}, u32[]{:S(2)}, u32[]{:S(2)}) collective-permute-start(bf16[4,104,1600]{2,1,0:T(8,128)(2,1)} %collective-permute-done.5), channel_id=1, source_target_pairs={{0,28},{1,29},{2,30},{3,31},{4,0},{5,1},{6,2},{7,3},{8,4},{9,5},{1... | collective-permute-start | bytes 3993608 | tf_op jit(solution)/shard_map/ppermute | solution.py:25
  45.5 0.3 collective-permute-done.10
  45.8 0.8 copy-done.9
  46.6 4.1 %collective-permute-done.11 = bf16[1,104,1600]{2,1,0:T(8,128)(2,1)S(1)} collective-permute-done((bf16[1,104,1600]{2,1,0:T(8,128)(2,1)S(1)}, bf16[1,104,1600]{2,1,0:T(8,128)(2,1)S(1)}, u32[]{:S(2)}, u32[]{:S(2)}) %collective-permute-start.11) | collective-permute-done | bytes 332832 | tf_op jit(solution)/shard_map/ppermute | solution.py:25
  50.7 0.7 copy-done.7
  51.4 0.9 slice.12
  52.4 0.4 collective-permute-start.12
  52.8 6.1 %collective-permute-start.17 = (bf16[4,104,1600]{2,1,0:T(8,128)(2,1)}, bf16[4,104,1600]{2,1,0:T(8,128)(2,1)S(1)}, u32[]{:S(2)}, u32[]{:S(2)}) collective-permute-start(bf16[4,104,1600]{2,1,0:T(8,128)(2,1)} %copy-done.1), channel_id=1, source_target_pairs={{0,32},{32,0},{1,33},{33,1},{2,34},{34,2},{3,35},{35,3},{4,36},{36... | collective-permute-start | bytes 3993608 | tf_op jit(solution)/shard_map/ppermute | solution.py:29
  58.8 0.1 slice.16
  58.9 0.1 collective-permute-start.14
  59.1 6.8 %collective-permute-done.12.low_ref = bf16[800,512]{1,0:T(8,128)(2,1)} collective-permute-done((bf16[800,512]{1,0:T(8,128)(2,1)}, bf16[800,512]{1,0:T(8,128)(2,1)}, u32[]{:S(2)}, u32[]{:S(2)}) %collective-permute-start.12) | collective-permute-done | bytes 819232 | tf_op jit(solution)/shard_map/ppermute | solution.py:14
  66.0 15.2 %collective-permute-start.19 = (bf16[4,104,1600]{2,1,0:T(8,128)(2,1)}, bf16[4,104,1600]{2,1,0:T(8,128)(2,1)S(1)}, u32[]{:S(2)}, u32[]{:S(2)}) collective-permute-start(bf16[4,104,1600]{2,1,0:T(8,128)(2,1)} %collective-permute-done.5), channel_id=1, source_target_pairs={{0,32},{32,0},{1,33},{33,1},{2,34},{34,2},{3,35},{35,3},{4,36},{36... | collective-permute-start | bytes 3993608 | tf_op jit(solution)/shard_map/ppermute | solution.py:29
  81.2 0.0 collective-permute-done.4
  81.2 0.1 collective-permute-start.18
  81.3 0.4 broadcast_select_fusion
  81.7 2.3 %collective-permute-start.21 = (bf16[4,104,1600]{2,1,0:T(8,128)(2,1)S(1)}, bf16[4,104,1600]{2,1,0:T(8,128)(2,1)S(1)}, u32[]{:S(2)}, u32[]{:S(2)}) collective-permute-start(bf16[4,104,1600]{2,1,0:T(8,128)(2,1)S(1)} %get-tuple-element.39), channel_id=1, source_target_pairs={{0,32},{32,0},{1,33},{33,1},{2,34},{34,2},{3,35},{35,3},{4,36},{36... | collective-permute-start | bytes 3993608 | tf_op jit(solution)/shard_map/ppermute | solution.py:29
  84.0 0.1 collective-permute-start.20
  84.1 0.0 collective-permute-done.17
  84.1 0.2 collective-permute-start.15
  84.3 0.0 collective-permute-done.19
  84.3 2.7 %collective-permute-start.16 = (bf16[4,104,1600]{2,1,0:T(8,128)(2,1)S(1)}, bf16[4,104,1600]{2,1,0:T(8,128)(2,1)S(1)}, u32[]{:S(2)}, u32[]{:S(2)}) collective-permute-start(bf16[4,104,1600]{2,1,0:T(8,128)(2,1)S(1)} %get-tuple-element.39), channel_id=1, source_target_pairs={{0,28},{1,29},{2,30},{3,31},{4,0},{5,1},{6,2},{7,3},{8,4},{9,5},{1... | collective-permute-start | bytes 3993608 | tf_op jit(solution)/shard_map/ppermute | solution.py:25
  87.0 4.7 %arrange.1 = (bf16[2,512,2080]{2,1,0:T(8,128)(2,1)S(1)}, bf16[2,512,832]{2,1,0:T(8,128)(2,1)S(1)}, bf16[2,512,416]{2,1,0:T(8,128)(2,1)S(1)}) custom-call(bf16[1600,512]{1,0:T(8,128)(2,1)} %own_ref.1, bf16[1600,512]{1,0:T(8,128)(2,1)S(1)} %collective-permute-done.7.near_ref, bf16[1600,512]{1,0:T(8,128)(2,1)S(1)} %collective-permute-done.13.other_ref, ...), custom_call_target="tpu_custom_call" | custom-call | bytes 13107200 | tf_op jit(solution)/shard_map/arrange/pallas_call | solution.py:101
  91.7 0.0 collective-permute-done.18
  91.7 0.0 collective-permute-done.20
  91.7 0.0 copy-start
  91.7 11.0 %first.1.total_ref = f32[512,1600]{1,0:T(8,128)S(1)} custom-call(bf16[2,512,2080]{2,1,0:T(8,128)(2,1)S(1)} %get-tuple-element.33.factor_ref, bf16[416,1600]{1,0:T(8,128)(2,1)S(1)} %bitcast.26, bf16[416,1600]{1,0:T(8,128)(2,1)} %bitcast.4.refs_1_, bf16[416,1600]{1,0:T(8,128)(2,1)} %bitcast.5.refs_2_, bf16[416,1600]{1,0:T(8,128)(2,1)} %bitcast.6.refs_3_, ...), custom_call_target="tpu_custom_call" | custom-call | flops 6815744000 | bytes 13312000 | tf_op jit(solution)/shard_map/first/pallas_call | solution.py:123
  102.7 0.4 collective-permute-done.15
  103.0 0.0 collective-permute-done.16
  103.1 1.1 collective-permute-start.22
  104.2 0.0 collective-permute-start.23
  104.2 0.1 slice.14
  104.2 0.1 collective-permute-start.24
  104.3 0.1 slice.15
  104.4 2.7 %collective-permute-start.25 = (bf16[2,104,1600]{2,1,0:T(8,128)(2,1)S(1)}, bf16[2,104,1600]{2,1,0:T(8,128)(2,1)S(1)}, u32[]{:S(2)}, u32[]{:S(2)}) collective-permute-start(bf16[2,104,1600]{2,1,0:T(8,128)(2,1)S(1)} %slice.15), channel_id=1, source_target_pairs={{0,28},{1,29},{2,30},{3,31},{4,0},{5,1},{6,2},{7,3},{8,4},{9,5},{1... | collective-permute-start | bytes 1996808 | tf_op jit(solution)/shard_map/ppermute | solution.py:25
  107.1 8.5 %collective-permute-done.24 = bf16[2,104,1600]{2,1,0:T(8,128)(2,1)S(1)} collective-permute-done((bf16[2,104,1600]{2,1,0:T(8,128)(2,1)S(1)}, bf16[2,104,1600]{2,1,0:T(8,128)(2,1)S(1)}, u32[]{:S(2)}, u32[]{:S(2)}) %collective-permute-start.24) | collective-permute-done | bytes 665632 | tf_op jit(solution)/shard_map/ppermute | solution.py:25
  115.6 1.4 %collective-permute-start.26 = (bf16[2,104,1600]{2,1,0:T(8,128)(2,1)S(1)}, bf16[2,104,1600]{2,1,0:T(8,128)(2,1)S(1)}, u32[]{:S(2)}, u32[]{:S(2)}) collective-permute-start(bf16[2,104,1600]{2,1,0:T(8,128)(2,1)S(1)} %collective-permute-done.24), channel_id=1, source_target_pairs={{0,32},{32,0},{1,33},{33,1},{2,34},{34,2},{3,35},{35,3},{4,36},{36... | collective-permute-start | bytes 1996808 | tf_op jit(solution)/shard_map/ppermute | solution.py:29
  117.0 0.0 collective-permute-start.27
  117.0 0.0 collective-permute-done.23
  117.0 4.0 %more.1.total_ref = f32[1600,512]{1,0:T(8,128)S(1)} custom-call(f32[1600,512]{1,0:T(8,128)S(1)} %bitcast.23, f32[512,1600]{1,0:T(8,128)S(1)} %first.1.total_ref, bf16[2,512,832]{2,1,0:T(8,128)(2,1)S(1)} %get-tuple-element.35.factor_ref, bf16[416,1600]{1,0:T(8,128)(2,1)S(1)} %bitcast.24, bf16[416,1600]{1,0:T(8,128)(2,1)S(1)} %bitcast.25, ...), custom_call_target="tpu_custom_call" | custom-call | flops 2726297600 | bytes 5324800 | tf_op jit(solution)/shard_map/more/pallas_call | solution.py:123
  121.0 0.0 collective-permute-done.26
  121.0 0.0 collective-permute-done.27
  121.0 3.3 %last.1 = f32[1600,512]{1,0:T(8,128)} custom-call(f32[1600,512]{1,0:T(8,128)S(1)} %more.1.total_ref, bf16[2,512,416]{2,1,0:T(8,128)(2,1)S(1)} %get-tuple-element.38.factor_ref, bf16[208,1600]{1,0:T(8,128)(2,1)S(1)} %bitcast.30, bf16[208,1600]{1,0:T(8,128)(2,1)S(1)} %bitcast.31, bf16[208,1600]{1,0:T(8,128)(2,1)S(1)} %bitcast.32, bf16[208,1600]{1,0:T(8,128)(2,1)S(1)} %bitcast.33), custom_call_target="tpu_custom_call" | custom-call | flops 1363148800 | bytes 2662400 | tf_op jit(solution)/shard_map/last/pallas_call | solution.py:123
  (29 shorter events, 0.2 us)
Async XLA Ops:
  0.0 35.2 %collective-permute-start.7 = (bf16[1600,512]{1,0:T(8,128)(2,1)}, bf16[1600,512]{1,0:T(8,128)(2,1)S(1)}, u32[]{:S(2)}, u32[]{:S(2)}) collective-permute-start(bf16[1600,512]{1,0:T(8,128)(2,1)} %own_ref.1), channel_id=1, source_target_pairs={{0,64},{32,224},{64,128},{96,32},{128,192},{160,96},{192,0},{224,1... | collective-permute-start | bytes 4915208 | tf_op jit(solution)/shard_map/ppermute | solution.py:14
  4.3 10.6 %collective-permute-start = (bf16[1,104,1600]{2,1,0:T(8,128)(2,1)S(1)}, bf16[1,104,1600]{2,1,0:T(8,128)(2,1)S(1)}, u32[]{:S(2)}, u32[]{:S(2)}) collective-permute-start(bf16[1,104,1600]{2,1,0:T(8,128)(2,1)S(1)} %pad.4), channel_id=1, source_target_pairs={{0,1},{1,2},{2,3},{3,0},{4,5},{5,6},{6,7},{7,4},{8,9},{9,10},{10,1... | collective-permute-start | bytes 998408 | tf_op jit(solution)/shard_map/ppermute | solution.py:25
  6.0 8.9 %collective-permute-start.1 = (bf16[1,104,1600]{2,1,0:T(8,128)(2,1)S(1)}, bf16[1,104,1600]{2,1,0:T(8,128)(2,1)S(1)}, u32[]{:S(2)}, u32[]{:S(2)}) collective-permute-start(bf16[1,104,1600]{2,1,0:T(8,128)(2,1)S(1)} %pad.4), channel_id=1, source_target_pairs={{0,3},{1,0},{2,1},{3,2},{4,7},{5,4},{6,5},{7,6},{8,11},{9,8},{10,9... | collective-permute-start | bytes 998408 | tf_op jit(solution)/shard_map/ppermute | solution.py:25
  14.9 7.6 %collective-permute-start.2 = (bf16[1,104,1600]{2,1,0:T(8,128)(2,1)S(1)}, bf16[1,104,1600]{2,1,0:T(8,128)(2,1)S(1)}, u32[]{:S(2)}, u32[]{:S(2)}) collective-permute-start(bf16[1,104,1600]{2,1,0:T(8,128)(2,1)S(1)} %collective-permute-done), channel_id=1, source_target_pairs={{0,1},{1,2},{2,3},{3,0},{4,5},{5,6},{6,7},{7,4},{8,9},{9,10},{10,1... | collective-permute-start | bytes 998408 | tf_op jit(solution)/shard_map/ppermute | solution.py:25
  14.9 12.7 %collective-permute-start.8 = (bf16[1,104,1600]{2,1,0:T(8,128)(2,1)S(1)}, bf16[1,104,1600]{2,1,0:T(8,128)(2,1)S(1)}, u32[]{:S(2)}, u32[]{:S(2)}) collective-permute-start(bf16[1,104,1600]{2,1,0:T(8,128)(2,1)S(1)} %collective-permute-done.1), channel_id=1, source_target_pairs={{32,60},{33,61},{34,62},{35,63},{36,32},{37,33},{38,34},{39,35},{4... | collective-permute-start | bytes 998408 | tf_op jit(solution)/shard_map/ppermute | solution.py:25
  22.6 12.7 %collective-permute-start.9 = (bf16[1,104,1600]{2,1,0:T(8,128)(2,1)S(1)}, bf16[1,104,1600]{2,1,0:T(8,128)(2,1)S(1)}, u32[]{:S(2)}, u32[]{:S(2)}) collective-permute-start(bf16[1,104,1600]{2,1,0:T(8,128)(2,1)S(1)} %collective-permute-done.2), channel_id=1, source_target_pairs={{32,36},{33,37},{34,38},{35,39},{36,40},{37,41},{38,42},{39,43},{4... | collective-permute-start | bytes 998408 | tf_op jit(solution)/shard_map/ppermute | solution.py:25
  24.7 10.5 %copy-start.1 = (bf16[4,104,1600]{2,1,0:T(8,128)(2,1)}, bf16[4,104,1600]{2,1,0:T(8,128)(2,1)S(1)}, u32[]{:S(2)}) copy-start(bf16[4,104,1600]{2,1,0:T(8,128)(2,1)S(1)} %pad_maximum_fusion) | copy-start | bytes 3993604
  24.7 19.0 %collective-permute-start.3 = (bf16[4,104,1600]{2,1,0:T(8,128)(2,1)S(1)}, bf16[4,104,1600]{2,1,0:T(8,128)(2,1)}, u32[]{:S(2)}, u32[]{:S(2)}) collective-permute-start(bf16[4,104,1600]{2,1,0:T(8,128)(2,1)S(1)} %pad_maximum_fusion), channel_id=1, source_target_pairs={{0,4},{1,5},{2,6},{3,7},{4,8},{5,9},{6,10},{7,11},{8,12},{9,13},{1... | collective-permute-start | bytes 3993608 | tf_op jit(solution)/shard_map/ppermute | solution.py:25
  26.1 17.7 %collective-permute-start.5 = (bf16[4,104,1600]{2,1,0:T(8,128)(2,1)S(1)}, bf16[4,104,1600]{2,1,0:T(8,128)(2,1)}, u32[]{:S(2)}, u32[]{:S(2)}) collective-permute-start(bf16[4,104,1600]{2,1,0:T(8,128)(2,1)S(1)} %pad_maximum_fusion), channel_id=1, source_target_pairs={{0,28},{1,29},{2,30},{3,31},{4,0},{5,1},{6,2},{7,3},{8,4},{9,5},{1... | collective-permute-start | bytes 3993608 | tf_op jit(solution)/shard_map/ppermute | solution.py:25
  27.6 16.1 %copy-start.3 = (bf16[1,104,1600]{2,1,0:T(8,128)(2,1)}, bf16[1,104,1600]{2,1,0:T(8,128)(2,1)S(1)}, u32[]{:S(2)}) copy-start(bf16[1,104,1600]{2,1,0:T(8,128)(2,1)S(1)} %collective-permute-done.8) | copy-start | bytes 998404
  35.2 10.6 %copy-start.5 = (bf16[1,104,1600]{2,1,0:T(8,128)(2,1)}, bf16[1,104,1600]{2,1,0:T(8,128)(2,1)S(1)}, u32[]{:S(2)}) copy-start(bf16[1,104,1600]{2,1,0:T(8,128)(2,1)S(1)} %collective-permute-done.9) | copy-start | bytes 998404
  35.2 23.6 %collective-permute-start.13 = (bf16[1600,512]{1,0:T(8,128)(2,1)}, bf16[1600,512]{1,0:T(8,128)(2,1)S(1)}, u32[]{:S(2)}, u32[]{:S(2)}) collective-permute-start(bf16[1600,512]{1,0:T(8,128)(2,1)} %own_ref.1), channel_id=1, source_target_pairs={{0,192},{32,96},{64,0},{96,160},{128,64},{160,224},{192,128},{224,... | collective-permute-start | bytes 4915208 | tf_op jit(solution)/shard_map/ppermute | solution.py:14
  35.3 10.5 %collective-permute-start.10 = (bf16[1,104,1600]{2,1,0:T(8,128)(2,1)S(1)}, bf16[1,104,1600]{2,1,0:T(8,128)(2,1)S(1)}, u32[]{:S(2)}, u32[]{:S(2)}) collective-permute-start(bf16[1,104,1600]{2,1,0:T(8,128)(2,1)S(1)} %collective-permute-done.8), channel_id=1, source_target_pairs={{32,60},{33,61},{34,62},{35,63},{36,32},{37,33},{38,34},{39,35},{4... | collective-permute-start | bytes 998408 | tf_op jit(solution)/shard_map/ppermute | solution.py:25
  37.3 13.4 %collective-permute-start.11 = (bf16[1,104,1600]{2,1,0:T(8,128)(2,1)S(1)}, bf16[1,104,1600]{2,1,0:T(8,128)(2,1)S(1)}, u32[]{:S(2)}, u32[]{:S(2)}) collective-permute-start(bf16[1,104,1600]{2,1,0:T(8,128)(2,1)S(1)} %collective-permute-done.9), channel_id=1, source_target_pairs={{32,36},{33,37},{34,38},{35,39},{36,40},{37,41},{38,42},{39,43},{4... | collective-permute-start | bytes 998408 | tf_op jit(solution)/shard_map/ppermute | solution.py:25
  43.7 37.5 %collective-permute-start.4 = (bf16[4,104,1600]{2,1,0:T(8,128)(2,1)}, bf16[4,104,1600]{2,1,0:T(8,128)(2,1)}, u32[]{:S(2)}, u32[]{:S(2)}) collective-permute-start(bf16[4,104,1600]{2,1,0:T(8,128)(2,1)} %collective-permute-done.3), channel_id=1, source_target_pairs={{0,4},{1,5},{2,6},{3,7},{4,8},{5,9},{6,10},{7,11},{8,12},{9,13},{1... | collective-permute-start | bytes 3993608 | tf_op jit(solution)/shard_map/ppermute | solution.py:25
  43.8 37.6 %collective-permute-start.6 = (bf16[4,104,1600]{2,1,0:T(8,128)(2,1)}, bf16[4,104,1600]{2,1,0:T(8,128)(2,1)}, u32[]{:S(2)}, u32[]{:S(2)}) collective-permute-start(bf16[4,104,1600]{2,1,0:T(8,128)(2,1)} %collective-permute-done.5), channel_id=1, source_target_pairs={{0,28},{1,29},{2,30},{3,31},{4,0},{5,1},{6,2},{7,3},{8,4},{9,5},{1... | collective-permute-start | bytes 3993608 | tf_op jit(solution)/shard_map/ppermute | solution.py:25
  45.8 0.8 copy-start.9
  50.7 0.8 copy-start.7
  52.4 13.6 %collective-permute-start.12 = (bf16[800,512]{1,0:T(8,128)(2,1)}, bf16[800,512]{1,0:T(8,128)(2,1)}, u32[]{:S(2)}, u32[]{:S(2)}) collective-permute-start(bf16[800,512]{1,0:T(8,128)(2,1)} %slice.12), channel_id=1, source_target_pairs={{0,64},{32,224},{64,128},{96,32},{128,192},{160,96},{192,0},{224,1... | collective-permute-start | bytes 2457608 | tf_op jit(solution)/shard_map/ppermute | solution.py:14
  52.8 6.3 %copy-start.4 = (bf16[1,104,1600]{2,1,0:T(8,128)(2,1)S(1)}, bf16[1,104,1600]{2,1,0:T(8,128)(2,1)}, u32[]{:S(2)}) copy-start(bf16[1,104,1600]{2,1,0:T(8,128)(2,1)} %copy-done.3) | copy-start | bytes 998404
  52.8 6.3 %copy-start.6 = (bf16[1,104,1600]{2,1,0:T(8,128)(2,1)S(1)}, bf16[1,104,1600]{2,1,0:T(8,128)(2,1)}, u32[]{:S(2)}) copy-start(bf16[1,104,1600]{2,1,0:T(8,128)(2,1)} %copy-done.5) | copy-start | bytes 998404
  52.8 6.3 %copy-start.10 = (bf16[1,104,1600]{2,1,0:T(8,128)(2,1)S(1)}, bf16[1,104,1600]{2,1,0:T(8,128)(2,1)}, u32[]{:S(2)}) copy-start(bf16[1,104,1600]{2,1,0:T(8,128)(2,1)} %copy-done.9) | copy-start | bytes 998404
  52.8 31.4 %collective-permute-start.17 = (bf16[4,104,1600]{2,1,0:T(8,128)(2,1)}, bf16[4,104,1600]{2,1,0:T(8,128)(2,1)S(1)}, u32[]{:S(2)}, u32[]{:S(2)}) collective-permute-start(bf16[4,104,1600]{2,1,0:T(8,128)(2,1)} %copy-done.1), channel_id=1, source_target_pairs={{0,32},{32,0},{1,33},{33,1},{2,34},{34,2},{3,35},{35,3},{4,36},{36... | collective-permute-start | bytes 3993608 | tf_op jit(solution)/shard_map/ppermute | solution.py:29
  58.9 22.3 %copy-start.8 = (bf16[1,104,1600]{2,1,0:T(8,128)(2,1)S(1)}, bf16[1,104,1600]{2,1,0:T(8,128)(2,1)}, u32[]{:S(2)}) copy-start(bf16[1,104,1600]{2,1,0:T(8,128)(2,1)} %copy-done.7) | copy-start | bytes 998404
  58.9 22.4 %collective-permute-start.14 = (bf16[800,512]{1,0:T(8,128)(2,1)S(1)}, bf16[800,512]{1,0:T(8,128)(2,1)S(1)}, u32[]{:S(2)}, u32[]{:S(2)}) collective-permute-start(bf16[800,512]{1,0:T(8,128)(2,1)S(1)} %slice.16), channel_id=1, source_target_pairs={{0,192},{32,96},{64,0},{96,160},{128,64},{160,224},{192,128},{224,... | collective-permute-start | bytes 2457608 | tf_op jit(solution)/shard_map/ppermute | solution.py:14
  66.0 18.4 %collective-permute-start.19 = (bf16[4,104,1600]{2,1,0:T(8,128)(2,1)}, bf16[4,104,1600]{2,1,0:T(8,128)(2,1)S(1)}, u32[]{:S(2)}, u32[]{:S(2)}) collective-permute-start(bf16[4,104,1600]{2,1,0:T(8,128)(2,1)} %collective-permute-done.5), channel_id=1, source_target_pairs={{0,32},{32,0},{1,33},{33,1},{2,34},{34,2},{3,35},{35,3},{4,36},{36... | collective-permute-start | bytes 3993608 | tf_op jit(solution)/shard_map/ppermute | solution.py:29
  81.2 10.5 %collective-permute-start.18 = (bf16[4,104,1600]{2,1,0:T(8,128)(2,1)}, bf16[4,104,1600]{2,1,0:T(8,128)(2,1)S(1)}, u32[]{:S(2)}, u32[]{:S(2)}) collective-permute-start(bf16[4,104,1600]{2,1,0:T(8,128)(2,1)} %collective-permute-done.3), channel_id=1, source_target_pairs={{0,32},{32,0},{1,33},{33,1},{2,34},{34,2},{3,35},{35,3},{4,36},{36... | collective-permute-start | bytes 3993608 | tf_op jit(solution)/shard_map/ppermute | solution.py:29
  81.7 10.0 %collective-permute-start.21 = (bf16[4,104,1600]{2,1,0:T(8,128)(2,1)S(1)}, bf16[4,104,1600]{2,1,0:T(8,128)(2,1)S(1)}, u32[]{:S(2)}, u32[]{:S(2)}) collective-permute-start(bf16[4,104,1600]{2,1,0:T(8,128)(2,1)S(1)} %get-tuple-element.39), channel_id=1, source_target_pairs={{0,32},{32,0},{1,33},{33,1},{2,34},{34,2},{3,35},{35,3},{4,36},{36... | collective-permute-start | bytes 3993608 | tf_op jit(solution)/shard_map/ppermute | solution.py:29
  84.0 7.7 %collective-permute-start.20 = (bf16[4,104,1600]{2,1,0:T(8,128)(2,1)}, bf16[4,104,1600]{2,1,0:T(8,128)(2,1)S(1)}, u32[]{:S(2)}, u32[]{:S(2)}) collective-permute-start(bf16[4,104,1600]{2,1,0:T(8,128)(2,1)} %collective-permute-done.4), channel_id=1, source_target_pairs={{0,32},{32,0},{1,33},{33,1},{2,34},{34,2},{3,35},{35,3},{4,36},{36... | collective-permute-start | bytes 3993608 | tf_op jit(solution)/shard_map/ppermute | solution.py:29
  84.1 7.6 %copy-start.2 = (bf16[4,104,1600]{2,1,0:T(8,128)(2,1)S(1)}, bf16[4,104,1600]{2,1,0:T(8,128)(2,1)}, u32[]{:S(2)}) copy-start(bf16[4,104,1600]{2,1,0:T(8,128)(2,1)} %copy-done.1) | copy-start | bytes 3993604
  84.1 18.9 %collective-permute-start.15 = (bf16[4,104,1600]{2,1,0:T(8,128)(2,1)S(1)}, bf16[4,104,1600]{2,1,0:T(8,128)(2,1)S(1)}, u32[]{:S(2)}, u32[]{:S(2)}) collective-permute-start(bf16[4,104,1600]{2,1,0:T(8,128)(2,1)S(1)} %get-tuple-element.40), channel_id=1, source_target_pairs={{0,4},{1,5},{2,6},{3,7},{4,8},{5,9},{6,10},{7,11},{8,12},{9,13},{1... | collective-permute-start | bytes 3993608 | tf_op jit(solution)/shard_map/ppermute | solution.py:25
  84.3 18.7 %collective-permute-start.16 = (bf16[4,104,1600]{2,1,0:T(8,128)(2,1)S(1)}, bf16[4,104,1600]{2,1,0:T(8,128)(2,1)S(1)}, u32[]{:S(2)}, u32[]{:S(2)}) collective-permute-start(bf16[4,104,1600]{2,1,0:T(8,128)(2,1)S(1)} %get-tuple-element.39), channel_id=1, source_target_pairs={{0,28},{1,29},{2,30},{3,31},{4,0},{5,1},{6,2},{7,3},{8,4},{9,5},{1... | collective-permute-start | bytes 3993608 | tf_op jit(solution)/shard_map/ppermute | solution.py:25
  91.7 25.3 %copy-start = (f32[512,1600]{0,1:T(8,128)S(1)}, f32[512,1600]{0,1:T(8,128)}, u32[]{:S(2)}) copy-start(f32[512,1600]{0,1:T(8,128)} %param.3) | copy-start | bytes 9830404
  103.1 14.0 %collective-permute-start.22 = (bf16[4,104,1600]{2,1,0:T(8,128)(2,1)S(1)}, bf16[4,104,1600]{2,1,0:T(8,128)(2,1)S(1)}, u32[]{:S(2)}, u32[]{:S(2)}) collective-permute-start(bf16[4,104,1600]{2,1,0:T(8,128)(2,1)S(1)} %collective-permute-done.15), channel_id=1, source_target_pairs={{0,32},{32,0},{1,33},{33,1},{2,34},{34,2},{3,35},{35,3},{4,36},{36... | collective-permute-start | bytes 3993608 | tf_op jit(solution)/shard_map/ppermute | solution.py:29
  104.2 12.9 %collective-permute-start.23 = (bf16[4,104,1600]{2,1,0:T(8,128)(2,1)S(1)}, bf16[4,104,1600]{2,1,0:T(8,128)(2,1)S(1)}, u32[]{:S(2)}, u32[]{:S(2)}) collective-permute-start(bf16[4,104,1600]{2,1,0:T(8,128)(2,1)S(1)} %collective-permute-done.16), channel_id=1, source_target_pairs={{0,32},{32,0},{1,33},{33,1},{2,34},{34,2},{3,35},{35,3},{4,36},{36... | collective-permute-start | bytes 3993608 | tf_op jit(solution)/shard_map/ppermute | solution.py:29
  104.2 11.4 %collective-permute-start.24 = (bf16[2,104,1600]{2,1,0:T(8,128)(2,1)S(1)}, bf16[2,104,1600]{2,1,0:T(8,128)(2,1)S(1)}, u32[]{:S(2)}, u32[]{:S(2)}) collective-permute-start(bf16[2,104,1600]{2,1,0:T(8,128)(2,1)S(1)} %slice.14), channel_id=1, source_target_pairs={{0,4},{1,5},{2,6},{3,7},{4,8},{5,9},{6,10},{7,11},{8,12},{9,13},{1... | collective-permute-start | bytes 1996808 | tf_op jit(solution)/shard_map/ppermute | solution.py:25
  104.4 12.6 %collective-permute-start.25 = (bf16[2,104,1600]{2,1,0:T(8,128)(2,1)S(1)}, bf16[2,104,1600]{2,1,0:T(8,128)(2,1)S(1)}, u32[]{:S(2)}, u32[]{:S(2)}) collective-permute-start(bf16[2,104,1600]{2,1,0:T(8,128)(2,1)S(1)} %slice.15), channel_id=1, source_target_pairs={{0,28},{1,29},{2,30},{3,31},{4,0},{5,1},{6,2},{7,3},{8,4},{9,5},{1... | collective-permute-start | bytes 1996808 | tf_op jit(solution)/shard_map/ppermute | solution.py:25
  115.6 5.4 %collective-permute-start.26 = (bf16[2,104,1600]{2,1,0:T(8,128)(2,1)S(1)}, bf16[2,104,1600]{2,1,0:T(8,128)(2,1)S(1)}, u32[]{:S(2)}, u32[]{:S(2)}) collective-permute-start(bf16[2,104,1600]{2,1,0:T(8,128)(2,1)S(1)} %collective-permute-done.24), channel_id=1, source_target_pairs={{0,32},{32,0},{1,33},{33,1},{2,34},{34,2},{3,35},{35,3},{4,36},{36... | collective-permute-start | bytes 1996808 | tf_op jit(solution)/shard_map/ppermute | solution.py:29
  117.0 4.0 %collective-permute-start.27 = (bf16[2,104,1600]{2,1,0:T(8,128)(2,1)S(1)}, bf16[2,104,1600]{2,1,0:T(8,128)(2,1)S(1)}, u32[]{:S(2)}, u32[]{:S(2)}) collective-permute-start(bf16[2,104,1600]{2,1,0:T(8,128)(2,1)S(1)} %collective-permute-done.25), channel_id=1, source_target_pairs={{0,32},{32,0},{1,33},{33,1},{2,34},{34,2},{3,35},{35,3},{4,36},{36... | collective-permute-start | bytes 1996808 | tf_op jit(solution)/shard_map/ppermute | solution.py:29

commit v6 on v5

--- a/solution.py
+++ b/solution.py
@@ -35,7 +35,7 @@
 
 
 def gather(block, height, amplitudes, rows, multiply_first):
-    count = amplitudes.shape[0]
+    cut = amplitudes.shape[0] // 4 * 3
     along, back = ((0, 1), (1, 0)), ((0, -1), (-1, 0))
     up, down = ((1, 0), (0, 1)), ((-1, 0), (0, -1))
     near = along_row(amplitudes, rows, 1, -1)
@@ -49,22 +49,24 @@
     other = along_row(own, rows, -1, 1)
     b3 = travel(b2, None, back[1])
     a4 = travel(a3, None, along[1])
-    near, b3, a4 = lax.optimization_barrier((near, b3, a4))
-    far_low = along_row(near[: count // 2], rows, 1, -1)
+    far_low = along_row(near[:cut], rows, 1, -1)
     rest = jnp.concatenate([b2, a3, b3, a4])
     u1, d1 = travel(pack, *up), travel(pack, *down)
     u2, d2 = travel(u1, *up), travel(d1, down[0], None)
-    far_high = along_row(other[count // 2 :], rows, -1, 1)
+    far_high = along_row(other[cut:], rows, -1, 1)
     u2, d2, far_low, far_high = lax.optimization_barrier((u2, d2, far_low, far_high))
     first = lax.axis_index("col") == 0
     kept = jnp.where(first, d2, rest)
     u3, d3 = travel(jnp.where(first, u2, rest), *up), travel(kept, *down)
+    early = [pack, u1, d1, u2, kept]
+    early = early + [swap(piece) for piece in early]
     factors = arrange(amplitudes, near, other, far_low, far_high, rows, height, [20, 8, 4])
-    early = [pack, u1, d1, u2, kept]
-    total = multiply_first(factors[0], early + [swap(piece) for piece in early])
-    u3, d3, total = lax.optimization_barrier((u3, d3, total))
+    u3, d3, factors, early = lax.optimization_barrier((u3, d3, factors, early))
     u4, d4 = travel(u3[:2], *up), travel(d3[2:], *down)
-    return factors[1:], total, [u3, d3, swap(u3), swap(d3)], [u4, d4, swap(u4), swap(d4)]
+    more = [u3, d3, swap(u3), swap(d3)]
+    total = multiply_first(factors[0], early)
+    u4, d4, total = lax.optimization_barrier((u4, d4, total))
+    return factors[1:], total, more, [u4, d4, swap(u4), swap(d4)]
 
 
 def arrange(own, near, other, far_low, far_high, rows, height, cuts):
@@ -78,7 +80,7 @@
         z, y = depth // Y, lax.rem(depth, Y)
         held[:, :, height:, :] = jnp.zeros((2, Z * Y, full - height, width), held.dtype)
         steps = rows - 1 + core * (2 - rows), 1 + core * (rows - 2)
-        sources = [(own_ref, 0, 0), (near_ref, steps[0], 0), (other_ref, steps[1], 0), (low_ref, 2, 0), (high_ref, 2, count // 2)]
+        sources = [(own_ref, 0, 0), (near_ref, steps[0], 0), (other_ref, steps[1], 0), (low_ref, 2, 0), (high_ref, 2, far_low.shape[0] // height)]
         for ref, step, start in sources:
             block_row = lax.rem(x + step, rows)
             half = block_row // (rows // 2)

time: 125 us -> 122 us (0.976)
  starting transfers between devices: 58.1 us -> 41.8 us
  waiting for transfers between devices: 38.6 us -> 49.5 us
  local copies, waits for them, and re-layouts: 3.78 us -> 6.18 us
    ppermute x9, starting transfers between devices: 26.3 us -> 9.21 us  [swap(): return lax.ppermute(array, 'col', [(0, 1), (1, 0)])]
    ppermute x15, waiting for transfers between devices: 31.8 us -> 40.3 us  [travel(): return lax.ppermute(array, ('col', 'depth'), pairs)]
    ppermute x4, waiting for transfers between devices: 6.81 us -> 9.25 us  [along_row(): return lax.ppermute(array, ('row', 'col'), pairs)]
    ppermute x4, starting transfers between devices: 3.88 us -> 6.06 us  [along_row(): return lax.ppermute(array, ('row', 'col'), pairs)]
    ppermute x15, starting transfers between devices: 27.9 us -> 26.5 us  [travel(): return lax.ppermute(array, ('col', 'depth'), pairs)]
    unnamed x25 -> x15, local copies, waits for them, and re-layouts: 1.64 us -> 2.88 us
  transfers between devices with their start and end apart: 28 -> 28, of which waited for: 9 -> 9; matrix products, arithmetic and copies ran while one was open for 2% -> 5% of each run, Pallas kernels for 16% -> 16%
where the time goes in v6:
time: 122 us
  waiting for transfers between devices  49.5 us (41%)
  starting transfers between devices  41.8 us (34%)
  Pallas kernels  23.3 us (19%)
  local copies, waits for them, and re-layouts  6.18 us (5%)
    ppermute x15, waiting for transfers between devices, travel(): return lax.ppermute(array, ('col', 'depth'), pairs)  40.3 us
    ppermute x15, starting transfers between devices, travel(): return lax.ppermute(array, ('col', 'depth'), pairs)  26.5 us
    pallas_call x3, Pallas kernels, multiply(): pl.pallas_call(body, out_shape=jax.ShapeDtypeStruct(shape, jnp.float32),...  18.5 us
    ppermute x4, waiting for transfers between devices, along_row(): return lax.ppermute(array, ('row', 'col'), pairs)  9.25 us
    ppermute x9, starting transfers between devices, swap(): return lax.ppermute(array, 'col', [(0, 1), (1, 0)])  9.21 us
    ppermute x4, starting transfers between devices, along_row(): return lax.ppermute(array, ('row', 'col'), pairs)  6.06 us
    pallas_call x1, Pallas kernels, arrange(): pl.pallas_call(kernel, out_shape=[jax.ShapeDtypeStruct((2, width, blocks...  4.82 us
    unnamed x15, local copies, waits for them, and re-layouts  2.88 us
  transfers between devices with their start and end apart: 28, of which 9 were waited for; matrix products, arithmetic and copies ran while one was open for 5% of the time, Pallas kernels for 16%

profile of v6, /device:TPU:1, one launch (start us, length us, event | category | flops | bytes accessed | tf_op | source)
XLA Modules:
  0.0 121.7 jit_solution(17676919926097869968)
XLA Ops:
  0.0 3.3 %collective-permute-start.7 = (bf16[1600,512]{1,0:T(8,128)(2,1)}, bf16[1600,512]{1,0:T(8,128)(2,1)S(1)}, u32[]{:S(2)}, u32[]{:S(2)}) collective-permute-start(bf16[1600,512]{1,0:T(8,128)(2,1)} %own_ref.1), channel_id=1, source_target_pairs={{0,64},{32,224},{64,128},{96,32},{128,192},{160,96},{192,0},{224,1... | collective-permute-start | bytes 4915208 | tf_op jit(solution)/shard_map/ppermute | solution.py:14
  3.3 1.0 pad.4
  4.3 1.7 %collective-permute-start = (bf16[1,104,1600]{2,1,0:T(8,128)(2,1)S(1)}, bf16[1,104,1600]{2,1,0:T(8,128)(2,1)S(1)}, u32[]{:S(2)}, u32[]{:S(2)}) collective-permute-start(bf16[1,104,1600]{2,1,0:T(8,128)(2,1)S(1)} %pad.4), channel_id=1, source_target_pairs={{0,1},{1,2},{2,3},{3,0},{4,5},{5,6},{6,7},{7,4},{8,9},{9,10},{10,1... | collective-permute-start | bytes 998408 | tf_op jit(solution)/shard_map/ppermute | solution.py:25
  6.0 4.0 %collective-permute-start.1 = (bf16[1,104,1600]{2,1,0:T(8,128)(2,1)S(1)}, bf16[1,104,1600]{2,1,0:T(8,128)(2,1)S(1)}, u32[]{:S(2)}, u32[]{:S(2)}) collective-permute-start(bf16[1,104,1600]{2,1,0:T(8,128)(2,1)S(1)} %pad.4), channel_id=1, source_target_pairs={{0,3},{1,0},{2,1},{3,2},{4,7},{5,4},{6,5},{7,6},{8,11},{9,8},{10,9... | collective-permute-start | bytes 998408 | tf_op jit(solution)/shard_map/ppermute | solution.py:25
  10.1 4.9 %collective-permute-done = bf16[1,104,1600]{2,1,0:T(8,128)(2,1)S(1)} collective-permute-done((bf16[1,104,1600]{2,1,0:T(8,128)(2,1)S(1)}, bf16[1,104,1600]{2,1,0:T(8,128)(2,1)S(1)}, u32[]{:S(2)}, u32[]{:S(2)}) %collective-permute-start) | collective-permute-done | bytes 332832 | tf_op jit(solution)/shard_map/ppermute | solution.py:25
  14.9 0.0 collective-permute-start.2
  14.9 0.0 collective-permute-done.1
  14.9 4.7 %collective-permute-start.8 = (bf16[1,104,1600]{2,1,0:T(8,128)(2,1)S(1)}, bf16[1,104,1600]{2,1,0:T(8,128)(2,1)S(1)}, u32[]{:S(2)}, u32[]{:S(2)}) collective-permute-start(bf16[1,104,1600]{2,1,0:T(8,128)(2,1)S(1)} %collective-permute-done.1), channel_id=1, source_target_pairs={{32,60},{33,61},{34,62},{35,63},{36,32},{37,33},{38,34},{39,35},{4... | collective-permute-start | bytes 998408 | tf_op jit(solution)/shard_map/ppermute | solution.py:25
  19.6 3.0 %collective-permute-done.2 = bf16[1,104,1600]{2,1,0:T(8,128)(2,1)S(1)} collective-permute-done((bf16[1,104,1600]{2,1,0:T(8,128)(2,1)S(1)}, bf16[1,104,1600]{2,1,0:T(8,128)(2,1)S(1)}, u32[]{:S(2)}, u32[]{:S(2)}) %collective-permute-start.2) | collective-permute-done | bytes 332832 | tf_op jit(solution)/shard_map/ppermute | solution.py:25
  22.6 1.9 %collective-permute-start.9 = (bf16[1,104,1600]{2,1,0:T(8,128)(2,1)S(1)}, bf16[1,104,1600]{2,1,0:T(8,128)(2,1)}, u32[]{:S(2)}, u32[]{:S(2)}) collective-permute-start(bf16[1,104,1600]{2,1,0:T(8,128)(2,1)S(1)} %collective-permute-done.2), channel_id=1, source_target_pairs={{32,36},{33,37},{34,38},{35,39},{36,40},{37,41},{38,42},{39,43},{4... | collective-permute-start | bytes 998408 | tf_op jit(solution)/shard_map/ppermute | solution.py:25
  24.5 0.2 pad_maximum_fusion
  24.7 0.0 copy-start.1
  24.7 1.4 %collective-permute-start.3 = (bf16[4,104,1600]{2,1,0:T(8,128)(2,1)S(1)}, bf16[4,104,1600]{2,1,0:T(8,128)(2,1)}, u32[]{:S(2)}, u32[]{:S(2)}) collective-permute-start(bf16[4,104,1600]{2,1,0:T(8,128)(2,1)S(1)} %pad_maximum_fusion), channel_id=1, source_target_pairs={{0,4},{1,5},{2,6},{3,7},{4,8},{5,9},{6,10},{7,11},{8,12},{9,13},{1... | collective-permute-start | bytes 3993608 | tf_op jit(solution)/shard_map/ppermute | solution.py:25
  26.1 1.5 %collective-permute-start.5 = (bf16[4,104,1600]{2,1,0:T(8,128)(2,1)S(1)}, bf16[4,104,1600]{2,1,0:T(8,128)(2,1)}, u32[]{:S(2)}, u32[]{:S(2)}) collective-permute-start(bf16[4,104,1600]{2,1,0:T(8,128)(2,1)S(1)} %pad_maximum_fusion), channel_id=1, source_target_pairs={{0,28},{1,29},{2,30},{3,31},{4,0},{5,1},{6,2},{7,3},{8,4},{9,5},{1... | collective-permute-start | bytes 3993608 | tf_op jit(solution)/shard_map/ppermute | solution.py:25
  27.6 0.0 collective-permute-done.8
  27.6 6.8 %collective-permute-done.9 = bf16[1,104,1600]{2,1,0:T(8,128)(2,1)} collective-permute-done((bf16[1,104,1600]{2,1,0:T(8,128)(2,1)S(1)}, bf16[1,104,1600]{2,1,0:T(8,128)(2,1)}, u32[]{:S(2)}, u32[]{:S(2)}) %collective-permute-start.9) | collective-permute-done | bytes 332832 | tf_op jit(solution)/shard_map/ppermute | solution.py:25
  34.4 0.0 collective-permute-done.7.near_ref
  34.4 0.0 collective-permute-start.11
  34.4 1.2 slice.12
  35.6 2.7 %collective-permute-start.10 = (bf16[1200,512]{1,0:T(8,128)(2,1)}, bf16[1200,512]{1,0:T(8,128)(2,1)}, u32[]{:S(2)}, u32[]{:S(2)}) collective-permute-start(bf16[1200,512]{1,0:T(8,128)(2,1)} %slice.12), channel_id=1, source_target_pairs={{0,64},{32,224},{64,128},{96,32},{128,192},{160,96},{192,0},{224,1... | collective-permute-start | bytes 3686408 | tf_op jit(solution)/shard_map/ppermute | solution.py:14
  38.2 1.9 %collective-permute-start.13 = (bf16[1,104,1600]{2,1,0:T(8,128)(2,1)S(1)}, bf16[1,104,1600]{2,1,0:T(8,128)(2,1)S(1)}, u32[]{:S(2)}, u32[]{:S(2)}) collective-permute-start(bf16[1,104,1600]{2,1,0:T(8,128)(2,1)S(1)} %collective-permute-done.8), channel_id=1, source_target_pairs={{32,60},{33,61},{34,62},{35,63},{36,32},{37,33},{38,34},{39,35},{4... | collective-permute-start | bytes 998408 | tf_op jit(solution)/shard_map/ppermute | solution.py:25
  40.2 3.6 %collective-permute-done.3 = bf16[4,104,1600]{2,1,0:T(8,128)(2,1)} collective-permute-done((bf16[4,104,1600]{2,1,0:T(8,128)(2,1)S(1)}, bf16[4,104,1600]{2,1,0:T(8,128)(2,1)}, u32[]{:S(2)}, u32[]{:S(2)}) %collective-permute-start.3) | collective-permute-done | bytes 1331232 | tf_op jit(solution)/shard_map/ppermute | solution.py:25
  43.7 0.0 collective-permute-start.4
  43.7 0.0 collective-permute-done.5
  43.8 1.8 %collective-permute-start.6 = (bf16[4,104,1600]{2,1,0:T(8,128)(2,1)}, bf16[4,104,1600]{2,1,0:T(8,128)(2,1)}, u32[]{:S(2)}, u32[]{:S(2)}) collective-permute-start(bf16[4,104,1600]{2,1,0:T(8,128)(2,1)} %collective-permute-done.5), channel_id=1, source_target_pairs={{0,28},{1,29},{2,30},{3,31},{4,0},{5,1},{6,2},{7,3},{8,4},{9,5},{1... | collective-permute-start | bytes 3993608 | tf_op jit(solution)/shard_map/ppermute | solution.py:25
  45.5 2.4 %collective-permute-done.13 = bf16[1,104,1600]{2,1,0:T(8,128)(2,1)S(1)} collective-permute-done((bf16[1,104,1600]{2,1,0:T(8,128)(2,1)S(1)}, bf16[1,104,1600]{2,1,0:T(8,128)(2,1)S(1)}, u32[]{:S(2)}, u32[]{:S(2)}) %collective-permute-start.13) | collective-permute-done | bytes 332832 | tf_op jit(solution)/shard_map/ppermute | solution.py:25
  48.0 0.7 copy-done.4
  48.7 2.1 %collective-permute-start.14 = (bf16[1,104,1600]{2,1,0:T(8,128)(2,1)}, bf16[1,104,1600]{2,1,0:T(8,128)(2,1)}, u32[]{:S(2)}, u32[]{:S(2)}) collective-permute-start(bf16[1,104,1600]{2,1,0:T(8,128)(2,1)} %collective-permute-done.9), channel_id=1, source_target_pairs={{32,36},{33,37},{34,38},{35,39},{36,40},{37,41},{38,42},{39,43},{4... | collective-permute-start | bytes 998408 | tf_op jit(solution)/shard_map/ppermute | solution.py:25
  50.8 1.1 constant_dynamic-update-slice_fusion.3
  51.9 11.3 %collective-permute-done.14 = bf16[1,104,1600]{2,1,0:T(8,128)(2,1)} collective-permute-done((bf16[1,104,1600]{2,1,0:T(8,128)(2,1)}, bf16[1,104,1600]{2,1,0:T(8,128)(2,1)}, u32[]{:S(2)}, u32[]{:S(2)}) %collective-permute-start.14) | collective-permute-done | bytes 332832 | tf_op jit(solution)/shard_map/ppermute | solution.py:25
  63.2 0.0 collective-permute-start.17
  63.2 4.0 %collective-permute-done.11.other_ref = bf16[1600,512]{1,0:T(8,128)(2,1)S(1)} collective-permute-done((bf16[1600,512]{1,0:T(8,128)(2,1)}, bf16[1600,512]{1,0:T(8,128)(2,1)S(1)}, u32[]{:S(2)}, u32[]{:S(2)}) %collective-permute-start.11) | collective-permute-done | bytes 1638432 | tf_op jit(solution)/shard_map/ppermute | solution.py:14
  67.1 0.0 collective-permute-start.18
  67.2 1.0 constant_dynamic-update-slice_fusion.2
  68.2 0.0 collective-permute-done.10.low_ref
  68.2 0.1 collective-permute-start.12
  68.4 1.0 constant_dynamic-update-slice_fusion
  69.4 1.7 %collective-permute-start.19 = (bf16[4,104,1600]{2,1,0:T(8,128)(2,1)}, bf16[4,104,1600]{2,1,0:T(8,128)(2,1)S(1)}, u32[]{:S(2)}, u32[]{:S(2)}) collective-permute-start(bf16[4,104,1600]{2,1,0:T(8,128)(2,1)} %collective-permute-done.5), channel_id=1, source_target_pairs={{0,32},{32,0},{1,33},{33,1},{2,34},{34,2},{3,35},{35,3},{4,36},{36... | collective-permute-start | bytes 3993608 | tf_op jit(solution)/shard_map/ppermute | solution.py:29
  71.0 5.3 %collective-permute-done.12.high_ref = bf16[400,512]{1,0:T(8,128)(2,1)S(1)} collective-permute-done((bf16[400,512]{1,0:T(8,128)(2,1)S(1)}, bf16[400,512]{1,0:T(8,128)(2,1)S(1)}, u32[]{:S(2)}, u32[]{:S(2)}) %collective-permute-start.12) | collective-permute-done | bytes 409632 | tf_op jit(solution)/shard_map/ppermute | solution.py:14
  76.3 0.3 broadcast_select_fusion
  76.6 0.1 collective-permute-start.15
  76.7 2.7 %collective-permute-start.16 = (bf16[4,104,1600]{2,1,0:T(8,128)(2,1)S(1)}, bf16[4,104,1600]{2,1,0:T(8,128)(2,1)S(1)}, u32[]{:S(2)}, u32[]{:S(2)}) collective-permute-start(bf16[4,104,1600]{2,1,0:T(8,128)(2,1)S(1)} %get-tuple-element.52), channel_id=1, source_target_pairs={{0,28},{1,29},{2,30},{3,31},{4,0},{5,1},{6,2},{7,3},{8,4},{9,5},{1... | collective-permute-start | bytes 3993608 | tf_op jit(solution)/shard_map/ppermute | solution.py:25
  79.3 2.8 %collective-permute-start.21 = (bf16[4,104,1600]{2,1,0:T(8,128)(2,1)S(1)}, bf16[4,104,1600]{2,1,0:T(8,128)(2,1)S(1)}, u32[]{:S(2)}, u32[]{:S(2)}) collective-permute-start(bf16[4,104,1600]{2,1,0:T(8,128)(2,1)S(1)} %get-tuple-element.52), channel_id=1, source_target_pairs={{0,32},{32,0},{1,33},{33,1},{2,34},{34,2},{3,35},{35,3},{4,36},{36... | collective-permute-start | bytes 3993608 | tf_op jit(solution)/shard_map/ppermute | solution.py:29
  82.1 0.0 collective-permute-done.18
  82.1 0.1 collective-permute-start.20
  82.2 4.8 %arrange.1 = (bf16[2,512,2080]{2,1,0:T(8,128)(2,1)S(1)}, bf16[2,512,832]{2,1,0:T(8,128)(2,1)S(1)}, bf16[2,512,416]{2,1,0:T(8,128)(2,1)S(1)}) custom-call(bf16[1600,512]{1,0:T(8,128)(2,1)} %own_ref.1, bf16[1600,512]{1,0:T(8,128)(2,1)S(1)} %collective-permute-done.7.near_ref, bf16[1600,512]{1,0:T(8,128)(2,1)S(1)} %collective-permute-done.11.other_ref, ...), custom_call_target="tpu_custom_call" | custom-call | bytes 13107200 | tf_op jit(solution)/shard_map/arrange/pallas_call | solution.py:103
  87.0 8.4 %collective-permute-done.15 = bf16[4,104,1600]{2,1,0:T(8,128)(2,1)S(1)} collective-permute-done((bf16[4,104,1600]{2,1,0:T(8,128)(2,1)S(1)}, bf16[4,104,1600]{2,1,0:T(8,128)(2,1)S(1)}, u32[]{:S(2)}, u32[]{:S(2)}) %collective-permute-start.15) | collective-permute-done | bytes 1331232 | tf_op jit(solution)/shard_map/ppermute | solution.py:25
  95.4 0.0 collective-permute-done.16
  95.4 0.0 collective-permute-done.21
  95.4 0.0 collective-permute-done.20
  95.4 0.0 copy-start.2
  95.4 3.1 %collective-permute-start.24 = (bf16[4,104,1600]{2,1,0:T(8,128)(2,1)S(1)}, bf16[4,104,1600]{2,1,0:T(8,128)(2,1)S(1)}, u32[]{:S(2)}, u32[]{:S(2)}) collective-permute-start(bf16[4,104,1600]{2,1,0:T(8,128)(2,1)S(1)} %collective-permute-done.15), channel_id=1, source_target_pairs={{0,32},{32,0},{1,33},{33,1},{2,34},{34,2},{3,35},{35,3},{4,36},{36... | collective-permute-start | bytes 3993608 | tf_op jit(solution)/shard_map/ppermute | solution.py:29
  98.6 0.1 collective-permute-start.25
  98.7 0.1 slice.14
  98.7 0.1 slice.15
  98.8 0.1 collective-permute-start.22
  98.9 2.7 %collective-permute-start.23 = (bf16[2,104,1600]{2,1,0:T(8,128)(2,1)S(1)}, bf16[2,104,1600]{2,1,0:T(8,128)(2,1)S(1)}, u32[]{:S(2)}, u32[]{:S(2)}) collective-permute-start(bf16[2,104,1600]{2,1,0:T(8,128)(2,1)S(1)} %slice.15), channel_id=1, source_target_pairs={{0,28},{1,29},{2,30},{3,31},{4,0},{5,1},{6,2},{7,3},{8,4},{9,5},{1... | collective-permute-start | bytes 1996808 | tf_op jit(solution)/shard_map/ppermute | solution.py:25
  101.5 11.0 %first.1.total_ref = f32[512,1600]{1,0:T(8,128)S(1)} custom-call(bf16[2,512,2080]{2,1,0:T(8,128)(2,1)S(1)} %get-tuple-element.47.factor_ref, bf16[416,1600]{1,0:T(8,128)(2,1)S(1)} %bitcast.26, bf16[416,1600]{1,0:T(8,128)(2,1)} %bitcast.4.refs_1_, bf16[416,1600]{1,0:T(8,128)(2,1)} %bitcast.5.refs_2_, bf16[416,1600]{1,0:T(8,128)(2,1)} %bitcast.6.refs_3_, ...), custom_call_target="tpu_custom_call" | custom-call | flops 6815744000 | bytes 13312000 | tf_op jit(solution)/shard_map/first/pallas_call | solution.py:125
  112.5 0.0 collective-permute-done.22
  112.5 1.1 collective-permute-start.26
  113.7 0.3 collective-permute-start.27
  114.0 4.1 %more.1.total_ref = f32[1600,512]{1,0:T(8,128)S(1)} custom-call(f32[1600,512]{1,0:T(8,128)S(1)} %bitcast.23, f32[512,1600]{1,0:T(8,128)S(1)} %first.1.total_ref, bf16[2,512,832]{2,1,0:T(8,128)(2,1)S(1)} %get-tuple-element.59.factor_ref, bf16[416,1600]{1,0:T(8,128)(2,1)S(1)} %bitcast.24, bf16[416,1600]{1,0:T(8,128)(2,1)S(1)} %bitcast.25, ...), custom_call_target="tpu_custom_call" | custom-call | flops 2726297600 | bytes 5324800 | tf_op jit(solution)/shard_map/more/pallas_call | solution.py:125
  118.1 0.0 collective-permute-done.26
  118.1 3.4 %last.1 = f32[1600,512]{1,0:T(8,128)} custom-call(f32[1600,512]{1,0:T(8,128)S(1)} %more.1.total_ref, bf16[2,512,416]{2,1,0:T(8,128)(2,1)S(1)} %get-tuple-element.60.factor_ref, bf16[208,1600]{1,0:T(8,128)(2,1)S(1)} %bitcast.30, bf16[208,1600]{1,0:T(8,128)(2,1)S(1)} %bitcast.31, bf16[208,1600]{1,0:T(8,128)(2,1)S(1)} %bitcast.32, bf16[208,1600]{1,0:T(8,128)(2,1)S(1)} %bitcast.33), custom_call_target="tpu_custom_call" | custom-call | flops 1363148800 | bytes 2662400 | tf_op jit(solution)/shard_map/last/pallas_call | solution.py:125
  (19 shorter events, 0.1 us)
Async XLA Ops:
  0.0 34.4 %collective-permute-start.7 = (bf16[1600,512]{1,0:T(8,128)(2,1)}, bf16[1600,512]{1,0:T(8,128)(2,1)S(1)}, u32[]{:S(2)}, u32[]{:S(2)}) collective-permute-start(bf16[1600,512]{1,0:T(8,128)(2,1)} %own_ref.1), channel_id=1, source_target_pairs={{0,64},{32,224},{64,128},{96,32},{128,192},{160,96},{192,0},{224,1... | collective-permute-start | bytes 4915208 | tf_op jit(solution)/shard_map/ppermute | solution.py:14
  4.3 10.6 %collective-permute-start = (bf16[1,104,1600]{2,1,0:T(8,128)(2,1)S(1)}, bf16[1,104,1600]{2,1,0:T(8,128)(2,1)S(1)}, u32[]{:S(2)}, u32[]{:S(2)}) collective-permute-start(bf16[1,104,1600]{2,1,0:T(8,128)(2,1)S(1)} %pad.4), channel_id=1, source_target_pairs={{0,1},{1,2},{2,3},{3,0},{4,5},{5,6},{6,7},{7,4},{8,9},{9,10},{10,1... | collective-permute-start | bytes 998408 | tf_op jit(solution)/shard_map/ppermute | solution.py:25
  6.0 8.9 %collective-permute-start.1 = (bf16[1,104,1600]{2,1,0:T(8,128)(2,1)S(1)}, bf16[1,104,1600]{2,1,0:T(8,128)(2,1)S(1)}, u32[]{:S(2)}, u32[]{:S(2)}) collective-permute-start(bf16[1,104,1600]{2,1,0:T(8,128)(2,1)S(1)} %pad.4), channel_id=1, source_target_pairs={{0,3},{1,0},{2,1},{3,2},{4,7},{5,4},{6,5},{7,6},{8,11},{9,8},{10,9... | collective-permute-start | bytes 998408 | tf_op jit(solution)/shard_map/ppermute | solution.py:25
  14.9 7.6 %collective-permute-start.2 = (bf16[1,104,1600]{2,1,0:T(8,128)(2,1)S(1)}, bf16[1,104,1600]{2,1,0:T(8,128)(2,1)S(1)}, u32[]{:S(2)}, u32[]{:S(2)}) collective-permute-start(bf16[1,104,1600]{2,1,0:T(8,128)(2,1)S(1)} %collective-permute-done), channel_id=1, source_target_pairs={{0,1},{1,2},{2,3},{3,0},{4,5},{5,6},{6,7},{7,4},{8,9},{9,10},{10,1... | collective-permute-start | bytes 998408 | tf_op jit(solution)/shard_map/ppermute | solution.py:25
  14.9 12.7 %collective-permute-start.8 = (bf16[1,104,1600]{2,1,0:T(8,128)(2,1)S(1)}, bf16[1,104,1600]{2,1,0:T(8,128)(2,1)S(1)}, u32[]{:S(2)}, u32[]{:S(2)}) collective-permute-start(bf16[1,104,1600]{2,1,0:T(8,128)(2,1)S(1)} %collective-permute-done.1), channel_id=1, source_target_pairs={{32,60},{33,61},{34,62},{35,63},{36,32},{37,33},{38,34},{39,35},{4... | collective-permute-start | bytes 998408 | tf_op jit(solution)/shard_map/ppermute | solution.py:25
  22.6 11.8 %collective-permute-start.9 = (bf16[1,104,1600]{2,1,0:T(8,128)(2,1)S(1)}, bf16[1,104,1600]{2,1,0:T(8,128)(2,1)}, u32[]{:S(2)}, u32[]{:S(2)}) collective-permute-start(bf16[1,104,1600]{2,1,0:T(8,128)(2,1)S(1)} %collective-permute-done.2), channel_id=1, source_target_pairs={{32,36},{33,37},{34,38},{35,39},{36,40},{37,41},{38,42},{39,43},{4... | collective-permute-start | bytes 998408 | tf_op jit(solution)/shard_map/ppermute | solution.py:25
  24.7 9.7 %copy-start.1 = (bf16[4,104,1600]{2,1,0:T(8,128)(2,1)}, bf16[4,104,1600]{2,1,0:T(8,128)(2,1)S(1)}, u32[]{:S(2)}) copy-start(bf16[4,104,1600]{2,1,0:T(8,128)(2,1)S(1)} %pad_maximum_fusion) | copy-start | bytes 3993604
  24.7 19.0 %collective-permute-start.3 = (bf16[4,104,1600]{2,1,0:T(8,128)(2,1)S(1)}, bf16[4,104,1600]{2,1,0:T(8,128)(2,1)}, u32[]{:S(2)}, u32[]{:S(2)}) collective-permute-start(bf16[4,104,1600]{2,1,0:T(8,128)(2,1)S(1)} %pad_maximum_fusion), channel_id=1, source_target_pairs={{0,4},{1,5},{2,6},{3,7},{4,8},{5,9},{6,10},{7,11},{8,12},{9,13},{1... | collective-permute-start | bytes 3993608 | tf_op jit(solution)/shard_map/ppermute | solution.py:25
  26.1 17.7 %collective-permute-start.5 = (bf16[4,104,1600]{2,1,0:T(8,128)(2,1)S(1)}, bf16[4,104,1600]{2,1,0:T(8,128)(2,1)}, u32[]{:S(2)}, u32[]{:S(2)}) collective-permute-start(bf16[4,104,1600]{2,1,0:T(8,128)(2,1)S(1)} %pad_maximum_fusion), channel_id=1, source_target_pairs={{0,28},{1,29},{2,30},{3,31},{4,0},{5,1},{6,2},{7,3},{8,4},{9,5},{1... | collective-permute-start | bytes 3993608 | tf_op jit(solution)/shard_map/ppermute | solution.py:25
  27.6 16.1 %copy-start.3 = (bf16[1,104,1600]{2,1,0:T(8,128)(2,1)}, bf16[1,104,1600]{2,1,0:T(8,128)(2,1)S(1)}, u32[]{:S(2)}) copy-start(bf16[1,104,1600]{2,1,0:T(8,128)(2,1)S(1)} %collective-permute-done.8) | copy-start | bytes 998404
  34.4 32.7 %collective-permute-start.11 = (bf16[1600,512]{1,0:T(8,128)(2,1)}, bf16[1600,512]{1,0:T(8,128)(2,1)S(1)}, u32[]{:S(2)}, u32[]{:S(2)}) collective-permute-start(bf16[1600,512]{1,0:T(8,128)(2,1)} %own_ref.1), channel_id=1, source_target_pairs={{0,192},{32,96},{64,0},{96,160},{128,64},{160,224},{192,128},{224,... | collective-permute-start | bytes 4915208 | tf_op jit(solution)/shard_map/ppermute | solution.py:14
  35.6 32.6 %collective-permute-start.10 = (bf16[1200,512]{1,0:T(8,128)(2,1)}, bf16[1200,512]{1,0:T(8,128)(2,1)}, u32[]{:S(2)}, u32[]{:S(2)}) collective-permute-start(bf16[1200,512]{1,0:T(8,128)(2,1)} %slice.12), channel_id=1, source_target_pairs={{0,64},{32,224},{64,128},{96,32},{128,192},{160,96},{192,0},{224,1... | collective-permute-start | bytes 3686408 | tf_op jit(solution)/shard_map/ppermute | solution.py:14
  38.2 9.7 %collective-permute-start.13 = (bf16[1,104,1600]{2,1,0:T(8,128)(2,1)S(1)}, bf16[1,104,1600]{2,1,0:T(8,128)(2,1)S(1)}, u32[]{:S(2)}, u32[]{:S(2)}) collective-permute-start(bf16[1,104,1600]{2,1,0:T(8,128)(2,1)S(1)} %collective-permute-done.8), channel_id=1, source_target_pairs={{32,60},{33,61},{34,62},{35,63},{36,32},{37,33},{38,34},{39,35},{4... | collective-permute-start | bytes 998408 | tf_op jit(solution)/shard_map/ppermute | solution.py:25
  43.7 25.6 %collective-permute-start.4 = (bf16[4,104,1600]{2,1,0:T(8,128)(2,1)}, bf16[4,104,1600]{2,1,0:T(8,128)(2,1)}, u32[]{:S(2)}, u32[]{:S(2)}) collective-permute-start(bf16[4,104,1600]{2,1,0:T(8,128)(2,1)} %collective-permute-done.3), channel_id=1, source_target_pairs={{0,4},{1,5},{2,6},{3,7},{4,8},{5,9},{6,10},{7,11},{8,12},{9,13},{1... | collective-permute-start | bytes 3993608 | tf_op jit(solution)/shard_map/ppermute | solution.py:25
  43.8 27.3 %collective-permute-start.6 = (bf16[4,104,1600]{2,1,0:T(8,128)(2,1)}, bf16[4,104,1600]{2,1,0:T(8,128)(2,1)}, u32[]{:S(2)}, u32[]{:S(2)}) collective-permute-start(bf16[4,104,1600]{2,1,0:T(8,128)(2,1)} %collective-permute-done.5), channel_id=1, source_target_pairs={{0,28},{1,29},{2,30},{3,31},{4,0},{5,1},{6,2},{7,3},{8,4},{9,5},{1... | collective-permute-start | bytes 3993608 | tf_op jit(solution)/shard_map/ppermute | solution.py:25
  48.0 0.8 copy-start.4
  48.7 14.4 %collective-permute-start.14 = (bf16[1,104,1600]{2,1,0:T(8,128)(2,1)}, bf16[1,104,1600]{2,1,0:T(8,128)(2,1)}, u32[]{:S(2)}, u32[]{:S(2)}) collective-permute-start(bf16[1,104,1600]{2,1,0:T(8,128)(2,1)} %collective-permute-done.9), channel_id=1, source_target_pairs={{32,36},{33,37},{34,38},{35,39},{36,40},{37,41},{38,42},{39,43},{4... | collective-permute-start | bytes 998408 | tf_op jit(solution)/shard_map/ppermute | solution.py:25
  50.8 17.5 %copy-start.5 = (bf16[1,104,1600]{2,1,0:T(8,128)(2,1)S(1)}, bf16[1,104,1600]{2,1,0:T(8,128)(2,1)}, u32[]{:S(2)}) copy-start(bf16[1,104,1600]{2,1,0:T(8,128)(2,1)} %copy-done.4) | copy-start | bytes 998404
  63.2 16.2 %collective-permute-start.17 = (bf16[4,104,1600]{2,1,0:T(8,128)(2,1)}, bf16[4,104,1600]{2,1,0:T(8,128)(2,1)S(1)}, u32[]{:S(2)}, u32[]{:S(2)}) collective-permute-start(bf16[4,104,1600]{2,1,0:T(8,128)(2,1)} %copy-done.1), channel_id=1, source_target_pairs={{0,32},{32,0},{1,33},{33,1},{2,34},{34,2},{3,35},{35,3},{4,36},{36... | collective-permute-start | bytes 3993608 | tf_op jit(solution)/shard_map/ppermute | solution.py:29
  67.1 14.9 %collective-permute-start.18 = (bf16[4,104,1600]{2,1,0:T(8,128)(2,1)}, bf16[4,104,1600]{2,1,0:T(8,128)(2,1)S(1)}, u32[]{:S(2)}, u32[]{:S(2)}) collective-permute-start(bf16[4,104,1600]{2,1,0:T(8,128)(2,1)} %collective-permute-done.3), channel_id=1, source_target_pairs={{0,32},{32,0},{1,33},{33,1},{2,34},{34,2},{3,35},{35,3},{4,36},{36... | collective-permute-start | bytes 3993608 | tf_op jit(solution)/shard_map/ppermute | solution.py:29
  68.2 8.1 %collective-permute-start.12 = (bf16[400,512]{1,0:T(8,128)(2,1)S(1)}, bf16[400,512]{1,0:T(8,128)(2,1)S(1)}, u32[]{:S(2)}, u32[]{:S(2)}) collective-permute-start(bf16[400,512]{1,0:T(8,128)(2,1)S(1)} %slice.16), channel_id=1, source_target_pairs={{0,192},{32,96},{64,0},{96,160},{128,64},{160,224},{192,128},{224,... | collective-permute-start | bytes 1228808 | tf_op jit(solution)/shard_map/ppermute | solution.py:14
  69.4 17.6 %collective-permute-start.19 = (bf16[4,104,1600]{2,1,0:T(8,128)(2,1)}, bf16[4,104,1600]{2,1,0:T(8,128)(2,1)S(1)}, u32[]{:S(2)}, u32[]{:S(2)}) collective-permute-start(bf16[4,104,1600]{2,1,0:T(8,128)(2,1)} %collective-permute-done.5), channel_id=1, source_target_pairs={{0,32},{32,0},{1,33},{33,1},{2,34},{34,2},{3,35},{35,3},{4,36},{36... | collective-permute-start | bytes 3993608 | tf_op jit(solution)/shard_map/ppermute | solution.py:29
  76.6 18.8 %collective-permute-start.15 = (bf16[4,104,1600]{2,1,0:T(8,128)(2,1)S(1)}, bf16[4,104,1600]{2,1,0:T(8,128)(2,1)S(1)}, u32[]{:S(2)}, u32[]{:S(2)}) collective-permute-start(bf16[4,104,1600]{2,1,0:T(8,128)(2,1)S(1)} %get-tuple-element.64), channel_id=1, source_target_pairs={{0,4},{1,5},{2,6},{3,7},{4,8},{5,9},{6,10},{7,11},{8,12},{9,13},{1... | collective-permute-start | bytes 3993608 | tf_op jit(solution)/shard_map/ppermute | solution.py:25
  76.7 18.7 %collective-permute-start.16 = (bf16[4,104,1600]{2,1,0:T(8,128)(2,1)S(1)}, bf16[4,104,1600]{2,1,0:T(8,128)(2,1)S(1)}, u32[]{:S(2)}, u32[]{:S(2)}) collective-permute-start(bf16[4,104,1600]{2,1,0:T(8,128)(2,1)S(1)} %get-tuple-element.52), channel_id=1, source_target_pairs={{0,28},{1,29},{2,30},{3,31},{4,0},{5,1},{6,2},{7,3},{8,4},{9,5},{1... | collective-permute-start | bytes 3993608 | tf_op jit(solution)/shard_map/ppermute | solution.py:25
  79.3 16.1 %collective-permute-start.21 = (bf16[4,104,1600]{2,1,0:T(8,128)(2,1)S(1)}, bf16[4,104,1600]{2,1,0:T(8,128)(2,1)S(1)}, u32[]{:S(2)}, u32[]{:S(2)}) collective-permute-start(bf16[4,104,1600]{2,1,0:T(8,128)(2,1)S(1)} %get-tuple-element.52), channel_id=1, source_target_pairs={{0,32},{32,0},{1,33},{33,1},{2,34},{34,2},{3,35},{35,3},{4,36},{36... | collective-permute-start | bytes 3993608 | tf_op jit(solution)/shard_map/ppermute | solution.py:29
  82.1 13.3 %collective-permute-start.20 = (bf16[4,104,1600]{2,1,0:T(8,128)(2,1)}, bf16[4,104,1600]{2,1,0:T(8,128)(2,1)S(1)}, u32[]{:S(2)}, u32[]{:S(2)}) collective-permute-start(bf16[4,104,1600]{2,1,0:T(8,128)(2,1)} %collective-permute-done.4), channel_id=1, source_target_pairs={{0,32},{32,0},{1,33},{33,1},{2,34},{34,2},{3,35},{35,3},{4,36},{36... | collective-permute-start | bytes 3993608 | tf_op jit(solution)/shard_map/ppermute | solution.py:29
  95.4 6.1 %copy-start.2 = (bf16[4,104,1600]{2,1,0:T(8,128)(2,1)S(1)}, bf16[4,104,1600]{2,1,0:T(8,128)(2,1)}, u32[]{:S(2)}) copy-start(bf16[4,104,1600]{2,1,0:T(8,128)(2,1)} %copy-done.1) | copy-start | bytes 3993604
  95.4 18.6 %collective-permute-start.24 = (bf16[4,104,1600]{2,1,0:T(8,128)(2,1)S(1)}, bf16[4,104,1600]{2,1,0:T(8,128)(2,1)S(1)}, u32[]{:S(2)}, u32[]{:S(2)}) collective-permute-start(bf16[4,104,1600]{2,1,0:T(8,128)(2,1)S(1)} %collective-permute-done.15), channel_id=1, source_target_pairs={{0,32},{32,0},{1,33},{33,1},{2,34},{34,2},{3,35},{35,3},{4,36},{36... | collective-permute-start | bytes 3993608 | tf_op jit(solution)/shard_map/ppermute | solution.py:29
  98.6 15.4 %collective-permute-start.25 = (bf16[4,104,1600]{2,1,0:T(8,128)(2,1)S(1)}, bf16[4,104,1600]{2,1,0:T(8,128)(2,1)S(1)}, u32[]{:S(2)}, u32[]{:S(2)}) collective-permute-start(bf16[4,104,1600]{2,1,0:T(8,128)(2,1)S(1)} %collective-permute-done.16), channel_id=1, source_target_pairs={{0,32},{32,0},{1,33},{33,1},{2,34},{34,2},{3,35},{35,3},{4,36},{36... | collective-permute-start | bytes 3993608 | tf_op jit(solution)/shard_map/ppermute | solution.py:29
  98.8 13.7 %collective-permute-start.22 = (bf16[2,104,1600]{2,1,0:T(8,128)(2,1)S(1)}, bf16[2,104,1600]{2,1,0:T(8,128)(2,1)S(1)}, u32[]{:S(2)}, u32[]{:S(2)}) collective-permute-start(bf16[2,104,1600]{2,1,0:T(8,128)(2,1)S(1)} %slice.14), channel_id=1, source_target_pairs={{0,4},{1,5},{2,6},{3,7},{4,8},{5,9},{6,10},{7,11},{8,12},{9,13},{1... | collective-permute-start | bytes 1996808 | tf_op jit(solution)/shard_map/ppermute | solution.py:25
  98.9 13.7 %collective-permute-start.23 = (bf16[2,104,1600]{2,1,0:T(8,128)(2,1)S(1)}, bf16[2,104,1600]{2,1,0:T(8,128)(2,1)S(1)}, u32[]{:S(2)}, u32[]{:S(2)}) collective-permute-start(bf16[2,104,1600]{2,1,0:T(8,128)(2,1)S(1)} %slice.15), channel_id=1, source_target_pairs={{0,28},{1,29},{2,30},{3,31},{4,0},{5,1},{6,2},{7,3},{8,4},{9,5},{1... | collective-permute-start | bytes 1996808 | tf_op jit(solution)/shard_map/ppermute | solution.py:25
  101.5 12.5 %copy-start = (f32[512,1600]{0,1:T(8,128)S(1)}, f32[512,1600]{0,1:T(8,128)}, u32[]{:S(2)}) copy-start(f32[512,1600]{0,1:T(8,128)} %param.3) | copy-start | bytes 9830404
  112.5 5.6 %collective-permute-start.26 = (bf16[2,104,1600]{2,1,0:T(8,128)(2,1)S(1)}, bf16[2,104,1600]{2,1,0:T(8,128)(2,1)S(1)}, u32[]{:S(2)}, u32[]{:S(2)}) collective-permute-start(bf16[2,104,1600]{2,1,0:T(8,128)(2,1)S(1)} %collective-permute-done.22), channel_id=1, source_target_pairs={{0,32},{32,0},{1,33},{33,1},{2,34},{34,2},{3,35},{35,3},{4,36},{36... | collective-permute-start | bytes 1996808 | tf_op jit(solution)/shard_map/ppermute | solution.py:29
  113.7 4.5 %collective-permute-start.27 = (bf16[2,104,1600]{2,1,0:T(8,128)(2,1)S(1)}, bf16[2,104,1600]{2,1,0:T(8,128)(2,1)S(1)}, u32[]{:S(2)}, u32[]{:S(2)}) collective-permute-start(bf16[2,104,1600]{2,1,0:T(8,128)(2,1)S(1)} %collective-permute-done.23), channel_id=1, source_target_pairs={{0,32},{32,0},{1,33},{33,1},{2,34},{34,2},{3,35},{35,3},{4,36},{36... | collective-permute-start | bytes 1996808 | tf_op jit(solution)/shard_map/ppermute | solution.py:29

commit v7 on v6

--- a/solution.py
+++ b/solution.py
@@ -53,8 +53,8 @@
     rest = jnp.concatenate([b2, a3, b3, a4])
     u1, d1 = travel(pack, *up), travel(pack, *down)
     u2, d2 = travel(u1, *up), travel(d1, down[0], None)
+    u2, d2, other, far_low = lax.optimization_barrier((u2, d2, other, far_low))
     far_high = along_row(other[cut:], rows, -1, 1)
-    u2, d2, far_low, far_high = lax.optimization_barrier((u2, d2, far_low, far_high))
     first = lax.axis_index("col") == 0
     kept = jnp.where(first, d2, rest)
     u3, d3 = travel(jnp.where(first, u2, rest), *up), travel(kept, *down)

time: 122 us -> 118 us (0.967)
  waiting for transfers between devices: 49.5 us -> 40.7 us
  starting transfers between devices: 41.8 us -> 46.3 us
    ppermute x4, waiting for transfers between devices: 9.25 us -> 0.01 us  [along_row(): return lax.ppermute(array, ('row', 'col'), pairs)]
    ppermute x9, starting transfers between devices: 9.21 us -> 14.5 us  [swap(): return lax.ppermute(array, 'col', [(0, 1), (1, 0)])]
  transfers between devices with their start and end apart: 28 -> 28, of which waited for: 9 -> 8; matrix products, arithmetic and copies ran while one was open for 5% -> 4% of each run, Pallas kernels for 16% -> 17%
where the time goes in v7:
time: 118 us; the launch traced here: 117 us
  starting transfers between devices  46.3 us (39%)
  waiting for transfers between devices  40.7 us (34%)
  Pallas kernels  23.1 us (20%)
  local copies, waits for them, and re-layouts  6.18 us (5%)
    ppermute x15, waiting for transfers between devices, travel(): return lax.ppermute(array, ('col', 'depth'), pairs)  40.6 us
    ppermute x15, starting transfers between devices, travel(): return lax.ppermute(array, ('col', 'depth'), pairs)  25.9 us
    pallas_call x3, Pallas kernels, multiply(): pl.pallas_call(body, out_shape=jax.ShapeDtypeStruct(shape, jnp.float32),...  18.3 us
    ppermute x9, starting transfers between devices, swap(): return lax.ppermute(array, 'col', [(0, 1), (1, 0)])  14.5 us
    ppermute x4, starting transfers between devices, along_row(): return lax.ppermute(array, ('row', 'col'), pairs)  5.88 us
    pallas_call x1, Pallas kernels, arrange(): pl.pallas_call(kernel, out_shape=[jax.ShapeDtypeStruct((2, width, blocks...  4.82 us
    unnamed x15, local copies, waits for them, and re-layouts  2.87 us
  transfers between devices with their start and end apart: 28, of which 8 were waited for; matrix products, arithmetic and copies ran while one was open for 4% of the time, Pallas kernels for 17%

profile of v7, /device:TPU:1, one launch (start us, length us, event | category | flops | bytes accessed | tf_op | source)
XLA Modules:
  0.0 117.3 jit_solution(16696322869463807428)
XLA Ops:
  0.0 1.0 pad.4
  1.0 2.5 %collective-permute-start = (bf16[1,104,1600]{2,1,0:T(8,128)(2,1)S(1)}, bf16[1,104,1600]{2,1,0:T(8,128)(2,1)S(1)}, u32[]{:S(2)}, u32[]{:S(2)}) collective-permute-start(bf16[1,104,1600]{2,1,0:T(8,128)(2,1)S(1)} %pad.4), channel_id=1, source_target_pairs={{0,1},{1,2},{2,3},{3,0},{4,5},{5,6},{6,7},{7,4},{8,9},{9,10},{10,1... | collective-permute-start | bytes 998408 | tf_op jit(solution)/shard_map/ppermute | solution.py:25
  3.6 2.5 %collective-permute-start.7 = (bf16[1600,512]{1,0:T(8,128)(2,1)}, bf16[1600,512]{1,0:T(8,128)(2,1)S(1)}, u32[]{:S(2)}, u32[]{:S(2)}) collective-permute-start(bf16[1600,512]{1,0:T(8,128)(2,1)} %own_ref.1), channel_id=1, source_target_pairs={{0,64},{32,224},{64,128},{96,32},{128,192},{160,96},{192,0},{224,1... | collective-permute-start | bytes 4915208 | tf_op jit(solution)/shard_map/ppermute | solution.py:14
  6.0 4.0 %collective-permute-start.1 = (bf16[1,104,1600]{2,1,0:T(8,128)(2,1)S(1)}, bf16[1,104,1600]{2,1,0:T(8,128)(2,1)S(1)}, u32[]{:S(2)}, u32[]{:S(2)}) collective-permute-start(bf16[1,104,1600]{2,1,0:T(8,128)(2,1)S(1)} %pad.4), channel_id=1, source_target_pairs={{0,3},{1,0},{2,1},{3,2},{4,7},{5,4},{6,5},{7,6},{8,11},{9,8},{10,9... | collective-permute-start | bytes 998408 | tf_op jit(solution)/shard_map/ppermute | solution.py:25
  10.1 2.4 %collective-permute-done = bf16[1,104,1600]{2,1,0:T(8,128)(2,1)S(1)} collective-permute-done((bf16[1,104,1600]{2,1,0:T(8,128)(2,1)S(1)}, bf16[1,104,1600]{2,1,0:T(8,128)(2,1)S(1)}, u32[]{:S(2)}, u32[]{:S(2)}) %collective-permute-start) | collective-permute-done | bytes 332832 | tf_op jit(solution)/shard_map/ppermute | solution.py:25
  12.5 0.0 collective-permute-start.2
  12.5 1.8 %collective-permute-done.1 = bf16[1,104,1600]{2,1,0:T(8,128)(2,1)S(1)} collective-permute-done((bf16[1,104,1600]{2,1,0:T(8,128)(2,1)S(1)}, bf16[1,104,1600]{2,1,0:T(8,128)(2,1)S(1)}, u32[]{:S(2)}, u32[]{:S(2)}) %collective-permute-start.1) | collective-permute-done | bytes 332832 | tf_op jit(solution)/shard_map/ppermute | solution.py:25
  14.3 5.8 %collective-permute-done.2 = bf16[1,104,1600]{2,1,0:T(8,128)(2,1)S(1)} collective-permute-done((bf16[1,104,1600]{2,1,0:T(8,128)(2,1)S(1)}, bf16[1,104,1600]{2,1,0:T(8,128)(2,1)S(1)}, u32[]{:S(2)}, u32[]{:S(2)}) %collective-permute-start.2) | collective-permute-done | bytes 332832 | tf_op jit(solution)/shard_map/ppermute | solution.py:25
  20.1 0.2 pad_maximum_fusion
  20.3 0.0 copy-start.1
  20.3 1.4 %collective-permute-start.3 = (bf16[4,104,1600]{2,1,0:T(8,128)(2,1)S(1)}, bf16[4,104,1600]{2,1,0:T(8,128)(2,1)}, u32[]{:S(2)}, u32[]{:S(2)}) collective-permute-start(bf16[4,104,1600]{2,1,0:T(8,128)(2,1)S(1)} %pad_maximum_fusion), channel_id=1, source_target_pairs={{0,4},{1,5},{2,6},{3,7},{4,8},{5,9},{6,10},{7,11},{8,12},{9,13},{1... | collective-permute-start | bytes 3993608 | tf_op jit(solution)/shard_map/ppermute | solution.py:25
  21.7 1.5 %collective-permute-start.5 = (bf16[4,104,1600]{2,1,0:T(8,128)(2,1)S(1)}, bf16[4,104,1600]{2,1,0:T(8,128)(2,1)}, u32[]{:S(2)}, u32[]{:S(2)}) collective-permute-start(bf16[4,104,1600]{2,1,0:T(8,128)(2,1)S(1)} %pad_maximum_fusion), channel_id=1, source_target_pairs={{0,28},{1,29},{2,30},{3,31},{4,0},{5,1},{6,2},{7,3},{8,4},{9,5},{1... | collective-permute-start | bytes 3993608 | tf_op jit(solution)/shard_map/ppermute | solution.py:25
  23.2 2.1 %collective-permute-start.8 = (bf16[1,104,1600]{2,1,0:T(8,128)(2,1)S(1)}, bf16[1,104,1600]{2,1,0:T(8,128)(2,1)S(1)}, u32[]{:S(2)}, u32[]{:S(2)}) collective-permute-start(bf16[1,104,1600]{2,1,0:T(8,128)(2,1)S(1)} %collective-permute-done.1), channel_id=1, source_target_pairs={{32,60},{33,61},{34,62},{35,63},{36,32},{37,33},{38,34},{39,35},{4... | collective-permute-start | bytes 998408 | tf_op jit(solution)/shard_map/ppermute | solution.py:25
  25.4 3.1 %collective-permute-start.9 = (bf16[1,104,1600]{2,1,0:T(8,128)(2,1)S(1)}, bf16[1,104,1600]{2,1,0:T(8,128)(2,1)}, u32[]{:S(2)}, u32[]{:S(2)}) collective-permute-start(bf16[1,104,1600]{2,1,0:T(8,128)(2,1)S(1)} %collective-permute-done.2), channel_id=1, source_target_pairs={{32,36},{33,37},{34,38},{35,39},{36,40},{37,41},{38,42},{39,43},{4... | collective-permute-start | bytes 998408 | tf_op jit(solution)/shard_map/ppermute | solution.py:25
  28.5 6.9 %collective-permute-done.8 = bf16[1,104,1600]{2,1,0:T(8,128)(2,1)S(1)} collective-permute-done((bf16[1,104,1600]{2,1,0:T(8,128)(2,1)S(1)}, bf16[1,104,1600]{2,1,0:T(8,128)(2,1)S(1)}, u32[]{:S(2)}, u32[]{:S(2)}) %collective-permute-start.8) | collective-permute-done | bytes 332832 | tf_op jit(solution)/shard_map/ppermute | solution.py:25
  35.4 3.4 %collective-permute-done.9 = bf16[1,104,1600]{2,1,0:T(8,128)(2,1)} collective-permute-done((bf16[1,104,1600]{2,1,0:T(8,128)(2,1)S(1)}, bf16[1,104,1600]{2,1,0:T(8,128)(2,1)}, u32[]{:S(2)}, u32[]{:S(2)}) %collective-permute-start.9) | collective-permute-done | bytes 332832 | tf_op jit(solution)/shard_map/ppermute | solution.py:25
  38.8 0.0 collective-permute-done.7.near_ref
  38.8 1.2 slice.12
  39.9 2.5 %collective-permute-start.11 = (bf16[1200,512]{1,0:T(8,128)(2,1)}, bf16[1200,512]{1,0:T(8,128)(2,1)}, u32[]{:S(2)}, u32[]{:S(2)}) collective-permute-start(bf16[1200,512]{1,0:T(8,128)(2,1)} %slice.12), channel_id=1, source_target_pairs={{0,64},{32,224},{64,128},{96,32},{128,192},{160,96},{192,0},{224,1... | collective-permute-start | bytes 3686408 | tf_op jit(solution)/shard_map/ppermute | solution.py:14
  42.4 0.0 collective-permute-start.10
  42.4 1.9 %collective-permute-start.12 = (bf16[1,104,1600]{2,1,0:T(8,128)(2,1)S(1)}, bf16[1,104,1600]{2,1,0:T(8,128)(2,1)S(1)}, u32[]{:S(2)}, u32[]{:S(2)}) collective-permute-start(bf16[1,104,1600]{2,1,0:T(8,128)(2,1)S(1)} %collective-permute-done.8), channel_id=1, source_target_pairs={{32,60},{33,61},{34,62},{35,63},{36,32},{37,33},{38,34},{39,35},{4... | collective-permute-start | bytes 998408 | tf_op jit(solution)/shard_map/ppermute | solution.py:25
  44.3 0.0 collective-permute-done.3
  44.4 0.1 collective-permute-start.4
  44.4 0.0 collective-permute-done.5
  44.5 1.8 %collective-permute-start.6 = (bf16[4,104,1600]{2,1,0:T(8,128)(2,1)}, bf16[4,104,1600]{2,1,0:T(8,128)(2,1)}, u32[]{:S(2)}, u32[]{:S(2)}) collective-permute-start(bf16[4,104,1600]{2,1,0:T(8,128)(2,1)} %collective-permute-done.5), channel_id=1, source_target_pairs={{0,28},{1,29},{2,30},{3,31},{4,0},{5,1},{6,2},{7,3},{8,4},{9,5},{1... | collective-permute-start | bytes 3993608 | tf_op jit(solution)/shard_map/ppermute | solution.py:25
  46.3 4.6 %collective-permute-done.12 = bf16[1,104,1600]{2,1,0:T(8,128)(2,1)S(1)} collective-permute-done((bf16[1,104,1600]{2,1,0:T(8,128)(2,1)S(1)}, bf16[1,104,1600]{2,1,0:T(8,128)(2,1)S(1)}, u32[]{:S(2)}, u32[]{:S(2)}) %collective-permute-start.12) | collective-permute-done | bytes 332832 | tf_op jit(solution)/shard_map/ppermute | solution.py:25
  50.8 0.7 copy-done.4
  51.6 1.9 %collective-permute-start.13 = (bf16[1,104,1600]{2,1,0:T(8,128)(2,1)}, bf16[1,104,1600]{2,1,0:T(8,128)(2,1)}, u32[]{:S(2)}, u32[]{:S(2)}) collective-permute-start(bf16[1,104,1600]{2,1,0:T(8,128)(2,1)} %collective-permute-done.9), channel_id=1, source_target_pairs={{32,36},{33,37},{34,38},{35,39},{36,40},{37,41},{38,42},{39,43},{4... | collective-permute-start | bytes 998408 | tf_op jit(solution)/shard_map/ppermute | solution.py:25
  53.5 1.1 constant_dynamic-update-slice_fusion.3
  54.6 10.6 %collective-permute-done.13 = bf16[1,104,1600]{2,1,0:T(8,128)(2,1)} collective-permute-done((bf16[1,104,1600]{2,1,0:T(8,128)(2,1)}, bf16[1,104,1600]{2,1,0:T(8,128)(2,1)}, u32[]{:S(2)}, u32[]{:S(2)}) %collective-permute-start.13) | collective-permute-done | bytes 332832 | tf_op jit(solution)/shard_map/ppermute | solution.py:25
  65.2 0.0 collective-permute-start.17
  65.2 0.0 collective-permute-done.11.low_ref
  65.2 0.5 collective-permute-start.18
  65.7 1.0 constant_dynamic-update-slice_fusion.2
  66.8 1.0 constant_dynamic-update-slice_fusion
  67.8 0.0 collective-permute-done.10.other_ref
  67.8 0.1 collective-permute-start.19
  67.9 0.0 collective-permute-done.4
  67.9 0.0 collective-permute-done.6
  67.9 0.9 collective-permute-start.16
  68.9 0.3 broadcast_select_fusion
  69.1 0.1 collective-permute-start.14
  69.2 0.0 collective-permute-done.17
  69.2 2.7 %collective-permute-start.15 = (bf16[4,104,1600]{2,1,0:T(8,128)(2,1)S(1)}, bf16[4,104,1600]{2,1,0:T(8,128)(2,1)S(1)}, u32[]{:S(2)}, u32[]{:S(2)}) collective-permute-start(bf16[4,104,1600]{2,1,0:T(8,128)(2,1)S(1)} %get-tuple-element.52), channel_id=1, source_target_pairs={{0,28},{1,29},{2,30},{3,31},{4,0},{5,1},{6,2},{7,3},{8,4},{9,5},{1... | collective-permute-start | bytes 3993608 | tf_op jit(solution)/shard_map/ppermute | solution.py:25
  71.9 0.0 collective-permute-done.18
  71.9 5.9 %collective-permute-start.21 = (bf16[4,104,1600]{2,1,0:T(8,128)(2,1)S(1)}, bf16[4,104,1600]{2,1,0:T(8,128)(2,1)S(1)}, u32[]{:S(2)}, u32[]{:S(2)}) collective-permute-start(bf16[4,104,1600]{2,1,0:T(8,128)(2,1)S(1)} %get-tuple-element.52), channel_id=1, source_target_pairs={{0,32},{32,0},{1,33},{33,1},{2,34},{34,2},{3,35},{35,3},{4,36},{36... | collective-permute-start | bytes 3993608 | tf_op jit(solution)/shard_map/ppermute | solution.py:29
  77.8 0.1 collective-permute-start.20
  77.9 4.8 %arrange.1 = (bf16[2,512,2080]{2,1,0:T(8,128)(2,1)S(1)}, bf16[2,512,832]{2,1,0:T(8,128)(2,1)S(1)}, bf16[2,512,416]{2,1,0:T(8,128)(2,1)S(1)}) custom-call(bf16[1600,512]{1,0:T(8,128)(2,1)} %own_ref.1, bf16[1600,512]{1,0:T(8,128)(2,1)S(1)} %collective-permute-done.7.near_ref, bf16[1600,512]{1,0:T(8,128)(2,1)S(1)} %collective-permute-done.10.other_ref, ...), custom_call_target="tpu_custom_call" | custom-call | bytes 13107200 | tf_op jit(solution)/shard_map/arrange/pallas_call | solution.py:103
  82.8 0.0 collective-permute-done.19
  82.8 5.2 %collective-permute-done.14 = bf16[4,104,1600]{2,1,0:T(8,128)(2,1)S(1)} collective-permute-done((bf16[4,104,1600]{2,1,0:T(8,128)(2,1)S(1)}, bf16[4,104,1600]{2,1,0:T(8,128)(2,1)S(1)}, u32[]{:S(2)}, u32[]{:S(2)}) %collective-permute-start.14) | collective-permute-done | bytes 1331232 | tf_op jit(solution)/shard_map/ppermute | solution.py:25
  88.0 0.0 collective-permute-done.15
  88.0 0.0 copy-start.2
  88.0 6.3 %collective-permute-start.24 = (bf16[4,104,1600]{2,1,0:T(8,128)(2,1)S(1)}, bf16[4,104,1600]{2,1,0:T(8,128)(2,1)S(1)}, u32[]{:S(2)}, u32[]{:S(2)}) collective-permute-start(bf16[4,104,1600]{2,1,0:T(8,128)(2,1)S(1)} %collective-permute-done.14), channel_id=1, source_target_pairs={{0,32},{32,0},{1,33},{33,1},{2,34},{34,2},{3,35},{35,3},{4,36},{36... | collective-permute-start | bytes 3993608 | tf_op jit(solution)/shard_map/ppermute | solution.py:29
  94.3 0.1 collective-permute-start.25
  94.4 0.1 slice.14
  94.4 0.1 slice.15
  94.5 0.2 collective-permute-start.22
  94.7 2.6 %collective-permute-start.23 = (bf16[2,104,1600]{2,1,0:T(8,128)(2,1)S(1)}, bf16[2,104,1600]{2,1,0:T(8,128)(2,1)S(1)}, u32[]{:S(2)}, u32[]{:S(2)}) collective-permute-start(bf16[2,104,1600]{2,1,0:T(8,128)(2,1)S(1)} %slice.15), channel_id=1, source_target_pairs={{0,28},{1,29},{2,30},{3,31},{4,0},{5,1},{6,2},{7,3},{8,4},{9,5},{1... | collective-permute-start | bytes 1996808 | tf_op jit(solution)/shard_map/ppermute | solution.py:25
  97.3 11.0 %first.1.total_ref = f32[512,1600]{1,0:T(8,128)S(1)} custom-call(bf16[2,512,2080]{2,1,0:T(8,128)(2,1)S(1)} %get-tuple-element.47.factor_ref, bf16[416,1600]{1,0:T(8,128)(2,1)S(1)} %bitcast.26, bf16[416,1600]{1,0:T(8,128)(2,1)} %bitcast.4.refs_1_, bf16[416,1600]{1,0:T(8,128)(2,1)} %bitcast.5.refs_2_, bf16[416,1600]{1,0:T(8,128)(2,1)} %bitcast.6.refs_3_, ...), custom_call_target="tpu_custom_call" | custom-call | flops 6815744000 | bytes 13312000 | tf_op jit(solution)/shard_map/first/pallas_call | solution.py:125
  108.2 1.1 collective-permute-start.26
  109.4 0.3 collective-permute-start.27
  109.7 0.0 collective-permute-done.24
  109.7 4.0 %more.1.total_ref = f32[1600,512]{1,0:T(8,128)S(1)} custom-call(f32[1600,512]{1,0:T(8,128)S(1)} %bitcast.23, f32[512,1600]{1,0:T(8,128)S(1)} %first.1.total_ref, bf16[2,512,832]{2,1,0:T(8,128)(2,1)S(1)} %get-tuple-element.59.factor_ref, bf16[416,1600]{1,0:T(8,128)(2,1)S(1)} %bitcast.24, bf16[416,1600]{1,0:T(8,128)(2,1)S(1)} %bitcast.25, ...), custom_call_target="tpu_custom_call" | custom-call | flops 2726297600 | bytes 5324800 | tf_op jit(solution)/shard_map/more/pallas_call | solution.py:125
  113.7 3.4 %last.1 = f32[1600,512]{1,0:T(8,128)} custom-call(f32[1600,512]{1,0:T(8,128)S(1)} %more.1.total_ref, bf16[2,512,416]{2,1,0:T(8,128)(2,1)S(1)} %get-tuple-element.60.factor_ref, bf16[208,1600]{1,0:T(8,128)(2,1)S(1)} %bitcast.30, bf16[208,1600]{1,0:T(8,128)(2,1)S(1)} %bitcast.31, bf16[208,1600]{1,0:T(8,128)(2,1)S(1)} %bitcast.32, bf16[208,1600]{1,0:T(8,128)(2,1)S(1)} %bitcast.33), custom_call_target="tpu_custom_call" | custom-call | flops 1363148800 | bytes 2662400 | tf_op jit(solution)/shard_map/last/pallas_call | solution.py:125
  (19 shorter events, 0.1 us)
Async XLA Ops:
  1.0 11.4 %collective-permute-start = (bf16[1,104,1600]{2,1,0:T(8,128)(2,1)S(1)}, bf16[1,104,1600]{2,1,0:T(8,128)(2,1)S(1)}, u32[]{:S(2)}, u32[]{:S(2)}) collective-permute-start(bf16[1,104,1600]{2,1,0:T(8,128)(2,1)S(1)} %pad.4), channel_id=1, source_target_pairs={{0,1},{1,2},{2,3},{3,0},{4,5},{5,6},{6,7},{7,4},{8,9},{9,10},{10,1... | collective-permute-start | bytes 998408 | tf_op jit(solution)/shard_map/ppermute | solution.py:25
  3.6 35.2 %collective-permute-start.7 = (bf16[1600,512]{1,0:T(8,128)(2,1)}, bf16[1600,512]{1,0:T(8,128)(2,1)S(1)}, u32[]{:S(2)}, u32[]{:S(2)}) collective-permute-start(bf16[1600,512]{1,0:T(8,128)(2,1)} %own_ref.1), channel_id=1, source_target_pairs={{0,64},{32,224},{64,128},{96,32},{128,192},{160,96},{192,0},{224,1... | collective-permute-start | bytes 4915208 | tf_op jit(solution)/shard_map/ppermute | solution.py:14
  6.0 8.2 %collective-permute-start.1 = (bf16[1,104,1600]{2,1,0:T(8,128)(2,1)S(1)}, bf16[1,104,1600]{2,1,0:T(8,128)(2,1)S(1)}, u32[]{:S(2)}, u32[]{:S(2)}) collective-permute-start(bf16[1,104,1600]{2,1,0:T(8,128)(2,1)S(1)} %pad.4), channel_id=1, source_target_pairs={{0,3},{1,0},{2,1},{3,2},{4,7},{5,4},{6,5},{7,6},{8,11},{9,8},{10,9... | collective-permute-start | bytes 998408 | tf_op jit(solution)/shard_map/ppermute | solution.py:25
  12.5 7.6 %collective-permute-start.2 = (bf16[1,104,1600]{2,1,0:T(8,128)(2,1)S(1)}, bf16[1,104,1600]{2,1,0:T(8,128)(2,1)S(1)}, u32[]{:S(2)}, u32[]{:S(2)}) collective-permute-start(bf16[1,104,1600]{2,1,0:T(8,128)(2,1)S(1)} %collective-permute-done), channel_id=1, source_target_pairs={{0,1},{1,2},{2,3},{3,0},{4,5},{5,6},{6,7},{7,4},{8,9},{9,10},{10,1... | collective-permute-start | bytes 998408 | tf_op jit(solution)/shard_map/ppermute | solution.py:25
  20.3 19.6 %copy-start.1 = (bf16[4,104,1600]{2,1,0:T(8,128)(2,1)}, bf16[4,104,1600]{2,1,0:T(8,128)(2,1)S(1)}, u32[]{:S(2)}) copy-start(bf16[4,104,1600]{2,1,0:T(8,128)(2,1)S(1)} %pad_maximum_fusion) | copy-start | bytes 3993604
  20.3 24.0 %collective-permute-start.3 = (bf16[4,104,1600]{2,1,0:T(8,128)(2,1)S(1)}, bf16[4,104,1600]{2,1,0:T(8,128)(2,1)}, u32[]{:S(2)}, u32[]{:S(2)}) collective-permute-start(bf16[4,104,1600]{2,1,0:T(8,128)(2,1)S(1)} %pad_maximum_fusion), channel_id=1, source_target_pairs={{0,4},{1,5},{2,6},{3,7},{4,8},{5,9},{6,10},{7,11},{8,12},{9,13},{1... | collective-permute-start | bytes 3993608 | tf_op jit(solution)/shard_map/ppermute | solution.py:25
  21.7 22.7 %collective-permute-start.5 = (bf16[4,104,1600]{2,1,0:T(8,128)(2,1)S(1)}, bf16[4,104,1600]{2,1,0:T(8,128)(2,1)}, u32[]{:S(2)}, u32[]{:S(2)}) collective-permute-start(bf16[4,104,1600]{2,1,0:T(8,128)(2,1)S(1)} %pad_maximum_fusion), channel_id=1, source_target_pairs={{0,28},{1,29},{2,30},{3,31},{4,0},{5,1},{6,2},{7,3},{8,4},{9,5},{1... | collective-permute-start | bytes 3993608 | tf_op jit(solution)/shard_map/ppermute | solution.py:25
  23.2 12.2 %collective-permute-start.8 = (bf16[1,104,1600]{2,1,0:T(8,128)(2,1)S(1)}, bf16[1,104,1600]{2,1,0:T(8,128)(2,1)S(1)}, u32[]{:S(2)}, u32[]{:S(2)}) collective-permute-start(bf16[1,104,1600]{2,1,0:T(8,128)(2,1)S(1)} %collective-permute-done.1), channel_id=1, source_target_pairs={{32,60},{33,61},{34,62},{35,63},{36,32},{37,33},{38,34},{39,35},{4... | collective-permute-start | bytes 998408 | tf_op jit(solution)/shard_map/ppermute | solution.py:25
  25.4 13.4 %collective-permute-start.9 = (bf16[1,104,1600]{2,1,0:T(8,128)(2,1)S(1)}, bf16[1,104,1600]{2,1,0:T(8,128)(2,1)}, u32[]{:S(2)}, u32[]{:S(2)}) collective-permute-start(bf16[1,104,1600]{2,1,0:T(8,128)(2,1)S(1)} %collective-permute-done.2), channel_id=1, source_target_pairs={{32,36},{33,37},{34,38},{35,39},{36,40},{37,41},{38,42},{39,43},{4... | collective-permute-start | bytes 998408 | tf_op jit(solution)/shard_map/ppermute | solution.py:25
  35.4 9.1 %copy-start.3 = (bf16[1,104,1600]{2,1,0:T(8,128)(2,1)}, bf16[1,104,1600]{2,1,0:T(8,128)(2,1)S(1)}, u32[]{:S(2)}) copy-start(bf16[1,104,1600]{2,1,0:T(8,128)(2,1)S(1)} %collective-permute-done.8) | copy-start | bytes 998404
  39.9 25.2 %collective-permute-start.11 = (bf16[1200,512]{1,0:T(8,128)(2,1)}, bf16[1200,512]{1,0:T(8,128)(2,1)}, u32[]{:S(2)}, u32[]{:S(2)}) collective-permute-start(bf16[1200,512]{1,0:T(8,128)(2,1)} %slice.12), channel_id=1, source_target_pairs={{0,64},{32,224},{64,128},{96,32},{128,192},{160,96},{192,0},{224,1... | collective-permute-start | bytes 3686408 | tf_op jit(solution)/shard_map/ppermute | solution.py:14
  42.4 25.4 %collective-permute-start.10 = (bf16[1600,512]{1,0:T(8,128)(2,1)}, bf16[1600,512]{1,0:T(8,128)(2,1)S(1)}, u32[]{:S(2)}, u32[]{:S(2)}) collective-permute-start(bf16[1600,512]{1,0:T(8,128)(2,1)} %own_ref.1), channel_id=1, source_target_pairs={{0,192},{32,96},{64,0},{96,160},{128,64},{160,224},{192,128},{224,... | collective-permute-start | bytes 4915208 | tf_op jit(solution)/shard_map/ppermute | solution.py:14
  42.4 8.4 %collective-permute-start.12 = (bf16[1,104,1600]{2,1,0:T(8,128)(2,1)S(1)}, bf16[1,104,1600]{2,1,0:T(8,128)(2,1)S(1)}, u32[]{:S(2)}, u32[]{:S(2)}) collective-permute-start(bf16[1,104,1600]{2,1,0:T(8,128)(2,1)S(1)} %collective-permute-done.8), channel_id=1, source_target_pairs={{32,60},{33,61},{34,62},{35,63},{36,32},{37,33},{38,34},{39,35},{4... | collective-permute-start | bytes 998408 | tf_op jit(solution)/shard_map/ppermute | solution.py:25
  44.4 23.5 %collective-permute-start.4 = (bf16[4,104,1600]{2,1,0:T(8,128)(2,1)}, bf16[4,104,1600]{2,1,0:T(8,128)(2,1)}, u32[]{:S(2)}, u32[]{:S(2)}) collective-permute-start(bf16[4,104,1600]{2,1,0:T(8,128)(2,1)} %collective-permute-done.3), channel_id=1, source_target_pairs={{0,4},{1,5},{2,6},{3,7},{4,8},{5,9},{6,10},{7,11},{8,12},{9,13},{1... | collective-permute-start | bytes 3993608 | tf_op jit(solution)/shard_map/ppermute | solution.py:25
  44.5 23.4 %collective-permute-start.6 = (bf16[4,104,1600]{2,1,0:T(8,128)(2,1)}, bf16[4,104,1600]{2,1,0:T(8,128)(2,1)}, u32[]{:S(2)}, u32[]{:S(2)}) collective-permute-start(bf16[4,104,1600]{2,1,0:T(8,128)(2,1)} %collective-permute-done.5), channel_id=1, source_target_pairs={{0,28},{1,29},{2,30},{3,31},{4,0},{5,1},{6,2},{7,3},{8,4},{9,5},{1... | collective-permute-start | bytes 3993608 | tf_op jit(solution)/shard_map/ppermute | solution.py:25
  50.8 0.8 copy-start.4
  51.6 13.6 %collective-permute-start.13 = (bf16[1,104,1600]{2,1,0:T(8,128)(2,1)}, bf16[1,104,1600]{2,1,0:T(8,128)(2,1)}, u32[]{:S(2)}, u32[]{:S(2)}) collective-permute-start(bf16[1,104,1600]{2,1,0:T(8,128)(2,1)} %collective-permute-done.9), channel_id=1, source_target_pairs={{32,36},{33,37},{34,38},{35,39},{36,40},{37,41},{38,42},{39,43},{4... | collective-permute-start | bytes 998408 | tf_op jit(solution)/shard_map/ppermute | solution.py:25
  53.5 13.2 %copy-start.5 = (bf16[1,104,1600]{2,1,0:T(8,128)(2,1)S(1)}, bf16[1,104,1600]{2,1,0:T(8,128)(2,1)}, u32[]{:S(2)}) copy-start(bf16[1,104,1600]{2,1,0:T(8,128)(2,1)} %copy-done.4) | copy-start | bytes 998404
  65.2 4.0 %collective-permute-start.17 = (bf16[4,104,1600]{2,1,0:T(8,128)(2,1)}, bf16[4,104,1600]{2,1,0:T(8,128)(2,1)S(1)}, u32[]{:S(2)}, u32[]{:S(2)}) collective-permute-start(bf16[4,104,1600]{2,1,0:T(8,128)(2,1)} %copy-done.1), channel_id=1, source_target_pairs={{0,32},{32,0},{1,33},{33,1},{2,34},{34,2},{3,35},{35,3},{4,36},{36... | collective-permute-start | bytes 3993608 | tf_op jit(solution)/shard_map/ppermute | solution.py:29
  65.2 6.7 %collective-permute-start.18 = (bf16[4,104,1600]{2,1,0:T(8,128)(2,1)}, bf16[4,104,1600]{2,1,0:T(8,128)(2,1)S(1)}, u32[]{:S(2)}, u32[]{:S(2)}) collective-permute-start(bf16[4,104,1600]{2,1,0:T(8,128)(2,1)} %collective-permute-done.3), channel_id=1, source_target_pairs={{0,32},{32,0},{1,33},{33,1},{2,34},{34,2},{3,35},{35,3},{4,36},{36... | collective-permute-start | bytes 3993608 | tf_op jit(solution)/shard_map/ppermute | solution.py:29
  67.8 15.0 %collective-permute-start.19 = (bf16[4,104,1600]{2,1,0:T(8,128)(2,1)}, bf16[4,104,1600]{2,1,0:T(8,128)(2,1)S(1)}, u32[]{:S(2)}, u32[]{:S(2)}) collective-permute-start(bf16[4,104,1600]{2,1,0:T(8,128)(2,1)} %collective-permute-done.5), channel_id=1, source_target_pairs={{0,32},{32,0},{1,33},{33,1},{2,34},{34,2},{3,35},{35,3},{4,36},{36... | collective-permute-start | bytes 3993608 | tf_op jit(solution)/shard_map/ppermute | solution.py:29
  67.9 9.9 %collective-permute-start.16 = (bf16[400,512]{1,0:T(8,128)(2,1)S(1)}, bf16[400,512]{1,0:T(8,128)(2,1)S(1)}, u32[]{:S(2)}, u32[]{:S(2)}) collective-permute-start(bf16[400,512]{1,0:T(8,128)(2,1)S(1)} %slice.13), channel_id=1, source_target_pairs={{0,192},{32,96},{64,0},{96,160},{128,64},{160,224},{192,128},{224,... | collective-permute-start | bytes 1228808 | tf_op jit(solution)/shard_map/ppermute | solution.py:14
  69.1 18.8 %collective-permute-start.14 = (bf16[4,104,1600]{2,1,0:T(8,128)(2,1)S(1)}, bf16[4,104,1600]{2,1,0:T(8,128)(2,1)S(1)}, u32[]{:S(2)}, u32[]{:S(2)}) collective-permute-start(bf16[4,104,1600]{2,1,0:T(8,128)(2,1)S(1)} %get-tuple-element.64), channel_id=1, source_target_pairs={{0,4},{1,5},{2,6},{3,7},{4,8},{5,9},{6,10},{7,11},{8,12},{9,13},{1... | collective-permute-start | bytes 3993608 | tf_op jit(solution)/shard_map/ppermute | solution.py:25
  69.2 18.7 %collective-permute-start.15 = (bf16[4,104,1600]{2,1,0:T(8,128)(2,1)S(1)}, bf16[4,104,1600]{2,1,0:T(8,128)(2,1)S(1)}, u32[]{:S(2)}, u32[]{:S(2)}) collective-permute-start(bf16[4,104,1600]{2,1,0:T(8,128)(2,1)S(1)} %get-tuple-element.52), channel_id=1, source_target_pairs={{0,28},{1,29},{2,30},{3,31},{4,0},{5,1},{6,2},{7,3},{8,4},{9,5},{1... | collective-permute-start | bytes 3993608 | tf_op jit(solution)/shard_map/ppermute | solution.py:25
  71.9 16.1 %collective-permute-start.21 = (bf16[4,104,1600]{2,1,0:T(8,128)(2,1)S(1)}, bf16[4,104,1600]{2,1,0:T(8,128)(2,1)S(1)}, u32[]{:S(2)}, u32[]{:S(2)}) collective-permute-start(bf16[4,104,1600]{2,1,0:T(8,128)(2,1)S(1)} %get-tuple-element.52), channel_id=1, source_target_pairs={{0,32},{32,0},{1,33},{33,1},{2,34},{34,2},{3,35},{35,3},{4,36},{36... | collective-permute-start | bytes 3993608 | tf_op jit(solution)/shard_map/ppermute | solution.py:29
  77.8 10.2 %collective-permute-start.20 = (bf16[4,104,1600]{2,1,0:T(8,128)(2,1)}, bf16[4,104,1600]{2,1,0:T(8,128)(2,1)S(1)}, u32[]{:S(2)}, u32[]{:S(2)}) collective-permute-start(bf16[4,104,1600]{2,1,0:T(8,128)(2,1)} %collective-permute-done.4), channel_id=1, source_target_pairs={{0,32},{32,0},{1,33},{33,1},{2,34},{34,2},{3,35},{35,3},{4,36},{36... | collective-permute-start | bytes 3993608 | tf_op jit(solution)/shard_map/ppermute | solution.py:29
  88.0 9.3 %copy-start.2 = (bf16[4,104,1600]{2,1,0:T(8,128)(2,1)S(1)}, bf16[4,104,1600]{2,1,0:T(8,128)(2,1)}, u32[]{:S(2)}) copy-start(bf16[4,104,1600]{2,1,0:T(8,128)(2,1)} %copy-done.1) | copy-start | bytes 3993604
  88.0 21.7 %collective-permute-start.24 = (bf16[4,104,1600]{2,1,0:T(8,128)(2,1)S(1)}, bf16[4,104,1600]{2,1,0:T(8,128)(2,1)S(1)}, u32[]{:S(2)}, u32[]{:S(2)}) collective-permute-start(bf16[4,104,1600]{2,1,0:T(8,128)(2,1)S(1)} %collective-permute-done.14), channel_id=1, source_target_pairs={{0,32},{32,0},{1,33},{33,1},{2,34},{34,2},{3,35},{35,3},{4,36},{36... | collective-permute-start | bytes 3993608 | tf_op jit(solution)/shard_map/ppermute | solution.py:29
  94.3 15.4 %collective-permute-start.25 = (bf16[4,104,1600]{2,1,0:T(8,128)(2,1)S(1)}, bf16[4,104,1600]{2,1,0:T(8,128)(2,1)S(1)}, u32[]{:S(2)}, u32[]{:S(2)}) collective-permute-start(bf16[4,104,1600]{2,1,0:T(8,128)(2,1)S(1)} %collective-permute-done.15), channel_id=1, source_target_pairs={{0,32},{32,0},{1,33},{33,1},{2,34},{34,2},{3,35},{35,3},{4,36},{36... | collective-permute-start | bytes 3993608 | tf_op jit(solution)/shard_map/ppermute | solution.py:29
  94.5 13.7 %collective-permute-start.22 = (bf16[2,104,1600]{2,1,0:T(8,128)(2,1)S(1)}, bf16[2,104,1600]{2,1,0:T(8,128)(2,1)S(1)}, u32[]{:S(2)}, u32[]{:S(2)}) collective-permute-start(bf16[2,104,1600]{2,1,0:T(8,128)(2,1)S(1)} %slice.14), channel_id=1, source_target_pairs={{0,4},{1,5},{2,6},{3,7},{4,8},{5,9},{6,10},{7,11},{8,12},{9,13},{1... | collective-permute-start | bytes 1996808 | tf_op jit(solution)/shard_map/ppermute | solution.py:25
  94.7 13.6 %collective-permute-start.23 = (bf16[2,104,1600]{2,1,0:T(8,128)(2,1)S(1)}, bf16[2,104,1600]{2,1,0:T(8,128)(2,1)S(1)}, u32[]{:S(2)}, u32[]{:S(2)}) collective-permute-start(bf16[2,104,1600]{2,1,0:T(8,128)(2,1)S(1)} %slice.15), channel_id=1, source_target_pairs={{0,28},{1,29},{2,30},{3,31},{4,0},{5,1},{6,2},{7,3},{8,4},{9,5},{1... | collective-permute-start | bytes 1996808 | tf_op jit(solution)/shard_map/ppermute | solution.py:25
  97.3 12.4 %copy-start = (f32[512,1600]{0,1:T(8,128)S(1)}, f32[512,1600]{0,1:T(8,128)}, u32[]{:S(2)}) copy-start(f32[512,1600]{0,1:T(8,128)} %param.3) | copy-start | bytes 9830404
  108.2 5.5 %collective-permute-start.26 = (bf16[2,104,1600]{2,1,0:T(8,128)(2,1)S(1)}, bf16[2,104,1600]{2,1,0:T(8,128)(2,1)S(1)}, u32[]{:S(2)}, u32[]{:S(2)}) collective-permute-start(bf16[2,104,1600]{2,1,0:T(8,128)(2,1)S(1)} %collective-permute-done.22), channel_id=1, source_target_pairs={{0,32},{32,0},{1,33},{33,1},{2,34},{34,2},{3,35},{35,3},{4,36},{36... | collective-permute-start | bytes 1996808 | tf_op jit(solution)/shard_map/ppermute | solution.py:29
  109.4 4.3 %collective-permute-start.27 = (bf16[2,104,1600]{2,1,0:T(8,128)(2,1)S(1)}, bf16[2,104,1600]{2,1,0:T(8,128)(2,1)S(1)}, u32[]{:S(2)}, u32[]{:S(2)}) collective-permute-start(bf16[2,104,1600]{2,1,0:T(8,128)(2,1)S(1)} %collective-permute-done.23), channel_id=1, source_target_pairs={{0,32},{32,0},{1,33},{33,1},{2,34},{34,2},{3,35},{35,3},{4,36},{36... | collective-permute-start | bytes 1996808 | tf_op jit(solution)/shard_map/ppermute | solution.py:29

commit v8 on v7

v8 whole, which is shorter than its diff:
```python
import jax
import jax.numpy as jnp
from jax import lax
from jax.experimental import pallas as pl
from jax.experimental.pallas import tpu as pltpu
from jax.sharding import PartitionSpec as P

Z, Y = 8, 4
VMEM = 16 << 20
TIE = 1


def along_row(array, size, first, second):
    pairs = [((row * 2 + core), (row + step) % size * 2 + core) for row in range(size) for core, step in enumerate((first, second))]
    return lax.ppermute(array, ("row", "col"), pairs)


def travel(array, first, second):
    pairs = []
    for core, step in enumerate((first, second)):
        if step is not None:
            for z in range(Z):
                for y in range(Y):
                    target = (z + step[0]) % Z * Y + (y + step[1]) % Y
                    pairs.append(((core * Z + z) * Y + y, core * Z * Y + target))
    return lax.ppermute(array, ("col", "depth"), pairs)


def swap(array):
    return lax.ppermute(array, "col", [(0, 1), (1, 0)])


def padded(blocks, rows):
    parts = blocks.reshape(-1, rows, blocks.shape[-1])
    return jnp.pad(parts, ((0, 0), (0, -rows % 8), (0, 0)))


def ladder(block, height, amplitudes, rows, residual):
    cut = amplitudes.shape[0] // 4 * 3
    along, back = ((0, 1), (1, 0)), ((0, -1), (-1, 0))
    up, down = ((1, 0), (0, 1)), ((-1, 0), (0, -1))
    near = along_row(amplitudes, rows, 1, -1)
    a1 = travel(block, *along)
    b1 = travel(block, *back)
    a2 = travel(block, (0, 2), (2, 0))
    pack = jnp.concatenate([block, a1, b1, a2])
    b2 = travel(b1, None, back[1])
    a3 = travel(a2, None, along[1])
    own, near, b2, a3 = lax.optimization_barrier((amplitudes, near, b2, a3))
    other = along_row(own, rows, -1, 1)
    b3 = travel(b2, None, back[1])
    a4 = travel(a3, None, along[1])
    far_low = along_row(near[:cut], rows, 1, -1)
    rest = jnp.concatenate([b2, a3, b3, a4])
    u1, d1 = travel(pack, *up), travel(pack, *down)
    u2, d2 = travel(u1, *up), travel(d1, down[0], None)
    u2, d2, other, far_low = lax.optimization_barrier((u2, d2, other, far_low))
    first = lax.axis_index("col") == 0
    kept = jnp.where(first, d2, rest)
    u3, d3 = travel(jnp.where(first, u2, rest), *up), travel(kept, *down)
    theirs = [swap(piece) for piece in (pack, u1, d1, u2, kept)]
    other, theirs[TIE] = lax.optimization_barrier((other, theirs[TIE]))
    far_high = along_row(other[cut:], rows, -1, 1)
    own_factors, their_factors = arrange(amplitudes, near, other, far_low, far_high, rows, height)
    total = first_products([own_factors[0], their_factors[0]], [[pack], theirs[:1]])
    u3, d3, total = lax.optimization_barrier((u3, d3, total))
    u4, d4 = travel(u3[:2], *up), travel(d3[2:], *down)
    total = second_products(total, [own_factors[1], their_factors[1]], [[u1, d1, u2, kept], theirs[1:]])
    theirs = [swap(u3), swap(d3)]
    u4, d4, total = lax.optimization_barrier((u4, d4, total))
    total = more_products(residual, total, [own_factors[2], their_factors[2]], [[u3, d3, u4, d4], theirs])
    return last_products(total, their_factors[3], [swap(u4), swap(d4)])


def arrange(own, near, other, far_low, far_high, rows, height):
    cuts = [(0, blocks) for blocks in (4, 16, 12)] + [(1, blocks) for blocks in (4, 16, 8, 4)]
    width = own.shape[1]
    count = own.shape[0] // height
    full = height + -height % 8

    def kernel(own_ref, near_ref, other_ref, low_ref, high_ref, *refs):
        out_refs, held = refs[:-1], refs[-1]
        x, core, depth = (lax.axis_index(name) for name in ("row", "col", "depth"))
        z, y = depth // Y, lax.rem(depth, Y)
        held[:, :, height:, :] = jnp.zeros((2, Z * Y, full - height, width), held.dtype)
        steps = rows - 1 + core * (2 - rows), 1 + core * (rows - 2)
        sources = [(own_ref, 0, 0), (near_ref, steps[0], 0), (other_ref, steps[1], 0), (low_ref, 2, 0), (high_ref, 2, far_low.shape[0] // height)]
        for ref, step, start in sources:
            block_row = lax.rem(x + step, rows)
            half = block_row // (rows // 2)
            for i in range(ref.shape[0] // height):
                there = lax.rem(block_row, rows // 2) * count + start + i
                dz = lax.rem(there // Y - z + Z, Z)
                dy = lax.rem((start + i) % Y - y + Y, Y)
                oz = jnp.where(dz < Z // 2, 2 * dz, 2 * (Z - dz) - 1)
                oy = jnp.where(dy < Y // 2, 2 * dy, 2 * (Y - dy) - 1)
                place = jnp.where(half == 0, oz * Y + oy, oz // Y * (Y * Y) + oy * Y + lax.rem(oz, Y))
                held[lax.rem(half + core, 2), place, pl.ds(0, height), :] = ref[pl.ds(i * height, height), :]
        at = [0, 0]
        for out_ref, (side, blocks) in zip(out_refs, cuts):
            part = held[side, pl.ds(at[side], blocks)].reshape(blocks * full, width)
            out_ref[...] = part if out_ref is out_refs[-1] else part.T
            at[side] += blocks

    size = 2 * own.size * rows
    shapes = [(width, blocks * full) for _, blocks in cuts]
    shapes[-1] = shapes[-1][::-1]
    factors = pl.pallas_call(
        kernel,
        out_shape=[jax.ShapeDtypeStruct(shape, own.dtype) for shape in shapes],
        scratch_shapes=[pltpu.VMEM((2, Z * Y, full, width), own.dtype)],
        compiler_params=pltpu.CompilerParams(vmem_limit_bytes=VMEM),
        cost_estimate=pl.CostEstimate(flops=0, bytes_accessed=2 * size, transcendentals=0),
        name="arrange",
    )(own, near, other, far_low, far_high)
    return factors[:3], factors[3:]


def products(refs, counts, start, width):
    share, at = 0.0, 0
    for count in counts:
        part = jnp.concatenate([ref[:, pl.ds(start, width)] for ref in refs[at + 1 : at + 1 + count]])
        share += jnp.dot(refs[at][...], part, preferred_element_type=jnp.float32)
        at += count + 1
    return share


def multiply(body, shape, factors, pieces, *operands, **options):
    columns = pieces[0][0].shape[-1]
    flops = 2 * sum(factor.size for factor in factors) * columns
    flat = []
    for factor, group in zip(factors, pieces):
        flat += [factor, *[piece.reshape(-1, columns) for piece in group]]
    return pl.pallas_call(
        body,
        out_shape=jax.ShapeDtypeStruct(shape, jnp.float32),
        compiler_params=pltpu.CompilerParams(vmem_limit_bytes=VMEM),
        cost_estimate=pl.CostEstimate(flops=flops, bytes_accessed=flops // 512, transcendentals=0),
        **options,
    )(*operands, *flat)


def tiles(columns, tile=256):
    return [(start, min(tile, columns - start)) for start in range(0, columns, tile)]


def first_products(factors, pieces):
    counts = [len(group) for group in pieces]

    def body(*refs):
        for start, width in tiles(refs[-1].shape[1]):
            refs[-1][:, pl.ds(start, width)] = products(refs, counts, start, width)

    return multiply(body, (factors[0].shape[0], pieces[0][0].shape[-1]), factors, pieces, name="first")


def second_products(total, factors, pieces):
    counts = [len(group) for group in pieces]

    def body(total_ref, *refs):
        for start, width in tiles(refs[-1].shape[1]):
            part = pl.ds(start, width)
            refs[-1][:, part] = total_ref[:, part] + products(refs, counts, start, width)

    return multiply(body, total.shape, factors, pieces, total, name="second")


def more_products(residual, total, factors, pieces):
    counts = [len(group) for group in pieces]

    def body(residual_ref, total_ref, *refs):
        for start, width in tiles(refs[-1].shape[0]):
            part = pl.ds(start, width)
            share = total_ref[:, part] + products(refs, counts, start, width)
            refs[-1][part, :] = residual_ref[part, :] + share.T

    return multiply(body, residual.shape, factors, pieces, residual, total, name="more")


def last_products(total, factor, pieces):
    parts = tiles(total.shape[0])

    def body(total_ref, factor_ref, *refs):
        *piece_refs, out_ref, held, sems = refs
        copies = []
        for number, (start, width) in enumerate(parts):
            part = pl.ds(start, width)
            piece = jnp.concatenate([ref[:, part] for ref in piece_refs])
            share = lax.dot_general(piece, factor_ref[...], (((0,), (0,)), ((), ())), preferred_element_type=jnp.float32)
            held[part, :] = total_ref[part, :] + share
            copies.append(pltpu.make_async_copy(held.at[part], out_ref.at[part], sems.at[number]))
            copies[-1].start()
        for copy in copies:
            copy.wait()

    return multiply(
        body,
        total.shape,
        [factor],
        [pieces],
        total,
        out_specs=pl.BlockSpec(memory_space=pl.ANY),
        scratch_shapes=[pltpu.VMEM(total.shape, jnp.float32), pltpu.SemaphoreType.DMA((len(parts),))],
        name="last",
    )


def solution(mesh):
    rows = mesh.shape["row"]

    def per_device(residual_in, integrals, amplitudes):
        height = integrals.shape[1]
        block = padded(integrals.T, height)
        return ladder(block, height, amplitudes, rows, residual_in.T).T

    placed = (P(("col", "depth"), "row"), P("row", ("col", "depth")), P("row", ("col", "depth")))
    return jax.shard_map(
        per_device, mesh=mesh, in_specs=placed, out_specs=P(("col", "depth"), "row"), check_vma=False
    )
```

time: 118 us -> 113 us (0.958)
  starting transfers between devices: 46.3 us -> 39 us
  waiting for transfers between devices: 40.7 us -> 44.6 us
    ppermute x9, starting transfers between devices: 14.5 us -> 7.02 us  [swap(): return lax.ppermute(array, 'col', [(0, 1), (1, 0)])]
    ppermute x4, waiting for transfers between devices: 0.01 us -> 4.29 us  [along_row(): return lax.ppermute(array, ('row', 'col'), pairs)]
    unnamed x15 -> x13, local copies, waits for them, and re-layouts: 2.87 us -> 0.87 us
    pallas_call x3 -> x4, Pallas kernels: 18.3 us -> 17.5 us  [multiply(): pl.pallas_call(body, out_shape=jax.ShapeDtypeStruct(shape, jnp.float32),...]
  transfers between devices with their start and end apart: 28 -> 28, of which waited for: 8 -> 8; matrix products, arithmetic and copies ran while one was open for 4% -> 5% of each run, Pallas kernels for 17% -> 18%
where the time goes in v8:
time: 113 us
  waiting for transfers between devices  44.6 us (39%)
  starting transfers between devices  39 us (35%)
  Pallas kernels  22.6 us (20%)
  local copies, waits for them, and re-layouts  5.3 us (5%)
    ppermute x15, waiting for transfers between devices, travel(): return lax.ppermute(array, ('col', 'depth'), pairs)  40.3 us
    ppermute x15, starting transfers between devices, travel(): return lax.ppermute(array, ('col', 'depth'), pairs)  26.1 us
    pallas_call x4, Pallas kernels, multiply(): pl.pallas_call(body, out_shape=jax.ShapeDtypeStruct(shape, jnp.float32),...  17.5 us
    ppermute x9, starting transfers between devices, swap(): return lax.ppermute(array, 'col', [(0, 1), (1, 0)])  7.02 us
    ppermute x4, starting transfers between devices, along_row(): return lax.ppermute(array, ('row', 'col'), pairs)  5.87 us
    pallas_call x1, Pallas kernels, arrange(): pl.pallas_call(kernel, out_shape=[jax.ShapeDtypeStruct(shape, own.dtype)...  5.14 us
    ppermute x4, waiting for transfers between devices, along_row(): return lax.ppermute(array, ('row', 'col'), pairs)  4.29 us
  transfers between devices with their start and end apart: 28, of which 8 were waited for; matrix products, arithmetic and copies ran while one was open for 5% of the time, Pallas kernels for 18%

profile of v8, /device:TPU:1, one launch (start us, length us, event | category | flops | bytes accessed | tf_op | source)
XLA Modules:
  0.0 112.6 jit_solution(17425891393325567042)
XLA Ops:
  0.0 3.3 %collective-permute-start.7 = (bf16[1600,512]{1,0:T(8,128)(2,1)}, bf16[1600,512]{1,0:T(8,128)(2,1)S(1)}, u32[]{:S(2)}, u32[]{:S(2)}) collective-permute-start(bf16[1600,512]{1,0:T(8,128)(2,1)} %own_ref.1), channel_id=1, source_target_pairs={{0,64},{32,224},{64,128},{96,32},{128,192},{160,96},{192,0},{224,1... | collective-permute-start | bytes 4915208 | tf_op jit(solution)/shard_map/ppermute | solution.py:15
  3.3 1.0 pad.4
  4.3 5.7 %collective-permute-start.1 = (bf16[1,104,1600]{2,1,0:T(8,128)(2,1)S(1)}, bf16[1,104,1600]{2,1,0:T(8,128)(2,1)S(1)}, u32[]{:S(2)}, u32[]{:S(2)}) collective-permute-start(bf16[1,104,1600]{2,1,0:T(8,128)(2,1)S(1)} %pad.4), channel_id=1, source_target_pairs={{0,3},{1,0},{2,1},{3,2},{4,7},{5,4},{6,5},{7,6},{8,11},{9,8},{10,9... | collective-permute-start | bytes 998408 | tf_op jit(solution)/shard_map/ppermute | solution.py:26
  10.0 0.0 collective-permute-start.2
  10.0 0.0 collective-permute-start
  10.0 4.2 %collective-permute-done.1 = bf16[1,104,1600]{2,1,0:T(8,128)(2,1)S(1)} collective-permute-done((bf16[1,104,1600]{2,1,0:T(8,128)(2,1)S(1)}, bf16[1,104,1600]{2,1,0:T(8,128)(2,1)S(1)}, u32[]{:S(2)}, u32[]{:S(2)}) %collective-permute-start.1) | collective-permute-done | bytes 332832 | tf_op jit(solution)/shard_map/ppermute | solution.py:26
  14.2 7.3 %collective-permute-done.2 = bf16[1,104,1600]{2,1,0:T(8,128)(2,1)S(1)} collective-permute-done((bf16[1,104,1600]{2,1,0:T(8,128)(2,1)S(1)}, bf16[1,104,1600]{2,1,0:T(8,128)(2,1)S(1)}, u32[]{:S(2)}, u32[]{:S(2)}) %collective-permute-start.2) | collective-permute-done | bytes 332832 | tf_op jit(solution)/shard_map/ppermute | solution.py:26
  21.5 1.6 %collective-permute-done = bf16[1,104,1600]{2,1,0:T(8,128)(2,1)S(1)} collective-permute-done((bf16[1,104,1600]{2,1,0:T(8,128)(2,1)S(1)}, bf16[1,104,1600]{2,1,0:T(8,128)(2,1)S(1)}, u32[]{:S(2)}, u32[]{:S(2)}) %collective-permute-start) | collective-permute-done | bytes 332832 | tf_op jit(solution)/shard_map/ppermute | solution.py:26
  23.1 0.2 pad_maximum_fusion
  23.3 1.5 %collective-permute-start.3 = (bf16[4,104,1600]{2,1,0:T(8,128)(2,1)S(1)}, bf16[4,104,1600]{2,1,0:T(8,128)(2,1)}, u32[]{:S(2)}, u32[]{:S(2)}) collective-permute-start(bf16[4,104,1600]{2,1,0:T(8,128)(2,1)S(1)} %pad_maximum_fusion), channel_id=1, source_target_pairs={{0,4},{1,5},{2,6},{3,7},{4,8},{5,9},{6,10},{7,11},{8,12},{9,13},{1... | collective-permute-start | bytes 3993608 | tf_op jit(solution)/shard_map/ppermute | solution.py:26
  24.8 1.5 %collective-permute-start.5 = (bf16[4,104,1600]{2,1,0:T(8,128)(2,1)S(1)}, bf16[4,104,1600]{2,1,0:T(8,128)(2,1)}, u32[]{:S(2)}, u32[]{:S(2)}) collective-permute-start(bf16[4,104,1600]{2,1,0:T(8,128)(2,1)S(1)} %pad_maximum_fusion), channel_id=1, source_target_pairs={{0,28},{1,29},{2,30},{3,31},{4,0},{5,1},{6,2},{7,3},{8,4},{9,5},{1... | collective-permute-start | bytes 3993608 | tf_op jit(solution)/shard_map/ppermute | solution.py:26
  26.4 4.4 %collective-permute-start.8 = (bf16[1,104,1600]{2,1,0:T(8,128)(2,1)S(1)}, bf16[1,104,1600]{2,1,0:T(8,128)(2,1)S(1)}, u32[]{:S(2)}, u32[]{:S(2)}) collective-permute-start(bf16[1,104,1600]{2,1,0:T(8,128)(2,1)S(1)} %collective-permute-done.1), channel_id=1, source_target_pairs={{32,60},{33,61},{34,62},{35,63},{36,32},{37,33},{38,34},{39,35},{4... | collective-permute-start | bytes 998408 | tf_op jit(solution)/shard_map/ppermute | solution.py:26
  30.7 1.9 %collective-permute-start.9 = (bf16[1,104,1600]{2,1,0:T(8,128)(2,1)S(1)}, bf16[1,104,1600]{2,1,0:T(8,128)(2,1)S(1)}, u32[]{:S(2)}, u32[]{:S(2)}) collective-permute-start(bf16[1,104,1600]{2,1,0:T(8,128)(2,1)S(1)} %collective-permute-done.2), channel_id=1, source_target_pairs={{32,36},{33,37},{34,38},{35,39},{36,40},{37,41},{38,42},{39,43},{4... | collective-permute-start | bytes 998408 | tf_op jit(solution)/shard_map/ppermute | solution.py:26
  32.7 6.7 %collective-permute-done.8 = bf16[1,104,1600]{2,1,0:T(8,128)(2,1)S(1)} collective-permute-done((bf16[1,104,1600]{2,1,0:T(8,128)(2,1)S(1)}, bf16[1,104,1600]{2,1,0:T(8,128)(2,1)S(1)}, u32[]{:S(2)}, u32[]{:S(2)}) %collective-permute-start.8) | collective-permute-done | bytes 332832 | tf_op jit(solution)/shard_map/ppermute | solution.py:26
  39.4 4.7 %collective-permute-done.9 = bf16[1,104,1600]{2,1,0:T(8,128)(2,1)S(1)} collective-permute-done((bf16[1,104,1600]{2,1,0:T(8,128)(2,1)S(1)}, bf16[1,104,1600]{2,1,0:T(8,128)(2,1)S(1)}, u32[]{:S(2)}, u32[]{:S(2)}) %collective-permute-start.9) | collective-permute-done | bytes 332832 | tf_op jit(solution)/shard_map/ppermute | solution.py:26
  44.1 0.0 collective-permute-done.7.near_ref
  44.1 1.3 %slice.12 = bf16[1200,512]{1,0:T(8,128)(2,1)} slice(bf16[1600,512]{1,0:T(8,128)(2,1)S(1)} %collective-permute-done.7.near_ref), slice={[0:1200], [0:512]} | slice | bytes 2457600 | tf_op jit(solution)/shard_map/slice | solution.py:53
  45.4 0.5 collective-permute-start.11
  46.0 0.9 collective-permute-start.10
  46.9 1.9 %collective-permute-start.12 = (bf16[1,104,1600]{2,1,0:T(8,128)(2,1)S(1)}, bf16[1,104,1600]{2,1,0:T(8,128)(2,1)S(1)}, u32[]{:S(2)}, u32[]{:S(2)}) collective-permute-start(bf16[1,104,1600]{2,1,0:T(8,128)(2,1)S(1)} %collective-permute-done.8), channel_id=1, source_target_pairs={{32,60},{33,61},{34,62},{35,63},{36,32},{37,33},{38,34},{39,35},{4... | collective-permute-start | bytes 998408 | tf_op jit(solution)/shard_map/ppermute | solution.py:26
  48.8 0.0 collective-permute-done.3
  48.8 0.1 collective-permute-start.4
  48.9 0.0 collective-permute-done.5
  48.9 1.8 %collective-permute-start.6 = (bf16[4,104,1600]{2,1,0:T(8,128)(2,1)}, bf16[4,104,1600]{2,1,0:T(8,128)(2,1)}, u32[]{:S(2)}, u32[]{:S(2)}) collective-permute-start(bf16[4,104,1600]{2,1,0:T(8,128)(2,1)} %collective-permute-done.5), channel_id=1, source_target_pairs={{0,28},{1,29},{2,30},{3,31},{4,0},{5,1},{6,2},{7,3},{8,4},{9,5},{1... | collective-permute-start | bytes 3993608 | tf_op jit(solution)/shard_map/ppermute | solution.py:26
  50.7 8.3 %collective-permute-done.12 = bf16[1,104,1600]{2,1,0:T(8,128)(2,1)S(1)} collective-permute-done((bf16[1,104,1600]{2,1,0:T(8,128)(2,1)S(1)}, bf16[1,104,1600]{2,1,0:T(8,128)(2,1)S(1)}, u32[]{:S(2)}, u32[]{:S(2)}) %collective-permute-start.12) | collective-permute-done | bytes 332832 | tf_op jit(solution)/shard_map/ppermute | solution.py:26
  59.0 0.8 copy-done.3
  59.8 1.9 %collective-permute-start.13 = (bf16[1,104,1600]{2,1,0:T(8,128)(2,1)S(1)}, bf16[1,104,1600]{2,1,0:T(8,128)(2,1)}, u32[]{:S(2)}, u32[]{:S(2)}) collective-permute-start(bf16[1,104,1600]{2,1,0:T(8,128)(2,1)S(1)} %collective-permute-done.9), channel_id=1, source_target_pairs={{32,36},{33,37},{34,38},{35,39},{36,40},{37,41},{38,42},{39,43},{4... | collective-permute-start | bytes 998408 | tf_op jit(solution)/shard_map/ppermute | solution.py:26
  61.7 7.4 %collective-permute-done.13 = bf16[1,104,1600]{2,1,0:T(8,128)(2,1)} collective-permute-done((bf16[1,104,1600]{2,1,0:T(8,128)(2,1)S(1)}, bf16[1,104,1600]{2,1,0:T(8,128)(2,1)}, u32[]{:S(2)}, u32[]{:S(2)}) %collective-permute-start.13) | collective-permute-done | bytes 332832 | tf_op jit(solution)/shard_map/ppermute | solution.py:26
  69.1 0.0 collective-permute-start.16
  69.1 0.0 collective-permute-done.11.low_ref
  69.1 0.6 collective-permute-start.18
  69.8 1.0 constant_dynamic-update-slice_fusion
  70.8 0.0 collective-permute-done.4
  70.8 0.0 collective-permute-done.6
  70.8 0.0 collective-permute-done.10.other_ref
  70.8 0.0 copy-start.1
  70.8 0.3 broadcast_select_fusion
  71.2 0.1 collective-permute-start.14
  71.3 2.7 %collective-permute-start.15 = (bf16[4,104,1600]{2,1,0:T(8,128)(2,1)S(1)}, bf16[4,104,1600]{2,1,0:T(8,128)(2,1)S(1)}, u32[]{:S(2)}, u32[]{:S(2)}) collective-permute-start(bf16[4,104,1600]{2,1,0:T(8,128)(2,1)S(1)} %get-tuple-element.51), channel_id=1, source_target_pairs={{0,28},{1,29},{2,30},{3,31},{4,0},{5,1},{6,2},{7,3},{8,4},{9,5},{1... | collective-permute-start | bytes 3993608 | tf_op jit(solution)/shard_map/ppermute | solution.py:26
  73.9 0.0 collective-permute-done.16
  73.9 1.0 slice.13
  75.0 1.1 collective-permute-start.17
  76.1 3.0 %collective-permute-start.21 = (bf16[4,104,1600]{2,1,0:T(8,128)(2,1)}, bf16[4,104,1600]{2,1,0:T(8,128)(2,1)S(1)}, u32[]{:S(2)}, u32[]{:S(2)}) collective-permute-start(bf16[4,104,1600]{2,1,0:T(8,128)(2,1)} %collective-permute-done.5), channel_id=1, source_target_pairs={{0,32},{32,0},{1,33},{33,1},{2,34},{34,2},{3,35},{35,3},{4,36},{36... | collective-permute-start | bytes 3993608 | tf_op jit(solution)/shard_map/ppermute | solution.py:30
  79.1 0.0 collective-permute-start.23
  79.1 4.3 %collective-permute-done.17.high_ref = bf16[400,512]{1,0:T(8,128)(2,1)S(1)} collective-permute-done((bf16[400,512]{1,0:T(8,128)(2,1)S(1)}, bf16[400,512]{1,0:T(8,128)(2,1)S(1)}, u32[]{:S(2)}, u32[]{:S(2)}) %collective-permute-start.17) | collective-permute-done | bytes 409632 | tf_op jit(solution)/shard_map/ppermute | solution.py:15
  83.3 1.7 %collective-permute-start.22 = (bf16[4,104,1600]{2,1,0:T(8,128)(2,1)S(1)}, bf16[4,104,1600]{2,1,0:T(8,128)(2,1)S(1)}, u32[]{:S(2)}, u32[]{:S(2)}) collective-permute-start(bf16[4,104,1600]{2,1,0:T(8,128)(2,1)S(1)} %collective-permute-done.4), channel_id=1, source_target_pairs={{0,32},{32,0},{1,33},{33,1},{2,34},{34,2},{3,35},{35,3},{4,36},{36... | collective-permute-start | bytes 3993608 | tf_op jit(solution)/shard_map/ppermute | solution.py:30
  85.0 5.1 %arrange.1 = (bf16[512,416]{1,0:T(8,128)(2,1)S(1)}, bf16[512,1664]{1,0:T(8,128)(2,1)S(1)}, bf16[512,1248]{1,0:T(8,128)(2,1)S(1)}, bf16[512,416]{1,0:T(8,128)(2,1...) custom-call(bf16[1600,512]{1,0:T(8,128)(2,1)} %own_ref.1, ...), custom_call_target="tpu_custom_call" | custom-call | bytes 13107200 | tf_op jit(solution)/shard_map/arrange/pallas_call | solution.py:108
  90.2 2.1 %first.1.total_ref = f32[512,1600]{1,0:T(8,128)S(1)} custom-call(bf16[512,416]{1,0:T(8,128)(2,1)S(1)} %get-tuple-element.37.refs_0_, bf16[416,1600]{1,0:T(8,128)(2,1)S(1)} %bitcast.23, bf16[512,416]{1,0:T(8,128)(2,1)S(1)} %get-tuple-element.38.refs_2_, bf16[416,1600]{1,0:T(8,128)(2,1)S(1)} %bitcast.29), custom_call_target="tpu_custom_call" | custom-call | flops 1363148800 | bytes 2662400 | tf_op jit(solution)/shard_map/first/pallas_call | solution.py:134
  92.3 0.0 collective-permute-done.15
  92.3 0.1 collective-permute-start.24
  92.4 0.5 collective-permute-start.25
  92.9 0.1 slice.14
  92.9 0.1 slice.15
  93.0 0.1 collective-permute-start.19
  93.1 2.7 %collective-permute-start.20 = (bf16[2,104,1600]{2,1,0:T(8,128)(2,1)S(1)}, bf16[2,104,1600]{2,1,0:T(8,128)(2,1)S(1)}, u32[]{:S(2)}, u32[]{:S(2)}) collective-permute-start(bf16[2,104,1600]{2,1,0:T(8,128)(2,1)S(1)} %slice.15), channel_id=1, source_target_pairs={{0,28},{1,29},{2,30},{3,31},{4,0},{5,1},{6,2},{7,3},{8,4},{9,5},{1... | collective-permute-start | bytes 1996808 | tf_op jit(solution)/shard_map/ppermute | solution.py:26
  95.8 0.0 collective-permute-done.22
  95.8 8.7 %second.1.total_ref = f32[512,1600]{1,0:T(8,128)S(1)} custom-call(f32[512,1600]{1,0:T(8,128)S(1)} %first.1.total_ref, bf16[512,1664]{1,0:T(8,128)(2,1)S(1)} %get-tuple-element.42.refs_0_, bf16[416,1600]{1,0:T(8,128)(2,1)} %bitcast.5.refs_1_, bf16[416,1600]{1,0:T(8,128)(2,1)} %bitcast.6.refs_2_, bf16[416,1600]{1,0:T(8,128)(2,1)S(1)} %bitcast.24, ...), custom_call_target="tpu_custom_call" | custom-call | flops 5452595200 | bytes 10649600 | tf_op jit(solution)/shard_map/second/pallas_call | solution.py:134
  104.5 0.9 collective-permute-start.26
  105.4 0.2 collective-permute-start.27
  105.6 0.0 collective-permute-done.24
  105.6 0.0 collective-permute-done.25
  105.6 4.7 %more.1.total_ref = f32[1600,512]{1,0:T(8,128)S(1)} custom-call(f32[1600,512]{1,0:T(8,128)S(1)} %bitcast.26, f32[512,1600]{1,0:T(8,128)S(1)} %second.1.total_ref, bf16[512,1248]{1,0:T(8,128)(2,1)S(1)} %get-tuple-element.46.refs_0_, bf16[416,1600]{1,0:T(8,128)(2,1)S(1)} %bitcast.27, bf16[416,1600]{1,0:T(8,128)(2,1)S(1)} %bitcast.28, ...), custom_call_target="tpu_custom_call" | custom-call | flops 3407872000 | bytes 6656000 | tf_op jit(solution)/shard_map/more/pallas_call | solution.py:134
  110.3 0.0 collective-permute-done.27
  110.3 2.1 %last.1 = f32[1600,512]{1,0:T(8,128)} custom-call(f32[1600,512]{1,0:T(8,128)S(1)} %more.1.total_ref, bf16[416,512]{1,0:T(8,128)(2,1)S(1)} %get-tuple-element.50.factor_ref, bf16[208,1600]{1,0:T(8,128)(2,1)S(1)} %bitcast.36, bf16[208,1600]{1,0:T(8,128)(2,1)S(1)} %bitcast.37), custom_call_target="tpu_custom_call" | custom-call | flops 681574400 | bytes 1331200 | tf_op jit(solution)/shard_map/last/pallas_call | solution.py:134
  (18 shorter events, 0.1 us)
Async XLA Ops:
  0.0 44.1 %collective-permute-start.7 = (bf16[1600,512]{1,0:T(8,128)(2,1)}, bf16[1600,512]{1,0:T(8,128)(2,1)S(1)}, u32[]{:S(2)}, u32[]{:S(2)}) collective-permute-start(bf16[1600,512]{1,0:T(8,128)(2,1)} %own_ref.1), channel_id=1, source_target_pairs={{0,64},{32,224},{64,128},{96,32},{128,192},{160,96},{192,0},{224,1... | collective-permute-start | bytes 4915208 | tf_op jit(solution)/shard_map/ppermute | solution.py:15
  4.3 9.9 %collective-permute-start.1 = (bf16[1,104,1600]{2,1,0:T(8,128)(2,1)S(1)}, bf16[1,104,1600]{2,1,0:T(8,128)(2,1)S(1)}, u32[]{:S(2)}, u32[]{:S(2)}) collective-permute-start(bf16[1,104,1600]{2,1,0:T(8,128)(2,1)S(1)} %pad.4), channel_id=1, source_target_pairs={{0,3},{1,0},{2,1},{3,2},{4,7},{5,4},{6,5},{7,6},{8,11},{9,8},{10,9... | collective-permute-start | bytes 998408 | tf_op jit(solution)/shard_map/ppermute | solution.py:26
  10.0 11.5 %collective-permute-start.2 = (bf16[1,104,1600]{2,1,0:T(8,128)(2,1)S(1)}, bf16[1,104,1600]{2,1,0:T(8,128)(2,1)S(1)}, u32[]{:S(2)}, u32[]{:S(2)}) collective-permute-start(bf16[1,104,1600]{2,1,0:T(8,128)(2,1)S(1)} %pad.4), channel_id=1, source_target_pairs={{0,2},{1,3},{2,0},{3,1},{4,6},{5,7},{6,4},{7,5},{8,10},{9,11},{10,... | collective-permute-start | bytes 998408 | tf_op jit(solution)/shard_map/ppermute | solution.py:26
  10.0 13.1 %collective-permute-start = (bf16[1,104,1600]{2,1,0:T(8,128)(2,1)S(1)}, bf16[1,104,1600]{2,1,0:T(8,128)(2,1)S(1)}, u32[]{:S(2)}, u32[]{:S(2)}) collective-permute-start(bf16[1,104,1600]{2,1,0:T(8,128)(2,1)S(1)} %pad.4), channel_id=1, source_target_pairs={{0,1},{1,2},{2,3},{3,0},{4,5},{5,6},{6,7},{7,4},{8,9},{9,10},{10,1... | collective-permute-start | bytes 998408 | tf_op jit(solution)/shard_map/ppermute | solution.py:26
  23.3 25.5 %collective-permute-start.3 = (bf16[4,104,1600]{2,1,0:T(8,128)(2,1)S(1)}, bf16[4,104,1600]{2,1,0:T(8,128)(2,1)}, u32[]{:S(2)}, u32[]{:S(2)}) collective-permute-start(bf16[4,104,1600]{2,1,0:T(8,128)(2,1)S(1)} %pad_maximum_fusion), channel_id=1, source_target_pairs={{0,4},{1,5},{2,6},{3,7},{4,8},{5,9},{6,10},{7,11},{8,12},{9,13},{1... | collective-permute-start | bytes 3993608 | tf_op jit(solution)/shard_map/ppermute | solution.py:26
  24.8 24.1 %collective-permute-start.5 = (bf16[4,104,1600]{2,1,0:T(8,128)(2,1)S(1)}, bf16[4,104,1600]{2,1,0:T(8,128)(2,1)}, u32[]{:S(2)}, u32[]{:S(2)}) collective-permute-start(bf16[4,104,1600]{2,1,0:T(8,128)(2,1)S(1)} %pad_maximum_fusion), channel_id=1, source_target_pairs={{0,28},{1,29},{2,30},{3,31},{4,0},{5,1},{6,2},{7,3},{8,4},{9,5},{1... | collective-permute-start | bytes 3993608 | tf_op jit(solution)/shard_map/ppermute | solution.py:26
  26.4 13.0 %collective-permute-start.8 = (bf16[1,104,1600]{2,1,0:T(8,128)(2,1)S(1)}, bf16[1,104,1600]{2,1,0:T(8,128)(2,1)S(1)}, u32[]{:S(2)}, u32[]{:S(2)}) collective-permute-start(bf16[1,104,1600]{2,1,0:T(8,128)(2,1)S(1)} %collective-permute-done.1), channel_id=1, source_target_pairs={{32,60},{33,61},{34,62},{35,63},{36,32},{37,33},{38,34},{39,35},{4... | collective-permute-start | bytes 998408 | tf_op jit(solution)/shard_map/ppermute | solution.py:26
  30.7 13.4 %collective-permute-start.9 = (bf16[1,104,1600]{2,1,0:T(8,128)(2,1)S(1)}, bf16[1,104,1600]{2,1,0:T(8,128)(2,1)S(1)}, u32[]{:S(2)}, u32[]{:S(2)}) collective-permute-start(bf16[1,104,1600]{2,1,0:T(8,128)(2,1)S(1)} %collective-permute-done.2), channel_id=1, source_target_pairs={{32,36},{33,37},{34,38},{35,39},{36,40},{37,41},{38,42},{39,43},{4... | collective-permute-start | bytes 998408 | tf_op jit(solution)/shard_map/ppermute | solution.py:26
  44.1 4.8 %copy-start = (bf16[1600,512]{1,0:T(8,128)(2,1)}, bf16[1600,512]{1,0:T(8,128)(2,1)S(1)}, u32[]{:S(2)}) copy-start(bf16[1600,512]{1,0:T(8,128)(2,1)S(1)} %collective-permute-done.7.near_ref) | copy-start | bytes 4915204
  45.4 23.7 %collective-permute-start.11 = (bf16[1200,512]{1,0:T(8,128)(2,1)}, bf16[1200,512]{1,0:T(8,128)(2,1)}, u32[]{:S(2)}, u32[]{:S(2)}) collective-permute-start(bf16[1200,512]{1,0:T(8,128)(2,1)} %slice.12), channel_id=1, source_target_pairs={{0,64},{32,224},{64,128},{96,32},{128,192},{160,96},{192,0},{224,1... | collective-permute-start | bytes 3686408 | tf_op jit(solution)/shard_map/ppermute | solution.py:15
  46.0 24.8 %collective-permute-start.10 = (bf16[1600,512]{1,0:T(8,128)(2,1)}, bf16[1600,512]{1,0:T(8,128)(2,1)}, u32[]{:S(2)}, u32[]{:S(2)}) collective-permute-start(bf16[1600,512]{1,0:T(8,128)(2,1)} %own_ref.1), channel_id=1, source_target_pairs={{0,192},{32,96},{64,0},{96,160},{128,64},{160,224},{192,128},{224,... | collective-permute-start | bytes 4915208 | tf_op jit(solution)/shard_map/ppermute | solution.py:15
  46.9 12.1 %collective-permute-start.12 = (bf16[1,104,1600]{2,1,0:T(8,128)(2,1)S(1)}, bf16[1,104,1600]{2,1,0:T(8,128)(2,1)S(1)}, u32[]{:S(2)}, u32[]{:S(2)}) collective-permute-start(bf16[1,104,1600]{2,1,0:T(8,128)(2,1)S(1)} %collective-permute-done.8), channel_id=1, source_target_pairs={{32,60},{33,61},{34,62},{35,63},{36,32},{37,33},{38,34},{39,35},{4... | collective-permute-start | bytes 998408 | tf_op jit(solution)/shard_map/ppermute | solution.py:26
  48.8 22.0 %collective-permute-start.4 = (bf16[4,104,1600]{2,1,0:T(8,128)(2,1)}, bf16[4,104,1600]{2,1,0:T(8,128)(2,1)S(1)}, u32[]{:S(2)}, u32[]{:S(2)}) collective-permute-start(bf16[4,104,1600]{2,1,0:T(8,128)(2,1)} %collective-permute-done.3), channel_id=1, source_target_pairs={{0,4},{1,5},{2,6},{3,7},{4,8},{5,9},{6,10},{7,11},{8,12},{9,13},{1... | collective-permute-start | bytes 3993608 | tf_op jit(solution)/shard_map/ppermute | solution.py:26
  48.9 21.9 %collective-permute-start.6 = (bf16[4,104,1600]{2,1,0:T(8,128)(2,1)}, bf16[4,104,1600]{2,1,0:T(8,128)(2,1)}, u32[]{:S(2)}, u32[]{:S(2)}) collective-permute-start(bf16[4,104,1600]{2,1,0:T(8,128)(2,1)} %collective-permute-done.5), channel_id=1, source_target_pairs={{0,28},{1,29},{2,30},{3,31},{4,0},{5,1},{6,2},{7,3},{8,4},{9,5},{1... | collective-permute-start | bytes 3993608 | tf_op jit(solution)/shard_map/ppermute | solution.py:26
  59.0 0.8 copy-start.3
  59.8 9.3 %collective-permute-start.13 = (bf16[1,104,1600]{2,1,0:T(8,128)(2,1)S(1)}, bf16[1,104,1600]{2,1,0:T(8,128)(2,1)}, u32[]{:S(2)}, u32[]{:S(2)}) collective-permute-start(bf16[1,104,1600]{2,1,0:T(8,128)(2,1)S(1)} %collective-permute-done.9), channel_id=1, source_target_pairs={{32,36},{33,37},{34,38},{35,39},{36,40},{37,41},{38,42},{39,43},{4... | collective-permute-start | bytes 998408 | tf_op jit(solution)/shard_map/ppermute | solution.py:26
  61.7 8.0 %copy-start.4 = (bf16[1,104,1600]{2,1,0:T(8,128)(2,1)S(1)}, bf16[1,104,1600]{2,1,0:T(8,128)(2,1)}, u32[]{:S(2)}) copy-start(bf16[1,104,1600]{2,1,0:T(8,128)(2,1)} %copy-done.3) | copy-start | bytes 998404
  69.1 4.8 %collective-permute-start.16 = (bf16[4,104,1600]{2,1,0:T(8,128)(2,1)}, bf16[4,104,1600]{2,1,0:T(8,128)(2,1)S(1)}, u32[]{:S(2)}, u32[]{:S(2)}) collective-permute-start(bf16[4,104,1600]{2,1,0:T(8,128)(2,1)} %collective-permute-done.3), channel_id=1, source_target_pairs={{0,32},{32,0},{1,33},{33,1},{2,34},{34,2},{3,35},{35,3},{4,36},{36... | collective-permute-start | bytes 3993608 | tf_op jit(solution)/shard_map/ppermute | solution.py:30
  69.1 9.9 %collective-permute-start.18 = (bf16[4,104,1600]{2,1,0:T(8,128)(2,1)S(1)}, bf16[4,104,1600]{2,1,0:T(8,128)(2,1)S(1)}, u32[]{:S(2)}, u32[]{:S(2)}) collective-permute-start(bf16[4,104,1600]{2,1,0:T(8,128)(2,1)S(1)} %pad_maximum_fusion), channel_id=1, source_target_pairs={{0,32},{32,0},{1,33},{33,1},{2,34},{34,2},{3,35},{35,3},{4,36},{36... | collective-permute-start | bytes 3993608 | tf_op jit(solution)/shard_map/ppermute | solution.py:30
  70.8 14.2 %copy-start.1 = (bf16[1600,512]{1,0:T(8,128)(2,1)S(1)}, bf16[1600,512]{1,0:T(8,128)(2,1)}, u32[]{:S(2)}) copy-start(bf16[1600,512]{1,0:T(8,128)(2,1)} %copy-done) | copy-start | bytes 4915204
  71.2 21.1 %collective-permute-start.14 = (bf16[4,104,1600]{2,1,0:T(8,128)(2,1)S(1)}, bf16[4,104,1600]{2,1,0:T(8,128)(2,1)S(1)}, u32[]{:S(2)}, u32[]{:S(2)}) collective-permute-start(bf16[4,104,1600]{2,1,0:T(8,128)(2,1)S(1)} %get-tuple-element.52), channel_id=1, source_target_pairs={{0,4},{1,5},{2,6},{3,7},{4,8},{5,9},{6,10},{7,11},{8,12},{9,13},{1... | collective-permute-start | bytes 3993608 | tf_op jit(solution)/shard_map/ppermute | solution.py:26
  71.3 21.0 %collective-permute-start.15 = (bf16[4,104,1600]{2,1,0:T(8,128)(2,1)S(1)}, bf16[4,104,1600]{2,1,0:T(8,128)(2,1)S(1)}, u32[]{:S(2)}, u32[]{:S(2)}) collective-permute-start(bf16[4,104,1600]{2,1,0:T(8,128)(2,1)S(1)} %get-tuple-element.51), channel_id=1, source_target_pairs={{0,28},{1,29},{2,30},{3,31},{4,0},{5,1},{6,2},{7,3},{8,4},{9,5},{1... | collective-permute-start | bytes 3993608 | tf_op jit(solution)/shard_map/ppermute | solution.py:26
  75.0 8.4 %collective-permute-start.17 = (bf16[400,512]{1,0:T(8,128)(2,1)S(1)}, bf16[400,512]{1,0:T(8,128)(2,1)S(1)}, u32[]{:S(2)}, u32[]{:S(2)}) collective-permute-start(bf16[400,512]{1,0:T(8,128)(2,1)S(1)} %slice.13), channel_id=1, source_target_pairs={{0,192},{32,96},{64,0},{96,160},{128,64},{160,224},{192,128},{224,... | collective-permute-start | bytes 1228808 | tf_op jit(solution)/shard_map/ppermute | solution.py:15
  76.1 16.9 %collective-permute-start.21 = (bf16[4,104,1600]{2,1,0:T(8,128)(2,1)}, bf16[4,104,1600]{2,1,0:T(8,128)(2,1)S(1)}, u32[]{:S(2)}, u32[]{:S(2)}) collective-permute-start(bf16[4,104,1600]{2,1,0:T(8,128)(2,1)} %collective-permute-done.5), channel_id=1, source_target_pairs={{0,32},{32,0},{1,33},{33,1},{2,34},{34,2},{3,35},{35,3},{4,36},{36... | collective-permute-start | bytes 3993608 | tf_op jit(solution)/shard_map/ppermute | solution.py:30
  79.1 14.0 %collective-permute-start.23 = (bf16[4,104,1600]{2,1,0:T(8,128)(2,1)S(1)}, bf16[4,104,1600]{2,1,0:T(8,128)(2,1)S(1)}, u32[]{:S(2)}, u32[]{:S(2)}) collective-permute-start(bf16[4,104,1600]{2,1,0:T(8,128)(2,1)S(1)} %get-tuple-element.51), channel_id=1, source_target_pairs={{0,32},{32,0},{1,33},{33,1},{2,34},{34,2},{3,35},{35,3},{4,36},{36... | collective-permute-start | bytes 3993608 | tf_op jit(solution)/shard_map/ppermute | solution.py:30
  83.3 12.4 %collective-permute-start.22 = (bf16[4,104,1600]{2,1,0:T(8,128)(2,1)S(1)}, bf16[4,104,1600]{2,1,0:T(8,128)(2,1)S(1)}, u32[]{:S(2)}, u32[]{:S(2)}) collective-permute-start(bf16[4,104,1600]{2,1,0:T(8,128)(2,1)S(1)} %collective-permute-done.4), channel_id=1, source_target_pairs={{0,32},{32,0},{1,33},{33,1},{2,34},{34,2},{3,35},{35,3},{4,36},{36... | collective-permute-start | bytes 3993608 | tf_op jit(solution)/shard_map/ppermute | solution.py:30
  92.3 13.3 %collective-permute-start.24 = (bf16[4,104,1600]{2,1,0:T(8,128)(2,1)S(1)}, bf16[4,104,1600]{2,1,0:T(8,128)(2,1)S(1)}, u32[]{:S(2)}, u32[]{:S(2)}) collective-permute-start(bf16[4,104,1600]{2,1,0:T(8,128)(2,1)S(1)} %collective-permute-done.14), channel_id=1, source_target_pairs={{0,32},{32,0},{1,33},{33,1},{2,34},{34,2},{3,35},{35,3},{4,36},{36... | collective-permute-start | bytes 3993608 | tf_op jit(solution)/shard_map/ppermute | solution.py:30
  92.4 13.2 %collective-permute-start.25 = (bf16[4,104,1600]{2,1,0:T(8,128)(2,1)S(1)}, bf16[4,104,1600]{2,1,0:T(8,128)(2,1)S(1)}, u32[]{:S(2)}, u32[]{:S(2)}) collective-permute-start(bf16[4,104,1600]{2,1,0:T(8,128)(2,1)S(1)} %collective-permute-done.15), channel_id=1, source_target_pairs={{0,32},{32,0},{1,33},{33,1},{2,34},{34,2},{3,35},{35,3},{4,36},{36... | collective-permute-start | bytes 3993608 | tf_op jit(solution)/shard_map/ppermute | solution.py:30
  93.0 11.5 %collective-permute-start.19 = (bf16[2,104,1600]{2,1,0:T(8,128)(2,1)S(1)}, bf16[2,104,1600]{2,1,0:T(8,128)(2,1)S(1)}, u32[]{:S(2)}, u32[]{:S(2)}) collective-permute-start(bf16[2,104,1600]{2,1,0:T(8,128)(2,1)S(1)} %slice.14), channel_id=1, source_target_pairs={{0,4},{1,5},{2,6},{3,7},{4,8},{5,9},{6,10},{7,11},{8,12},{9,13},{1... | collective-permute-start | bytes 1996808 | tf_op jit(solution)/shard_map/ppermute | solution.py:26
  93.1 11.4 %collective-permute-start.20 = (bf16[2,104,1600]{2,1,0:T(8,128)(2,1)S(1)}, bf16[2,104,1600]{2,1,0:T(8,128)(2,1)S(1)}, u32[]{:S(2)}, u32[]{:S(2)}) collective-permute-start(bf16[2,104,1600]{2,1,0:T(8,128)(2,1)S(1)} %slice.15), channel_id=1, source_target_pairs={{0,28},{1,29},{2,30},{3,31},{4,0},{5,1},{6,2},{7,3},{8,4},{9,5},{1... | collective-permute-start | bytes 1996808 | tf_op jit(solution)/shard_map/ppermute | solution.py:26
  95.8 9.9 %copy-start.2 = (f32[512,1600]{0,1:T(8,128)S(1)}, f32[512,1600]{0,1:T(8,128)}, u32[]{:S(2)}) copy-start(f32[512,1600]{0,1:T(8,128)} %param.3) | copy-start | bytes 9830404
  104.5 5.8 %collective-permute-start.26 = (bf16[2,104,1600]{2,1,0:T(8,128)(2,1)S(1)}, bf16[2,104,1600]{2,1,0:T(8,128)(2,1)S(1)}, u32[]{:S(2)}, u32[]{:S(2)}) collective-permute-start(bf16[2,104,1600]{2,1,0:T(8,128)(2,1)S(1)} %collective-permute-done.19), channel_id=1, source_target_pairs={{0,32},{32,0},{1,33},{33,1},{2,34},{34,2},{3,35},{35,3},{4,36},{36... | collective-permute-start | bytes 1996808 | tf_op jit(solution)/shard_map/ppermute | solution.py:30
  105.4 4.9 %collective-permute-start.27 = (bf16[2,104,1600]{2,1,0:T(8,128)(2,1)S(1)}, bf16[2,104,1600]{2,1,0:T(8,128)(2,1)S(1)}, u32[]{:S(2)}, u32[]{:S(2)}) collective-permute-start(bf16[2,104,1600]{2,1,0:T(8,128)(2,1)S(1)} %collective-permute-done.20), channel_id=1, source_target_pairs={{0,32},{32,0},{1,33},{33,1},{2,34},{34,2},{3,35},{35,3},{4,36},{36... | collective-permute-start | bytes 1996808 | tf_op jit(solution)/shard_map/ppermute | solution.py:30

commit v9 on v8

--- a/solution.py
+++ b/solution.py
@@ -7,7 +7,6 @@
 
 Z, Y = 8, 4
 VMEM = 16 << 20
-TIE = 1
 
 
 def along_row(array, size, first, second):
@@ -36,7 +35,6 @@
 
 
 def ladder(block, height, amplitudes, rows, residual):
-    cut = amplitudes.shape[0] // 4 * 3
     along, back = ((0, 1), (1, 0)), ((0, -1), (-1, 0))
     up, down = ((1, 0), (0, 1)), ((-1, 0), (0, -1))
     near = along_row(amplitudes, rows, 1, -1)
@@ -50,48 +48,45 @@
     other = along_row(own, rows, -1, 1)
     b3 = travel(b2, None, back[1])
     a4 = travel(a3, None, along[1])
-    far_low = along_row(near[:cut], rows, 1, -1)
+    far = along_row(near, rows, 1, -1)
     rest = jnp.concatenate([b2, a3, b3, a4])
     u1, d1 = travel(pack, *up), travel(pack, *down)
     u2, d2 = travel(u1, *up), travel(d1, down[0], None)
-    u2, d2, other, far_low = lax.optimization_barrier((u2, d2, other, far_low))
+    u2, d2, other, far = lax.optimization_barrier((u2, d2, other, far))
     first = lax.axis_index("col") == 0
     kept = jnp.where(first, d2, rest)
     u3, d3 = travel(jnp.where(first, u2, rest), *up), travel(kept, *down)
     theirs = [swap(piece) for piece in (pack, u1, d1, u2, kept)]
-    other, theirs[TIE] = lax.optimization_barrier((other, theirs[TIE]))
-    far_high = along_row(other[cut:], rows, -1, 1)
-    own_factors, their_factors = arrange(amplitudes, near, other, far_low, far_high, rows, height)
-    total = first_products([own_factors[0], their_factors[0]], [[pack], theirs[:1]])
+    own_factors, their_factors = arrange(amplitudes, near, other, far, rows, height)
+    total = first_products([own_factors[0], their_factors[0]], [[pack, u1, d1], theirs[:3]])
     u3, d3, total = lax.optimization_barrier((u3, d3, total))
     u4, d4 = travel(u3[:2], *up), travel(d3[2:], *down)
-    total = second_products(total, [own_factors[1], their_factors[1]], [[u1, d1, u2, kept], theirs[1:]])
+    total = second_products(total, [own_factors[1], their_factors[1]], [[u2, kept], theirs[3:]])
     theirs = [swap(u3), swap(d3)]
     u4, d4, total = lax.optimization_barrier((u4, d4, total))
     total = more_products(residual, total, [own_factors[2], their_factors[2]], [[u3, d3, u4, d4], theirs])
     return last_products(total, their_factors[3], [swap(u4), swap(d4)])
 
 
-def arrange(own, near, other, far_low, far_high, rows, height):
-    cuts = [(0, blocks) for blocks in (4, 16, 12)] + [(1, blocks) for blocks in (4, 16, 8, 4)]
+def arrange(own, near, other, far, rows, height):
+    cuts = [(0, blocks) for blocks in (12, 8, 12)] + [(1, blocks) for blocks in (12, 8, 8, 4)]
     width = own.shape[1]
     count = own.shape[0] // height
     full = height + -height % 8
 
-    def kernel(own_ref, near_ref, other_ref, low_ref, high_ref, *refs):
+    def kernel(own_ref, near_ref, other_ref, far_ref, *refs):
         out_refs, held = refs[:-1], refs[-1]
         x, core, depth = (lax.axis_index(name) for name in ("row", "col", "depth"))
         z, y = depth // Y, lax.rem(depth, Y)
         held[:, :, height:, :] = jnp.zeros((2, Z * Y, full - height, width), held.dtype)
         steps = rows - 1 + core * (2 - rows), 1 + core * (rows - 2)
-        sources = [(own_ref, 0, 0), (near_ref, steps[0], 0), (other_ref, steps[1], 0), (low_ref, 2, 0), (high_ref, 2, far_low.shape[0] // height)]
-        for ref, step, start in sources:
+        for ref, step in (own_ref, 0), (near_ref, steps[0]), (other_ref, steps[1]), (far_ref, 2):
             block_row = lax.rem(x + step, rows)
             half = block_row // (rows // 2)
-            for i in range(ref.shape[0] // height):
-                there = lax.rem(block_row, rows // 2) * count + start + i
+            for i in range(count):
+                there = lax.rem(block_row, rows // 2) * count + i
                 dz = lax.rem(there // Y - z + Z, Z)
-                dy = lax.rem((start + i) % Y - y + Y, Y)
+                dy = lax.rem(i % Y - y + Y, Y)
                 oz = jnp.where(dz < Z // 2, 2 * dz, 2 * (Z - dz) - 1)
                 oy = jnp.where(dy < Y // 2, 2 * dy, 2 * (Y - dy) - 1)
                 place = jnp.where(half == 0, oz * Y + oy, oz // Y * (Y * Y) + oy * Y + lax.rem(oz, Y))
@@ -112,7 +107,7 @@
         compiler_params=pltpu.CompilerParams(vmem_limit_bytes=VMEM),
         cost_estimate=pl.CostEstimate(flops=0, bytes_accessed=2 * size, transcendentals=0),
         name="arrange",
-    )(own, near, other, far_low, far_high)
+    )(own, near, other, far)
     return factors[:3], factors[3:]
 
 

time: 113 us -> 113 us (level)
  waiting for transfers between devices: 44.6 us -> 47.6 us
  local copies, waits for them, and re-layouts: 5.3 us -> 3.24 us
    ppermute x15, waiting for transfers between devices: 40.3 us -> 47.6 us  [travel(): return lax.ppermute(array, ('col', 'depth'), pairs)]
    ppermute x4 -> x3, waiting for transfers between devices: 4.29 us -> 0.01 us  [along_row(): return lax.ppermute(array, ('row', 'col'), pairs)]
    slice x2 -> x0, local copies, waits for them, and re-layouts: 2.31 us -> none  [the longest x1 1.28 us: ladder(): far_low = along_row(near[:cut], rows, 1, -1)]
    unnamed x13, local copies, waits for them, and re-layouts: 0.87 us -> 2.09 us
    ppermute x4 -> x3, starting transfers between devices: 5.87 us -> 4.77 us  [along_row(): return lax.ppermute(array, ('row', 'col'), pairs)]
  transfers between devices with their start and end apart: 28 -> 27, of which waited for: 8 -> 9; matrix products, arithmetic and copies ran while one was open for 5% -> 3% of each run, Pallas kernels for 18% -> 18%
where the time goes in v9:
time: 113 us
  waiting for transfers between devices  47.6 us (42%)
  starting transfers between devices  38.3 us (34%)
  Pallas kernels  22.6 us (20%)
  local copies, waits for them, and re-layouts  3.24 us (3%)
    ppermute x15, waiting for transfers between devices, travel(): return lax.ppermute(array, ('col', 'depth'), pairs)  47.6 us
    ppermute x15, starting transfers between devices, travel(): return lax.ppermute(array, ('col', 'depth'), pairs)  26.5 us
    pallas_call x4, Pallas kernels, multiply(): pl.pallas_call(body, out_shape=jax.ShapeDtypeStruct(shape, jnp.float32),...  17.3 us
    ppermute x9, starting transfers between devices, swap(): return lax.ppermute(array, 'col', [(0, 1), (1, 0)])  7.02 us
    pallas_call x1, Pallas kernels, arrange(): pl.pallas_call(kernel, out_shape=[jax.ShapeDtypeStruct(shape, own.dtype)...  5.27 us
    ppermute x3, starting transfers between devices, along_row(): return lax.ppermute(array, ('row', 'col'), pairs)  4.77 us
  transfers between devices with their start and end apart: 27, of which 9 were waited for; matrix products, arithmetic and copies ran while one was open for 3% of the time, Pallas kernels for 18%

profile of v9, /device:TPU:1, one launch (start us, length us, event | category | flops | bytes accessed | tf_op | source)
XLA Modules:
  0.0 112.7 jit_solution(6719824236549635671)
XLA Ops:
  0.0 3.3 %collective-permute-start.7 = (bf16[1600,512]{1,0:T(8,128)(2,1)}, bf16[1600,512]{1,0:T(8,128)(2,1)}, u32[]{:S(2)}, u32[]{:S(2)}) collective-permute-start(bf16[1600,512]{1,0:T(8,128)(2,1)} %own_ref.1), channel_id=1, source_target_pairs={{0,64},{32,224},{64,128},{96,32},{128,192},{160,96},{192,0},{224,1... | collective-permute-start | bytes 4915208 | tf_op jit(solution)/shard_map/ppermute | solution.py:14
  3.3 1.0 pad.4
  4.3 0.0 copy-start.1
  4.3 5.7 %collective-permute-start.1 = (bf16[1,104,1600]{2,1,0:T(8,128)(2,1)S(1)}, bf16[1,104,1600]{2,1,0:T(8,128)(2,1)S(1)}, u32[]{:S(2)}, u32[]{:S(2)}) collective-permute-start(bf16[1,104,1600]{2,1,0:T(8,128)(2,1)S(1)} %pad.4), channel_id=1, source_target_pairs={{0,3},{1,0},{2,1},{3,2},{4,7},{5,4},{6,5},{7,6},{8,11},{9,8},{10,9... | collective-permute-start | bytes 998408 | tf_op jit(solution)/shard_map/ppermute | solution.py:25
  10.0 0.0 collective-permute-start.2
  10.0 0.0 collective-permute-start
  10.0 4.2 %collective-permute-done.1 = bf16[1,104,1600]{2,1,0:T(8,128)(2,1)S(1)} collective-permute-done((bf16[1,104,1600]{2,1,0:T(8,128)(2,1)S(1)}, bf16[1,104,1600]{2,1,0:T(8,128)(2,1)S(1)}, u32[]{:S(2)}, u32[]{:S(2)}) %collective-permute-start.1) | collective-permute-done | bytes 332832 | tf_op jit(solution)/shard_map/ppermute | solution.py:25
  14.2 7.3 %collective-permute-done.2 = bf16[1,104,1600]{2,1,0:T(8,128)(2,1)S(1)} collective-permute-done((bf16[1,104,1600]{2,1,0:T(8,128)(2,1)S(1)}, bf16[1,104,1600]{2,1,0:T(8,128)(2,1)S(1)}, u32[]{:S(2)}, u32[]{:S(2)}) %collective-permute-start.2) | collective-permute-done | bytes 332832 | tf_op jit(solution)/shard_map/ppermute | solution.py:25
  21.5 1.7 %collective-permute-done = bf16[1,104,1600]{2,1,0:T(8,128)(2,1)S(1)} collective-permute-done((bf16[1,104,1600]{2,1,0:T(8,128)(2,1)S(1)}, bf16[1,104,1600]{2,1,0:T(8,128)(2,1)S(1)}, u32[]{:S(2)}, u32[]{:S(2)}) %collective-permute-start) | collective-permute-done | bytes 332832 | tf_op jit(solution)/shard_map/ppermute | solution.py:25
  23.2 0.2 pad_maximum_fusion
  23.5 0.0 copy-start.2
  23.5 1.4 %collective-permute-start.3 = (bf16[4,104,1600]{2,1,0:T(8,128)(2,1)S(1)}, bf16[4,104,1600]{2,1,0:T(8,128)(2,1)}, u32[]{:S(2)}, u32[]{:S(2)}) collective-permute-start(bf16[4,104,1600]{2,1,0:T(8,128)(2,1)S(1)} %pad_maximum_fusion), channel_id=1, source_target_pairs={{0,4},{1,5},{2,6},{3,7},{4,8},{5,9},{6,10},{7,11},{8,12},{9,13},{1... | collective-permute-start | bytes 3993608 | tf_op jit(solution)/shard_map/ppermute | solution.py:25
  24.9 1.5 %collective-permute-start.5 = (bf16[4,104,1600]{2,1,0:T(8,128)(2,1)S(1)}, bf16[4,104,1600]{2,1,0:T(8,128)(2,1)}, u32[]{:S(2)}, u32[]{:S(2)}) collective-permute-start(bf16[4,104,1600]{2,1,0:T(8,128)(2,1)S(1)} %pad_maximum_fusion), channel_id=1, source_target_pairs={{0,28},{1,29},{2,30},{3,31},{4,0},{5,1},{6,2},{7,3},{8,4},{9,5},{1... | collective-permute-start | bytes 3993608 | tf_op jit(solution)/shard_map/ppermute | solution.py:25
  26.4 4.5 %collective-permute-start.8 = (bf16[1,104,1600]{2,1,0:T(8,128)(2,1)S(1)}, bf16[1,104,1600]{2,1,0:T(8,128)(2,1)S(1)}, u32[]{:S(2)}, u32[]{:S(2)}) collective-permute-start(bf16[1,104,1600]{2,1,0:T(8,128)(2,1)S(1)} %collective-permute-done.1), channel_id=1, source_target_pairs={{32,60},{33,61},{34,62},{35,63},{36,32},{37,33},{38,34},{39,35},{4... | collective-permute-start | bytes 998408 | tf_op jit(solution)/shard_map/ppermute | solution.py:25
  30.9 1.9 %collective-permute-start.9 = (bf16[1,104,1600]{2,1,0:T(8,128)(2,1)S(1)}, bf16[1,104,1600]{2,1,0:T(8,128)(2,1)S(1)}, u32[]{:S(2)}, u32[]{:S(2)}) collective-permute-start(bf16[1,104,1600]{2,1,0:T(8,128)(2,1)S(1)} %collective-permute-done.2), channel_id=1, source_target_pairs={{32,36},{33,37},{34,38},{35,39},{36,40},{37,41},{38,42},{39,43},{4... | collective-permute-start | bytes 998408 | tf_op jit(solution)/shard_map/ppermute | solution.py:25
  32.8 6.6 %collective-permute-done.8 = bf16[1,104,1600]{2,1,0:T(8,128)(2,1)S(1)} collective-permute-done((bf16[1,104,1600]{2,1,0:T(8,128)(2,1)S(1)}, bf16[1,104,1600]{2,1,0:T(8,128)(2,1)S(1)}, u32[]{:S(2)}, u32[]{:S(2)}) %collective-permute-start.8) | collective-permute-done | bytes 332832 | tf_op jit(solution)/shard_map/ppermute | solution.py:25
  39.4 4.8 %collective-permute-done.9 = bf16[1,104,1600]{2,1,0:T(8,128)(2,1)S(1)} collective-permute-done((bf16[1,104,1600]{2,1,0:T(8,128)(2,1)S(1)}, bf16[1,104,1600]{2,1,0:T(8,128)(2,1)S(1)}, u32[]{:S(2)}, u32[]{:S(2)}) %collective-permute-start.9) | collective-permute-done | bytes 332832 | tf_op jit(solution)/shard_map/ppermute | solution.py:25
  44.3 0.0 collective-permute-done.7.near_ref
  44.3 0.6 collective-permute-start.11
  44.8 0.9 collective-permute-start.10
  45.7 0.0 collective-permute-done.3
  45.8 0.1 collective-permute-start.4
  45.8 0.0 collective-permute-done.5
  45.9 1.9 %collective-permute-start.6 = (bf16[4,104,1600]{2,1,0:T(8,128)(2,1)}, bf16[4,104,1600]{2,1,0:T(8,128)(2,1)}, u32[]{:S(2)}, u32[]{:S(2)}) collective-permute-start(bf16[4,104,1600]{2,1,0:T(8,128)(2,1)} %collective-permute-done.5), channel_id=1, source_target_pairs={{0,28},{1,29},{2,30},{3,31},{4,0},{5,1},{6,2},{7,3},{8,4},{9,5},{1... | collective-permute-start | bytes 3993608 | tf_op jit(solution)/shard_map/ppermute | solution.py:25
  47.7 1.9 %collective-permute-start.12 = (bf16[1,104,1600]{2,1,0:T(8,128)(2,1)S(1)}, bf16[1,104,1600]{2,1,0:T(8,128)(2,1)}, u32[]{:S(2)}, u32[]{:S(2)}) collective-permute-start(bf16[1,104,1600]{2,1,0:T(8,128)(2,1)S(1)} %collective-permute-done.8), channel_id=1, source_target_pairs={{32,60},{33,61},{34,62},{35,63},{36,32},{37,33},{38,34},{39,35},{4... | collective-permute-start | bytes 998408 | tf_op jit(solution)/shard_map/ppermute | solution.py:25
  49.6 0.0 copy-start.3
  49.6 10.2 %collective-permute-done.12 = bf16[1,104,1600]{2,1,0:T(8,128)(2,1)} collective-permute-done((bf16[1,104,1600]{2,1,0:T(8,128)(2,1)S(1)}, bf16[1,104,1600]{2,1,0:T(8,128)(2,1)}, u32[]{:S(2)}, u32[]{:S(2)}) %collective-permute-start.12) | collective-permute-done | bytes 332832 | tf_op jit(solution)/shard_map/ppermute | solution.py:25
  59.8 1.9 %collective-permute-start.13 = (bf16[1,104,1600]{2,1,0:T(8,128)(2,1)}, bf16[1,104,1600]{2,1,0:T(8,128)(2,1)S(1)}, u32[]{:S(2)}, u32[]{:S(2)}) collective-permute-start(bf16[1,104,1600]{2,1,0:T(8,128)(2,1)} %copy-done.4), channel_id=1, source_target_pairs={{32,36},{33,37},{34,38},{35,39},{36,40},{37,41},{38,42},{39,43},{4... | collective-permute-start | bytes 998408 | tf_op jit(solution)/shard_map/ppermute | solution.py:25
  61.8 1.0 constant_dynamic-update-slice_fusion.2
  62.8 6.4 %collective-permute-done.13 = bf16[1,104,1600]{2,1,0:T(8,128)(2,1)S(1)} collective-permute-done((bf16[1,104,1600]{2,1,0:T(8,128)(2,1)}, bf16[1,104,1600]{2,1,0:T(8,128)(2,1)S(1)}, u32[]{:S(2)}, u32[]{:S(2)}) %collective-permute-start.13) | collective-permute-done | bytes 332832 | tf_op jit(solution)/shard_map/ppermute | solution.py:25
  69.3 0.0 collective-permute-start.16
  69.3 1.0 constant_dynamic-update-slice_fusion.1
  70.3 0.0 collective-permute-done.4
  70.3 0.6 collective-permute-start.17
  70.9 0.0 collective-permute-done.6
  70.9 0.1 collective-permute-start.18
  71.0 0.0 collective-permute-done.11.far_ref
  71.0 0.0 collective-permute-done.10.other_ref
  71.0 0.4 broadcast_select_fusion
  71.4 1.3 %collective-permute-start.14 = (bf16[4,104,1600]{2,1,0:T(8,128)(2,1)S(1)}, bf16[4,104,1600]{2,1,0:T(8,128)(2,1)S(1)}, u32[]{:S(2)}, u32[]{:S(2)}) collective-permute-start(bf16[4,104,1600]{2,1,0:T(8,128)(2,1)S(1)} %get-tuple-element.48), channel_id=1, source_target_pairs={{0,4},{1,5},{2,6},{3,7},{4,8},{5,9},{6,10},{7,11},{8,12},{9,13},{1... | collective-permute-start | bytes 3993608 | tf_op jit(solution)/shard_map/ppermute | solution.py:25
  72.8 1.5 %collective-permute-start.15 = (bf16[4,104,1600]{2,1,0:T(8,128)(2,1)S(1)}, bf16[4,104,1600]{2,1,0:T(8,128)(2,1)S(1)}, u32[]{:S(2)}, u32[]{:S(2)}) collective-permute-start(bf16[4,104,1600]{2,1,0:T(8,128)(2,1)S(1)} %get-tuple-element.47), channel_id=1, source_target_pairs={{0,28},{1,29},{2,30},{3,31},{4,0},{5,1},{6,2},{7,3},{8,4},{9,5},{1... | collective-permute-start | bytes 3993608 | tf_op jit(solution)/shard_map/ppermute | solution.py:25
  74.3 2.2 %collective-permute-start.22 = (bf16[4,104,1600]{2,1,0:T(8,128)(2,1)S(1)}, bf16[4,104,1600]{2,1,0:T(8,128)(2,1)S(1)}, u32[]{:S(2)}, u32[]{:S(2)}) collective-permute-start(bf16[4,104,1600]{2,1,0:T(8,128)(2,1)S(1)} %get-tuple-element.47), channel_id=1, source_target_pairs={{0,32},{32,0},{1,33},{33,1},{2,34},{34,2},{3,35},{35,3},{4,36},{36... | collective-permute-start | bytes 3993608 | tf_op jit(solution)/shard_map/ppermute | solution.py:29
  76.5 0.0 collective-permute-done.17
  76.5 0.3 collective-permute-start.21
  76.7 5.3 %arrange.1 = (bf16[512,1248]{1,0:T(8,128)(2,1)S(1)}, bf16[512,832]{1,0:T(8,128)(2,1)S(1)}, bf16[512,1248]{1,0:T(8,128)(2,1)S(1)}, bf16[512,1248]{1,0:T(8,128)(2,...) custom-call(bf16[1600,512]{1,0:T(8,128)(2,1)S(1)} %copy-done.1, ...), custom_call_target="tpu_custom_call" | custom-call | bytes 13107200 | tf_op jit(solution)/shard_map/arrange/pallas_call | solution.py:103
  82.0 0.0 collective-permute-done.18
  82.0 6.7 %first.1.total_ref = f32[512,1600]{1,0:T(8,128)S(1)} custom-call(bf16[512,1248]{1,0:T(8,128)(2,1)S(1)} %get-tuple-element.34.refs_0_, bf16[416,1600]{1,0:T(8,128)(2,1)S(1)} %bitcast.30, bf16[416,1600]{1,0:T(8,128)(2,1)} %bitcast.4.refs_2_, bf16[416,1600]{1,0:T(8,128)(2,1)} %bitcast.5.refs_3_, bf16[512,1248]{1,0:T(8,128)(2,1)S(1)} %get-tuple-element.35.refs_4_, ...), custom_call_target="tpu_custom_call" | custom-call | flops 4089446400 | bytes 7987200 | tf_op jit(solution)/shard_map/first/pallas_call | solution.py:129
  88.7 1.6 %collective-permute-done.14 = bf16[4,104,1600]{2,1,0:T(8,128)(2,1)S(1)} collective-permute-done((bf16[4,104,1600]{2,1,0:T(8,128)(2,1)S(1)}, bf16[4,104,1600]{2,1,0:T(8,128)(2,1)S(1)}, u32[]{:S(2)}, u32[]{:S(2)}) %collective-permute-start.14) | collective-permute-done | bytes 1331232 | tf_op jit(solution)/shard_map/ppermute | solution.py:25
  90.3 0.0 collective-permute-done.15
  90.3 2.5 %collective-permute-start.23 = (bf16[4,104,1600]{2,1,0:T(8,128)(2,1)S(1)}, bf16[4,104,1600]{2,1,0:T(8,128)(2,1)S(1)}, u32[]{:S(2)}, u32[]{:S(2)}) collective-permute-start(bf16[4,104,1600]{2,1,0:T(8,128)(2,1)S(1)} %collective-permute-done.14), channel_id=1, source_target_pairs={{0,32},{32,0},{1,33},{33,1},{2,34},{34,2},{3,35},{35,3},{4,36},{36... | collective-permute-start | bytes 3993608 | tf_op jit(solution)/shard_map/ppermute | solution.py:29
  92.8 0.0 collective-permute-start.24
  92.8 0.1 slice.6
  92.9 0.1 slice.7
  93.0 1.3 %collective-permute-start.19 = (bf16[2,104,1600]{2,1,0:T(8,128)(2,1)S(1)}, bf16[2,104,1600]{2,1,0:T(8,128)(2,1)S(1)}, u32[]{:S(2)}, u32[]{:S(2)}) collective-permute-start(bf16[2,104,1600]{2,1,0:T(8,128)(2,1)S(1)} %slice.6), channel_id=1, source_target_pairs={{0,4},{1,5},{2,6},{3,7},{4,8},{5,9},{6,10},{7,11},{8,12},{9,13},{1... | collective-permute-start | bytes 1996808 | tf_op jit(solution)/shard_map/ppermute | solution.py:25
  94.3 0.0 collective-permute-done.22
  94.3 1.5 %collective-permute-start.20 = (bf16[2,104,1600]{2,1,0:T(8,128)(2,1)S(1)}, bf16[2,104,1600]{2,1,0:T(8,128)(2,1)S(1)}, u32[]{:S(2)}, u32[]{:S(2)}) collective-permute-start(bf16[2,104,1600]{2,1,0:T(8,128)(2,1)S(1)} %slice.7), channel_id=1, source_target_pairs={{0,28},{1,29},{2,30},{3,31},{4,0},{5,1},{6,2},{7,3},{8,4},{9,5},{1... | collective-permute-start | bytes 1996808 | tf_op jit(solution)/shard_map/ppermute | solution.py:25
  95.8 0.0 collective-permute-done.21
  95.9 3.9 %second.1.total_ref = f32[512,1600]{1,0:T(8,128)S(1)} custom-call(f32[512,1600]{1,0:T(8,128)S(1)} %first.1.total_ref, bf16[512,832]{1,0:T(8,128)(2,1)S(1)} %get-tuple-element.39.refs_0_, bf16[416,1600]{1,0:T(8,128)(2,1)S(1)} %bitcast.23, bf16[416,1600]{1,0:T(8,128)(2,1)S(1)} %bitcast.24, bf16[512,832]{1,0:T(8,128)(2,1)S(1)} %get-tuple-element.40.refs_3_, ...), custom_call_target="tpu_custom_call" | custom-call | flops 2726297600 | bytes 5324800 | tf_op jit(solution)/shard_map/second/pallas_call | solution.py:129
  99.8 4.6 %collective-permute-done.19 = bf16[2,104,1600]{2,1,0:T(8,128)(2,1)S(1)} collective-permute-done((bf16[2,104,1600]{2,1,0:T(8,128)(2,1)S(1)}, bf16[2,104,1600]{2,1,0:T(8,128)(2,1)S(1)}, u32[]{:S(2)}, u32[]{:S(2)}) %collective-permute-start.19) | collective-permute-done | bytes 665632 | tf_op jit(solution)/shard_map/ppermute | solution.py:25
  104.4 0.0 collective-permute-done.20
  104.4 1.3 %collective-permute-start.25 = (bf16[2,104,1600]{2,1,0:T(8,128)(2,1)S(1)}, bf16[2,104,1600]{2,1,0:T(8,128)(2,1)S(1)}, u32[]{:S(2)}, u32[]{:S(2)}) collective-permute-start(bf16[2,104,1600]{2,1,0:T(8,128)(2,1)S(1)} %collective-permute-done.19), channel_id=1, source_target_pairs={{0,32},{32,0},{1,33},{33,1},{2,34},{34,2},{3,35},{35,3},{4,36},{36... | collective-permute-start | bytes 1996808 | tf_op jit(solution)/shard_map/ppermute | solution.py:29
  105.7 0.0 collective-permute-start.26
  105.8 4.6 %more.1.total_ref = f32[1600,512]{1,0:T(8,128)S(1)} custom-call(f32[1600,512]{1,0:T(8,128)S(1)} %bitcast.25, f32[512,1600]{1,0:T(8,128)S(1)} %second.1.total_ref, bf16[512,1248]{1,0:T(8,128)(2,1)S(1)} %get-tuple-element.42.refs_0_, bf16[416,1600]{1,0:T(8,128)(2,1)S(1)} %bitcast.26, bf16[416,1600]{1,0:T(8,128)(2,1)S(1)} %bitcast.27, ...), custom_call_target="tpu_custom_call" | custom-call | flops 3407872000 | bytes 6656000 | tf_op jit(solution)/shard_map/more/pallas_call | solution.py:129
  110.4 2.1 %last.1 = f32[1600,512]{1,0:T(8,128)} custom-call(f32[1600,512]{1,0:T(8,128)S(1)} %more.1.total_ref, bf16[416,512]{1,0:T(8,128)(2,1)S(1)} %get-tuple-element.46.factor_ref, bf16[208,1600]{1,0:T(8,128)(2,1)S(1)} %bitcast.33, bf16[208,1600]{1,0:T(8,128)(2,1)S(1)} %bitcast.34), custom_call_target="tpu_custom_call" | custom-call | flops 681574400 | bytes 1331200 | tf_op jit(solution)/shard_map/last/pallas_call | solution.py:129
  (14 shorter events, 0.1 us)
Async XLA Ops:
  0.0 44.3 %collective-permute-start.7 = (bf16[1600,512]{1,0:T(8,128)(2,1)}, bf16[1600,512]{1,0:T(8,128)(2,1)}, u32[]{:S(2)}, u32[]{:S(2)}) collective-permute-start(bf16[1600,512]{1,0:T(8,128)(2,1)} %own_ref.1), channel_id=1, source_target_pairs={{0,64},{32,224},{64,128},{96,32},{128,192},{160,96},{192,0},{224,1... | collective-permute-start | bytes 4915208 | tf_op jit(solution)/shard_map/ppermute | solution.py:14
  4.3 40.5 %copy-start.1 = (bf16[1600,512]{1,0:T(8,128)(2,1)S(1)}, bf16[1600,512]{1,0:T(8,128)(2,1)}, u32[]{:S(2)}) copy-start(bf16[1600,512]{1,0:T(8,128)(2,1)} %own_ref.1) | copy-start | bytes 4915204
  4.3 9.9 %collective-permute-start.1 = (bf16[1,104,1600]{2,1,0:T(8,128)(2,1)S(1)}, bf16[1,104,1600]{2,1,0:T(8,128)(2,1)S(1)}, u32[]{:S(2)}, u32[]{:S(2)}) collective-permute-start(bf16[1,104,1600]{2,1,0:T(8,128)(2,1)S(1)} %pad.4), channel_id=1, source_target_pairs={{0,3},{1,0},{2,1},{3,2},{4,7},{5,4},{6,5},{7,6},{8,11},{9,8},{10,9... | collective-permute-start | bytes 998408 | tf_op jit(solution)/shard_map/ppermute | solution.py:25
  10.0 11.5 %collective-permute-start.2 = (bf16[1,104,1600]{2,1,0:T(8,128)(2,1)S(1)}, bf16[1,104,1600]{2,1,0:T(8,128)(2,1)S(1)}, u32[]{:S(2)}, u32[]{:S(2)}) collective-permute-start(bf16[1,104,1600]{2,1,0:T(8,128)(2,1)S(1)} %pad.4), channel_id=1, source_target_pairs={{0,2},{1,3},{2,0},{3,1},{4,6},{5,7},{6,4},{7,5},{8,10},{9,11},{10,... | collective-permute-start | bytes 998408 | tf_op jit(solution)/shard_map/ppermute | solution.py:25
  10.0 13.2 %collective-permute-start = (bf16[1,104,1600]{2,1,0:T(8,128)(2,1)S(1)}, bf16[1,104,1600]{2,1,0:T(8,128)(2,1)S(1)}, u32[]{:S(2)}, u32[]{:S(2)}) collective-permute-start(bf16[1,104,1600]{2,1,0:T(8,128)(2,1)S(1)} %pad.4), channel_id=1, source_target_pairs={{0,1},{1,2},{2,3},{3,0},{4,5},{5,6},{6,7},{7,4},{8,9},{9,10},{10,1... | collective-permute-start | bytes 998408 | tf_op jit(solution)/shard_map/ppermute | solution.py:25
  23.5 22.3 %copy-start.2 = (bf16[4,104,1600]{2,1,0:T(8,128)(2,1)}, bf16[4,104,1600]{2,1,0:T(8,128)(2,1)S(1)}, u32[]{:S(2)}) copy-start(bf16[4,104,1600]{2,1,0:T(8,128)(2,1)S(1)} %pad_maximum_fusion) | copy-start | bytes 3993604
  23.5 22.3 %collective-permute-start.3 = (bf16[4,104,1600]{2,1,0:T(8,128)(2,1)S(1)}, bf16[4,104,1600]{2,1,0:T(8,128)(2,1)}, u32[]{:S(2)}, u32[]{:S(2)}) collective-permute-start(bf16[4,104,1600]{2,1,0:T(8,128)(2,1)S(1)} %pad_maximum_fusion), channel_id=1, source_target_pairs={{0,4},{1,5},{2,6},{3,7},{4,8},{5,9},{6,10},{7,11},{8,12},{9,13},{1... | collective-permute-start | bytes 3993608 | tf_op jit(solution)/shard_map/ppermute | solution.py:25
  24.9 21.0 %collective-permute-start.5 = (bf16[4,104,1600]{2,1,0:T(8,128)(2,1)S(1)}, bf16[4,104,1600]{2,1,0:T(8,128)(2,1)}, u32[]{:S(2)}, u32[]{:S(2)}) collective-permute-start(bf16[4,104,1600]{2,1,0:T(8,128)(2,1)S(1)} %pad_maximum_fusion), channel_id=1, source_target_pairs={{0,28},{1,29},{2,30},{3,31},{4,0},{5,1},{6,2},{7,3},{8,4},{9,5},{1... | collective-permute-start | bytes 3993608 | tf_op jit(solution)/shard_map/ppermute | solution.py:25
  26.4 13.0 %collective-permute-start.8 = (bf16[1,104,1600]{2,1,0:T(8,128)(2,1)S(1)}, bf16[1,104,1600]{2,1,0:T(8,128)(2,1)S(1)}, u32[]{:S(2)}, u32[]{:S(2)}) collective-permute-start(bf16[1,104,1600]{2,1,0:T(8,128)(2,1)S(1)} %collective-permute-done.1), channel_id=1, source_target_pairs={{32,60},{33,61},{34,62},{35,63},{36,32},{37,33},{38,34},{39,35},{4... | collective-permute-start | bytes 998408 | tf_op jit(solution)/shard_map/ppermute | solution.py:25
  30.9 13.4 %collective-permute-start.9 = (bf16[1,104,1600]{2,1,0:T(8,128)(2,1)S(1)}, bf16[1,104,1600]{2,1,0:T(8,128)(2,1)S(1)}, u32[]{:S(2)}, u32[]{:S(2)}) collective-permute-start(bf16[1,104,1600]{2,1,0:T(8,128)(2,1)S(1)} %collective-permute-done.2), channel_id=1, source_target_pairs={{32,36},{33,37},{34,38},{35,39},{36,40},{37,41},{38,42},{39,43},{4... | collective-permute-start | bytes 998408 | tf_op jit(solution)/shard_map/ppermute | solution.py:25
  44.3 1.5 %copy-start.4 = (bf16[1,104,1600]{2,1,0:T(8,128)(2,1)}, bf16[1,104,1600]{2,1,0:T(8,128)(2,1)S(1)}, u32[]{:S(2)}) copy-start(bf16[1,104,1600]{2,1,0:T(8,128)(2,1)S(1)} %collective-permute-done.9) | copy-start | bytes 998404
  44.3 26.8 %collective-permute-start.11 = (bf16[1600,512]{1,0:T(8,128)(2,1)}, bf16[1600,512]{1,0:T(8,128)(2,1)}, u32[]{:S(2)}, u32[]{:S(2)}) collective-permute-start(bf16[1600,512]{1,0:T(8,128)(2,1)} %collective-permute-done.7.near_ref), channel_id=1, source_target_pairs={{0,64},{32,224},{64,128},{96,32},{128,192},{160,96},{192,0},{224,1... | collective-permute-start | bytes 4915208 | tf_op jit(solution)/shard_map/ppermute | solution.py:14
  44.8 26.2 %collective-permute-start.10 = (bf16[1600,512]{1,0:T(8,128)(2,1)S(1)}, bf16[1600,512]{1,0:T(8,128)(2,1)}, u32[]{:S(2)}, u32[]{:S(2)}) collective-permute-start(bf16[1600,512]{1,0:T(8,128)(2,1)S(1)} %copy-done.1), channel_id=1, source_target_pairs={{0,192},{32,96},{64,0},{96,160},{128,64},{160,224},{192,128},{224,... | collective-permute-start | bytes 4915208 | tf_op jit(solution)/shard_map/ppermute | solution.py:14
  45.8 24.6 %collective-permute-start.4 = (bf16[4,104,1600]{2,1,0:T(8,128)(2,1)}, bf16[4,104,1600]{2,1,0:T(8,128)(2,1)S(1)}, u32[]{:S(2)}, u32[]{:S(2)}) collective-permute-start(bf16[4,104,1600]{2,1,0:T(8,128)(2,1)} %collective-permute-done.3), channel_id=1, source_target_pairs={{0,4},{1,5},{2,6},{3,7},{4,8},{5,9},{6,10},{7,11},{8,12},{9,13},{1... | collective-permute-start | bytes 3993608 | tf_op jit(solution)/shard_map/ppermute | solution.py:25
  45.9 25.1 %collective-permute-start.6 = (bf16[4,104,1600]{2,1,0:T(8,128)(2,1)}, bf16[4,104,1600]{2,1,0:T(8,128)(2,1)}, u32[]{:S(2)}, u32[]{:S(2)}) collective-permute-start(bf16[4,104,1600]{2,1,0:T(8,128)(2,1)} %collective-permute-done.5), channel_id=1, source_target_pairs={{0,28},{1,29},{2,30},{3,31},{4,0},{5,1},{6,2},{7,3},{8,4},{9,5},{1... | collective-permute-start | bytes 3993608 | tf_op jit(solution)/shard_map/ppermute | solution.py:25
  47.7 12.1 %collective-permute-start.12 = (bf16[1,104,1600]{2,1,0:T(8,128)(2,1)S(1)}, bf16[1,104,1600]{2,1,0:T(8,128)(2,1)}, u32[]{:S(2)}, u32[]{:S(2)}) collective-permute-start(bf16[1,104,1600]{2,1,0:T(8,128)(2,1)S(1)} %collective-permute-done.8), channel_id=1, source_target_pairs={{32,60},{33,61},{34,62},{35,63},{36,32},{37,33},{38,34},{39,35},{4... | collective-permute-start | bytes 998408 | tf_op jit(solution)/shard_map/ppermute | solution.py:25
  49.6 19.6 %copy-start.3 = (bf16[4,104,1600]{2,1,0:T(8,128)(2,1)S(1)}, bf16[4,104,1600]{2,1,0:T(8,128)(2,1)}, u32[]{:S(2)}) copy-start(bf16[4,104,1600]{2,1,0:T(8,128)(2,1)} %copy-done.2) | copy-start | bytes 3993604
  59.8 9.4 %collective-permute-start.13 = (bf16[1,104,1600]{2,1,0:T(8,128)(2,1)}, bf16[1,104,1600]{2,1,0:T(8,128)(2,1)S(1)}, u32[]{:S(2)}, u32[]{:S(2)}) collective-permute-start(bf16[1,104,1600]{2,1,0:T(8,128)(2,1)} %copy-done.4), channel_id=1, source_target_pairs={{32,36},{33,37},{34,38},{35,39},{36,40},{37,41},{38,42},{39,43},{4... | collective-permute-start | bytes 998408 | tf_op jit(solution)/shard_map/ppermute | solution.py:25
  69.3 5.0 %collective-permute-start.16 = (bf16[4,104,1600]{2,1,0:T(8,128)(2,1)S(1)}, bf16[4,104,1600]{2,1,0:T(8,128)(2,1)S(1)}, u32[]{:S(2)}, u32[]{:S(2)}) collective-permute-start(bf16[4,104,1600]{2,1,0:T(8,128)(2,1)S(1)} %copy-done.3), channel_id=1, source_target_pairs={{0,32},{32,0},{1,33},{33,1},{2,34},{34,2},{3,35},{35,3},{4,36},{36... | collective-permute-start | bytes 3993608 | tf_op jit(solution)/shard_map/ppermute | solution.py:29
  70.3 6.2 %collective-permute-start.17 = (bf16[4,104,1600]{2,1,0:T(8,128)(2,1)}, bf16[4,104,1600]{2,1,0:T(8,128)(2,1)S(1)}, u32[]{:S(2)}, u32[]{:S(2)}) collective-permute-start(bf16[4,104,1600]{2,1,0:T(8,128)(2,1)} %collective-permute-done.3), channel_id=1, source_target_pairs={{0,32},{32,0},{1,33},{33,1},{2,34},{34,2},{3,35},{35,3},{4,36},{36... | collective-permute-start | bytes 3993608 | tf_op jit(solution)/shard_map/ppermute | solution.py:29
  70.9 11.1 %collective-permute-start.18 = (bf16[4,104,1600]{2,1,0:T(8,128)(2,1)}, bf16[4,104,1600]{2,1,0:T(8,128)(2,1)S(1)}, u32[]{:S(2)}, u32[]{:S(2)}) collective-permute-start(bf16[4,104,1600]{2,1,0:T(8,128)(2,1)} %collective-permute-done.5), channel_id=1, source_target_pairs={{0,32},{32,0},{1,33},{33,1},{2,34},{34,2},{3,35},{35,3},{4,36},{36... | collective-permute-start | bytes 3993608 | tf_op jit(solution)/shard_map/ppermute | solution.py:29
  71.4 18.9 %collective-permute-start.14 = (bf16[4,104,1600]{2,1,0:T(8,128)(2,1)S(1)}, bf16[4,104,1600]{2,1,0:T(8,128)(2,1)S(1)}, u32[]{:S(2)}, u32[]{:S(2)}) collective-permute-start(bf16[4,104,1600]{2,1,0:T(8,128)(2,1)S(1)} %get-tuple-element.48), channel_id=1, source_target_pairs={{0,4},{1,5},{2,6},{3,7},{4,8},{5,9},{6,10},{7,11},{8,12},{9,13},{1... | collective-permute-start | bytes 3993608 | tf_op jit(solution)/shard_map/ppermute | solution.py:25
  72.8 17.5 %collective-permute-start.15 = (bf16[4,104,1600]{2,1,0:T(8,128)(2,1)S(1)}, bf16[4,104,1600]{2,1,0:T(8,128)(2,1)S(1)}, u32[]{:S(2)}, u32[]{:S(2)}) collective-permute-start(bf16[4,104,1600]{2,1,0:T(8,128)(2,1)S(1)} %get-tuple-element.47), channel_id=1, source_target_pairs={{0,28},{1,29},{2,30},{3,31},{4,0},{5,1},{6,2},{7,3},{8,4},{9,5},{1... | collective-permute-start | bytes 3993608 | tf_op jit(solution)/shard_map/ppermute | solution.py:25
  74.3 20.0 %collective-permute-start.22 = (bf16[4,104,1600]{2,1,0:T(8,128)(2,1)S(1)}, bf16[4,104,1600]{2,1,0:T(8,128)(2,1)S(1)}, u32[]{:S(2)}, u32[]{:S(2)}) collective-permute-start(bf16[4,104,1600]{2,1,0:T(8,128)(2,1)S(1)} %get-tuple-element.47), channel_id=1, source_target_pairs={{0,32},{32,0},{1,33},{33,1},{2,34},{34,2},{3,35},{35,3},{4,36},{36... | collective-permute-start | bytes 3993608 | tf_op jit(solution)/shard_map/ppermute | solution.py:29
  76.5 19.4 %collective-permute-start.21 = (bf16[4,104,1600]{2,1,0:T(8,128)(2,1)S(1)}, bf16[4,104,1600]{2,1,0:T(8,128)(2,1)S(1)}, u32[]{:S(2)}, u32[]{:S(2)}) collective-permute-start(bf16[4,104,1600]{2,1,0:T(8,128)(2,1)S(1)} %collective-permute-done.4), channel_id=1, source_target_pairs={{0,32},{32,0},{1,33},{33,1},{2,34},{34,2},{3,35},{35,3},{4,36},{36... | collective-permute-start | bytes 3993608 | tf_op jit(solution)/shard_map/ppermute | solution.py:29
  90.3 15.5 %collective-permute-start.23 = (bf16[4,104,1600]{2,1,0:T(8,128)(2,1)S(1)}, bf16[4,104,1600]{2,1,0:T(8,128)(2,1)S(1)}, u32[]{:S(2)}, u32[]{:S(2)}) collective-permute-start(bf16[4,104,1600]{2,1,0:T(8,128)(2,1)S(1)} %collective-permute-done.14), channel_id=1, source_target_pairs={{0,32},{32,0},{1,33},{33,1},{2,34},{34,2},{3,35},{35,3},{4,36},{36... | collective-permute-start | bytes 3993608 | tf_op jit(solution)/shard_map/ppermute | solution.py:29
  92.8 12.9 %collective-permute-start.24 = (bf16[4,104,1600]{2,1,0:T(8,128)(2,1)S(1)}, bf16[4,104,1600]{2,1,0:T(8,128)(2,1)S(1)}, u32[]{:S(2)}, u32[]{:S(2)}) collective-permute-start(bf16[4,104,1600]{2,1,0:T(8,128)(2,1)S(1)} %collective-permute-done.15), channel_id=1, source_target_pairs={{0,32},{32,0},{1,33},{33,1},{2,34},{34,2},{3,35},{35,3},{4,36},{36... | collective-permute-start | bytes 3993608 | tf_op jit(solution)/shard_map/ppermute | solution.py:29
  93.0 11.4 %collective-permute-start.19 = (bf16[2,104,1600]{2,1,0:T(8,128)(2,1)S(1)}, bf16[2,104,1600]{2,1,0:T(8,128)(2,1)S(1)}, u32[]{:S(2)}, u32[]{:S(2)}) collective-permute-start(bf16[2,104,1600]{2,1,0:T(8,128)(2,1)S(1)} %slice.6), channel_id=1, source_target_pairs={{0,4},{1,5},{2,6},{3,7},{4,8},{5,9},{6,10},{7,11},{8,12},{9,13},{1... | collective-permute-start | bytes 1996808 | tf_op jit(solution)/shard_map/ppermute | solution.py:25
  94.3 10.1 %collective-permute-start.20 = (bf16[2,104,1600]{2,1,0:T(8,128)(2,1)S(1)}, bf16[2,104,1600]{2,1,0:T(8,128)(2,1)S(1)}, u32[]{:S(2)}, u32[]{:S(2)}) collective-permute-start(bf16[2,104,1600]{2,1,0:T(8,128)(2,1)S(1)} %slice.7), channel_id=1, source_target_pairs={{0,28},{1,29},{2,30},{3,31},{4,0},{5,1},{6,2},{7,3},{8,4},{9,5},{1... | collective-permute-start | bytes 1996808 | tf_op jit(solution)/shard_map/ppermute | solution.py:25
  95.9 9.9 %copy-start = (f32[512,1600]{0,1:T(8,128)S(1)}, f32[512,1600]{0,1:T(8,128)}, u32[]{:S(2)}) copy-start(f32[512,1600]{0,1:T(8,128)} %param.3) | copy-start | bytes 9830404
  104.4 6.0 %collective-permute-start.25 = (bf16[2,104,1600]{2,1,0:T(8,128)(2,1)S(1)}, bf16[2,104,1600]{2,1,0:T(8,128)(2,1)S(1)}, u32[]{:S(2)}, u32[]{:S(2)}) collective-permute-start(bf16[2,104,1600]{2,1,0:T(8,128)(2,1)S(1)} %collective-permute-done.19), channel_id=1, source_target_pairs={{0,32},{32,0},{1,33},{33,1},{2,34},{34,2},{3,35},{35,3},{4,36},{36... | collective-permute-start | bytes 1996808 | tf_op jit(solution)/shard_map/ppermute | solution.py:29
  105.7 4.7 %collective-permute-start.26 = (bf16[2,104,1600]{2,1,0:T(8,128)(2,1)S(1)}, bf16[2,104,1600]{2,1,0:T(8,128)(2,1)S(1)}, u32[]{:S(2)}, u32[]{:S(2)}) collective-permute-start(bf16[2,104,1600]{2,1,0:T(8,128)(2,1)S(1)} %collective-permute-done.20), channel_id=1, source_target_pairs={{0,32},{32,0},{1,33},{33,1},{2,34},{34,2},{3,35},{35,3},{4,36},{36... | collective-permute-start | bytes 1996808 | tf_op jit(solution)/shard_map/ppermute | solution.py:29

commit v10 on v9

--- a/solution.py
+++ b/solution.py
@@ -29,9 +29,8 @@
     return lax.ppermute(array, "col", [(0, 1), (1, 0)])
 
 
-def padded(blocks, rows):
-    parts = blocks.reshape(-1, rows, blocks.shape[-1])
-    return jnp.pad(parts, ((0, 0), (0, -rows % 8), (0, 0)))
+def packed(*blocks):
+    return jnp.concatenate([jnp.pad(block, ((0, 0), (0, -block.shape[1] % 8), (0, 0))) for block in blocks])
 
 
 def ladder(block, height, amplitudes, rows, residual):
@@ -40,28 +39,29 @@
     near = along_row(amplitudes, rows, 1, -1)
     a1 = travel(block, *along)
     b1 = travel(block, *back)
-    a2 = travel(block, (0, 2), (2, 0))
-    pack = jnp.concatenate([block, a1, b1, a2])
+    a2 = travel(a1, *along)
+    pack = packed(block, a1, b1, a2)
     b2 = travel(b1, None, back[1])
     a3 = travel(a2, None, along[1])
     own, near, b2, a3 = lax.optimization_barrier((amplitudes, near, b2, a3))
     other = along_row(own, rows, -1, 1)
     b3 = travel(b2, None, back[1])
     a4 = travel(a3, None, along[1])
-    far = along_row(near, rows, 1, -1)
-    rest = jnp.concatenate([b2, a3, b3, a4])
+    near_again, b3 = lax.optimization_barrier((near, b3))
+    far = along_row(near_again, rows, 1, -1)
+    rest = lax.optimization_barrier(packed(b2, a3, b3, a4))
     u1, d1 = travel(pack, *up), travel(pack, *down)
     u2, d2 = travel(u1, *up), travel(d1, down[0], None)
-    u2, d2, other, far = lax.optimization_barrier((u2, d2, other, far))
+    u2, d2, other = lax.optimization_barrier((u2, d2, other))
     first = lax.axis_index("col") == 0
     kept = jnp.where(first, d2, rest)
     u3, d3 = travel(jnp.where(first, u2, rest), *up), travel(kept, *down)
     theirs = [swap(piece) for piece in (pack, u1, d1, u2, kept)]
     own_factors, their_factors = arrange(amplitudes, near, other, far, rows, height)
-    total = first_products([own_factors[0], their_factors[0]], [[pack, u1, d1], theirs[:3]])
+    total = first_products([own_factors[0], their_factors[0]], [[pack, u1], theirs[:2]])
     u3, d3, total = lax.optimization_barrier((u3, d3, total))
     u4, d4 = travel(u3[:2], *up), travel(d3[2:], *down)
-    total = second_products(total, [own_factors[1], their_factors[1]], [[u2, kept], theirs[3:]])
+    total = second_products(total, [own_factors[1], their_factors[1]], [[d1, u2, kept], theirs[2:]])
     theirs = [swap(u3), swap(d3)]
     u4, d4, total = lax.optimization_barrier((u4, d4, total))
     total = more_products(residual, total, [own_factors[2], their_factors[2]], [[u3, d3, u4, d4], theirs])
@@ -69,7 +69,7 @@
 
 
 def arrange(own, near, other, far, rows, height):
-    cuts = [(0, blocks) for blocks in (12, 8, 12)] + [(1, blocks) for blocks in (12, 8, 8, 4)]
+    cuts = [(0, blocks) for blocks in (8, 12, 12)] + [(1, blocks) for blocks in (8, 12, 8, 4)]
     width = own.shape[1]
     count = own.shape[0] // height
     full = height + -height % 8
@@ -205,8 +205,7 @@
 
     def per_device(residual_in, integrals, amplitudes):
         height = integrals.shape[1]
-        block = padded(integrals.T, height)
-        return ladder(block, height, amplitudes, rows, residual_in.T).T
+        return ladder(integrals.T[None], height, amplitudes, rows, residual_in.T).T
 
     placed = (P(("col", "depth"), "row"), P("row", ("col", "depth")), P("row", ("col", "depth")))
     return jax.shard_map(

time: 113 us -> 111 us (0.982)
  waiting for transfers between devices: 47.6 us -> 36.3 us
  starting transfers between devices: 38.3 us -> 47.7 us
  local copies, waits for them, and re-layouts: 3.24 us -> 0.11 us
  other arithmetic: 0.61 us -> 2.58 us
    ppermute x15, waiting for transfers between devices: 47.6 us -> 28.3 us  [travel(): return lax.ppermute(array, ('col', 'depth'), pairs)]
    ppermute x9, starting transfers between devices: 7.02 us -> 15.4 us  [swap(): return lax.ppermute(array, 'col', [(0, 1), (1, 0)])]
    ppermute x3, waiting for transfers between devices: 0.01 us -> 7.99 us  [along_row(): return lax.ppermute(array, ('row', 'col'), pairs)]
    unnamed x13 -> x2, local copies, waits for them, and re-layouts: 2.09 us -> 0.01 us
    concatenate x1 -> x2, other arithmetic: 0.23 us -> 2.31 us  [packed(): jnp.concatenate([jnp.pad(block, ((0, 0), (0, -block.shape[1] % 8), (0, 0)...]
  transfers between devices with their start and end apart: 27 -> 27, of which waited for: 9 -> 10; matrix products, arithmetic and copies ran while one was open for 3% -> 2% of each run, Pallas kernels for 18% -> 19%
where the time goes in v10:
time: 111 us
  starting transfers between devices  47.7 us (43%)
  waiting for transfers between devices  36.3 us (33%)
  Pallas kernels  23.6 us (21%)
  other arithmetic  2.58 us (2%)
    ppermute x15, waiting for transfers between devices, travel(): return lax.ppermute(array, ('col', 'depth'), pairs)  28.3 us
    ppermute x15, starting transfers between devices, travel(): return lax.ppermute(array, ('col', 'depth'), pairs)  27.1 us
    pallas_call x4, Pallas kernels, multiply(): pl.pallas_call(body, out_shape=jax.ShapeDtypeStruct(shape, jnp.float32),...  18.4 us
    ppermute x9, starting transfers between devices, swap(): return lax.ppermute(array, 'col', [(0, 1), (1, 0)])  15.4 us
    ppermute x3, waiting for transfers between devices, along_row(): return lax.ppermute(array, ('row', 'col'), pairs)  7.99 us
    pallas_call x1, Pallas kernels, arrange(): pl.pallas_call(kernel, out_shape=[jax.ShapeDtypeStruct(shape, own.dtype)...  5.27 us
    ppermute x3, starting transfers between devices, along_row(): return lax.ppermute(array, ('row', 'col'), pairs)  5.25 us
    concatenate x2, other arithmetic, packed(): jnp.concatenate([jnp.pad(block, ((0, 0), (0, -block.shape[1] % 8), (0, 0)...  2.31 us
  transfers between devices with their start and end apart: 27, of which 10 were waited for; matrix products, arithmetic and copies ran while one was open for 2% of the time, Pallas kernels for 19%

profile of v10, /device:TPU:1, one launch (start us, length us, event | category | flops | bytes accessed | tf_op | source)
XLA Modules:
  0.0 110.7 jit_solution(11780186275461517129)
XLA Ops:
  0.0 2.5 %collective-permute-start = (bf16[1,100,1600]{2,1,0:T(8,128)(2,1)}, bf16[1,100,1600]{2,1,0:T(8,128)(2,1)S(1)}, u32[]{:S(2)}, u32[]{:S(2)}) collective-permute-start(bf16[1,100,1600]{2,1,0:T(8,128)(2,1)} %bitcast.40), channel_id=1, source_target_pairs={{0,1},{1,2},{2,3},{3,0},{4,5},{5,6},{6,7},{7,4},{8,9},{9,10},{10,1... | collective-permute-start | bytes 960008 | tf_op jit(solution)/shard_map/ppermute | solution.py:25
  2.5 2.5 %collective-permute-start.7 = (bf16[1600,512]{1,0:T(8,128)(2,1)}, bf16[1600,512]{1,0:T(8,128)(2,1)}, u32[]{:S(2)}, u32[]{:S(2)}) collective-permute-start(bf16[1600,512]{1,0:T(8,128)(2,1)} %own_ref.1), channel_id=1, source_target_pairs={{0,64},{32,224},{64,128},{96,32},{128,192},{160,96},{192,0},{224,1... | collective-permute-start | bytes 4915208 | tf_op jit(solution)/shard_map/ppermute | solution.py:14
  4.9 3.9 %collective-permute-start.1 = (bf16[1,100,1600]{2,1,0:T(8,128)(2,1)}, bf16[1,100,1600]{2,1,0:T(8,128)(2,1)S(1)}, u32[]{:S(2)}, u32[]{:S(2)}) collective-permute-start(bf16[1,100,1600]{2,1,0:T(8,128)(2,1)} %bitcast.41), channel_id=1, source_target_pairs={{0,3},{1,0},{2,1},{3,2},{4,7},{5,4},{6,5},{7,6},{8,11},{9,8},{10,9... | collective-permute-start | bytes 960008 | tf_op jit(solution)/shard_map/ppermute | solution.py:25
  8.9 2.8 %collective-permute-done = bf16[1,100,1600]{2,1,0:T(8,128)(2,1)S(1)} collective-permute-done((bf16[1,100,1600]{2,1,0:T(8,128)(2,1)}, bf16[1,100,1600]{2,1,0:T(8,128)(2,1)S(1)}, u32[]{:S(2)}, u32[]{:S(2)}) %collective-permute-start) | collective-permute-done | bytes 320032 | tf_op jit(solution)/shard_map/ppermute | solution.py:25
  11.7 0.0 collective-permute-start.2
  11.7 1.7 %collective-permute-done.1 = bf16[1,100,1600]{2,1,0:T(8,128)(2,1)S(1)} collective-permute-done((bf16[1,100,1600]{2,1,0:T(8,128)(2,1)}, bf16[1,100,1600]{2,1,0:T(8,128)(2,1)S(1)}, u32[]{:S(2)}, u32[]{:S(2)}) %collective-permute-start.1) | collective-permute-done | bytes 320032 | tf_op jit(solution)/shard_map/ppermute | solution.py:25
  13.4 6.0 %collective-permute-done.2 = bf16[1,100,1600]{2,1,0:T(8,128)(2,1)S(1)} collective-permute-done((bf16[1,100,1600]{2,1,0:T(8,128)(2,1)S(1)}, bf16[1,100,1600]{2,1,0:T(8,128)(2,1)S(1)}, u32[]{:S(2)}, u32[]{:S(2)}) %collective-permute-start.2) | collective-permute-done | bytes 320032 | tf_op jit(solution)/shard_map/ppermute | solution.py:25
  19.4 1.1 %fusion.12 = bf16[4,104,1600]{2,1,0:T(8,128)(2,1)S(1)} fusion(bf16[1,100,1600]{2,1,0:T(8,128)(2,1)S(1)} %collective-permute-done.2, bf16[1,100,1600]{2,1,0:T(8,128)(2,1)S(1)} %collective-permute-done.1, bf16[1,100,1600]{2,1,0:T(8,128)(2,1)S(1)} %collective-permute-done, bf16[1,100,1600]{2,1,0:T(8,128)(2,1)} %bitcast.42), kind=kLoop, calls=%fused_computation.18 | loop fusion | flops 13312000 | bytes 2611200 | tf_op jit(solution)/shard_map/concatenate | solution.py:33
  20.5 1.4 %collective-permute-start.3 = (bf16[4,104,1600]{2,1,0:T(8,128)(2,1)S(1)}, bf16[4,104,1600]{2,1,0:T(8,128)(2,1)}, u32[]{:S(2)}, u32[]{:S(2)}) collective-permute-start(bf16[4,104,1600]{2,1,0:T(8,128)(2,1)S(1)} %fusion.12), channel_id=1, source_target_pairs={{0,4},{1,5},{2,6},{3,7},{4,8},{5,9},{6,10},{7,11},{8,12},{9,13},{1... | collective-permute-start | bytes 3993608 | tf_op jit(solution)/shard_map/ppermute | solution.py:25
  21.9 1.5 %collective-permute-start.5 = (bf16[4,104,1600]{2,1,0:T(8,128)(2,1)S(1)}, bf16[4,104,1600]{2,1,0:T(8,128)(2,1)}, u32[]{:S(2)}, u32[]{:S(2)}) collective-permute-start(bf16[4,104,1600]{2,1,0:T(8,128)(2,1)S(1)} %fusion.12), channel_id=1, source_target_pairs={{0,28},{1,29},{2,30},{3,31},{4,0},{5,1},{6,2},{7,3},{8,4},{9,5},{1... | collective-permute-start | bytes 3993608 | tf_op jit(solution)/shard_map/ppermute | solution.py:25
  23.4 2.1 %collective-permute-start.8 = (bf16[1,100,1600]{2,1,0:T(8,128)(2,1)S(1)}, bf16[1,100,1600]{2,1,0:T(8,128)(2,1)S(1)}, u32[]{:S(2)}, u32[]{:S(2)}) collective-permute-start(bf16[1,100,1600]{2,1,0:T(8,128)(2,1)S(1)} %collective-permute-done.1), channel_id=1, source_target_pairs={{32,60},{33,61},{34,62},{35,63},{36,32},{37,33},{38,34},{39,35},{4... | collective-permute-start | bytes 960008 | tf_op jit(solution)/shard_map/ppermute | solution.py:25
  25.6 3.1 %collective-permute-start.9 = (bf16[1,100,1600]{2,1,0:T(8,128)(2,1)S(1)}, bf16[1,100,1600]{2,1,0:T(8,128)(2,1)S(1)}, u32[]{:S(2)}, u32[]{:S(2)}) collective-permute-start(bf16[1,100,1600]{2,1,0:T(8,128)(2,1)S(1)} %collective-permute-done.2), channel_id=1, source_target_pairs={{32,36},{33,37},{34,38},{35,39},{36,40},{37,41},{38,42},{39,43},{4... | collective-permute-start | bytes 960008 | tf_op jit(solution)/shard_map/ppermute | solution.py:25
  28.7 6.9 %collective-permute-done.8 = bf16[1,100,1600]{2,1,0:T(8,128)(2,1)S(1)} collective-permute-done((bf16[1,100,1600]{2,1,0:T(8,128)(2,1)S(1)}, bf16[1,100,1600]{2,1,0:T(8,128)(2,1)S(1)}, u32[]{:S(2)}, u32[]{:S(2)}) %collective-permute-start.8) | collective-permute-done | bytes 320032 | tf_op jit(solution)/shard_map/ppermute | solution.py:25
  35.6 3.4 %collective-permute-done.9 = bf16[1,100,1600]{2,1,0:T(8,128)(2,1)S(1)} collective-permute-done((bf16[1,100,1600]{2,1,0:T(8,128)(2,1)S(1)}, bf16[1,100,1600]{2,1,0:T(8,128)(2,1)S(1)}, u32[]{:S(2)}, u32[]{:S(2)}) %collective-permute-start.9) | collective-permute-done | bytes 320032 | tf_op jit(solution)/shard_map/ppermute | solution.py:25
  39.0 0.0 collective-permute-done.7.near_ref
  39.0 1.2 %collective-permute-start.10 = (bf16[1600,512]{1,0:T(8,128)(2,1)}, bf16[1600,512]{1,0:T(8,128)(2,1)}, u32[]{:S(2)}, u32[]{:S(2)}) collective-permute-start(bf16[1600,512]{1,0:T(8,128)(2,1)} %own_ref.1), channel_id=1, source_target_pairs={{0,192},{32,96},{64,0},{96,160},{128,64},{160,224},{192,128},{224,... | collective-permute-start | bytes 4915208 | tf_op jit(solution)/shard_map/ppermute | solution.py:14
  40.2 0.0 collective-permute-done.3
  40.2 0.0 collective-permute-start.4
  40.2 0.0 collective-permute-done.5
  40.2 1.7 %collective-permute-start.6 = (bf16[4,104,1600]{2,1,0:T(8,128)(2,1)}, bf16[4,104,1600]{2,1,0:T(8,128)(2,1)}, u32[]{:S(2)}, u32[]{:S(2)}) collective-permute-start(bf16[4,104,1600]{2,1,0:T(8,128)(2,1)} %collective-permute-done.5), channel_id=1, source_target_pairs={{0,28},{1,29},{2,30},{3,31},{4,0},{5,1},{6,2},{7,3},{8,4},{9,5},{1... | collective-permute-start | bytes 3993608 | tf_op jit(solution)/shard_map/ppermute | solution.py:25
  42.0 1.9 %collective-permute-start.11 = (bf16[1,100,1600]{2,1,0:T(8,128)(2,1)S(1)}, bf16[1,100,1600]{2,1,0:T(8,128)(2,1)}, u32[]{:S(2)}, u32[]{:S(2)}) collective-permute-start(bf16[1,100,1600]{2,1,0:T(8,128)(2,1)S(1)} %collective-permute-done.8), channel_id=1, source_target_pairs={{32,60},{33,61},{34,62},{35,63},{36,32},{37,33},{38,34},{39,35},{4... | collective-permute-start | bytes 960008 | tf_op jit(solution)/shard_map/ppermute | solution.py:25
  43.9 3.4 %collective-permute-start.12 = (bf16[1,100,1600]{2,1,0:T(8,128)(2,1)S(1)}, bf16[1,100,1600]{2,1,0:T(8,128)(2,1)}, u32[]{:S(2)}, u32[]{:S(2)}) collective-permute-start(bf16[1,100,1600]{2,1,0:T(8,128)(2,1)S(1)} %collective-permute-done.9), channel_id=1, source_target_pairs={{32,36},{33,37},{34,38},{35,39},{36,40},{37,41},{38,42},{39,43},{4... | collective-permute-start | bytes 960008 | tf_op jit(solution)/shard_map/ppermute | solution.py:25
  47.3 2.8 %collective-permute-done.11 = bf16[1,100,1600]{2,1,0:T(8,128)(2,1)} collective-permute-done((bf16[1,100,1600]{2,1,0:T(8,128)(2,1)S(1)}, bf16[1,100,1600]{2,1,0:T(8,128)(2,1)}, u32[]{:S(2)}, u32[]{:S(2)}) %collective-permute-start.11) | collective-permute-done | bytes 320032 | tf_op jit(solution)/shard_map/ppermute | solution.py:25
  50.1 3.8 %collective-permute-start.16 = (bf16[4,104,1600]{2,1,0:T(8,128)(2,1)S(1)}, bf16[4,104,1600]{2,1,0:T(8,128)(2,1)S(1)}, u32[]{:S(2)}, u32[]{:S(2)}) collective-permute-start(bf16[4,104,1600]{2,1,0:T(8,128)(2,1)S(1)} %fusion.12), channel_id=1, source_target_pairs={{0,32},{32,0},{1,33},{33,1},{2,34},{34,2},{3,35},{35,3},{4,36},{36... | collective-permute-start | bytes 3993608 | tf_op jit(solution)/shard_map/ppermute | solution.py:29
  53.9 2.4 %collective-permute-done.12 = bf16[1,100,1600]{2,1,0:T(8,128)(2,1)} collective-permute-done((bf16[1,100,1600]{2,1,0:T(8,128)(2,1)S(1)}, bf16[1,100,1600]{2,1,0:T(8,128)(2,1)}, u32[]{:S(2)}, u32[]{:S(2)}) %collective-permute-start.12) | collective-permute-done | bytes 320032 | tf_op jit(solution)/shard_map/ppermute | solution.py:25
  56.3 1.6 %collective-permute-start.15 = (bf16[1600,512]{1,0:T(8,128)(2,1)}, bf16[1600,512]{1,0:T(8,128)(2,1)S(1)}, u32[]{:S(2)}, u32[]{:S(2)}) collective-permute-start(bf16[1600,512]{1,0:T(8,128)(2,1)} %collective-permute-done.7.near_ref), channel_id=1, source_target_pairs={{0,64},{32,224},{64,128},{96,32},{128,192},{160,96},{192,0},{224,1... | collective-permute-start | bytes 4915208 | tf_op jit(solution)/shard_map/ppermute | solution.py:14
  57.9 4.8 %collective-permute-done.10.other_ref = bf16[1600,512]{1,0:T(8,128)(2,1)} collective-permute-done((bf16[1600,512]{1,0:T(8,128)(2,1)}, bf16[1600,512]{1,0:T(8,128)(2,1)}, u32[]{:S(2)}, u32[]{:S(2)}) %collective-permute-start.10) | collective-permute-done | bytes 1638432 | tf_op jit(solution)/shard_map/ppermute | solution.py:14
  62.7 0.0 collective-permute-start.17
  62.7 1.2 %fusion.15 = bf16[4,104,1600]{2,1,0:T(8,128)(2,1)S(1)} fusion(bf16[1,100,1600]{2,1,0:T(8,128)(2,1)} %collective-permute-done.12, bf16[1,100,1600]{2,1,0:T(8,128)(2,1)} %collective-permute-done.11, bf16[1,100,1600]{2,1,0:T(8,128)(2,1)S(1)} %collective-permute-done.9, bf16[1,100,1600]{2,1,0:T(8,128)(2,1)S(1)} %collective-permute-done.8), kind=kLoop, calls=%fused_computation.21 | loop fusion | flops 13312000 | bytes 2611200 | tf_op jit(solution)/shard_map/concatenate | solution.py:33
  63.9 0.0 collective-permute-done.4
  63.9 0.0 collective-permute-done.6
  63.9 0.3 broadcast_select_fusion
  64.2 0.3 collective-permute-start.13
  64.5 2.5 %collective-permute-start.14 = (bf16[4,104,1600]{2,1,0:T(8,128)(2,1)S(1)}, bf16[4,104,1600]{2,1,0:T(8,128)(2,1)S(1)}, u32[]{:S(2)}, u32[]{:S(2)}) collective-permute-start(bf16[4,104,1600]{2,1,0:T(8,128)(2,1)S(1)} %get-tuple-element.49), channel_id=1, source_target_pairs={{0,28},{1,29},{2,30},{3,31},{4,0},{5,1},{6,2},{7,3},{8,4},{9,5},{1... | collective-permute-start | bytes 3993608 | tf_op jit(solution)/shard_map/ppermute | solution.py:25
  67.0 0.0 collective-permute-done.16
  67.0 6.6 %collective-permute-start.20 = (bf16[4,104,1600]{2,1,0:T(8,128)(2,1)}, bf16[4,104,1600]{2,1,0:T(8,128)(2,1)S(1)}, u32[]{:S(2)}, u32[]{:S(2)}) collective-permute-start(bf16[4,104,1600]{2,1,0:T(8,128)(2,1)} %collective-permute-done.5), channel_id=1, source_target_pairs={{0,32},{32,0},{1,33},{33,1},{2,34},{34,2},{3,35},{35,3},{4,36},{36... | collective-permute-start | bytes 3993608 | tf_op jit(solution)/shard_map/ppermute | solution.py:29
  73.6 0.0 collective-permute-done.17
  73.6 0.1 collective-permute-start.22
  73.7 3.1 %collective-permute-done.15.far_ref = bf16[1600,512]{1,0:T(8,128)(2,1)S(1)} collective-permute-done((bf16[1600,512]{1,0:T(8,128)(2,1)}, bf16[1600,512]{1,0:T(8,128)(2,1)S(1)}, u32[]{:S(2)}, u32[]{:S(2)}) %collective-permute-start.15) | collective-permute-done | bytes 1638432 | tf_op jit(solution)/shard_map/ppermute | solution.py:14
  76.8 1.8 %collective-permute-start.21 = (bf16[4,104,1600]{2,1,0:T(8,128)(2,1)S(1)}, bf16[4,104,1600]{2,1,0:T(8,128)(2,1)S(1)}, u32[]{:S(2)}, u32[]{:S(2)}) collective-permute-start(bf16[4,104,1600]{2,1,0:T(8,128)(2,1)S(1)} %collective-permute-done.4), channel_id=1, source_target_pairs={{0,32},{32,0},{1,33},{33,1},{2,34},{34,2},{3,35},{35,3},{4,36},{36... | collective-permute-start | bytes 3993608 | tf_op jit(solution)/shard_map/ppermute | solution.py:29
  78.6 5.3 %arrange.1 = (bf16[512,832]{1,0:T(8,128)(2,1)S(1)}, bf16[512,1248]{1,0:T(8,128)(2,1)S(1)}, bf16[512,1248]{1,0:T(8,128)(2,1)S(1)}, bf16[512,832]{1,0:T(8,128)(2,1...) custom-call(bf16[1600,512]{1,0:T(8,128)(2,1)} %own_ref.1, ...), custom_call_target="tpu_custom_call" | custom-call | bytes 13107200 | tf_op jit(solution)/shard_map/arrange/pallas_call | solution.py:103
  83.9 5.2 %first.1.total_ref = f32[512,1600]{1,0:T(8,128)S(1)} custom-call(bf16[512,832]{1,0:T(8,128)(2,1)S(1)} %get-tuple-element.36.refs_0_, bf16[416,1600]{1,0:T(8,128)(2,1)S(1)} %bitcast.24, bf16[416,1600]{1,0:T(8,128)(2,1)} %bitcast.5.refs_2_, bf16[512,832]{1,0:T(8,128)(2,1)S(1)} %get-tuple-element.37.refs_3_, bf16[416,1600]{1,0:T(8,128)(2,1)S(1)} %bitcast.29, ...), custom_call_target="tpu_custom_call" | custom-call | flops 2726297600 | bytes 5324800 | tf_op jit(solution)/shard_map/first/pallas_call | solution.py:129
  89.1 0.0 collective-permute-done.13
  89.2 0.0 collective-permute-done.14
  89.2 0.8 collective-permute-start.23
  89.9 0.0 collective-permute-start.24
  89.9 0.1 slice.6
  90.0 0.1 slice.7
  90.0 0.0 collective-permute-done.20
  90.1 0.3 collective-permute-start.18
  90.3 0.0 collective-permute-done.22
  90.3 2.5 %collective-permute-start.19 = (bf16[2,104,1600]{2,1,0:T(8,128)(2,1)S(1)}, bf16[2,104,1600]{2,1,0:T(8,128)(2,1)S(1)}, u32[]{:S(2)}, u32[]{:S(2)}) collective-permute-start(bf16[2,104,1600]{2,1,0:T(8,128)(2,1)S(1)} %slice.7), channel_id=1, source_target_pairs={{0,28},{1,29},{2,30},{3,31},{4,0},{5,1},{6,2},{7,3},{8,4},{9,5},{1... | collective-permute-start | bytes 1996808 | tf_op jit(solution)/shard_map/ppermute | solution.py:25
  92.8 0.0 collective-permute-done.21
  92.8 6.4 %second.1.total_ref = f32[512,1600]{1,0:T(8,128)S(1)} custom-call(f32[512,1600]{1,0:T(8,128)S(1)} %first.1.total_ref, bf16[512,1248]{1,0:T(8,128)(2,1)S(1)} %get-tuple-element.41.refs_0_, bf16[416,1600]{1,0:T(8,128)(2,1)} %bitcast.8.refs_1_, bf16[416,1600]{1,0:T(8,128)(2,1)S(1)} %bitcast.23, bf16[416,1600]{1,0:T(8,128)(2,1)S(1)} %bitcast.25, ...), custom_call_target="tpu_custom_call" | custom-call | flops 4089446400 | bytes 7987200 | tf_op jit(solution)/shard_map/second/pallas_call | solution.py:129
  99.2 2.2 %collective-permute-done.18 = bf16[2,104,1600]{2,1,0:T(8,128)(2,1)S(1)} collective-permute-done((bf16[2,104,1600]{2,1,0:T(8,128)(2,1)S(1)}, bf16[2,104,1600]{2,1,0:T(8,128)(2,1)S(1)}, u32[]{:S(2)}, u32[]{:S(2)}) %collective-permute-start.18) | collective-permute-done | bytes 665632 | tf_op jit(solution)/shard_map/ppermute | solution.py:25
  101.5 0.0 collective-permute-done.19
  101.5 2.3 %collective-permute-start.25 = (bf16[2,104,1600]{2,1,0:T(8,128)(2,1)S(1)}, bf16[2,104,1600]{2,1,0:T(8,128)(2,1)S(1)}, u32[]{:S(2)}, u32[]{:S(2)}) collective-permute-start(bf16[2,104,1600]{2,1,0:T(8,128)(2,1)S(1)} %collective-permute-done.18), channel_id=1, source_target_pairs={{0,32},{32,0},{1,33},{33,1},{2,34},{34,2},{3,35},{35,3},{4,36},{36... | collective-permute-start | bytes 1996808 | tf_op jit(solution)/shard_map/ppermute | solution.py:29
  103.7 0.0 collective-permute-start.26
  103.8 0.0 collective-permute-done.23
  103.8 0.0 collective-permute-done.24
  103.8 4.6 %more.1.total_ref = f32[1600,512]{1,0:T(8,128)S(1)} custom-call(f32[1600,512]{1,0:T(8,128)S(1)} %bitcast.26, f32[512,1600]{1,0:T(8,128)S(1)} %second.1.total_ref, bf16[512,1248]{1,0:T(8,128)(2,1)S(1)} %get-tuple-element.44.refs_0_, bf16[416,1600]{1,0:T(8,128)(2,1)S(1)} %bitcast.27, bf16[416,1600]{1,0:T(8,128)(2,1)S(1)} %bitcast.28, ...), custom_call_target="tpu_custom_call" | custom-call | flops 3407872000 | bytes 6656000 | tf_op jit(solution)/shard_map/more/pallas_call | solution.py:129
  108.4 0.0 collective-permute-done.25
  108.4 0.0 collective-permute-done.26
  108.4 2.1 %last.1 = f32[1600,512]{1,0:T(8,128)} custom-call(f32[1600,512]{1,0:T(8,128)S(1)} %more.1.total_ref, bf16[416,512]{1,0:T(8,128)(2,1)S(1)} %get-tuple-element.48.factor_ref, bf16[208,1600]{1,0:T(8,128)(2,1)S(1)} %bitcast.36, bf16[208,1600]{1,0:T(8,128)(2,1)S(1)} %bitcast.37), custom_call_target="tpu_custom_call" | custom-call | flops 681574400 | bytes 1331200 | tf_op jit(solution)/shard_map/last/pallas_call | solution.py:129
  (2 shorter events, 0.0 us)
Async XLA Ops:
  0.0 11.7 %collective-permute-start = (bf16[1,100,1600]{2,1,0:T(8,128)(2,1)}, bf16[1,100,1600]{2,1,0:T(8,128)(2,1)S(1)}, u32[]{:S(2)}, u32[]{:S(2)}) collective-permute-start(bf16[1,100,1600]{2,1,0:T(8,128)(2,1)} %bitcast.40), channel_id=1, source_target_pairs={{0,1},{1,2},{2,3},{3,0},{4,5},{5,6},{6,7},{7,4},{8,9},{9,10},{10,1... | collective-permute-start | bytes 960008 | tf_op jit(solution)/shard_map/ppermute | solution.py:25
  2.5 36.5 %collective-permute-start.7 = (bf16[1600,512]{1,0:T(8,128)(2,1)}, bf16[1600,512]{1,0:T(8,128)(2,1)}, u32[]{:S(2)}, u32[]{:S(2)}) collective-permute-start(bf16[1600,512]{1,0:T(8,128)(2,1)} %own_ref.1), channel_id=1, source_target_pairs={{0,64},{32,224},{64,128},{96,32},{128,192},{160,96},{192,0},{224,1... | collective-permute-start | bytes 4915208 | tf_op jit(solution)/shard_map/ppermute | solution.py:14
  4.9 8.5 %collective-permute-start.1 = (bf16[1,100,1600]{2,1,0:T(8,128)(2,1)}, bf16[1,100,1600]{2,1,0:T(8,128)(2,1)S(1)}, u32[]{:S(2)}, u32[]{:S(2)}) collective-permute-start(bf16[1,100,1600]{2,1,0:T(8,128)(2,1)} %bitcast.41), channel_id=1, source_target_pairs={{0,3},{1,0},{2,1},{3,2},{4,7},{5,4},{6,5},{7,6},{8,11},{9,8},{10,9... | collective-permute-start | bytes 960008 | tf_op jit(solution)/shard_map/ppermute | solution.py:25
  11.7 7.7 %collective-permute-start.2 = (bf16[1,100,1600]{2,1,0:T(8,128)(2,1)S(1)}, bf16[1,100,1600]{2,1,0:T(8,128)(2,1)S(1)}, u32[]{:S(2)}, u32[]{:S(2)}) collective-permute-start(bf16[1,100,1600]{2,1,0:T(8,128)(2,1)S(1)} %collective-permute-done), channel_id=1, source_target_pairs={{0,1},{1,2},{2,3},{3,0},{4,5},{5,6},{6,7},{7,4},{8,9},{9,10},{10,1... | collective-permute-start | bytes 960008 | tf_op jit(solution)/shard_map/ppermute | solution.py:25
  20.5 19.7 %collective-permute-start.3 = (bf16[4,104,1600]{2,1,0:T(8,128)(2,1)S(1)}, bf16[4,104,1600]{2,1,0:T(8,128)(2,1)}, u32[]{:S(2)}, u32[]{:S(2)}) collective-permute-start(bf16[4,104,1600]{2,1,0:T(8,128)(2,1)S(1)} %fusion.12), channel_id=1, source_target_pairs={{0,4},{1,5},{2,6},{3,7},{4,8},{5,9},{6,10},{7,11},{8,12},{9,13},{1... | collective-permute-start | bytes 3993608 | tf_op jit(solution)/shard_map/ppermute | solution.py:25
  21.9 18.3 %collective-permute-start.5 = (bf16[4,104,1600]{2,1,0:T(8,128)(2,1)S(1)}, bf16[4,104,1600]{2,1,0:T(8,128)(2,1)}, u32[]{:S(2)}, u32[]{:S(2)}) collective-permute-start(bf16[4,104,1600]{2,1,0:T(8,128)(2,1)S(1)} %fusion.12), channel_id=1, source_target_pairs={{0,28},{1,29},{2,30},{3,31},{4,0},{5,1},{6,2},{7,3},{8,4},{9,5},{1... | collective-permute-start | bytes 3993608 | tf_op jit(solution)/shard_map/ppermute | solution.py:25
  23.4 12.2 %collective-permute-start.8 = (bf16[1,100,1600]{2,1,0:T(8,128)(2,1)S(1)}, bf16[1,100,1600]{2,1,0:T(8,128)(2,1)S(1)}, u32[]{:S(2)}, u32[]{:S(2)}) collective-permute-start(bf16[1,100,1600]{2,1,0:T(8,128)(2,1)S(1)} %collective-permute-done.1), channel_id=1, source_target_pairs={{32,60},{33,61},{34,62},{35,63},{36,32},{37,33},{38,34},{39,35},{4... | collective-permute-start | bytes 960008 | tf_op jit(solution)/shard_map/ppermute | solution.py:25
  25.6 13.4 %collective-permute-start.9 = (bf16[1,100,1600]{2,1,0:T(8,128)(2,1)S(1)}, bf16[1,100,1600]{2,1,0:T(8,128)(2,1)S(1)}, u32[]{:S(2)}, u32[]{:S(2)}) collective-permute-start(bf16[1,100,1600]{2,1,0:T(8,128)(2,1)S(1)} %collective-permute-done.2), channel_id=1, source_target_pairs={{32,36},{33,37},{34,38},{35,39},{36,40},{37,41},{38,42},{39,43},{4... | collective-permute-start | bytes 960008 | tf_op jit(solution)/shard_map/ppermute | solution.py:25
  39.0 23.7 %collective-permute-start.10 = (bf16[1600,512]{1,0:T(8,128)(2,1)}, bf16[1600,512]{1,0:T(8,128)(2,1)}, u32[]{:S(2)}, u32[]{:S(2)}) collective-permute-start(bf16[1600,512]{1,0:T(8,128)(2,1)} %own_ref.1), channel_id=1, source_target_pairs={{0,192},{32,96},{64,0},{96,160},{128,64},{160,224},{192,128},{224,... | collective-permute-start | bytes 4915208 | tf_op jit(solution)/shard_map/ppermute | solution.py:14
  40.2 23.7 %collective-permute-start.4 = (bf16[4,104,1600]{2,1,0:T(8,128)(2,1)}, bf16[4,104,1600]{2,1,0:T(8,128)(2,1)S(1)}, u32[]{:S(2)}, u32[]{:S(2)}) collective-permute-start(bf16[4,104,1600]{2,1,0:T(8,128)(2,1)} %collective-permute-done.3), channel_id=1, source_target_pairs={{0,4},{1,5},{2,6},{3,7},{4,8},{5,9},{6,10},{7,11},{8,12},{9,13},{1... | collective-permute-start | bytes 3993608 | tf_op jit(solution)/shard_map/ppermute | solution.py:25
  40.2 23.7 %collective-permute-start.6 = (bf16[4,104,1600]{2,1,0:T(8,128)(2,1)}, bf16[4,104,1600]{2,1,0:T(8,128)(2,1)}, u32[]{:S(2)}, u32[]{:S(2)}) collective-permute-start(bf16[4,104,1600]{2,1,0:T(8,128)(2,1)} %collective-permute-done.5), channel_id=1, source_target_pairs={{0,28},{1,29},{2,30},{3,31},{4,0},{5,1},{6,2},{7,3},{8,4},{9,5},{1... | collective-permute-start | bytes 3993608 | tf_op jit(solution)/shard_map/ppermute | solution.py:25
  42.0 8.1 %collective-permute-start.11 = (bf16[1,100,1600]{2,1,0:T(8,128)(2,1)S(1)}, bf16[1,100,1600]{2,1,0:T(8,128)(2,1)}, u32[]{:S(2)}, u32[]{:S(2)}) collective-permute-start(bf16[1,100,1600]{2,1,0:T(8,128)(2,1)S(1)} %collective-permute-done.8), channel_id=1, source_target_pairs={{32,60},{33,61},{34,62},{35,63},{36,32},{37,33},{38,34},{39,35},{4... | collective-permute-start | bytes 960008 | tf_op jit(solution)/shard_map/ppermute | solution.py:25
  43.9 12.4 %collective-permute-start.12 = (bf16[1,100,1600]{2,1,0:T(8,128)(2,1)S(1)}, bf16[1,100,1600]{2,1,0:T(8,128)(2,1)}, u32[]{:S(2)}, u32[]{:S(2)}) collective-permute-start(bf16[1,100,1600]{2,1,0:T(8,128)(2,1)S(1)} %collective-permute-done.9), channel_id=1, source_target_pairs={{32,36},{33,37},{34,38},{35,39},{36,40},{37,41},{38,42},{39,43},{4... | collective-permute-start | bytes 960008 | tf_op jit(solution)/shard_map/ppermute | solution.py:25
  50.1 16.9 %collective-permute-start.16 = (bf16[4,104,1600]{2,1,0:T(8,128)(2,1)S(1)}, bf16[4,104,1600]{2,1,0:T(8,128)(2,1)S(1)}, u32[]{:S(2)}, u32[]{:S(2)}) collective-permute-start(bf16[4,104,1600]{2,1,0:T(8,128)(2,1)S(1)} %fusion.12), channel_id=1, source_target_pairs={{0,32},{32,0},{1,33},{33,1},{2,34},{34,2},{3,35},{35,3},{4,36},{36... | collective-permute-start | bytes 3993608 | tf_op jit(solution)/shard_map/ppermute | solution.py:29
  56.3 20.5 %collective-permute-start.15 = (bf16[1600,512]{1,0:T(8,128)(2,1)}, bf16[1600,512]{1,0:T(8,128)(2,1)S(1)}, u32[]{:S(2)}, u32[]{:S(2)}) collective-permute-start(bf16[1600,512]{1,0:T(8,128)(2,1)} %collective-permute-done.7.near_ref), channel_id=1, source_target_pairs={{0,64},{32,224},{64,128},{96,32},{128,192},{160,96},{192,0},{224,1... | collective-permute-start | bytes 4915208 | tf_op jit(solution)/shard_map/ppermute | solution.py:14
  62.7 10.8 %collective-permute-start.17 = (bf16[4,104,1600]{2,1,0:T(8,128)(2,1)}, bf16[4,104,1600]{2,1,0:T(8,128)(2,1)S(1)}, u32[]{:S(2)}, u32[]{:S(2)}) collective-permute-start(bf16[4,104,1600]{2,1,0:T(8,128)(2,1)} %collective-permute-done.3), channel_id=1, source_target_pairs={{0,32},{32,0},{1,33},{33,1},{2,34},{34,2},{3,35},{35,3},{4,36},{36... | collective-permute-start | bytes 3993608 | tf_op jit(solution)/shard_map/ppermute | solution.py:29
  64.2 24.9 %collective-permute-start.13 = (bf16[4,104,1600]{2,1,0:T(8,128)(2,1)S(1)}, bf16[4,104,1600]{2,1,0:T(8,128)(2,1)S(1)}, u32[]{:S(2)}, u32[]{:S(2)}) collective-permute-start(bf16[4,104,1600]{2,1,0:T(8,128)(2,1)S(1)} %get-tuple-element.50), channel_id=1, source_target_pairs={{0,4},{1,5},{2,6},{3,7},{4,8},{5,9},{6,10},{7,11},{8,12},{9,13},{1... | collective-permute-start | bytes 3993608 | tf_op jit(solution)/shard_map/ppermute | solution.py:25
  64.5 24.7 %collective-permute-start.14 = (bf16[4,104,1600]{2,1,0:T(8,128)(2,1)S(1)}, bf16[4,104,1600]{2,1,0:T(8,128)(2,1)S(1)}, u32[]{:S(2)}, u32[]{:S(2)}) collective-permute-start(bf16[4,104,1600]{2,1,0:T(8,128)(2,1)S(1)} %get-tuple-element.49), channel_id=1, source_target_pairs={{0,28},{1,29},{2,30},{3,31},{4,0},{5,1},{6,2},{7,3},{8,4},{9,5},{1... | collective-permute-start | bytes 3993608 | tf_op jit(solution)/shard_map/ppermute | solution.py:25
  67.0 23.1 %collective-permute-start.20 = (bf16[4,104,1600]{2,1,0:T(8,128)(2,1)}, bf16[4,104,1600]{2,1,0:T(8,128)(2,1)S(1)}, u32[]{:S(2)}, u32[]{:S(2)}) collective-permute-start(bf16[4,104,1600]{2,1,0:T(8,128)(2,1)} %collective-permute-done.5), channel_id=1, source_target_pairs={{0,32},{32,0},{1,33},{33,1},{2,34},{34,2},{3,35},{35,3},{4,36},{36... | collective-permute-start | bytes 3993608 | tf_op jit(solution)/shard_map/ppermute | solution.py:29
  73.6 16.8 %collective-permute-start.22 = (bf16[4,104,1600]{2,1,0:T(8,128)(2,1)S(1)}, bf16[4,104,1600]{2,1,0:T(8,128)(2,1)S(1)}, u32[]{:S(2)}, u32[]{:S(2)}) collective-permute-start(bf16[4,104,1600]{2,1,0:T(8,128)(2,1)S(1)} %get-tuple-element.49), channel_id=1, source_target_pairs={{0,32},{32,0},{1,33},{33,1},{2,34},{34,2},{3,35},{35,3},{4,36},{36... | collective-permute-start | bytes 3993608 | tf_op jit(solution)/shard_map/ppermute | solution.py:29
  76.8 16.0 %collective-permute-start.21 = (bf16[4,104,1600]{2,1,0:T(8,128)(2,1)S(1)}, bf16[4,104,1600]{2,1,0:T(8,128)(2,1)S(1)}, u32[]{:S(2)}, u32[]{:S(2)}) collective-permute-start(bf16[4,104,1600]{2,1,0:T(8,128)(2,1)S(1)} %collective-permute-done.4), channel_id=1, source_target_pairs={{0,32},{32,0},{1,33},{33,1},{2,34},{34,2},{3,35},{35,3},{4,36},{36... | collective-permute-start | bytes 3993608 | tf_op jit(solution)/shard_map/ppermute | solution.py:29
  89.2 14.6 %collective-permute-start.23 = (bf16[4,104,1600]{2,1,0:T(8,128)(2,1)S(1)}, bf16[4,104,1600]{2,1,0:T(8,128)(2,1)S(1)}, u32[]{:S(2)}, u32[]{:S(2)}) collective-permute-start(bf16[4,104,1600]{2,1,0:T(8,128)(2,1)S(1)} %collective-permute-done.13), channel_id=1, source_target_pairs={{0,32},{32,0},{1,33},{33,1},{2,34},{34,2},{3,35},{35,3},{4,36},{36... | collective-permute-start | bytes 3993608 | tf_op jit(solution)/shard_map/ppermute | solution.py:29
  89.9 13.8 %collective-permute-start.24 = (bf16[4,104,1600]{2,1,0:T(8,128)(2,1)S(1)}, bf16[4,104,1600]{2,1,0:T(8,128)(2,1)S(1)}, u32[]{:S(2)}, u32[]{:S(2)}) collective-permute-start(bf16[4,104,1600]{2,1,0:T(8,128)(2,1)S(1)} %collective-permute-done.14), channel_id=1, source_target_pairs={{0,32},{32,0},{1,33},{33,1},{2,34},{34,2},{3,35},{35,3},{4,36},{36... | collective-permute-start | bytes 3993608 | tf_op jit(solution)/shard_map/ppermute | solution.py:29
  90.1 11.4 %collective-permute-start.18 = (bf16[2,104,1600]{2,1,0:T(8,128)(2,1)S(1)}, bf16[2,104,1600]{2,1,0:T(8,128)(2,1)S(1)}, u32[]{:S(2)}, u32[]{:S(2)}) collective-permute-start(bf16[2,104,1600]{2,1,0:T(8,128)(2,1)S(1)} %slice.6), channel_id=1, source_target_pairs={{0,4},{1,5},{2,6},{3,7},{4,8},{5,9},{6,10},{7,11},{8,12},{9,13},{1... | collective-permute-start | bytes 1996808 | tf_op jit(solution)/shard_map/ppermute | solution.py:25
  90.3 11.2 %collective-permute-start.19 = (bf16[2,104,1600]{2,1,0:T(8,128)(2,1)S(1)}, bf16[2,104,1600]{2,1,0:T(8,128)(2,1)S(1)}, u32[]{:S(2)}, u32[]{:S(2)}) collective-permute-start(bf16[2,104,1600]{2,1,0:T(8,128)(2,1)S(1)} %slice.7), channel_id=1, source_target_pairs={{0,28},{1,29},{2,30},{3,31},{4,0},{5,1},{6,2},{7,3},{8,4},{9,5},{1... | collective-permute-start | bytes 1996808 | tf_op jit(solution)/shard_map/ppermute | solution.py:25
  92.8 10.9 %copy-start = (f32[512,1600]{0,1:T(8,128)S(1)}, f32[512,1600]{0,1:T(8,128)}, u32[]{:S(2)}) copy-start(f32[512,1600]{0,1:T(8,128)} %param.3) | copy-start | bytes 9830404
  101.5 6.9 %collective-permute-start.25 = (bf16[2,104,1600]{2,1,0:T(8,128)(2,1)S(1)}, bf16[2,104,1600]{2,1,0:T(8,128)(2,1)S(1)}, u32[]{:S(2)}, u32[]{:S(2)}) collective-permute-start(bf16[2,104,1600]{2,1,0:T(8,128)(2,1)S(1)} %collective-permute-done.18), channel_id=1, source_target_pairs={{0,32},{32,0},{1,33},{33,1},{2,34},{34,2},{3,35},{35,3},{4,36},{36... | collective-permute-start | bytes 1996808 | tf_op jit(solution)/shard_map/ppermute | solution.py:29
  103.7 4.7 %collective-permute-start.26 = (bf16[2,104,1600]{2,1,0:T(8,128)(2,1)S(1)}, bf16[2,104,1600]{2,1,0:T(8,128)(2,1)S(1)}, u32[]{:S(2)}, u32[]{:S(2)}) collective-permute-start(bf16[2,104,1600]{2,1,0:T(8,128)(2,1)S(1)} %collective-permute-done.19), channel_id=1, source_target_pairs={{0,32},{32,0},{1,33},{33,1},{2,34},{34,2},{3,35},{35,3},{4,36},{36... | collective-permute-start | bytes 1996808 | tf_op jit(solution)/shard_map/ppermute | solution.py:29

commit v11 on v10

--- a/solution.py
+++ b/solution.py
@@ -58,10 +58,11 @@
     u3, d3 = travel(jnp.where(first, u2, rest), *up), travel(kept, *down)
     theirs = [swap(piece) for piece in (pack, u1, d1, u2, kept)]
     own_factors, their_factors = arrange(amplitudes, near, other, far, rows, height)
-    total = first_products([own_factors[0], their_factors[0]], [[pack, u1], theirs[:2]])
+    theirs[:2] = lax.optimization_barrier(theirs[:2])
+    total = first_products([own_factors[0], their_factors[0]], [[pack], theirs[:1]])
     u3, d3, total = lax.optimization_barrier((u3, d3, total))
     u4, d4 = travel(u3[:2], *up), travel(d3[2:], *down)
-    total = second_products(total, [own_factors[1], their_factors[1]], [[d1, u2, kept], theirs[2:]])
+    total = second_products(total, [own_factors[1], their_factors[1]], [[u1, d1, u2, kept], theirs[1:]])
     theirs = [swap(u3), swap(d3)]
     u4, d4, total = lax.optimization_barrier((u4, d4, total))
     total = more_products(residual, total, [own_factors[2], their_factors[2]], [[u3, d3, u4, d4], theirs])
@@ -69,7 +70,7 @@
 
 
 def arrange(own, near, other, far, rows, height):
-    cuts = [(0, blocks) for blocks in (8, 12, 12)] + [(1, blocks) for blocks in (8, 12, 8, 4)]
+    cuts = [(0, blocks) for blocks in (4, 16, 12)] + [(1, blocks) for blocks in (4, 16, 8, 4)]
     width = own.shape[1]
     count = own.shape[0] // height
     full = height + -height % 8

time: 111 us -> 111 us (level)
  starting transfers between devices: 47.7 us -> 49.8 us
  waiting for transfers between devices: 36.3 us -> 34.6 us
    ppermute x9, starting transfers between devices: 15.4 us -> 17.1 us  [swap(): return lax.ppermute(array, 'col', [(0, 1), (1, 0)])]
    ppermute x3, waiting for transfers between devices: 7.99 us -> 6.42 us  [along_row(): return lax.ppermute(array, ('row', 'col'), pairs)]
  transfers between devices with their start and end apart: 27 -> 27, of which waited for: 10 -> 8; matrix products, arithmetic and copies ran while one was open for 2% -> 2% of each run, Pallas kernels for 19% -> 19%
where the time goes in v11:
time: 111 us
  starting transfers between devices  49.8 us (45%)
  waiting for transfers between devices  34.6 us (31%)
  Pallas kernels  23.2 us (21%)
  other arithmetic  2.66 us (2%)
    ppermute x15, waiting for transfers between devices, travel(): return lax.ppermute(array, ('col', 'depth'), pairs)  28.2 us
    ppermute x15, starting transfers between devices, travel(): return lax.ppermute(array, ('col', 'depth'), pairs)  27.2 us
    pallas_call x4, Pallas kernels, multiply(): pl.pallas_call(body, out_shape=jax.ShapeDtypeStruct(shape, jnp.float32),...  17.5 us
    ppermute x9, starting transfers between devices, swap(): return lax.ppermute(array, 'col', [(0, 1), (1, 0)])  17.1 us
    ppermute x3, waiting for transfers between devices, along_row(): return lax.ppermute(array, ('row', 'col'), pairs)  6.42 us
    pallas_call x1, Pallas kernels, arrange(): pl.pallas_call(kernel, out_shape=[jax.ShapeDtypeStruct(shape, own.dtype)...  5.76 us
    ppermute x3, starting transfers between devices, along_row(): return lax.ppermute(array, ('row', 'col'), pairs)  5.45 us
    concatenate x2, other arithmetic, packed(): jnp.concatenate([jnp.pad(block, ((0, 0), (0, -block.shape[1] % 8), (0, 0)...  2.32 us
  transfers between devices with their start and end apart: 27, of which 8 were waited for; matrix products, arithmetic and copies ran while one was open for 2% of the time, Pallas kernels for 19%

profile of v11, /device:TPU:1, one launch (start us, length us, event | category | flops | bytes accessed | tf_op | source)
XLA Modules:
  0.0 110.8 jit_solution(9809141400883722698)
XLA Ops:
  0.0 2.5 %collective-permute-start = (bf16[1,100,1600]{2,1,0:T(8,128)(2,1)}, bf16[1,100,1600]{2,1,0:T(8,128)(2,1)S(1)}, u32[]{:S(2)}, u32[]{:S(2)}) collective-permute-start(bf16[1,100,1600]{2,1,0:T(8,128)(2,1)} %bitcast.40), channel_id=1, source_target_pairs={{0,1},{1,2},{2,3},{3,0},{4,5},{5,6},{6,7},{7,4},{8,9},{9,10},{10,1... | collective-permute-start | bytes 960008 | tf_op jit(solution)/shard_map/ppermute | solution.py:25
  2.5 2.5 %collective-permute-start.7 = (bf16[1600,512]{1,0:T(8,128)(2,1)}, bf16[1600,512]{1,0:T(8,128)(2,1)}, u32[]{:S(2)}, u32[]{:S(2)}) collective-permute-start(bf16[1600,512]{1,0:T(8,128)(2,1)} %own_ref.1), channel_id=1, source_target_pairs={{0,64},{32,224},{64,128},{96,32},{128,192},{160,96},{192,0},{224,1... | collective-permute-start | bytes 4915208 | tf_op jit(solution)/shard_map/ppermute | solution.py:14
  4.9 3.9 %collective-permute-start.1 = (bf16[1,100,1600]{2,1,0:T(8,128)(2,1)}, bf16[1,100,1600]{2,1,0:T(8,128)(2,1)S(1)}, u32[]{:S(2)}, u32[]{:S(2)}) collective-permute-start(bf16[1,100,1600]{2,1,0:T(8,128)(2,1)} %bitcast.41), channel_id=1, source_target_pairs={{0,3},{1,0},{2,1},{3,2},{4,7},{5,4},{6,5},{7,6},{8,11},{9,8},{10,9... | collective-permute-start | bytes 960008 | tf_op jit(solution)/shard_map/ppermute | solution.py:25
  8.9 2.8 %collective-permute-done = bf16[1,100,1600]{2,1,0:T(8,128)(2,1)S(1)} collective-permute-done((bf16[1,100,1600]{2,1,0:T(8,128)(2,1)}, bf16[1,100,1600]{2,1,0:T(8,128)(2,1)S(1)}, u32[]{:S(2)}, u32[]{:S(2)}) %collective-permute-start) | collective-permute-done | bytes 320032 | tf_op jit(solution)/shard_map/ppermute | solution.py:25
  11.7 0.0 collective-permute-start.2
  11.7 1.7 %collective-permute-done.1 = bf16[1,100,1600]{2,1,0:T(8,128)(2,1)S(1)} collective-permute-done((bf16[1,100,1600]{2,1,0:T(8,128)(2,1)}, bf16[1,100,1600]{2,1,0:T(8,128)(2,1)S(1)}, u32[]{:S(2)}, u32[]{:S(2)}) %collective-permute-start.1) | collective-permute-done | bytes 320032 | tf_op jit(solution)/shard_map/ppermute | solution.py:25
  13.4 6.0 %collective-permute-done.2 = bf16[1,100,1600]{2,1,0:T(8,128)(2,1)S(1)} collective-permute-done((bf16[1,100,1600]{2,1,0:T(8,128)(2,1)S(1)}, bf16[1,100,1600]{2,1,0:T(8,128)(2,1)S(1)}, u32[]{:S(2)}, u32[]{:S(2)}) %collective-permute-start.2) | collective-permute-done | bytes 320032 | tf_op jit(solution)/shard_map/ppermute | solution.py:25
  19.4 1.1 %fusion.12 = bf16[4,104,1600]{2,1,0:T(8,128)(2,1)S(1)} fusion(bf16[1,100,1600]{2,1,0:T(8,128)(2,1)S(1)} %collective-permute-done.2, bf16[1,100,1600]{2,1,0:T(8,128)(2,1)S(1)} %collective-permute-done.1, bf16[1,100,1600]{2,1,0:T(8,128)(2,1)S(1)} %collective-permute-done, bf16[1,100,1600]{2,1,0:T(8,128)(2,1)} %bitcast.42), kind=kLoop, calls=%fused_computation.18 | loop fusion | flops 13312000 | bytes 2611200 | tf_op jit(solution)/shard_map/concatenate | solution.py:33
  20.5 1.4 %collective-permute-start.3 = (bf16[4,104,1600]{2,1,0:T(8,128)(2,1)S(1)}, bf16[4,104,1600]{2,1,0:T(8,128)(2,1)}, u32[]{:S(2)}, u32[]{:S(2)}) collective-permute-start(bf16[4,104,1600]{2,1,0:T(8,128)(2,1)S(1)} %fusion.12), channel_id=1, source_target_pairs={{0,4},{1,5},{2,6},{3,7},{4,8},{5,9},{6,10},{7,11},{8,12},{9,13},{1... | collective-permute-start | bytes 3993608 | tf_op jit(solution)/shard_map/ppermute | solution.py:25
  21.9 1.5 %collective-permute-start.5 = (bf16[4,104,1600]{2,1,0:T(8,128)(2,1)S(1)}, bf16[4,104,1600]{2,1,0:T(8,128)(2,1)}, u32[]{:S(2)}, u32[]{:S(2)}) collective-permute-start(bf16[4,104,1600]{2,1,0:T(8,128)(2,1)S(1)} %fusion.12), channel_id=1, source_target_pairs={{0,28},{1,29},{2,30},{3,31},{4,0},{5,1},{6,2},{7,3},{8,4},{9,5},{1... | collective-permute-start | bytes 3993608 | tf_op jit(solution)/shard_map/ppermute | solution.py:25
  23.4 2.1 %collective-permute-start.8 = (bf16[1,100,1600]{2,1,0:T(8,128)(2,1)S(1)}, bf16[1,100,1600]{2,1,0:T(8,128)(2,1)S(1)}, u32[]{:S(2)}, u32[]{:S(2)}) collective-permute-start(bf16[1,100,1600]{2,1,0:T(8,128)(2,1)S(1)} %collective-permute-done.1), channel_id=1, source_target_pairs={{32,60},{33,61},{34,62},{35,63},{36,32},{37,33},{38,34},{39,35},{4... | collective-permute-start | bytes 960008 | tf_op jit(solution)/shard_map/ppermute | solution.py:25
  25.6 3.1 %collective-permute-start.9 = (bf16[1,100,1600]{2,1,0:T(8,128)(2,1)S(1)}, bf16[1,100,1600]{2,1,0:T(8,128)(2,1)S(1)}, u32[]{:S(2)}, u32[]{:S(2)}) collective-permute-start(bf16[1,100,1600]{2,1,0:T(8,128)(2,1)S(1)} %collective-permute-done.2), channel_id=1, source_target_pairs={{32,36},{33,37},{34,38},{35,39},{36,40},{37,41},{38,42},{39,43},{4... | collective-permute-start | bytes 960008 | tf_op jit(solution)/shard_map/ppermute | solution.py:25
  28.7 6.9 %collective-permute-done.8 = bf16[1,100,1600]{2,1,0:T(8,128)(2,1)S(1)} collective-permute-done((bf16[1,100,1600]{2,1,0:T(8,128)(2,1)S(1)}, bf16[1,100,1600]{2,1,0:T(8,128)(2,1)S(1)}, u32[]{:S(2)}, u32[]{:S(2)}) %collective-permute-start.8) | collective-permute-done | bytes 320032 | tf_op jit(solution)/shard_map/ppermute | solution.py:25
  35.6 3.4 %collective-permute-done.9 = bf16[1,100,1600]{2,1,0:T(8,128)(2,1)S(1)} collective-permute-done((bf16[1,100,1600]{2,1,0:T(8,128)(2,1)S(1)}, bf16[1,100,1600]{2,1,0:T(8,128)(2,1)S(1)}, u32[]{:S(2)}, u32[]{:S(2)}) %collective-permute-start.9) | collective-permute-done | bytes 320032 | tf_op jit(solution)/shard_map/ppermute | solution.py:25
  39.0 0.0 collective-permute-done.7.near_ref
  39.0 1.2 %collective-permute-start.10 = (bf16[1600,512]{1,0:T(8,128)(2,1)}, bf16[1600,512]{1,0:T(8,128)(2,1)}, u32[]{:S(2)}, u32[]{:S(2)}) collective-permute-start(bf16[1600,512]{1,0:T(8,128)(2,1)} %own_ref.1), channel_id=1, source_target_pairs={{0,192},{32,96},{64,0},{96,160},{128,64},{160,224},{192,128},{224,... | collective-permute-start | bytes 4915208 | tf_op jit(solution)/shard_map/ppermute | solution.py:14
  40.2 0.0 collective-permute-done.3
  40.2 0.0 collective-permute-start.4
  40.2 0.0 collective-permute-done.5
  40.2 1.8 %collective-permute-start.6 = (bf16[4,104,1600]{2,1,0:T(8,128)(2,1)}, bf16[4,104,1600]{2,1,0:T(8,128)(2,1)}, u32[]{:S(2)}, u32[]{:S(2)}) collective-permute-start(bf16[4,104,1600]{2,1,0:T(8,128)(2,1)} %collective-permute-done.5), channel_id=1, source_target_pairs={{0,28},{1,29},{2,30},{3,31},{4,0},{5,1},{6,2},{7,3},{8,4},{9,5},{1... | collective-permute-start | bytes 3993608 | tf_op jit(solution)/shard_map/ppermute | solution.py:25
  42.1 1.9 %collective-permute-start.11 = (bf16[1,100,1600]{2,1,0:T(8,128)(2,1)S(1)}, bf16[1,100,1600]{2,1,0:T(8,128)(2,1)}, u32[]{:S(2)}, u32[]{:S(2)}) collective-permute-start(bf16[1,100,1600]{2,1,0:T(8,128)(2,1)S(1)} %collective-permute-done.8), channel_id=1, source_target_pairs={{32,60},{33,61},{34,62},{35,63},{36,32},{37,33},{38,34},{39,35},{4... | collective-permute-start | bytes 960008 | tf_op jit(solution)/shard_map/ppermute | solution.py:25
  44.0 3.4 %collective-permute-start.12 = (bf16[1,100,1600]{2,1,0:T(8,128)(2,1)S(1)}, bf16[1,100,1600]{2,1,0:T(8,128)(2,1)}, u32[]{:S(2)}, u32[]{:S(2)}) collective-permute-start(bf16[1,100,1600]{2,1,0:T(8,128)(2,1)S(1)} %collective-permute-done.9), channel_id=1, source_target_pairs={{32,36},{33,37},{34,38},{35,39},{36,40},{37,41},{38,42},{39,43},{4... | collective-permute-start | bytes 960008 | tf_op jit(solution)/shard_map/ppermute | solution.py:25
  47.3 2.8 %collective-permute-done.11 = bf16[1,100,1600]{2,1,0:T(8,128)(2,1)} collective-permute-done((bf16[1,100,1600]{2,1,0:T(8,128)(2,1)S(1)}, bf16[1,100,1600]{2,1,0:T(8,128)(2,1)}, u32[]{:S(2)}, u32[]{:S(2)}) %collective-permute-start.11) | collective-permute-done | bytes 320032 | tf_op jit(solution)/shard_map/ppermute | solution.py:25
  50.2 1.8 %collective-permute-start.15 = (bf16[1600,512]{1,0:T(8,128)(2,1)}, bf16[1600,512]{1,0:T(8,128)(2,1)}, u32[]{:S(2)}, u32[]{:S(2)}) collective-permute-start(bf16[1600,512]{1,0:T(8,128)(2,1)} %collective-permute-done.7.near_ref), channel_id=1, source_target_pairs={{0,64},{32,224},{64,128},{96,32},{128,192},{160,96},{192,0},{224,1... | collective-permute-start | bytes 4915208 | tf_op jit(solution)/shard_map/ppermute | solution.py:14
  51.9 4.6 %collective-permute-done.12 = bf16[1,100,1600]{2,1,0:T(8,128)(2,1)} collective-permute-done((bf16[1,100,1600]{2,1,0:T(8,128)(2,1)S(1)}, bf16[1,100,1600]{2,1,0:T(8,128)(2,1)}, u32[]{:S(2)}, u32[]{:S(2)}) %collective-permute-start.12) | collective-permute-done | bytes 320032 | tf_op jit(solution)/shard_map/ppermute | solution.py:25
  56.5 0.0 collective-permute-start.16
  56.5 6.4 %collective-permute-done.10.other_ref = bf16[1600,512]{1,0:T(8,128)(2,1)} collective-permute-done((bf16[1600,512]{1,0:T(8,128)(2,1)}, bf16[1600,512]{1,0:T(8,128)(2,1)}, u32[]{:S(2)}, u32[]{:S(2)}) %collective-permute-start.10) | collective-permute-done | bytes 1638432 | tf_op jit(solution)/shard_map/ppermute | solution.py:14
  62.9 0.0 collective-permute-start.17
  62.9 1.2 %fusion.15 = bf16[4,104,1600]{2,1,0:T(8,128)(2,1)S(1)} fusion(bf16[1,100,1600]{2,1,0:T(8,128)(2,1)} %collective-permute-done.12, bf16[1,100,1600]{2,1,0:T(8,128)(2,1)} %collective-permute-done.11, bf16[1,100,1600]{2,1,0:T(8,128)(2,1)S(1)} %collective-permute-done.9, bf16[1,100,1600]{2,1,0:T(8,128)(2,1)S(1)} %collective-permute-done.8), kind=kLoop, calls=%fused_computation.21 | loop fusion | flops 13312000 | bytes 2611200 | tf_op jit(solution)/shard_map/concatenate | solution.py:33
  64.1 0.0 collective-permute-done.4
  64.1 0.0 collective-permute-done.6
  64.1 0.3 broadcast_select_fusion
  64.5 0.8 collective-permute-start.13
  65.3 2.0 %collective-permute-start.14 = (bf16[4,104,1600]{2,1,0:T(8,128)(2,1)S(1)}, bf16[4,104,1600]{2,1,0:T(8,128)(2,1)S(1)}, u32[]{:S(2)}, u32[]{:S(2)}) collective-permute-start(bf16[4,104,1600]{2,1,0:T(8,128)(2,1)S(1)} %get-tuple-element.53), channel_id=1, source_target_pairs={{0,28},{1,29},{2,30},{3,31},{4,0},{5,1},{6,2},{7,3},{8,4},{9,5},{1... | collective-permute-start | bytes 3993608 | tf_op jit(solution)/shard_map/ppermute | solution.py:25
  67.3 0.0 collective-permute-done.16
  67.3 6.5 %collective-permute-start.20 = (bf16[4,104,1600]{2,1,0:T(8,128)(2,1)}, bf16[4,104,1600]{2,1,0:T(8,128)(2,1)S(1)}, u32[]{:S(2)}, u32[]{:S(2)}) collective-permute-start(bf16[4,104,1600]{2,1,0:T(8,128)(2,1)} %collective-permute-done.5), channel_id=1, source_target_pairs={{0,32},{32,0},{1,33},{33,1},{2,34},{34,2},{3,35},{35,3},{4,36},{36... | collective-permute-start | bytes 3993608 | tf_op jit(solution)/shard_map/ppermute | solution.py:29
  73.7 0.0 collective-permute-done.17
  73.7 0.1 collective-permute-start.22
  73.8 0.0 collective-permute-done.15.far_ref
  73.8 4.9 %collective-permute-start.21 = (bf16[4,104,1600]{2,1,0:T(8,128)(2,1)S(1)}, bf16[4,104,1600]{2,1,0:T(8,128)(2,1)S(1)}, u32[]{:S(2)}, u32[]{:S(2)}) collective-permute-start(bf16[4,104,1600]{2,1,0:T(8,128)(2,1)S(1)} %collective-permute-done.4), channel_id=1, source_target_pairs={{0,32},{32,0},{1,33},{33,1},{2,34},{34,2},{3,35},{35,3},{4,36},{36... | collective-permute-start | bytes 3993608 | tf_op jit(solution)/shard_map/ppermute | solution.py:29
  78.7 5.8 %arrange.1 = (bf16[512,416]{1,0:T(8,128)(2,1)S(1)}, bf16[512,1664]{1,0:T(8,128)(2,1)S(1)}, bf16[512,1248]{1,0:T(8,128)(2,1)S(1)}, bf16[512,416]{1,0:T(8,128)(2,1...) custom-call(bf16[1600,512]{1,0:T(8,128)(2,1)} %own_ref.1, ...), custom_call_target="tpu_custom_call" | custom-call | bytes 13107200 | tf_op jit(solution)/shard_map/arrange/pallas_call | solution.py:104
  84.5 2.1 %first.1.total_ref = f32[512,1600]{1,0:T(8,128)S(1)} custom-call(bf16[512,416]{1,0:T(8,128)(2,1)S(1)} %get-tuple-element.38.refs_0_, bf16[416,1600]{1,0:T(8,128)(2,1)S(1)} %bitcast.23, bf16[512,416]{1,0:T(8,128)(2,1)S(1)} %get-tuple-element.39.refs_2_, bf16[416,1600]{1,0:T(8,128)(2,1)S(1)} %bitcast.29), custom_call_target="tpu_custom_call" | custom-call | flops 1363148800 | bytes 2662400 | tf_op jit(solution)/shard_map/first/pallas_call | solution.py:130
  86.6 0.0 collective-permute-done.13
  86.6 0.0 collective-permute-done.14
  86.6 3.5 %collective-permute-start.23 = (bf16[4,104,1600]{2,1,0:T(8,128)(2,1)S(1)}, bf16[4,104,1600]{2,1,0:T(8,128)(2,1)S(1)}, u32[]{:S(2)}, u32[]{:S(2)}) collective-permute-start(bf16[4,104,1600]{2,1,0:T(8,128)(2,1)S(1)} %collective-permute-done.13), channel_id=1, source_target_pairs={{0,32},{32,0},{1,33},{33,1},{2,34},{34,2},{3,35},{35,3},{4,36},{36... | collective-permute-start | bytes 3993608 | tf_op jit(solution)/shard_map/ppermute | solution.py:29
  90.1 0.0 collective-permute-start.24
  90.1 0.1 slice.6
  90.2 0.1 slice.7
  90.2 0.0 collective-permute-done.20
  90.2 0.1 collective-permute-start.18
  90.3 0.0 collective-permute-done.22
  90.3 2.7 %collective-permute-start.19 = (bf16[2,104,1600]{2,1,0:T(8,128)(2,1)S(1)}, bf16[2,104,1600]{2,1,0:T(8,128)(2,1)S(1)}, u32[]{:S(2)}, u32[]{:S(2)}) collective-permute-start(bf16[2,104,1600]{2,1,0:T(8,128)(2,1)S(1)} %slice.7), channel_id=1, source_target_pairs={{0,28},{1,29},{2,30},{3,31},{4,0},{5,1},{6,2},{7,3},{8,4},{9,5},{1... | collective-permute-start | bytes 1996808 | tf_op jit(solution)/shard_map/ppermute | solution.py:25
  93.0 0.0 collective-permute-done.21
  93.0 8.7 %second.1.total_ref = f32[512,1600]{1,0:T(8,128)S(1)} custom-call(f32[512,1600]{1,0:T(8,128)S(1)} %first.1.total_ref, bf16[512,1664]{1,0:T(8,128)(2,1)S(1)} %get-tuple-element.44.refs_0_, bf16[416,1600]{1,0:T(8,128)(2,1)} %bitcast.6.refs_1_, bf16[416,1600]{1,0:T(8,128)(2,1)} %bitcast.7.refs_2_, bf16[416,1600]{1,0:T(8,128)(2,1)S(1)} %bitcast.24, ...), custom_call_target="tpu_custom_call" | custom-call | flops 5452595200 | bytes 10649600 | tf_op jit(solution)/shard_map/second/pallas_call | solution.py:130
  101.7 0.0 collective-permute-done.18
  101.7 0.0 collective-permute-done.19
  101.7 2.1 %collective-permute-start.25 = (bf16[2,104,1600]{2,1,0:T(8,128)(2,1)S(1)}, bf16[2,104,1600]{2,1,0:T(8,128)(2,1)S(1)}, u32[]{:S(2)}, u32[]{:S(2)}) collective-permute-start(bf16[2,104,1600]{2,1,0:T(8,128)(2,1)S(1)} %collective-permute-done.18), channel_id=1, source_target_pairs={{0,32},{32,0},{1,33},{33,1},{2,34},{34,2},{3,35},{35,3},{4,36},{36... | collective-permute-start | bytes 1996808 | tf_op jit(solution)/shard_map/ppermute | solution.py:29
  103.8 0.0 collective-permute-start.26
  103.8 0.0 collective-permute-done.23
  103.8 0.0 collective-permute-done.24
  103.9 4.6 %more.1.total_ref = f32[1600,512]{1,0:T(8,128)S(1)} custom-call(f32[1600,512]{1,0:T(8,128)S(1)} %bitcast.26, f32[512,1600]{1,0:T(8,128)S(1)} %second.1.total_ref, bf16[512,1248]{1,0:T(8,128)(2,1)S(1)} %get-tuple-element.48.refs_0_, bf16[416,1600]{1,0:T(8,128)(2,1)S(1)} %bitcast.27, bf16[416,1600]{1,0:T(8,128)(2,1)S(1)} %bitcast.28, ...), custom_call_target="tpu_custom_call" | custom-call | flops 3407872000 | bytes 6656000 | tf_op jit(solution)/shard_map/more/pallas_call | solution.py:130
  108.5 0.0 collective-permute-done.25
  108.5 0.0 collective-permute-done.26
  108.5 2.1 %last.1 = f32[1600,512]{1,0:T(8,128)} custom-call(f32[1600,512]{1,0:T(8,128)S(1)} %more.1.total_ref, bf16[416,512]{1,0:T(8,128)(2,1)S(1)} %get-tuple-element.52.factor_ref, bf16[208,1600]{1,0:T(8,128)(2,1)S(1)} %bitcast.36, bf16[208,1600]{1,0:T(8,128)(2,1)S(1)} %bitcast.37), custom_call_target="tpu_custom_call" | custom-call | flops 681574400 | bytes 1331200 | tf_op jit(solution)/shard_map/last/pallas_call | solution.py:130
  (2 shorter events, 0.0 us)
Async XLA Ops:
  0.0 11.7 %collective-permute-start = (bf16[1,100,1600]{2,1,0:T(8,128)(2,1)}, bf16[1,100,1600]{2,1,0:T(8,128)(2,1)S(1)}, u32[]{:S(2)}, u32[]{:S(2)}) collective-permute-start(bf16[1,100,1600]{2,1,0:T(8,128)(2,1)} %bitcast.40), channel_id=1, source_target_pairs={{0,1},{1,2},{2,3},{3,0},{4,5},{5,6},{6,7},{7,4},{8,9},{9,10},{10,1... | collective-permute-start | bytes 960008 | tf_op jit(solution)/shard_map/ppermute | solution.py:25
  2.5 36.5 %collective-permute-start.7 = (bf16[1600,512]{1,0:T(8,128)(2,1)}, bf16[1600,512]{1,0:T(8,128)(2,1)}, u32[]{:S(2)}, u32[]{:S(2)}) collective-permute-start(bf16[1600,512]{1,0:T(8,128)(2,1)} %own_ref.1), channel_id=1, source_target_pairs={{0,64},{32,224},{64,128},{96,32},{128,192},{160,96},{192,0},{224,1... | collective-permute-start | bytes 4915208 | tf_op jit(solution)/shard_map/ppermute | solution.py:14
  4.9 8.5 %collective-permute-start.1 = (bf16[1,100,1600]{2,1,0:T(8,128)(2,1)}, bf16[1,100,1600]{2,1,0:T(8,128)(2,1)S(1)}, u32[]{:S(2)}, u32[]{:S(2)}) collective-permute-start(bf16[1,100,1600]{2,1,0:T(8,128)(2,1)} %bitcast.41), channel_id=1, source_target_pairs={{0,3},{1,0},{2,1},{3,2},{4,7},{5,4},{6,5},{7,6},{8,11},{9,8},{10,9... | collective-permute-start | bytes 960008 | tf_op jit(solution)/shard_map/ppermute | solution.py:25
  11.7 7.7 %collective-permute-start.2 = (bf16[1,100,1600]{2,1,0:T(8,128)(2,1)S(1)}, bf16[1,100,1600]{2,1,0:T(8,128)(2,1)S(1)}, u32[]{:S(2)}, u32[]{:S(2)}) collective-permute-start(bf16[1,100,1600]{2,1,0:T(8,128)(2,1)S(1)} %collective-permute-done), channel_id=1, source_target_pairs={{0,1},{1,2},{2,3},{3,0},{4,5},{5,6},{6,7},{7,4},{8,9},{9,10},{10,1... | collective-permute-start | bytes 960008 | tf_op jit(solution)/shard_map/ppermute | solution.py:25
  20.5 19.7 %collective-permute-start.3 = (bf16[4,104,1600]{2,1,0:T(8,128)(2,1)S(1)}, bf16[4,104,1600]{2,1,0:T(8,128)(2,1)}, u32[]{:S(2)}, u32[]{:S(2)}) collective-permute-start(bf16[4,104,1600]{2,1,0:T(8,128)(2,1)S(1)} %fusion.12), channel_id=1, source_target_pairs={{0,4},{1,5},{2,6},{3,7},{4,8},{5,9},{6,10},{7,11},{8,12},{9,13},{1... | collective-permute-start | bytes 3993608 | tf_op jit(solution)/shard_map/ppermute | solution.py:25
  21.9 18.3 %collective-permute-start.5 = (bf16[4,104,1600]{2,1,0:T(8,128)(2,1)S(1)}, bf16[4,104,1600]{2,1,0:T(8,128)(2,1)}, u32[]{:S(2)}, u32[]{:S(2)}) collective-permute-start(bf16[4,104,1600]{2,1,0:T(8,128)(2,1)S(1)} %fusion.12), channel_id=1, source_target_pairs={{0,28},{1,29},{2,30},{3,31},{4,0},{5,1},{6,2},{7,3},{8,4},{9,5},{1... | collective-permute-start | bytes 3993608 | tf_op jit(solution)/shard_map/ppermute | solution.py:25
  23.4 12.2 %collective-permute-start.8 = (bf16[1,100,1600]{2,1,0:T(8,128)(2,1)S(1)}, bf16[1,100,1600]{2,1,0:T(8,128)(2,1)S(1)}, u32[]{:S(2)}, u32[]{:S(2)}) collective-permute-start(bf16[1,100,1600]{2,1,0:T(8,128)(2,1)S(1)} %collective-permute-done.1), channel_id=1, source_target_pairs={{32,60},{33,61},{34,62},{35,63},{36,32},{37,33},{38,34},{39,35},{4... | collective-permute-start | bytes 960008 | tf_op jit(solution)/shard_map/ppermute | solution.py:25
  25.6 13.4 %collective-permute-start.9 = (bf16[1,100,1600]{2,1,0:T(8,128)(2,1)S(1)}, bf16[1,100,1600]{2,1,0:T(8,128)(2,1)S(1)}, u32[]{:S(2)}, u32[]{:S(2)}) collective-permute-start(bf16[1,100,1600]{2,1,0:T(8,128)(2,1)S(1)} %collective-permute-done.2), channel_id=1, source_target_pairs={{32,36},{33,37},{34,38},{35,39},{36,40},{37,41},{38,42},{39,43},{4... | collective-permute-start | bytes 960008 | tf_op jit(solution)/shard_map/ppermute | solution.py:25
  39.0 23.9 %collective-permute-start.10 = (bf16[1600,512]{1,0:T(8,128)(2,1)}, bf16[1600,512]{1,0:T(8,128)(2,1)}, u32[]{:S(2)}, u32[]{:S(2)}) collective-permute-start(bf16[1600,512]{1,0:T(8,128)(2,1)} %own_ref.1), channel_id=1, source_target_pairs={{0,192},{32,96},{64,0},{96,160},{128,64},{160,224},{192,128},{224,... | collective-permute-start | bytes 4915208 | tf_op jit(solution)/shard_map/ppermute | solution.py:14
  40.2 23.9 %collective-permute-start.4 = (bf16[4,104,1600]{2,1,0:T(8,128)(2,1)}, bf16[4,104,1600]{2,1,0:T(8,128)(2,1)S(1)}, u32[]{:S(2)}, u32[]{:S(2)}) collective-permute-start(bf16[4,104,1600]{2,1,0:T(8,128)(2,1)} %collective-permute-done.3), channel_id=1, source_target_pairs={{0,4},{1,5},{2,6},{3,7},{4,8},{5,9},{6,10},{7,11},{8,12},{9,13},{1... | collective-permute-start | bytes 3993608 | tf_op jit(solution)/shard_map/ppermute | solution.py:25
  40.2 23.9 %collective-permute-start.6 = (bf16[4,104,1600]{2,1,0:T(8,128)(2,1)}, bf16[4,104,1600]{2,1,0:T(8,128)(2,1)}, u32[]{:S(2)}, u32[]{:S(2)}) collective-permute-start(bf16[4,104,1600]{2,1,0:T(8,128)(2,1)} %collective-permute-done.5), channel_id=1, source_target_pairs={{0,28},{1,29},{2,30},{3,31},{4,0},{5,1},{6,2},{7,3},{8,4},{9,5},{1... | collective-permute-start | bytes 3993608 | tf_op jit(solution)/shard_map/ppermute | solution.py:25
  42.1 8.1 %collective-permute-start.11 = (bf16[1,100,1600]{2,1,0:T(8,128)(2,1)S(1)}, bf16[1,100,1600]{2,1,0:T(8,128)(2,1)}, u32[]{:S(2)}, u32[]{:S(2)}) collective-permute-start(bf16[1,100,1600]{2,1,0:T(8,128)(2,1)S(1)} %collective-permute-done.8), channel_id=1, source_target_pairs={{32,60},{33,61},{34,62},{35,63},{36,32},{37,33},{38,34},{39,35},{4... | collective-permute-start | bytes 960008 | tf_op jit(solution)/shard_map/ppermute | solution.py:25
  44.0 12.5 %collective-permute-start.12 = (bf16[1,100,1600]{2,1,0:T(8,128)(2,1)S(1)}, bf16[1,100,1600]{2,1,0:T(8,128)(2,1)}, u32[]{:S(2)}, u32[]{:S(2)}) collective-permute-start(bf16[1,100,1600]{2,1,0:T(8,128)(2,1)S(1)} %collective-permute-done.9), channel_id=1, source_target_pairs={{32,36},{33,37},{34,38},{35,39},{36,40},{37,41},{38,42},{39,43},{4... | collective-permute-start | bytes 960008 | tf_op jit(solution)/shard_map/ppermute | solution.py:25
  50.2 23.7 %collective-permute-start.15 = (bf16[1600,512]{1,0:T(8,128)(2,1)}, bf16[1600,512]{1,0:T(8,128)(2,1)}, u32[]{:S(2)}, u32[]{:S(2)}) collective-permute-start(bf16[1600,512]{1,0:T(8,128)(2,1)} %collective-permute-done.7.near_ref), channel_id=1, source_target_pairs={{0,64},{32,224},{64,128},{96,32},{128,192},{160,96},{192,0},{224,1... | collective-permute-start | bytes 4915208 | tf_op jit(solution)/shard_map/ppermute | solution.py:14
  56.5 10.7 %collective-permute-start.16 = (bf16[4,104,1600]{2,1,0:T(8,128)(2,1)S(1)}, bf16[4,104,1600]{2,1,0:T(8,128)(2,1)S(1)}, u32[]{:S(2)}, u32[]{:S(2)}) collective-permute-start(bf16[4,104,1600]{2,1,0:T(8,128)(2,1)S(1)} %fusion.12), channel_id=1, source_target_pairs={{0,32},{32,0},{1,33},{33,1},{2,34},{34,2},{3,35},{35,3},{4,36},{36... | collective-permute-start | bytes 3993608 | tf_op jit(solution)/shard_map/ppermute | solution.py:29
  62.9 10.8 %collective-permute-start.17 = (bf16[4,104,1600]{2,1,0:T(8,128)(2,1)}, bf16[4,104,1600]{2,1,0:T(8,128)(2,1)S(1)}, u32[]{:S(2)}, u32[]{:S(2)}) collective-permute-start(bf16[4,104,1600]{2,1,0:T(8,128)(2,1)} %collective-permute-done.3), channel_id=1, source_target_pairs={{0,32},{32,0},{1,33},{33,1},{2,34},{34,2},{3,35},{35,3},{4,36},{36... | collective-permute-start | bytes 3993608 | tf_op jit(solution)/shard_map/ppermute | solution.py:29
  64.5 22.1 %collective-permute-start.13 = (bf16[4,104,1600]{2,1,0:T(8,128)(2,1)S(1)}, bf16[4,104,1600]{2,1,0:T(8,128)(2,1)S(1)}, u32[]{:S(2)}, u32[]{:S(2)}) collective-permute-start(bf16[4,104,1600]{2,1,0:T(8,128)(2,1)S(1)} %get-tuple-element.54), channel_id=1, source_target_pairs={{0,4},{1,5},{2,6},{3,7},{4,8},{5,9},{6,10},{7,11},{8,12},{9,13},{1... | collective-permute-start | bytes 3993608 | tf_op jit(solution)/shard_map/ppermute | solution.py:25
  65.3 21.3 %collective-permute-start.14 = (bf16[4,104,1600]{2,1,0:T(8,128)(2,1)S(1)}, bf16[4,104,1600]{2,1,0:T(8,128)(2,1)S(1)}, u32[]{:S(2)}, u32[]{:S(2)}) collective-permute-start(bf16[4,104,1600]{2,1,0:T(8,128)(2,1)S(1)} %get-tuple-element.53), channel_id=1, source_target_pairs={{0,28},{1,29},{2,30},{3,31},{4,0},{5,1},{6,2},{7,3},{8,4},{9,5},{1... | collective-permute-start | bytes 3993608 | tf_op jit(solution)/shard_map/ppermute | solution.py:25
  67.3 23.0 %collective-permute-start.20 = (bf16[4,104,1600]{2,1,0:T(8,128)(2,1)}, bf16[4,104,1600]{2,1,0:T(8,128)(2,1)S(1)}, u32[]{:S(2)}, u32[]{:S(2)}) collective-permute-start(bf16[4,104,1600]{2,1,0:T(8,128)(2,1)} %collective-permute-done.5), channel_id=1, source_target_pairs={{0,32},{32,0},{1,33},{33,1},{2,34},{34,2},{3,35},{35,3},{4,36},{36... | collective-permute-start | bytes 3993608 | tf_op jit(solution)/shard_map/ppermute | solution.py:29
  73.7 16.6 %collective-permute-start.22 = (bf16[4,104,1600]{2,1,0:T(8,128)(2,1)S(1)}, bf16[4,104,1600]{2,1,0:T(8,128)(2,1)S(1)}, u32[]{:S(2)}, u32[]{:S(2)}) collective-permute-start(bf16[4,104,1600]{2,1,0:T(8,128)(2,1)S(1)} %get-tuple-element.53), channel_id=1, source_target_pairs={{0,32},{32,0},{1,33},{33,1},{2,34},{34,2},{3,35},{35,3},{4,36},{36... | collective-permute-start | bytes 3993608 | tf_op jit(solution)/shard_map/ppermute | solution.py:29
  73.8 19.2 %collective-permute-start.21 = (bf16[4,104,1600]{2,1,0:T(8,128)(2,1)S(1)}, bf16[4,104,1600]{2,1,0:T(8,128)(2,1)S(1)}, u32[]{:S(2)}, u32[]{:S(2)}) collective-permute-start(bf16[4,104,1600]{2,1,0:T(8,128)(2,1)S(1)} %collective-permute-done.4), channel_id=1, source_target_pairs={{0,32},{32,0},{1,33},{33,1},{2,34},{34,2},{3,35},{35,3},{4,36},{36... | collective-permute-start | bytes 3993608 | tf_op jit(solution)/shard_map/ppermute | solution.py:29
  86.6 17.2 %collective-permute-start.23 = (bf16[4,104,1600]{2,1,0:T(8,128)(2,1)S(1)}, bf16[4,104,1600]{2,1,0:T(8,128)(2,1)S(1)}, u32[]{:S(2)}, u32[]{:S(2)}) collective-permute-start(bf16[4,104,1600]{2,1,0:T(8,128)(2,1)S(1)} %collective-permute-done.13), channel_id=1, source_target_pairs={{0,32},{32,0},{1,33},{33,1},{2,34},{34,2},{3,35},{35,3},{4,36},{36... | collective-permute-start | bytes 3993608 | tf_op jit(solution)/shard_map/ppermute | solution.py:29
  90.1 13.7 %collective-permute-start.24 = (bf16[4,104,1600]{2,1,0:T(8,128)(2,1)S(1)}, bf16[4,104,1600]{2,1,0:T(8,128)(2,1)S(1)}, u32[]{:S(2)}, u32[]{:S(2)}) collective-permute-start(bf16[4,104,1600]{2,1,0:T(8,128)(2,1)S(1)} %collective-permute-done.14), channel_id=1, source_target_pairs={{0,32},{32,0},{1,33},{33,1},{2,34},{34,2},{3,35},{35,3},{4,36},{36... | collective-permute-start | bytes 3993608 | tf_op jit(solution)/shard_map/ppermute | solution.py:29
  90.2 11.5 %collective-permute-start.18 = (bf16[2,104,1600]{2,1,0:T(8,128)(2,1)S(1)}, bf16[2,104,1600]{2,1,0:T(8,128)(2,1)S(1)}, u32[]{:S(2)}, u32[]{:S(2)}) collective-permute-start(bf16[2,104,1600]{2,1,0:T(8,128)(2,1)S(1)} %slice.6), channel_id=1, source_target_pairs={{0,4},{1,5},{2,6},{3,7},{4,8},{5,9},{6,10},{7,11},{8,12},{9,13},{1... | collective-permute-start | bytes 1996808 | tf_op jit(solution)/shard_map/ppermute | solution.py:25
  90.3 11.4 %collective-permute-start.19 = (bf16[2,104,1600]{2,1,0:T(8,128)(2,1)S(1)}, bf16[2,104,1600]{2,1,0:T(8,128)(2,1)S(1)}, u32[]{:S(2)}, u32[]{:S(2)}) collective-permute-start(bf16[2,104,1600]{2,1,0:T(8,128)(2,1)S(1)} %slice.7), channel_id=1, source_target_pairs={{0,28},{1,29},{2,30},{3,31},{4,0},{5,1},{6,2},{7,3},{8,4},{9,5},{1... | collective-permute-start | bytes 1996808 | tf_op jit(solution)/shard_map/ppermute | solution.py:25
  93.0 10.9 %copy-start = (f32[512,1600]{0,1:T(8,128)S(1)}, f32[512,1600]{0,1:T(8,128)}, u32[]{:S(2)}) copy-start(f32[512,1600]{0,1:T(8,128)} %param.3) | copy-start | bytes 9830404
  101.7 6.8 %collective-permute-start.25 = (bf16[2,104,1600]{2,1,0:T(8,128)(2,1)S(1)}, bf16[2,104,1600]{2,1,0:T(8,128)(2,1)S(1)}, u32[]{:S(2)}, u32[]{:S(2)}) collective-permute-start(bf16[2,104,1600]{2,1,0:T(8,128)(2,1)S(1)} %collective-permute-done.18), channel_id=1, source_target_pairs={{0,32},{32,0},{1,33},{33,1},{2,34},{34,2},{3,35},{35,3},{4,36},{36... | collective-permute-start | bytes 1996808 | tf_op jit(solution)/shard_map/ppermute | solution.py:29
  103.8 4.7 %collective-permute-start.26 = (bf16[2,104,1600]{2,1,0:T(8,128)(2,1)S(1)}, bf16[2,104,1600]{2,1,0:T(8,128)(2,1)S(1)}, u32[]{:S(2)}, u32[]{:S(2)}) collective-permute-start(bf16[2,104,1600]{2,1,0:T(8,128)(2,1)S(1)} %collective-permute-done.19), channel_id=1, source_target_pairs={{0,32},{32,0},{1,33},{33,1},{2,34},{34,2},{3,35},{35,3},{4,36},{36... | collective-permute-start | bytes 1996808 | tf_op jit(solution)/shard_map/ppermute | solution.py:29

commit v12 on v11

--- a/solution.py
+++ b/solution.py
@@ -61,9 +61,10 @@
     theirs[:2] = lax.optimization_barrier(theirs[:2])
     total = first_products([own_factors[0], their_factors[0]], [[pack], theirs[:1]])
     u3, d3, total = lax.optimization_barrier((u3, d3, total))
-    u4, d4 = travel(u3[:2], *up), travel(d3[2:], *down)
+    halves = [u3[:2], u3[2:]]
+    u4, d4 = travel(halves[0], *up), travel(d3[2:], *down)
     total = second_products(total, [own_factors[1], their_factors[1]], [[u1, d1, u2, kept], theirs[1:]])
-    theirs = [swap(u3), swap(d3)]
+    theirs = [*[swap(piece) for piece in halves], swap(d3)]
     u4, d4, total = lax.optimization_barrier((u4, d4, total))
     total = more_products(residual, total, [own_factors[2], their_factors[2]], [[u3, d3, u4, d4], theirs])
     return last_products(total, their_factors[3], [swap(u4), swap(d4)])

time: 111 us -> 111 us (level)
  starting transfers between devices: 49.8 us -> 53 us
  waiting for transfers between devices: 34.6 us -> 31.9 us
    ppermute x9 -> x10, starting transfers between devices: 17.1 us -> 20.1 us  [swap(): return lax.ppermute(array, 'col', [(0, 1), (1, 0)])]
    ppermute x15, waiting for transfers between devices: 28.2 us -> 26 us  [travel(): return lax.ppermute(array, ('col', 'depth'), pairs)]
  transfers between devices with their start and end apart: 27 -> 28, of which waited for: 8 -> 8; matrix products, arithmetic and copies ran while one was open for 2% -> 3% of each run, Pallas kernels for 19% -> 18%
where the time goes in v12:
time: 111 us; the launch traced here: 110 us
  starting transfers between devices  53 us (48%)
  waiting for transfers between devices  31.9 us (29%)
  Pallas kernels  22.3 us (20%)
  other arithmetic  2.68 us (2%)
    ppermute x15, starting transfers between devices, travel(): return lax.ppermute(array, ('col', 'depth'), pairs)  27.2 us
    ppermute x15, waiting for transfers between devices, travel(): return lax.ppermute(array, ('col', 'depth'), pairs)  26 us
    ppermute x10, starting transfers between devices, swap(): return lax.ppermute(array, 'col', [(0, 1), (1, 0)])  20.1 us
    pallas_call x4, Pallas kernels, multiply(): pl.pallas_call(body, out_shape=jax.ShapeDtypeStruct(shape, jnp.float32),...  17.5 us
    ppermute x3, waiting for transfers between devices, along_row(): return lax.ppermute(array, ('row', 'col'), pairs)  5.89 us
    ppermute x3, starting transfers between devices, along_row(): return lax.ppermute(array, ('row', 'col'), pairs)  5.73 us
    pallas_call x1, Pallas kernels, arrange(): pl.pallas_call(kernel, out_shape=[jax.ShapeDtypeStruct(shape, own.dtype)...  4.79 us
    concatenate x2, other arithmetic, packed(): jnp.concatenate([jnp.pad(block, ((0, 0), (0, -block.shape[1] % 8), (0, 0)...  2.31 us
  transfers between devices with their start and end apart: 28, of which 8 were waited for; matrix products, arithmetic and copies ran while one was open for 3% of the time, Pallas kernels for 18%

profile of v12, /device:TPU:1, one launch (start us, length us, event | category | flops | bytes accessed | tf_op | source)
XLA Modules:
  0.0 110.5 jit_solution(16189373275229780604)
XLA Ops:
  0.0 2.5 %collective-permute-start = (bf16[1,100,1600]{2,1,0:T(8,128)(2,1)}, bf16[1,100,1600]{2,1,0:T(8,128)(2,1)S(1)}, u32[]{:S(2)}, u32[]{:S(2)}) collective-permute-start(bf16[1,100,1600]{2,1,0:T(8,128)(2,1)} %bitcast.42), channel_id=1, source_target_pairs={{0,1},{1,2},{2,3},{3,0},{4,5},{5,6},{6,7},{7,4},{8,9},{9,10},{10,1... | collective-permute-start | bytes 960008 | tf_op jit(solution)/shard_map/ppermute | solution.py:25
  2.5 3.9 %collective-permute-start.1 = (bf16[1,100,1600]{2,1,0:T(8,128)(2,1)}, bf16[1,100,1600]{2,1,0:T(8,128)(2,1)S(1)}, u32[]{:S(2)}, u32[]{:S(2)}) collective-permute-start(bf16[1,100,1600]{2,1,0:T(8,128)(2,1)} %bitcast.43), channel_id=1, source_target_pairs={{0,3},{1,0},{2,1},{3,2},{4,7},{5,4},{6,5},{7,6},{8,11},{9,8},{10,9... | collective-permute-start | bytes 960008 | tf_op jit(solution)/shard_map/ppermute | solution.py:25
  6.4 5.1 %collective-permute-done = bf16[1,100,1600]{2,1,0:T(8,128)(2,1)S(1)} collective-permute-done((bf16[1,100,1600]{2,1,0:T(8,128)(2,1)}, bf16[1,100,1600]{2,1,0:T(8,128)(2,1)S(1)}, u32[]{:S(2)}, u32[]{:S(2)}) %collective-permute-start) | collective-permute-done | bytes 320032 | tf_op jit(solution)/shard_map/ppermute | solution.py:25
  11.5 0.0 collective-permute-start.2
  11.5 2.2 %collective-permute-start.7 = (bf16[1600,512]{1,0:T(8,128)(2,1)}, bf16[1600,512]{1,0:T(8,128)(2,1)S(1)}, u32[]{:S(2)}, u32[]{:S(2)}) collective-permute-start(bf16[1600,512]{1,0:T(8,128)(2,1)} %own_ref.1), channel_id=1, source_target_pairs={{0,64},{32,224},{64,128},{96,32},{128,192},{160,96},{192,0},{224,1... | collective-permute-start | bytes 4915208 | tf_op jit(solution)/shard_map/ppermute | solution.py:14
  13.8 0.0 collective-permute-done.1
  13.8 5.4 %collective-permute-done.2 = bf16[1,100,1600]{2,1,0:T(8,128)(2,1)S(1)} collective-permute-done((bf16[1,100,1600]{2,1,0:T(8,128)(2,1)S(1)}, bf16[1,100,1600]{2,1,0:T(8,128)(2,1)S(1)}, u32[]{:S(2)}, u32[]{:S(2)}) %collective-permute-start.2) | collective-permute-done | bytes 320032 | tf_op jit(solution)/shard_map/ppermute | solution.py:25
  19.2 1.1 %fusion.12 = bf16[4,104,1600]{2,1,0:T(8,128)(2,1)S(1)} fusion(bf16[1,100,1600]{2,1,0:T(8,128)(2,1)S(1)} %collective-permute-done.2, bf16[1,100,1600]{2,1,0:T(8,128)(2,1)S(1)} %collective-permute-done.1, bf16[1,100,1600]{2,1,0:T(8,128)(2,1)S(1)} %collective-permute-done, bf16[1,100,1600]{2,1,0:T(8,128)(2,1)} %bitcast.44), kind=kLoop, calls=%fused_computation.18 | loop fusion | flops 13312000 | bytes 2611200 | tf_op jit(solution)/shard_map/concatenate | solution.py:33
  20.3 1.1 %collective-permute-start.3 = (bf16[4,104,1600]{2,1,0:T(8,128)(2,1)S(1)}, bf16[4,104,1600]{2,1,0:T(8,128)(2,1)}, u32[]{:S(2)}, u32[]{:S(2)}) collective-permute-start(bf16[4,104,1600]{2,1,0:T(8,128)(2,1)S(1)} %fusion.12), channel_id=1, source_target_pairs={{0,4},{1,5},{2,6},{3,7},{4,8},{5,9},{6,10},{7,11},{8,12},{9,13},{1... | collective-permute-start | bytes 3993608 | tf_op jit(solution)/shard_map/ppermute | solution.py:25
  21.4 1.8 %collective-permute-start.5 = (bf16[4,104,1600]{2,1,0:T(8,128)(2,1)S(1)}, bf16[4,104,1600]{2,1,0:T(8,128)(2,1)}, u32[]{:S(2)}, u32[]{:S(2)}) collective-permute-start(bf16[4,104,1600]{2,1,0:T(8,128)(2,1)S(1)} %fusion.12), channel_id=1, source_target_pairs={{0,28},{1,29},{2,30},{3,31},{4,0},{5,1},{6,2},{7,3},{8,4},{9,5},{1... | collective-permute-start | bytes 3993608 | tf_op jit(solution)/shard_map/ppermute | solution.py:25
  23.2 2.1 %collective-permute-start.8 = (bf16[1,100,1600]{2,1,0:T(8,128)(2,1)S(1)}, bf16[1,100,1600]{2,1,0:T(8,128)(2,1)S(1)}, u32[]{:S(2)}, u32[]{:S(2)}) collective-permute-start(bf16[1,100,1600]{2,1,0:T(8,128)(2,1)S(1)} %collective-permute-done.1), channel_id=1, source_target_pairs={{32,60},{33,61},{34,62},{35,63},{36,32},{37,33},{38,34},{39,35},{4... | collective-permute-start | bytes 960008 | tf_op jit(solution)/shard_map/ppermute | solution.py:25
  25.4 3.1 %collective-permute-start.9 = (bf16[1,100,1600]{2,1,0:T(8,128)(2,1)S(1)}, bf16[1,100,1600]{2,1,0:T(8,128)(2,1)S(1)}, u32[]{:S(2)}, u32[]{:S(2)}) collective-permute-start(bf16[1,100,1600]{2,1,0:T(8,128)(2,1)S(1)} %collective-permute-done.2), channel_id=1, source_target_pairs={{32,36},{33,37},{34,38},{35,39},{36,40},{37,41},{38,42},{39,43},{4... | collective-permute-start | bytes 960008 | tf_op jit(solution)/shard_map/ppermute | solution.py:25
  28.5 6.9 %collective-permute-done.8 = bf16[1,100,1600]{2,1,0:T(8,128)(2,1)S(1)} collective-permute-done((bf16[1,100,1600]{2,1,0:T(8,128)(2,1)S(1)}, bf16[1,100,1600]{2,1,0:T(8,128)(2,1)S(1)}, u32[]{:S(2)}, u32[]{:S(2)}) %collective-permute-start.8) | collective-permute-done | bytes 320032 | tf_op jit(solution)/shard_map/ppermute | solution.py:25
  35.4 3.4 %collective-permute-done.9 = bf16[1,100,1600]{2,1,0:T(8,128)(2,1)S(1)} collective-permute-done((bf16[1,100,1600]{2,1,0:T(8,128)(2,1)S(1)}, bf16[1,100,1600]{2,1,0:T(8,128)(2,1)S(1)}, u32[]{:S(2)}, u32[]{:S(2)}) %collective-permute-start.9) | collective-permute-done | bytes 320032 | tf_op jit(solution)/shard_map/ppermute | solution.py:25
  38.8 0.0 collective-permute-done.7.near_ref
  38.8 1.2 %collective-permute-start.10 = (bf16[1600,512]{1,0:T(8,128)(2,1)}, bf16[1600,512]{1,0:T(8,128)(2,1)}, u32[]{:S(2)}, u32[]{:S(2)}) collective-permute-start(bf16[1600,512]{1,0:T(8,128)(2,1)} %own_ref.1), channel_id=1, source_target_pairs={{0,192},{32,96},{64,0},{96,160},{128,64},{160,224},{192,128},{224,... | collective-permute-start | bytes 4915208 | tf_op jit(solution)/shard_map/ppermute | solution.py:14
  40.0 0.0 collective-permute-done.3
  40.0 0.0 collective-permute-start.4
  40.0 0.0 collective-permute-done.5
  40.0 1.8 %collective-permute-start.6 = (bf16[4,104,1600]{2,1,0:T(8,128)(2,1)}, bf16[4,104,1600]{2,1,0:T(8,128)(2,1)}, u32[]{:S(2)}, u32[]{:S(2)}) collective-permute-start(bf16[4,104,1600]{2,1,0:T(8,128)(2,1)} %collective-permute-done.5), channel_id=1, source_target_pairs={{0,28},{1,29},{2,30},{3,31},{4,0},{5,1},{6,2},{7,3},{8,4},{9,5},{1... | collective-permute-start | bytes 3993608 | tf_op jit(solution)/shard_map/ppermute | solution.py:25
  41.8 1.9 %collective-permute-start.11 = (bf16[1,100,1600]{2,1,0:T(8,128)(2,1)S(1)}, bf16[1,100,1600]{2,1,0:T(8,128)(2,1)}, u32[]{:S(2)}, u32[]{:S(2)}) collective-permute-start(bf16[1,100,1600]{2,1,0:T(8,128)(2,1)S(1)} %collective-permute-done.8), channel_id=1, source_target_pairs={{32,60},{33,61},{34,62},{35,63},{36,32},{37,33},{38,34},{39,35},{4... | collective-permute-start | bytes 960008 | tf_op jit(solution)/shard_map/ppermute | solution.py:25
  43.7 3.4 %collective-permute-start.12 = (bf16[1,100,1600]{2,1,0:T(8,128)(2,1)S(1)}, bf16[1,100,1600]{2,1,0:T(8,128)(2,1)}, u32[]{:S(2)}, u32[]{:S(2)}) collective-permute-start(bf16[1,100,1600]{2,1,0:T(8,128)(2,1)S(1)} %collective-permute-done.9), channel_id=1, source_target_pairs={{32,36},{33,37},{34,38},{35,39},{36,40},{37,41},{38,42},{39,43},{4... | collective-permute-start | bytes 960008 | tf_op jit(solution)/shard_map/ppermute | solution.py:25
  47.1 3.1 %collective-permute-done.11 = bf16[1,100,1600]{2,1,0:T(8,128)(2,1)} collective-permute-done((bf16[1,100,1600]{2,1,0:T(8,128)(2,1)S(1)}, bf16[1,100,1600]{2,1,0:T(8,128)(2,1)}, u32[]{:S(2)}, u32[]{:S(2)}) %collective-permute-start.11) | collective-permute-done | bytes 320032 | tf_op jit(solution)/shard_map/ppermute | solution.py:25
  50.2 3.7 %collective-permute-start.16 = (bf16[4,104,1600]{2,1,0:T(8,128)(2,1)S(1)}, bf16[4,104,1600]{2,1,0:T(8,128)(2,1)S(1)}, u32[]{:S(2)}, u32[]{:S(2)}) collective-permute-start(bf16[4,104,1600]{2,1,0:T(8,128)(2,1)S(1)} %fusion.12), channel_id=1, source_target_pairs={{0,32},{32,0},{1,33},{33,1},{2,34},{34,2},{3,35},{35,3},{4,36},{36... | collective-permute-start | bytes 3993608 | tf_op jit(solution)/shard_map/ppermute | solution.py:29
  53.9 2.1 %collective-permute-done.12 = bf16[1,100,1600]{2,1,0:T(8,128)(2,1)} collective-permute-done((bf16[1,100,1600]{2,1,0:T(8,128)(2,1)S(1)}, bf16[1,100,1600]{2,1,0:T(8,128)(2,1)}, u32[]{:S(2)}, u32[]{:S(2)}) %collective-permute-start.12) | collective-permute-done | bytes 320032 | tf_op jit(solution)/shard_map/ppermute | solution.py:25
  56.0 2.3 %collective-permute-start.15 = (bf16[1600,512]{1,0:T(8,128)(2,1)}, bf16[1600,512]{1,0:T(8,128)(2,1)S(1)}, u32[]{:S(2)}, u32[]{:S(2)}) collective-permute-start(bf16[1600,512]{1,0:T(8,128)(2,1)} %copy-done.1), channel_id=1, source_target_pairs={{0,64},{32,224},{64,128},{96,32},{128,192},{160,96},{192,0},{224,1... | collective-permute-start | bytes 4915208 | tf_op jit(solution)/shard_map/ppermute | solution.py:14
  58.3 1.2 %fusion.15 = bf16[4,104,1600]{2,1,0:T(8,128)(2,1)S(1)} fusion(bf16[1,100,1600]{2,1,0:T(8,128)(2,1)} %collective-permute-done.12, bf16[1,100,1600]{2,1,0:T(8,128)(2,1)} %collective-permute-done.11, bf16[1,100,1600]{2,1,0:T(8,128)(2,1)S(1)} %collective-permute-done.9, bf16[1,100,1600]{2,1,0:T(8,128)(2,1)S(1)} %collective-permute-done.8), kind=kLoop, calls=%fused_computation.21 | loop fusion | flops 13312000 | bytes 2611200 | tf_op jit(solution)/shard_map/concatenate | solution.py:33
  59.5 0.0 copy-start.2
  59.5 2.8 %collective-permute-done.10.other_ref = bf16[1600,512]{1,0:T(8,128)(2,1)} collective-permute-done((bf16[1600,512]{1,0:T(8,128)(2,1)}, bf16[1600,512]{1,0:T(8,128)(2,1)}, u32[]{:S(2)}, u32[]{:S(2)}) %collective-permute-start.10) | collective-permute-done | bytes 1638432 | tf_op jit(solution)/shard_map/ppermute | solution.py:14
  62.3 0.0 collective-permute-start.17
  62.3 0.0 collective-permute-done.4
  62.3 0.0 collective-permute-done.6
  62.3 0.4 broadcast_select_fusion
  62.7 0.8 collective-permute-start.13
  63.5 1.9 %collective-permute-start.14 = (bf16[4,104,1600]{2,1,0:T(8,128)(2,1)S(1)}, bf16[4,104,1600]{2,1,0:T(8,128)(2,1)S(1)}, u32[]{:S(2)}, u32[]{:S(2)}) collective-permute-start(bf16[4,104,1600]{2,1,0:T(8,128)(2,1)S(1)} %get-tuple-element.55), channel_id=1, source_target_pairs={{0,28},{1,29},{2,30},{3,31},{4,0},{5,1},{6,2},{7,3},{8,4},{9,5},{1... | collective-permute-start | bytes 3993608 | tf_op jit(solution)/shard_map/ppermute | solution.py:25
  65.5 0.0 collective-permute-done.16
  65.5 8.0 %collective-permute-start.20 = (bf16[4,104,1600]{2,1,0:T(8,128)(2,1)}, bf16[4,104,1600]{2,1,0:T(8,128)(2,1)S(1)}, u32[]{:S(2)}, u32[]{:S(2)}) collective-permute-start(bf16[4,104,1600]{2,1,0:T(8,128)(2,1)} %collective-permute-done.5), channel_id=1, source_target_pairs={{0,32},{32,0},{1,33},{33,1},{2,34},{34,2},{3,35},{35,3},{4,36},{36... | collective-permute-start | bytes 3993608 | tf_op jit(solution)/shard_map/ppermute | solution.py:29
  73.5 0.0 collective-permute-done.17
  73.5 0.1 collective-permute-start.22
  73.6 3.1 %collective-permute-done.15.far_ref = bf16[1600,512]{1,0:T(8,128)(2,1)S(1)} collective-permute-done((bf16[1600,512]{1,0:T(8,128)(2,1)}, bf16[1600,512]{1,0:T(8,128)(2,1)S(1)}, u32[]{:S(2)}, u32[]{:S(2)}) %collective-permute-start.15) | collective-permute-done | bytes 1638432 | tf_op jit(solution)/shard_map/ppermute | solution.py:14
  76.7 1.8 %collective-permute-start.21 = (bf16[4,104,1600]{2,1,0:T(8,128)(2,1)S(1)}, bf16[4,104,1600]{2,1,0:T(8,128)(2,1)S(1)}, u32[]{:S(2)}, u32[]{:S(2)}) collective-permute-start(bf16[4,104,1600]{2,1,0:T(8,128)(2,1)S(1)} %collective-permute-done.4), channel_id=1, source_target_pairs={{0,32},{32,0},{1,33},{33,1},{2,34},{34,2},{3,35},{35,3},{4,36},{36... | collective-permute-start | bytes 3993608 | tf_op jit(solution)/shard_map/ppermute | solution.py:29
  78.4 4.8 %arrange.1 = (bf16[512,416]{1,0:T(8,128)(2,1)S(1)}, bf16[512,1664]{1,0:T(8,128)(2,1)S(1)}, bf16[512,1248]{1,0:T(8,128)(2,1)S(1)}, bf16[512,416]{1,0:T(8,128)(2,1...) custom-call(bf16[1600,512]{1,0:T(8,128)(2,1)} %own_ref.1, ...), custom_call_target="tpu_custom_call" | custom-call | bytes 13107200 | tf_op jit(solution)/shard_map/arrange/pallas_call | solution.py:105
  83.2 2.1 %first.1.total_ref = f32[512,1600]{1,0:T(8,128)S(1)} custom-call(bf16[512,416]{1,0:T(8,128)(2,1)S(1)} %get-tuple-element.38.refs_0_, bf16[416,1600]{1,0:T(8,128)(2,1)S(1)} %bitcast.24, bf16[512,416]{1,0:T(8,128)(2,1)S(1)} %get-tuple-element.39.refs_2_, bf16[416,1600]{1,0:T(8,128)(2,1)S(1)} %bitcast.30), custom_call_target="tpu_custom_call" | custom-call | flops 1363148800 | bytes 2662400 | tf_op jit(solution)/shard_map/first/pallas_call | solution.py:131
  85.3 0.0 collective-permute-done.13
  85.3 0.0 collective-permute-done.14
  85.3 0.1 slice.10
  85.4 4.6 %collective-permute-start.25 = (bf16[4,104,1600]{2,1,0:T(8,128)(2,1)S(1)}, bf16[4,104,1600]{2,1,0:T(8,128)(2,1)S(1)}, u32[]{:S(2)}, u32[]{:S(2)}) collective-permute-start(bf16[4,104,1600]{2,1,0:T(8,128)(2,1)S(1)} %collective-permute-done.14), channel_id=1, source_target_pairs={{0,32},{32,0},{1,33},{33,1},{2,34},{34,2},{3,35},{35,3},{4,36},{36... | collective-permute-start | bytes 3993608 | tf_op jit(solution)/shard_map/ppermute | solution.py:29
  90.0 0.1 fusion.16
  90.1 0.1 collective-permute-start.18
  90.2 0.0 collective-permute-done.20
  90.2 2.7 %collective-permute-start.19 = (bf16[2,104,1600]{2,1,0:T(8,128)(2,1)S(1)}, bf16[2,104,1600]{2,1,0:T(8,128)(2,1)S(1)}, u32[]{:S(2)}, u32[]{:S(2)}) collective-permute-start(bf16[2,104,1600]{2,1,0:T(8,128)(2,1)S(1)} %slice.10), channel_id=1, source_target_pairs={{0,28},{1,29},{2,30},{3,31},{4,0},{5,1},{6,2},{7,3},{8,4},{9,5},{1... | collective-permute-start | bytes 1996808 | tf_op jit(solution)/shard_map/ppermute | solution.py:25
  92.9 0.0 collective-permute-done.22
  92.9 0.7 collective-permute-start.23
  93.5 0.0 collective-permute-done.21
  93.6 0.1 collective-permute-start.24
  93.6 8.7 %second.1.total_ref = f32[512,1600]{1,0:T(8,128)S(1)} custom-call(f32[512,1600]{1,0:T(8,128)S(1)} %first.1.total_ref, bf16[512,1664]{1,0:T(8,128)(2,1)S(1)} %get-tuple-element.44.refs_0_, bf16[416,1600]{1,0:T(8,128)(2,1)} %bitcast.6.refs_1_, bf16[416,1600]{1,0:T(8,128)(2,1)} %bitcast.7.refs_2_, bf16[416,1600]{1,0:T(8,128)(2,1)S(1)} %bitcast.25, ...), custom_call_target="tpu_custom_call" | custom-call | flops 5452595200 | bytes 10649600 | tf_op jit(solution)/shard_map/second/pallas_call | solution.py:131
  102.4 0.0 collective-permute-done.18
  102.4 0.0 collective-permute-done.19
  102.4 1.1 collective-permute-start.26
  103.5 0.0 collective-permute-start.27
  103.5 0.0 collective-permute-done.23
  103.5 4.7 %more.1.total_ref = f32[1600,512]{1,0:T(8,128)S(1)} custom-call(f32[1600,512]{1,0:T(8,128)S(1)} %bitcast.28, f32[512,1600]{1,0:T(8,128)S(1)} %second.1.total_ref, bf16[512,1248]{1,0:T(8,128)(2,1)S(1)} %get-tuple-element.48.refs_0_, bf16[416,1600]{1,0:T(8,128)(2,1)S(1)} %bitcast.26, bf16[416,1600]{1,0:T(8,128)(2,1)S(1)} %bitcast.29, ...), custom_call_target="tpu_custom_call" | custom-call | flops 3407872000 | bytes 6656000 | tf_op jit(solution)/shard_map/more/pallas_call | solution.py:131
  108.2 0.0 collective-permute-done.27
  108.2 2.1 %last.1 = f32[1600,512]{1,0:T(8,128)} custom-call(f32[1600,512]{1,0:T(8,128)S(1)} %more.1.total_ref, bf16[416,512]{1,0:T(8,128)(2,1)S(1)} %get-tuple-element.52.factor_ref, bf16[208,1600]{1,0:T(8,128)(2,1)S(1)} %bitcast.36, bf16[208,1600]{1,0:T(8,128)(2,1)S(1)} %bitcast.37), custom_call_target="tpu_custom_call" | custom-call | flops 681574400 | bytes 1331200 | tf_op jit(solution)/shard_map/last/pallas_call | solution.py:131
  (8 shorter events, 0.0 us)
Async XLA Ops:
  0.0 11.5 %collective-permute-start = (bf16[1,100,1600]{2,1,0:T(8,128)(2,1)}, bf16[1,100,1600]{2,1,0:T(8,128)(2,1)S(1)}, u32[]{:S(2)}, u32[]{:S(2)}) collective-permute-start(bf16[1,100,1600]{2,1,0:T(8,128)(2,1)} %bitcast.42), channel_id=1, source_target_pairs={{0,1},{1,2},{2,3},{3,0},{4,5},{5,6},{6,7},{7,4},{8,9},{9,10},{10,1... | collective-permute-start | bytes 960008 | tf_op jit(solution)/shard_map/ppermute | solution.py:25
  2.5 11.3 %collective-permute-start.1 = (bf16[1,100,1600]{2,1,0:T(8,128)(2,1)}, bf16[1,100,1600]{2,1,0:T(8,128)(2,1)S(1)}, u32[]{:S(2)}, u32[]{:S(2)}) collective-permute-start(bf16[1,100,1600]{2,1,0:T(8,128)(2,1)} %bitcast.43), channel_id=1, source_target_pairs={{0,3},{1,0},{2,1},{3,2},{4,7},{5,4},{6,5},{7,6},{8,11},{9,8},{10,9... | collective-permute-start | bytes 960008 | tf_op jit(solution)/shard_map/ppermute | solution.py:25
  11.5 7.6 %collective-permute-start.2 = (bf16[1,100,1600]{2,1,0:T(8,128)(2,1)S(1)}, bf16[1,100,1600]{2,1,0:T(8,128)(2,1)S(1)}, u32[]{:S(2)}, u32[]{:S(2)}) collective-permute-start(bf16[1,100,1600]{2,1,0:T(8,128)(2,1)S(1)} %collective-permute-done), channel_id=1, source_target_pairs={{0,1},{1,2},{2,3},{3,0},{4,5},{5,6},{6,7},{7,4},{8,9},{9,10},{10,1... | collective-permute-start | bytes 960008 | tf_op jit(solution)/shard_map/ppermute | solution.py:25
  11.5 27.2 %collective-permute-start.7 = (bf16[1600,512]{1,0:T(8,128)(2,1)}, bf16[1600,512]{1,0:T(8,128)(2,1)S(1)}, u32[]{:S(2)}, u32[]{:S(2)}) collective-permute-start(bf16[1600,512]{1,0:T(8,128)(2,1)} %own_ref.1), channel_id=1, source_target_pairs={{0,64},{32,224},{64,128},{96,32},{128,192},{160,96},{192,0},{224,1... | collective-permute-start | bytes 4915208 | tf_op jit(solution)/shard_map/ppermute | solution.py:14
  20.3 19.7 %collective-permute-start.3 = (bf16[4,104,1600]{2,1,0:T(8,128)(2,1)S(1)}, bf16[4,104,1600]{2,1,0:T(8,128)(2,1)}, u32[]{:S(2)}, u32[]{:S(2)}) collective-permute-start(bf16[4,104,1600]{2,1,0:T(8,128)(2,1)S(1)} %fusion.12), channel_id=1, source_target_pairs={{0,4},{1,5},{2,6},{3,7},{4,8},{5,9},{6,10},{7,11},{8,12},{9,13},{1... | collective-permute-start | bytes 3993608 | tf_op jit(solution)/shard_map/ppermute | solution.py:25
  21.4 18.6 %collective-permute-start.5 = (bf16[4,104,1600]{2,1,0:T(8,128)(2,1)S(1)}, bf16[4,104,1600]{2,1,0:T(8,128)(2,1)}, u32[]{:S(2)}, u32[]{:S(2)}) collective-permute-start(bf16[4,104,1600]{2,1,0:T(8,128)(2,1)S(1)} %fusion.12), channel_id=1, source_target_pairs={{0,28},{1,29},{2,30},{3,31},{4,0},{5,1},{6,2},{7,3},{8,4},{9,5},{1... | collective-permute-start | bytes 3993608 | tf_op jit(solution)/shard_map/ppermute | solution.py:25
  23.2 12.2 %collective-permute-start.8 = (bf16[1,100,1600]{2,1,0:T(8,128)(2,1)S(1)}, bf16[1,100,1600]{2,1,0:T(8,128)(2,1)S(1)}, u32[]{:S(2)}, u32[]{:S(2)}) collective-permute-start(bf16[1,100,1600]{2,1,0:T(8,128)(2,1)S(1)} %collective-permute-done.1), channel_id=1, source_target_pairs={{32,60},{33,61},{34,62},{35,63},{36,32},{37,33},{38,34},{39,35},{4... | collective-permute-start | bytes 960008 | tf_op jit(solution)/shard_map/ppermute | solution.py:25
  25.4 13.4 %collective-permute-start.9 = (bf16[1,100,1600]{2,1,0:T(8,128)(2,1)S(1)}, bf16[1,100,1600]{2,1,0:T(8,128)(2,1)S(1)}, u32[]{:S(2)}, u32[]{:S(2)}) collective-permute-start(bf16[1,100,1600]{2,1,0:T(8,128)(2,1)S(1)} %collective-permute-done.2), channel_id=1, source_target_pairs={{32,36},{33,37},{34,38},{35,39},{36,40},{37,41},{38,42},{39,43},{4... | collective-permute-start | bytes 960008 | tf_op jit(solution)/shard_map/ppermute | solution.py:25
  38.8 1.2 %copy-start.1 = (bf16[1600,512]{1,0:T(8,128)(2,1)}, bf16[1600,512]{1,0:T(8,128)(2,1)S(1)}, u32[]{:S(2)}) copy-start(bf16[1600,512]{1,0:T(8,128)(2,1)S(1)} %collective-permute-done.7.near_ref) | copy-start | bytes 4915204
  38.8 23.5 %collective-permute-start.10 = (bf16[1600,512]{1,0:T(8,128)(2,1)}, bf16[1600,512]{1,0:T(8,128)(2,1)}, u32[]{:S(2)}, u32[]{:S(2)}) collective-permute-start(bf16[1600,512]{1,0:T(8,128)(2,1)} %own_ref.1), channel_id=1, source_target_pairs={{0,192},{32,96},{64,0},{96,160},{128,64},{160,224},{192,128},{224,... | collective-permute-start | bytes 4915208 | tf_op jit(solution)/shard_map/ppermute | solution.py:14
  40.0 22.3 %collective-permute-start.4 = (bf16[4,104,1600]{2,1,0:T(8,128)(2,1)}, bf16[4,104,1600]{2,1,0:T(8,128)(2,1)S(1)}, u32[]{:S(2)}, u32[]{:S(2)}) collective-permute-start(bf16[4,104,1600]{2,1,0:T(8,128)(2,1)} %collective-permute-done.3), channel_id=1, source_target_pairs={{0,4},{1,5},{2,6},{3,7},{4,8},{5,9},{6,10},{7,11},{8,12},{9,13},{1... | collective-permute-start | bytes 3993608 | tf_op jit(solution)/shard_map/ppermute | solution.py:25
  40.0 22.3 %collective-permute-start.6 = (bf16[4,104,1600]{2,1,0:T(8,128)(2,1)}, bf16[4,104,1600]{2,1,0:T(8,128)(2,1)}, u32[]{:S(2)}, u32[]{:S(2)}) collective-permute-start(bf16[4,104,1600]{2,1,0:T(8,128)(2,1)} %collective-permute-done.5), channel_id=1, source_target_pairs={{0,28},{1,29},{2,30},{3,31},{4,0},{5,1},{6,2},{7,3},{8,4},{9,5},{1... | collective-permute-start | bytes 3993608 | tf_op jit(solution)/shard_map/ppermute | solution.py:25
  41.8 8.4 %collective-permute-start.11 = (bf16[1,100,1600]{2,1,0:T(8,128)(2,1)S(1)}, bf16[1,100,1600]{2,1,0:T(8,128)(2,1)}, u32[]{:S(2)}, u32[]{:S(2)}) collective-permute-start(bf16[1,100,1600]{2,1,0:T(8,128)(2,1)S(1)} %collective-permute-done.8), channel_id=1, source_target_pairs={{32,60},{33,61},{34,62},{35,63},{36,32},{37,33},{38,34},{39,35},{4... | collective-permute-start | bytes 960008 | tf_op jit(solution)/shard_map/ppermute | solution.py:25
  43.7 12.2 %collective-permute-start.12 = (bf16[1,100,1600]{2,1,0:T(8,128)(2,1)S(1)}, bf16[1,100,1600]{2,1,0:T(8,128)(2,1)}, u32[]{:S(2)}, u32[]{:S(2)}) collective-permute-start(bf16[1,100,1600]{2,1,0:T(8,128)(2,1)S(1)} %collective-permute-done.9), channel_id=1, source_target_pairs={{32,36},{33,37},{34,38},{35,39},{36,40},{37,41},{38,42},{39,43},{4... | collective-permute-start | bytes 960008 | tf_op jit(solution)/shard_map/ppermute | solution.py:25
  50.2 15.2 %collective-permute-start.16 = (bf16[4,104,1600]{2,1,0:T(8,128)(2,1)S(1)}, bf16[4,104,1600]{2,1,0:T(8,128)(2,1)S(1)}, u32[]{:S(2)}, u32[]{:S(2)}) collective-permute-start(bf16[4,104,1600]{2,1,0:T(8,128)(2,1)S(1)} %fusion.12), channel_id=1, source_target_pairs={{0,32},{32,0},{1,33},{33,1},{2,34},{34,2},{3,35},{35,3},{4,36},{36... | collective-permute-start | bytes 3993608 | tf_op jit(solution)/shard_map/ppermute | solution.py:29
  56.0 20.7 %collective-permute-start.15 = (bf16[1600,512]{1,0:T(8,128)(2,1)}, bf16[1600,512]{1,0:T(8,128)(2,1)S(1)}, u32[]{:S(2)}, u32[]{:S(2)}) collective-permute-start(bf16[1600,512]{1,0:T(8,128)(2,1)} %copy-done.1), channel_id=1, source_target_pairs={{0,64},{32,224},{64,128},{96,32},{128,192},{160,96},{192,0},{224,1... | collective-permute-start | bytes 4915208 | tf_op jit(solution)/shard_map/ppermute | solution.py:14
  59.5 19.0 %copy-start.2 = (bf16[1600,512]{1,0:T(8,128)(2,1)S(1)}, bf16[1600,512]{1,0:T(8,128)(2,1)}, u32[]{:S(2)}) copy-start(bf16[1600,512]{1,0:T(8,128)(2,1)} %copy-done.1) | copy-start | bytes 4915204
  62.3 11.2 %collective-permute-start.17 = (bf16[4,104,1600]{2,1,0:T(8,128)(2,1)}, bf16[4,104,1600]{2,1,0:T(8,128)(2,1)S(1)}, u32[]{:S(2)}, u32[]{:S(2)}) collective-permute-start(bf16[4,104,1600]{2,1,0:T(8,128)(2,1)} %collective-permute-done.3), channel_id=1, source_target_pairs={{0,32},{32,0},{1,33},{33,1},{2,34},{34,2},{3,35},{35,3},{4,36},{36... | collective-permute-start | bytes 3993608 | tf_op jit(solution)/shard_map/ppermute | solution.py:29
  62.7 22.6 %collective-permute-start.13 = (bf16[4,104,1600]{2,1,0:T(8,128)(2,1)S(1)}, bf16[4,104,1600]{2,1,0:T(8,128)(2,1)S(1)}, u32[]{:S(2)}, u32[]{:S(2)}) collective-permute-start(bf16[4,104,1600]{2,1,0:T(8,128)(2,1)S(1)} %get-tuple-element.56), channel_id=1, source_target_pairs={{0,4},{1,5},{2,6},{3,7},{4,8},{5,9},{6,10},{7,11},{8,12},{9,13},{1... | collective-permute-start | bytes 3993608 | tf_op jit(solution)/shard_map/ppermute | solution.py:25
  63.5 21.8 %collective-permute-start.14 = (bf16[4,104,1600]{2,1,0:T(8,128)(2,1)S(1)}, bf16[4,104,1600]{2,1,0:T(8,128)(2,1)S(1)}, u32[]{:S(2)}, u32[]{:S(2)}) collective-permute-start(bf16[4,104,1600]{2,1,0:T(8,128)(2,1)S(1)} %get-tuple-element.55), channel_id=1, source_target_pairs={{0,28},{1,29},{2,30},{3,31},{4,0},{5,1},{6,2},{7,3},{8,4},{9,5},{1... | collective-permute-start | bytes 3993608 | tf_op jit(solution)/shard_map/ppermute | solution.py:25
  65.5 24.8 %collective-permute-start.20 = (bf16[4,104,1600]{2,1,0:T(8,128)(2,1)}, bf16[4,104,1600]{2,1,0:T(8,128)(2,1)S(1)}, u32[]{:S(2)}, u32[]{:S(2)}) collective-permute-start(bf16[4,104,1600]{2,1,0:T(8,128)(2,1)} %collective-permute-done.5), channel_id=1, source_target_pairs={{0,32},{32,0},{1,33},{33,1},{2,34},{34,2},{3,35},{35,3},{4,36},{36... | collective-permute-start | bytes 3993608 | tf_op jit(solution)/shard_map/ppermute | solution.py:29
  73.5 19.4 %collective-permute-start.22 = (bf16[4,104,1600]{2,1,0:T(8,128)(2,1)S(1)}, bf16[4,104,1600]{2,1,0:T(8,128)(2,1)S(1)}, u32[]{:S(2)}, u32[]{:S(2)}) collective-permute-start(bf16[4,104,1600]{2,1,0:T(8,128)(2,1)S(1)} %get-tuple-element.55), channel_id=1, source_target_pairs={{0,32},{32,0},{1,33},{33,1},{2,34},{34,2},{3,35},{35,3},{4,36},{36... | collective-permute-start | bytes 3993608 | tf_op jit(solution)/shard_map/ppermute | solution.py:29
  76.7 16.9 %collective-permute-start.21 = (bf16[4,104,1600]{2,1,0:T(8,128)(2,1)S(1)}, bf16[4,104,1600]{2,1,0:T(8,128)(2,1)S(1)}, u32[]{:S(2)}, u32[]{:S(2)}) collective-permute-start(bf16[4,104,1600]{2,1,0:T(8,128)(2,1)S(1)} %collective-permute-done.4), channel_id=1, source_target_pairs={{0,32},{32,0},{1,33},{33,1},{2,34},{34,2},{3,35},{35,3},{4,36},{36... | collective-permute-start | bytes 3993608 | tf_op jit(solution)/shard_map/ppermute | solution.py:29
  85.4 18.1 %collective-permute-start.25 = (bf16[4,104,1600]{2,1,0:T(8,128)(2,1)S(1)}, bf16[4,104,1600]{2,1,0:T(8,128)(2,1)S(1)}, u32[]{:S(2)}, u32[]{:S(2)}) collective-permute-start(bf16[4,104,1600]{2,1,0:T(8,128)(2,1)S(1)} %collective-permute-done.14), channel_id=1, source_target_pairs={{0,32},{32,0},{1,33},{33,1},{2,34},{34,2},{3,35},{35,3},{4,36},{36... | collective-permute-start | bytes 3993608 | tf_op jit(solution)/shard_map/ppermute | solution.py:29
  90.1 12.2 %collective-permute-start.18 = (bf16[2,104,1600]{2,1,0:T(8,128)(2,1)S(1)}, bf16[2,104,1600]{2,1,0:T(8,128)(2,1)S(1)}, u32[]{:S(2)}, u32[]{:S(2)}) collective-permute-start(bf16[2,104,1600]{2,1,0:T(8,128)(2,1)S(1)} %get-tuple-element.54), channel_id=1, source_target_pairs={{0,4},{1,5},{2,6},{3,7},{4,8},{5,9},{6,10},{7,11},{8,12},{9,13},{1... | collective-permute-start | bytes 1996808 | tf_op jit(solution)/shard_map/ppermute | solution.py:25
  90.2 12.2 %collective-permute-start.19 = (bf16[2,104,1600]{2,1,0:T(8,128)(2,1)S(1)}, bf16[2,104,1600]{2,1,0:T(8,128)(2,1)S(1)}, u32[]{:S(2)}, u32[]{:S(2)}) collective-permute-start(bf16[2,104,1600]{2,1,0:T(8,128)(2,1)S(1)} %slice.10), channel_id=1, source_target_pairs={{0,28},{1,29},{2,30},{3,31},{4,0},{5,1},{6,2},{7,3},{8,4},{9,5},{1... | collective-permute-start | bytes 1996808 | tf_op jit(solution)/shard_map/ppermute | solution.py:25
  92.9 10.6 %collective-permute-start.23 = (bf16[2,104,1600]{2,1,0:T(8,128)(2,1)S(1)}, bf16[2,104,1600]{2,1,0:T(8,128)(2,1)S(1)}, u32[]{:S(2)}, u32[]{:S(2)}) collective-permute-start(bf16[2,104,1600]{2,1,0:T(8,128)(2,1)S(1)} %get-tuple-element.54), channel_id=1, source_target_pairs={{0,32},{32,0},{1,33},{33,1},{2,34},{34,2},{3,35},{35,3},{4,36},{36... | collective-permute-start | bytes 1996808 | tf_op jit(solution)/shard_map/ppermute | solution.py:29
  93.6 9.9 %collective-permute-start.24 = (bf16[2,104,1600]{2,1,0:T(8,128)(2,1)S(1)}, bf16[2,104,1600]{2,1,0:T(8,128)(2,1)S(1)}, u32[]{:S(2)}, u32[]{:S(2)}) collective-permute-start(bf16[2,104,1600]{2,1,0:T(8,128)(2,1)S(1)} %get-tuple-element.53), channel_id=1, source_target_pairs={{0,32},{32,0},{1,33},{33,1},{2,34},{34,2},{3,35},{35,3},{4,36},{36... | collective-permute-start | bytes 1996808 | tf_op jit(solution)/shard_map/ppermute | solution.py:29
  93.6 9.9 %copy-start = (f32[512,1600]{0,1:T(8,128)S(1)}, f32[512,1600]{0,1:T(8,128)}, u32[]{:S(2)}) copy-start(f32[512,1600]{0,1:T(8,128)} %param.3) | copy-start | bytes 9830404
  102.4 5.8 %collective-permute-start.26 = (bf16[2,104,1600]{2,1,0:T(8,128)(2,1)S(1)}, bf16[2,104,1600]{2,1,0:T(8,128)(2,1)S(1)}, u32[]{:S(2)}, u32[]{:S(2)}) collective-permute-start(bf16[2,104,1600]{2,1,0:T(8,128)(2,1)S(1)} %collective-permute-done.18), channel_id=1, source_target_pairs={{0,32},{32,0},{1,33},{33,1},{2,34},{34,2},{3,35},{35,3},{4,36},{36... | collective-permute-start | bytes 1996808 | tf_op jit(solution)/shard_map/ppermute | solution.py:29
  103.5 4.7 %collective-permute-start.27 = (bf16[2,104,1600]{2,1,0:T(8,128)(2,1)S(1)}, bf16[2,104,1600]{2,1,0:T(8,128)(2,1)S(1)}, u32[]{:S(2)}, u32[]{:S(2)}) collective-permute-start(bf16[2,104,1600]{2,1,0:T(8,128)(2,1)S(1)} %collective-permute-done.19), channel_id=1, source_target_pairs={{0,32},{32,0},{1,33},{33,1},{2,34},{34,2},{3,35},{35,3},{4,36},{36... | collective-permute-start | bytes 1996808 | tf_op jit(solution)/shard_map/ppermute | solution.py:29
